TPU v7x, 32 devices: a whole 2x2x4 slice. The times are simulated.
32 devices in a mesh: leaf: 8 (over y, x, core), sub: 4 (over z).
Axes of the slice: x: 2, y: 2, z: 4, core: 2. Of those that a mesh axis runs over, the one named last changes fastest.
Arguments:
- charges: bfloat16 [32, 524288], P(None, ('leaf', 'sub')), may hold values from -0.59765625 to 0.59765625
- points: float32 [3, 524288], P(None, ('leaf', 'sub')), as said below
- basis: bfloat16 [4096, 64, 128], P(('leaf', 'sub')), may hold values from -0.5 to 0.5
- transfer: float32 [2, 64, 64], replicated, may hold values from -0.625 to 0.625
- near_list: int32 [4096, 8], P(('leaf', 'sub')), may hold values from -1 to 4095, as said below
- coupling_list: int32 [4096, 8], P(('leaf', 'sub')), may hold values from -1 to 4095, as said below
Outputs:
- potential: float32 [32, 524288], P(None, ('leaf', 'sub'))
Inputs may be any that keep to these rules, and one draw needn't show every extreme that they name: `near_list`: every live slot of row i holds a leaf j with |j - i| <= 64 whose unit box touches the box of leaf i (the box corners differ by at most 1 in every coordinate); slot 0 holds i itself, slot 1 the leaf whose index differs from i in the lowest bit, slot 2 the leaf i - 4 (i + 4 where i < 4), slot 3 the leaf i + 4 (i - 4 where i + 4 >= 4096); other slots may repeat leaves; empty slots hold -1 and come after the live ones; at least four slots of every row are live, and how many are live varies from device to device. `coupling_list`: every live slot of row i holds a leaf j with 1 <= |j - i| <= 64 whose unit box does not touch the box of leaf i (the box corners differ by 2 or more in some coordinate); slot 1 holds a leaf exactly 64 away from i; other slots may repeat leaves; empty slots hold -1 and come after the live ones; at least two slots of every row are live, and how many are live varies from device to device. The points of leaf c lie in the unit box whose lower corner is (c % 2, (c // 2) % 2, c // 4).
All inputs are finite; a program needn't handle non-finite values.
Results may differ from a plain program's by a relative error of at most 0.00065.
The roundings to bfloat16 on the way count: a program that leaves them out, or rounds other values in their place, can miss the bound.
Values may be sent and summed in bfloat16 or wider, within the bound.
No kernel may reach another device: no remote copies, remote signals or barrier semaphores. Data moves between devices by JAX's collectives and lax.ppermute only.
A program may use at most 128 MiB of HBM per device.

v0:
```python
import math

import jax
import jax.numpy as jnp
from jax import lax
from jax.sharding import PartitionSpec as P

P_SIZE = 128
K = 64
R = 32
LD = 128


LENGTH_SCALE = 2.0
NUGGET_VARIANCE = 1.0
HIGHEST = lax.Precision.HIGHEST


def padded(block, sides, width):
    for axis, dim in sides:
        count = lax.axis_size(axis)
        forward = [(i, i + 1) for i in range(count - 1)]
        backward = [(target, source) for source, target in forward]
        low = lax.ppermute(
            lax.slice_in_dim(block, block.shape[dim] - width, None, axis=dim), axis, forward
        )
        high = lax.ppermute(lax.slice_in_dim(block, 0, width, axis=dim), axis, backward)
        block = jnp.concatenate([low, block, high], axis=dim)
    return block


def partner(value, axis, stride):
    mask = 2**stride
    pairs = [(source, source ^ mask) for source in range(lax.axis_size(axis))]
    return lax.ppermute(value, axis, pairs)


def unit_nodes():
    index_row = jnp.arange(64, dtype=jnp.int32)

    def axis_value(digit):
        return jnp.cos((2.0 * digit.astype(jnp.float32) + 1.0) * (math.pi / 8.0))

    return jnp.stack(
        [axis_value(index_row // 16), axis_value(index_row // 4 % 4), axis_value(index_row % 4)]
    )


def covariance(first, second):
    separation = first[..., :, None] - second[..., None, :]
    return jnp.exp(-jnp.sqrt(jnp.sum(separation * separation, axis=0)) / LENGTH_SCALE)


def cluster_nodes(centers, radii, reference_nodes):
    extra = (1,) * (centers.ndim - 1)
    shaped = reference_nodes.reshape((3,) + extra + (reference_nodes.shape[1],))
    return centers[..., None] + radii[None, ..., None] * shaped


def leaf_shapes(leaf_points):
    centers = jnp.mean(leaf_points, axis=2)
    offsets = leaf_points - centers[:, :, None]
    radii = jnp.max(jnp.sqrt(jnp.sum(offsets * offsets, axis=0)), axis=1)
    return (centers, radii)


def merge_shapes(centers, radii):
    paired = centers.reshape(3, -1, 2)
    spread = radii.reshape(-1, 2)
    separation = paired[:, :, 0] - paired[:, :, 1]
    joined = 0.5 * (paired[:, :, 0] + paired[:, :, 1])
    return (
        joined,
        jnp.maximum(spread[:, 0], spread[:, 1])
        + 0.5 * jnp.sqrt(jnp.sum(separation * separation, axis=0)),
    )


def merge_coefficients(coefficient, transfer):
    paired = coefficient.reshape(coefficient.shape[0], -1, 2, coefficient.shape[2])
    return jnp.einsum("rcsk,skj->rcj", paired, transfer, precision=HIGHEST)


def descend(downward, transfer):
    spread = jnp.einsum("rcj,skj->rcsk", downward, transfer, precision=HIGHEST)
    return spread.reshape(downward.shape[0], -1, downward.shape[2])


def sibling_coupling(coefficient, centers, radii, reference_nodes):
    nodes = cluster_nodes(centers, radii, reference_nodes)
    paired = nodes.reshape(3, -1, 2, nodes.shape[2])
    kernel_tile = covariance(paired[:, :, 0], paired[:, :, 1])
    coef_pairs = coefficient.reshape(coefficient.shape[0], -1, 2, coefficient.shape[2])
    to_left = jnp.einsum("rcq,cpq->rcp", coef_pairs[:, :, 1], kernel_tile, precision=HIGHEST)
    to_right = jnp.einsum("rcp,cpq->rcq", coef_pairs[:, :, 0], kernel_tile, precision=HIGHEST)
    return jnp.stack([to_left, to_right], axis=2).reshape(coefficient.shape)


def listed_coupling(
    all_coef, all_centers, all_radii, own_centers, own_radii, slot_rows, reference_nodes
):
    is_live = slot_rows >= 0
    safe_rows = jnp.where(is_live, slot_rows, 0)
    own_nodes = cluster_nodes(own_centers, own_radii, reference_nodes)
    far_nodes = cluster_nodes(
        jnp.take(all_centers, safe_rows, axis=1),
        jnp.take(all_radii, safe_rows, axis=0),
        reference_nodes,
    )
    kernel_tile = (
        covariance(own_nodes[:, :, None, :], far_nodes)
        * is_live.astype(jnp.float32)[:, :, None, None]
    )
    far_coef = jnp.take(all_coef, safe_rows, axis=1)
    return jnp.einsum("wspq,rwsq->rwp", kernel_tile, far_coef, precision=HIGHEST)


def near_tile(all_x, all_points, own_x, own_points, slot_rows):
    is_live = slot_rows >= 0
    safe_rows = jnp.where(is_live, slot_rows, 0)
    far_points = jnp.take(all_points, safe_rows, axis=1)
    kernel_tile = (
        covariance(own_points[:, :, None, :], far_points)
        * is_live.astype(jnp.float32)[:, :, None, None]
    ).astype(jnp.bfloat16)
    far_x = jnp.take(all_x, safe_rows, axis=1)
    summed = jnp.einsum("wspq,rwsq->rwp", kernel_tile, far_x, preferred_element_type=jnp.float32)
    return summed + NUGGET_VARIANCE * own_x.astype(jnp.float32)


def blocked(function, total_rows, block_size):
    starts = jnp.arange(total_rows // block_size, dtype=jnp.int32) * block_size
    pieces = lax.map(function, starts)
    return jnp.moveaxis(pieces, 0, 1).reshape(pieces.shape[1], total_rows, pieces.shape[3])


def pick_column(values, position):
    columns = jnp.arange(values.shape[-1], dtype=jnp.int32)
    return jnp.sum(jnp.where(columns == position, values, 0.0), axis=-1)


def per_device(charges, points, basis, transfer, near_list, coupling_list):
    reference_nodes = unit_nodes()
    device = lax.axis_index(("leaf", "sub"))
    devices_count = lax.axis_size(("leaf", "sub"))
    tree_depth = devices_count.bit_length() - 1
    margin = LD
    wide_x = padded(charges, ((("leaf", "sub"), 1),), margin * P_SIZE)
    wide_points = padded(points, ((("leaf", "sub"), 1),), margin * P_SIZE)
    leaf_x = charges.reshape(R, LD, P_SIZE)
    leaf_points = points.reshape(3, LD, P_SIZE)
    ext_x = wide_x.reshape(R, LD + 2 * margin, P_SIZE)
    ext_points = wide_points.reshape(3, LD + 2 * margin, P_SIZE)
    first_leaf = device * LD - margin
    local_near = jnp.where(near_list >= 0, near_list - first_leaf, -1)
    local_coupling = jnp.where(coupling_list >= 0, coupling_list - first_leaf, -1)
    block_size = min(16, LD)

    def near_block(start_leaf):
        return near_tile(
            ext_x,
            ext_points,
            lax.dynamic_slice_in_dim(leaf_x, start_leaf, block_size, 1),
            lax.dynamic_slice_in_dim(leaf_points, start_leaf, block_size, 1),
            lax.dynamic_slice_in_dim(local_near, start_leaf, block_size, 0),
        )

    near = blocked(near_block, LD, block_size)
    coefficient = jnp.einsum("rcp,ckp->rck", leaf_x, basis, preferred_element_type=jnp.float32)
    centers, radii = leaf_shapes(leaf_points)
    wide_coef = padded(coefficient, ((("leaf", "sub"), 1),), margin)
    ext_centers, ext_radii = leaf_shapes(ext_points)

    def couple_block(start_leaf):
        return listed_coupling(
            wide_coef,
            ext_centers,
            ext_radii,
            lax.dynamic_slice_in_dim(centers, start_leaf, block_size, 1),
            lax.dynamic_slice_in_dim(radii, start_leaf, block_size, 0),
            lax.dynamic_slice_in_dim(local_coupling, start_leaf, block_size, 0),
            reference_nodes,
        )

    leaf_couple = blocked(couple_block, LD, block_size)
    levels = [(coefficient, centers, radii)]
    while levels[-1][0].shape[1] > 1:
        last_coef, last_centers, last_radii = levels[-1]
        joined_centers, joined_radii = merge_shapes(last_centers, last_radii)
        levels.append((merge_coefficients(last_coef, transfer), joined_centers, joined_radii))
    root_coef = levels[-1][0][:, 0, :]
    root_centers, root_radii = (
        lax.all_gather(levels[-1][1], ("leaf", "sub"), axis=1, tiled=True),
        lax.all_gather(levels[-1][2], ("leaf", "sub"), axis=0, tiled=True),
    )
    top_shapes = [(root_centers, root_radii)]
    for level_index in range(tree_depth - 1):
        top_shapes.append(merge_shapes(top_shapes[-1][0], top_shapes[-1][1]))
    own_coef = root_coef
    couplings = []
    side_bits = []
    for level_index in range(tree_depth):
        sibling_coef = partner(own_coef, ("leaf", "sub"), level_index)
        node_index = jnp.right_shift(device, level_index)
        side_bit = node_index % 2
        level_centers, level_radii = top_shapes[level_index]
        own_nodes = cluster_nodes(
            pick_column(level_centers, node_index),
            pick_column(level_radii, node_index),
            reference_nodes,
        )
        far_nodes = cluster_nodes(
            pick_column(level_centers, node_index ^ 1),
            pick_column(level_radii, node_index ^ 1),
            reference_nodes,
        )
        kernel_tile = covariance(own_nodes, far_nodes)
        couplings.append(jnp.einsum("rq,pq->rp", sibling_coef, kernel_tile, precision=HIGHEST))
        side_bits.append(side_bit)
        if level_index + 1 < tree_depth:
            is_left = side_bit == 0
            left_coef = jnp.where(is_left, own_coef, sibling_coef)
            right_coef = jnp.where(is_left, sibling_coef, own_coef)
            own_coef = jnp.einsum(
                "rsk,skj->rj",
                jnp.stack([left_coef, right_coef], axis=1),
                transfer,
                precision=HIGHEST,
            )
    root_down = jnp.zeros((R, K), jnp.float32)
    for level_index in reversed(range(tree_depth)):
        chosen = jnp.where(side_bits[level_index] == 0, transfer[0], transfer[1])
        root_down = couplings[level_index] + jnp.einsum(
            "rj,kj->rk", root_down, chosen, precision=HIGHEST
        )
    downward = root_down[:, None, :]
    for level_index in range(len(levels) - 2, 0, -1):
        level_coef, level_centers, level_radii = levels[level_index]
        downward = descend(downward, transfer) + sibling_coupling(
            level_coef, level_centers, level_radii, reference_nodes
        )
    downward = descend(downward, transfer) + leaf_couple
    far = jnp.einsum(
        "rck,ckp->rcp", downward.astype(jnp.bfloat16), basis, preferred_element_type=jnp.float32
    )
    return (near + far).reshape(R, LD * P_SIZE)


def solution(mesh):
    in_specs = (
        P(None, ("leaf", "sub")),
        P(None, ("leaf", "sub")),
        P(("leaf", "sub"), None, None),
        P(),
        P(("leaf", "sub"), None),
        P(("leaf", "sub"), None),
    )
    out_specs = P(None, ("leaf", "sub"))
    return jax.shard_map(
        per_device, mesh=mesh, in_specs=in_specs, out_specs=out_specs, check_vma=False
    )
```

profile of v0, /device:TPU:4, one launch (start us, length us, event | category | flops | bytes accessed | tf_op | source)
XLA Modules:
  0.0 656.7 jit_solution(1692249100180969397)
XLA Ops:
  3.6 5.7 collective-permute-start.3
  18.7 7.2 %collective-permute-start.10 = (f32[32,128,64]{1,2,0:T(8,128)}, f32[32,128,64]{1,2,0:T(8,128)}, u32[]{:S(2)}, u32[]{:S(2)}) collective-permute-start(f32[32,128,64]{1,2,0:T(8,128)} %copy.236), channel_id=1, source_target_pairs={{1,0},{2,1},{3,2},{4,3},{5,4},{6,5},{7,6},{8,7},{9,8},{10,9},{11,1... | collective-permute-start | bytes 3145736 | tf_op jit(solution)/shard_map/ppermute | solution.py:27
  49.1 41.2 %all-reduce = f32[32]{0:T(128)} all-reduce(f32[32]{0:T(128)} %fusion.175), channel_id=1, replica_groups=mesh['leaf'=8,'sub'=4] {'leaf','sub'}, use_global_device_ids=true, to_apply=%add | all-reduce | flops 32 | bytes 256
  100.2 65.2 %all-gather = f32[3,32,1]{0,2,1:T(1,128)S(1)} all-gather(f32[3,1,1]{0,2,1:T(1,128)} %get-tuple-element.280), channel_id=2, replica_groups=mesh['leaf'=8,'sub'=4] {'leaf','sub'}, dimensions={1}, use_global_device_ids=true | all-gather | bytes 396 | tf_op jit(solution)/shard_map/all_gather | solution.py:193
  270.4 6.7 %collective-permute-start.1 = (bf16[32,16384]{1,0:T(8,128)(2,1)S(1)}, bf16[32,16384]{1,0:T(8,128)(2,1)}, u32[]{:S(2)}, u32[]{:S(2)}) collective-permute-start(bf16[32,16384]{1,0:T(8,128)(2,1)S(1)} %copy-done.2), channel_id=1, source_target_pairs={{1,0},{2,1},{3,2},{4,3},{5,4},{6,5},{7,6},{8,7},{9,8},{10,9},{11,1... | collective-permute-start | bytes 3145736 | tf_op jit(solution)/shard_map/ppermute | solution.py:27
  292.7 6.3 pad_maximum_fusion
  299.0 182.6 %while.21 = (s32[]{:T(128)}, f32[8,32,16,64]{3,1,2,0:T(8,128)}, s32[8]{0:T(128)S(1)}, s32[128,8]{0,1:T(8,128)S(1)}, f32[32,384,64]{2,0,1:T(8,128)}, /*index=5*/f...) while((s32[]{:T(128)}, f32[8,32,16,64]{3,1,2,0:T(8,128)}, ...), condition=%wide.region_53.54_spmd, body=%wide.region_51.53_spmd.sunk | while | flops 207414656 | bytes 10999095 | solution.py:133
  313.2 8.9 %fusion.248 = f32[8,32,16,64]{3,1,2,0:T(8,128)} fusion(f32[8,32,16,64]{3,1,2,0:T(8,128)} %get-tuple-element.431, s32[]{:T(128)} %get-tuple-element.430, f32[16,8,64,64]{3,2,1,0:T(8,128)} %multiply_reduce_fusion.31, f32[16,8]{1,0:T(8,128)S(1)} %compare_convert_fusion.5, f32[16,8,32,64]{3,2,1,0:T(8,128)} %bitcast.450, ...), kind=kOutput, calls=%fused_computation.38.clone.1 | convolution fusion | flops 203161600 | bytes 6554752 | tf_op jit(solution)/shard_map/while/body/eval_jaxpr/wspq,rwsq->rwp/dot_general | solution.py:115
  336.0 8.9 %fusion.248 = f32[8,32,16,64]{3,1,2,0:T(8,128)} fusion(f32[8,32,16,64]{3,1,2,0:T(8,128)} %get-tuple-element.431, s32[]{:T(128)} %get-tuple-element.430, f32[16,8,64,64]{3,2,1,0:T(8,128)} %multiply_reduce_fusion.31, f32[16,8]{1,0:T(8,128)S(1)} %compare_convert_fusion.5, f32[16,8,32,64]{3,2,1,0:T(8,128)} %bitcast.450, ...), kind=kOutput, calls=%fused_computation.38.clone.1 | convolution fusion | flops 203161600 | bytes 6554752 | tf_op jit(solution)/shard_map/while/body/eval_jaxpr/wspq,rwsq->rwp/dot_general | solution.py:115
  358.8 8.9 %fusion.248 = f32[8,32,16,64]{3,1,2,0:T(8,128)} fusion(f32[8,32,16,64]{3,1,2,0:T(8,128)} %get-tuple-element.431, s32[]{:T(128)} %get-tuple-element.430, f32[16,8,64,64]{3,2,1,0:T(8,128)} %multiply_reduce_fusion.31, f32[16,8]{1,0:T(8,128)S(1)} %compare_convert_fusion.5, f32[16,8,32,64]{3,2,1,0:T(8,128)} %bitcast.450, ...), kind=kOutput, calls=%fused_computation.38.clone.1 | convolution fusion | flops 203161600 | bytes 6554752 | tf_op jit(solution)/shard_map/while/body/eval_jaxpr/wspq,rwsq->rwp/dot_general | solution.py:115
  381.6 8.9 %fusion.248 = f32[8,32,16,64]{3,1,2,0:T(8,128)} fusion(f32[8,32,16,64]{3,1,2,0:T(8,128)} %get-tuple-element.431, s32[]{:T(128)} %get-tuple-element.430, f32[16,8,64,64]{3,2,1,0:T(8,128)} %multiply_reduce_fusion.31, f32[16,8]{1,0:T(8,128)S(1)} %compare_convert_fusion.5, f32[16,8,32,64]{3,2,1,0:T(8,128)} %bitcast.450, ...), kind=kOutput, calls=%fused_computation.38.clone.1 | convolution fusion | flops 203161600 | bytes 6554752 | tf_op jit(solution)/shard_map/while/body/eval_jaxpr/wspq,rwsq->rwp/dot_general | solution.py:115
  404.4 8.9 %fusion.248 = f32[8,32,16,64]{3,1,2,0:T(8,128)} fusion(f32[8,32,16,64]{3,1,2,0:T(8,128)} %get-tuple-element.431, s32[]{:T(128)} %get-tuple-element.430, f32[16,8,64,64]{3,2,1,0:T(8,128)} %multiply_reduce_fusion.31, f32[16,8]{1,0:T(8,128)S(1)} %compare_convert_fusion.5, f32[16,8,32,64]{3,2,1,0:T(8,128)} %bitcast.450, ...), kind=kOutput, calls=%fused_computation.38.clone.1 | convolution fusion | flops 203161600 | bytes 6554752 | tf_op jit(solution)/shard_map/while/body/eval_jaxpr/wspq,rwsq->rwp/dot_general | solution.py:115
  427.1 8.9 %fusion.248 = f32[8,32,16,64]{3,1,2,0:T(8,128)} fusion(f32[8,32,16,64]{3,1,2,0:T(8,128)} %get-tuple-element.431, s32[]{:T(128)} %get-tuple-element.430, f32[16,8,64,64]{3,2,1,0:T(8,128)} %multiply_reduce_fusion.31, f32[16,8]{1,0:T(8,128)S(1)} %compare_convert_fusion.5, f32[16,8,32,64]{3,2,1,0:T(8,128)} %bitcast.450, ...), kind=kOutput, calls=%fused_computation.38.clone.1 | convolution fusion | flops 203161600 | bytes 6554752 | tf_op jit(solution)/shard_map/while/body/eval_jaxpr/wspq,rwsq->rwp/dot_general | solution.py:115
  449.9 8.9 %fusion.248 = f32[8,32,16,64]{3,1,2,0:T(8,128)} fusion(f32[8,32,16,64]{3,1,2,0:T(8,128)} %get-tuple-element.431, s32[]{:T(128)} %get-tuple-element.430, f32[16,8,64,64]{3,2,1,0:T(8,128)} %multiply_reduce_fusion.31, f32[16,8]{1,0:T(8,128)S(1)} %compare_convert_fusion.5, f32[16,8,32,64]{3,2,1,0:T(8,128)} %bitcast.450, ...), kind=kOutput, calls=%fused_computation.38.clone.1 | convolution fusion | flops 203161600 | bytes 6554752 | tf_op jit(solution)/shard_map/while/body/eval_jaxpr/wspq,rwsq->rwp/dot_general | solution.py:115
  472.7 8.9 %fusion.248 = f32[8,32,16,64]{3,1,2,0:T(8,128)} fusion(f32[8,32,16,64]{3,1,2,0:T(8,128)} %get-tuple-element.431, s32[]{:T(128)} %get-tuple-element.430, f32[16,8,64,64]{3,2,1,0:T(8,128)} %multiply_reduce_fusion.31, f32[16,8]{1,0:T(8,128)S(1)} %compare_convert_fusion.5, f32[16,8,32,64]{3,2,1,0:T(8,128)} %bitcast.450, ...), kind=kOutput, calls=%fused_computation.38.clone.1 | convolution fusion | flops 203161600 | bytes 6554752 | tf_op jit(solution)/shard_map/while/body/eval_jaxpr/wspq,rwsq->rwp/dot_general | solution.py:115
  484.9 166.4 %while.20 = (s32[]{:T(128)}, f32[8,32,16,128]{3,1,2,0:T(8,128)}, s32[8]{0:T(128)S(1)}, s32[128,8]{0,1:T(8,128)S(1)}, bf16[32,384,128]{2,0,1:T(8,128)(2,1)}, /*in...) while((s32[]{:T(128)}, f32[8,32,16,128]{3,1,2,0:T(8,128)}, ...), condition=%wide.region_2.3_spmd, body=%wide.region_0.2_spmd.sunk | while | flops 160090880 | bytes 21778472 | solution.py:133
  499.2 6.7 %fusion.244 = f32[8,32,16,128]{3,1,2,0:T(8,128)} fusion(f32[8,32,16,128]{3,1,2,0:T(8,128)} %get-tuple-element.468, s32[]{:T(128)} %get-tuple-element.467, f32[16,8,128,128]{3,2,1,0:T(8,128)} %multiply_reduce_fusion.30, f32[16,8]{1,0:T(8,128)S(1)} %get-tuple-element.404, bf16[16,8,32,128]{3,2,1,0:T(8,128)(2,1)S(1)} %bitcast.454, ...), kind=kOutput, calls=%fused_computation.11.clone.1 | convolution fusion | flops 143261696 | bytes 9831556 | tf_op jit(solution)/shard_map/while/body/eval_jaxpr/wspq,rwsq->rwp/dot_general | solution.py:127
  520.0 6.7 %fusion.244 = f32[8,32,16,128]{3,1,2,0:T(8,128)} fusion(f32[8,32,16,128]{3,1,2,0:T(8,128)} %get-tuple-element.468, s32[]{:T(128)} %get-tuple-element.467, f32[16,8,128,128]{3,2,1,0:T(8,128)} %multiply_reduce_fusion.30, f32[16,8]{1,0:T(8,128)S(1)} %get-tuple-element.404, bf16[16,8,32,128]{3,2,1,0:T(8,128)(2,1)S(1)} %bitcast.454, ...), kind=kOutput, calls=%fused_computation.11.clone.1 | convolution fusion | flops 143261696 | bytes 9831556 | tf_op jit(solution)/shard_map/while/body/eval_jaxpr/wspq,rwsq->rwp/dot_general | solution.py:127
  540.7 6.7 %fusion.244 = f32[8,32,16,128]{3,1,2,0:T(8,128)} fusion(f32[8,32,16,128]{3,1,2,0:T(8,128)} %get-tuple-element.468, s32[]{:T(128)} %get-tuple-element.467, f32[16,8,128,128]{3,2,1,0:T(8,128)} %multiply_reduce_fusion.30, f32[16,8]{1,0:T(8,128)S(1)} %get-tuple-element.404, bf16[16,8,32,128]{3,2,1,0:T(8,128)(2,1)S(1)} %bitcast.454, ...), kind=kOutput, calls=%fused_computation.11.clone.1 | convolution fusion | flops 143261696 | bytes 9831556 | tf_op jit(solution)/shard_map/while/body/eval_jaxpr/wspq,rwsq->rwp/dot_general | solution.py:127
  561.5 6.7 %fusion.244 = f32[8,32,16,128]{3,1,2,0:T(8,128)} fusion(f32[8,32,16,128]{3,1,2,0:T(8,128)} %get-tuple-element.468, s32[]{:T(128)} %get-tuple-element.467, f32[16,8,128,128]{3,2,1,0:T(8,128)} %multiply_reduce_fusion.30, f32[16,8]{1,0:T(8,128)S(1)} %get-tuple-element.404, bf16[16,8,32,128]{3,2,1,0:T(8,128)(2,1)S(1)} %bitcast.454, ...), kind=kOutput, calls=%fused_computation.11.clone.1 | convolution fusion | flops 143261696 | bytes 9831556 | tf_op jit(solution)/shard_map/while/body/eval_jaxpr/wspq,rwsq->rwp/dot_general | solution.py:127
  582.3 6.7 %fusion.244 = f32[8,32,16,128]{3,1,2,0:T(8,128)} fusion(f32[8,32,16,128]{3,1,2,0:T(8,128)} %get-tuple-element.468, s32[]{:T(128)} %get-tuple-element.467, f32[16,8,128,128]{3,2,1,0:T(8,128)} %multiply_reduce_fusion.30, f32[16,8]{1,0:T(8,128)S(1)} %get-tuple-element.404, bf16[16,8,32,128]{3,2,1,0:T(8,128)(2,1)S(1)} %bitcast.454, ...), kind=kOutput, calls=%fused_computation.11.clone.1 | convolution fusion | flops 143261696 | bytes 9831556 | tf_op jit(solution)/shard_map/while/body/eval_jaxpr/wspq,rwsq->rwp/dot_general | solution.py:127
  603.1 6.7 %fusion.244 = f32[8,32,16,128]{3,1,2,0:T(8,128)} fusion(f32[8,32,16,128]{3,1,2,0:T(8,128)} %get-tuple-element.468, s32[]{:T(128)} %get-tuple-element.467, f32[16,8,128,128]{3,2,1,0:T(8,128)} %multiply_reduce_fusion.30, f32[16,8]{1,0:T(8,128)S(1)} %get-tuple-element.404, bf16[16,8,32,128]{3,2,1,0:T(8,128)(2,1)S(1)} %bitcast.454, ...), kind=kOutput, calls=%fused_computation.11.clone.1 | convolution fusion | flops 143261696 | bytes 9831556 | tf_op jit(solution)/shard_map/while/body/eval_jaxpr/wspq,rwsq->rwp/dot_general | solution.py:127
  623.9 6.7 %fusion.244 = f32[8,32,16,128]{3,1,2,0:T(8,128)} fusion(f32[8,32,16,128]{3,1,2,0:T(8,128)} %get-tuple-element.468, s32[]{:T(128)} %get-tuple-element.467, f32[16,8,128,128]{3,2,1,0:T(8,128)} %multiply_reduce_fusion.30, f32[16,8]{1,0:T(8,128)S(1)} %get-tuple-element.404, bf16[16,8,32,128]{3,2,1,0:T(8,128)(2,1)S(1)} %bitcast.454, ...), kind=kOutput, calls=%fused_computation.11.clone.1 | convolution fusion | flops 143261696 | bytes 9831556 | tf_op jit(solution)/shard_map/while/body/eval_jaxpr/wspq,rwsq->rwp/dot_general | solution.py:127
  644.6 6.7 %fusion.244 = f32[8,32,16,128]{3,1,2,0:T(8,128)} fusion(f32[8,32,16,128]{3,1,2,0:T(8,128)} %get-tuple-element.468, s32[]{:T(128)} %get-tuple-element.467, f32[16,8,128,128]{3,2,1,0:T(8,128)} %multiply_reduce_fusion.30, f32[16,8]{1,0:T(8,128)S(1)} %get-tuple-element.404, bf16[16,8,32,128]{3,2,1,0:T(8,128)(2,1)S(1)} %bitcast.454, ...), kind=kOutput, calls=%fused_computation.11.clone.1 | convolution fusion | flops 143261696 | bytes 9831556 | tf_op jit(solution)/shard_map/while/body/eval_jaxpr/wspq,rwsq->rwp/dot_general | solution.py:127
  (549 shorter events, 364.8 us)
Async XLA Ops:
  0.0 25.9 %copy-start.5 = (f32[3,16384]{1,0:T(4,128)S(1)}, f32[3,16384]{1,0:T(4,128)}, u32[]{:S(2)}) copy-start(f32[3,16384]{1,0:T(4,128)} %param.11) | copy-start | bytes 589828
  0.0 270.4 %collective-permute-start.2 = (f32[3,16384]{1,0:T(4,128)}, f32[3,16384]{1,0:T(4,128)}, u32[]{:S(2)}, u32[]{:S(2)}) collective-permute-start(f32[3,16384]{1,0:T(4,128)} %param.11), channel_id=1, source_target_pairs={{0,1},{1,2},{2,3},{3,4},{4,5},{5,6},{6,7},{7,8},{8,9},{9,10},{10,1... | collective-permute-start | bytes 589832 | tf_op jit(solution)/shard_map/ppermute | solution.py:24
  3.6 273.5 %collective-permute-start.3 = (f32[3,16384]{1,0:T(4,128)}, f32[3,16384]{1,0:T(4,128)}, u32[]{:S(2)}, u32[]{:S(2)}) collective-permute-start(f32[3,16384]{1,0:T(4,128)} %param.11), channel_id=1, source_target_pairs={{1,0},{2,1},{3,2},{4,3},{5,4},{6,5},{7,6},{8,7},{9,8},{10,9},{11,1... | collective-permute-start | bytes 589832 | tf_op jit(solution)/shard_map/ppermute | solution.py:27
  13.1 22.2 %copy-start.1 = (f32[2,64,64]{2,1,0:T(8,128)S(1)}, f32[2,64,64]{2,1,0:T(8,128)}, u32[]{:S(2)}) copy-start(f32[2,64,64]{2,1,0:T(8,128)} %param.13) | copy-start | bytes 98308
  16.8 267.8 %collective-permute-start.9 = (f32[32,128,64]{1,2,0:T(8,128)}, f32[32,128,64]{1,2,0:T(8,128)}, u32[]{:S(2)}, u32[]{:S(2)}) collective-permute-start(f32[32,128,64]{1,2,0:T(8,128)} %copy.236), channel_id=1, source_target_pairs={{0,1},{1,2},{2,3},{3,4},{4,5},{5,6},{6,7},{7,8},{8,9},{9,10},{10,1... | collective-permute-start | bytes 3145736 | tf_op jit(solution)/shard_map/ppermute | solution.py:24
  18.7 270.0 %collective-permute-start.10 = (f32[32,128,64]{1,2,0:T(8,128)}, f32[32,128,64]{1,2,0:T(8,128)}, u32[]{:S(2)}, u32[]{:S(2)}) collective-permute-start(f32[32,128,64]{1,2,0:T(8,128)} %copy.236), channel_id=1, source_target_pairs={{1,0},{2,1},{3,2},{4,3},{5,4},{6,5},{7,6},{8,7},{9,8},{10,9},{11,1... | collective-permute-start | bytes 3145736 | tf_op jit(solution)/shard_map/ppermute | solution.py:27
  49.1 182.4 %collective-permute-start.4 = (f32[32,64]{1,0:T(8,128)}, f32[32,64]{1,0:T(8,128)}, u32[]{:S(2)}, u32[]{:S(2)}) collective-permute-start(f32[32,64]{1,0:T(8,128)} %convolution_bitcast_fusion.16), channel_id=1, source_target_pairs={{0,1},{1,0},{2,3},{3,2},{4,5},{5,4},{6,7},{7,6},{8,9},{9,8},{10,11... | collective-permute-start | bytes 24584 | tf_op jit(solution)/shard_map/ppermute | solution.py:35
  176.7 18.5 %copy-start.25 = (f32[3,16,2]{1,0,2:T(4,128)S(1)}, f32[3,16,2]{1,0,2:T(4,128)}, u32[]{:S(2)}) copy-start(f32[3,16,2]{1,0,2:T(4,128)} %copy.222) | copy-start | bytes 1156
  195.2 15.1 %copy-start.8 = (f32[32,32,64]{2,1,0:T(8,128)S(1)}, f32[32,32,64]{2,1,0:T(8,128)}, u32[]{:S(2)}) copy-start(f32[32,32,64]{2,1,0:T(8,128)} %get-tuple-element.233) | copy-start | bytes 786436
  200.2 16.7 %copy-start.29 = (s32[128,8]{0,1:T(8,128)S(1)}, s32[128,8]{0,1:T(8,128)}, u32[]{:S(2)}) copy-start(s32[128,8]{0,1:T(8,128)} %param.15) | copy-start | bytes 12292
  200.2 16.7 %copy-start.30 = (s32[128,8]{0,1:T(8,128)S(1)}, s32[128,8]{0,1:T(8,128)}, u32[]{:S(2)}) copy-start(s32[128,8]{0,1:T(8,128)} %param.14) | copy-start | bytes 12292
  209.2 30.7 %copy-start.14 = (f32[32,2,64,1]{2,0,3,1:T(8,128)S(1)}, f32[32,2,64,1]{2,0,3,1:T(8,128)}, u32[]{:S(2)}) copy-start(f32[32,2,64,1]{2,0,3,1:T(8,128)} %copy-done.13) | copy-start | bytes 49156
  213.4 38.4 %copy-start.2 = (bf16[32,16384]{1,0:T(8,128)(2,1)S(1)}, bf16[32,16384]{1,0:T(8,128)(2,1)}, u32[]{:S(2)}) copy-start(bf16[32,16384]{1,0:T(8,128)(2,1)} %param.10) | copy-start | bytes 3145732
  213.4 47.4 %copy-start.19 = (f32[32,2,1,64]{3,0,2,1:T(8,128)S(1)}, f32[32,2,1,64]{3,0,2,1:T(8,128)}, u32[]{:S(2)}) copy-start(f32[32,2,1,64]{3,0,2,1:T(8,128)} %convolution_bitcast_fusion.9) | copy-start | bytes 49156
  213.4 47.4 %copy-start.20 = (f32[32,2,1,64]{3,0,2,1:T(8,128)S(1)}, f32[32,2,1,64]{3,0,2,1:T(8,128)}, u32[]{:S(2)}) copy-start(f32[32,2,1,64]{3,0,2,1:T(8,128)} %convolution_bitcast_fusion.8) | copy-start | bytes 49156
  213.4 49.0 %copy-start.12 = (f32[32,8,1,64]{3,0,2,1:T(8,128)S(1)}, f32[32,8,1,64]{3,0,2,1:T(8,128)}, u32[]{:S(2)}) copy-start(f32[32,8,1,64]{3,0,2,1:T(8,128)} %convolution_bitcast_fusion.4) | copy-start | bytes 196612
  233.1 5.1 collective-permute-start.5
  239.9 1.5 collective-permute-start.6
  243.0 4.1 collective-permute-start.7
  248.0 3.8 collective-permute-start.8
  251.8 229.8 %collective-permute-start = (bf16[32,16384]{1,0:T(8,128)(2,1)S(1)}, bf16[32,16384]{1,0:T(8,128)(2,1)}, u32[]{:S(2)}, u32[]{:S(2)}) collective-permute-start(bf16[32,16384]{1,0:T(8,128)(2,1)S(1)} %copy-done.2), channel_id=1, source_target_pairs={{0,1},{1,2},{2,3},{3,4},{4,5},{5,6},{6,7},{7,8},{8,9},{9,10},{10,1... | collective-permute-start | bytes 3145736 | tf_op jit(solution)/shard_map/ppermute | solution.py:24
  266.5 10.7 %copy-start.6 = (f32[3,16384]{1,0:T(4,128)S(1)}, f32[3,16384]{1,0:T(4,128)}, u32[]{:S(2)}) copy-start(f32[3,16384]{1,0:T(4,128)} %param.11) | copy-start | bytes 589828
  267.1 14.2 %copy-start.9 = (f32[3,128,128]{2,1,0:T(8,128)S(1)}, f32[3,128,128]{2,1,0:T(8,128)}, u32[]{:S(2)}) copy-start(f32[3,128,128]{2,1,0:T(8,128)} %get-tuple-element.461) | copy-start | bytes 589828
  270.4 211.3 %collective-permute-start.1 = (bf16[32,16384]{1,0:T(8,128)(2,1)S(1)}, bf16[32,16384]{1,0:T(8,128)(2,1)}, u32[]{:S(2)}, u32[]{:S(2)}) collective-permute-start(bf16[32,16384]{1,0:T(8,128)(2,1)S(1)} %copy-done.2), channel_id=1, source_target_pairs={{1,0},{2,1},{3,2},{4,3},{5,4},{6,5},{7,6},{8,7},{9,8},{10,9},{11,1... | collective-permute-start | bytes 3145736 | tf_op jit(solution)/shard_map/ppermute | solution.py:27
  (24 other events, 85.4 us)
where the time goes:
time: 669 us; the launch traced here: 657 us
  matrix products  177 us (26%)
  local copies, waits for them, and re-layouts  159 us (24%)
  other arithmetic  144 us (22%)
  blocking collectives  106 us (16%)
  loops' own time  31.6 us (5%)
  starting transfers between devices  27.8 us (4%)
  waiting for transfers between devices  8.22 us (1%)
    reduce_sum x27, other arithmetic, covariance(): jnp.sum(separation * separation, axis=0)  81.8 us
    dot_general x8, matrix products, listed_coupling(): jnp.einsum('wspq,rwsq->rwp', kernel_tile, far_coef, precision=HIGHEST)  71.1 us
    all_gather x1, blocking collectives, per_device(): lax.all_gather(levels[-1][1], ('leaf', 'sub'), axis=1, tiled=True)  65.2 us
    dot_general x8, matrix products, near_tile(): jnp.einsum('wspq,rwsq->rwp', kernel_tile, far_x, preferred_element_type=j...  53.8 us
    unnamed x1, blocking collectives  41.2 us
    gather x8, local copies, waits for them, and re-layouts, listed_coupling(): far_coef = jnp.take(all_coef, safe_rows, axis=1)  38.2 us
    another operation x2, loops' own time, blocked(): pieces = lax.map(function, starts)  31.6 us
    gather x8, local copies, waits for them, and re-layouts, near_tile(): far_x = jnp.take(all_x, safe_rows, axis=1)  21.2 us
  transfers between devices with their start and end apart: 11, of which 4 were waited for; matrix products, arithmetic and copies ran while one was open for 48% of the time, Pallas kernels for 0%

commit v1 on v0

v1 whole, which is shorter than its diff:
```python
import functools
import math

import jax
import jax.numpy as jnp
from jax import lax
from jax.experimental import pallas as pl
from jax.experimental.pallas import tpu as pltpu
from jax.sharding import PartitionSpec as P

P_SIZE = 128
K = 64
R = 32
LD = 128
PAIRS = LD // 2
GROUPS = LD // 4
HALF = LD // 2
NEAR_REACH = 8
FEATS = 48
BATCH = 8
LIST = 896
SEND = 40
SCALE = 0.5 * math.log2(math.e)
NODE = [math.cos((2 * a + 1) * math.pi / 8) for a in range(4)]
AXES = ("leaf", "sub")
F32 = jnp.float32
BF16 = jnp.bfloat16
NT = (((1,), (1,)), ((), ()))
TINY = 1e-30
VMEM_LIMIT = 56 * 1024 * 1024


def lanes(shape):
    return lax.broadcasted_iota(jnp.int32, shape, len(shape) - 1)


def rows(shape):
    return lax.broadcasted_iota(jnp.int32, shape, len(shape) - 2)


def dot(a, b):
    return jnp.dot(a, b, preferred_element_type=F32)


def dot_nt(a, b):
    return lax.dot_general(a, b, NT, preferred_element_type=F32)


def halves(value):
    high = value.astype(BF16)
    return high, (value - high.astype(F32)).astype(BF16)


def thirds(value):
    first = value.astype(BF16).astype(F32)
    rest = value - first
    second = rest.astype(BF16).astype(F32)
    return first, second, rest - second


def unit_node(index):
    return jnp.where(
        index == 0,
        NODE[0],
        jnp.where(index == 1, NODE[1], jnp.where(index == 2, NODE[2], NODE[3])),
    ).astype(F32)


def lane_nodes():
    b = lanes((8, 128)) & 63
    return [unit_node(b >> 4), unit_node((b >> 2) & 3), unit_node(b & 3)]


def row_nodes():
    r = rows((8, 128))
    return [unit_node(r >> 2), unit_node((r >> 2) + 2)], unit_node(r & 3)


def decay(t):
    t = jnp.maximum(t, TINY)
    return jnp.exp2(-(t * lax.rsqrt(t)))


def tile_from_axes(x_sq, y_sq, z_sq):
    yz = [y_sq[0] + z_sq, y_sq[1] + z_sq]
    return decay(jnp.concatenate([x_sq[k // 2] + yz[k % 2] for k in range(8)], axis=0))


def doubled_transfer(t_ref):
    flat = t_ref[...].reshape(2 * K, K)
    return jnp.concatenate([flat, flat], axis=1)


def device_index():
    return lax.axis_index("leaf") * lax.axis_size("sub") + lax.axis_index("sub")


def merge_up(pairs, t_high, t_low):
    n = pairs.shape[0]
    high, low = halves(pairs.reshape(n * R, 128))
    out = dot(high, t_high) + dot(high, t_low) + dot(low, t_high)
    return out.reshape(n, R, 128)


def pair_lanes(clusters):
    n = clusters.shape[0]
    split = clusters.reshape(n // 2, 2, R, 128)
    return jnp.where(lanes((1, R, 128)) < K, split[:, 0], split[:, 1])


def push_down(value, t_high, t_low):
    n = value.shape[0]
    high, low = halves(value.reshape(n * R, 128))
    out = dot_nt(high, t_high) + dot_nt(high, t_low) + dot_nt(low, t_high)
    return out.reshape(n, R, 128)


def children_of(pairs):
    lane = lanes((1, R, 128))
    left = jnp.where(lane < K, pairs, 0.0)
    right = jnp.where(lane < K, 0.0, pairs)
    return jnp.stack([left, right], axis=1).reshape(2 * pairs.shape[0], R, 128)


def merge_shape_rows(left, right):
    lane = lanes(left.shape)
    sep = left - right
    gap = jnp.sqrt(jnp.sum(jnp.where(lane < 3, sep * sep, 0.0), axis=1, keepdims=True))
    radius = jnp.maximum(left, right) + 0.5 * gap
    return jnp.where(lane == 3, radius, jnp.where(lane < 3, 0.5 * (left + right), 0.0))


def sibling_tile(left, right, lane_u, row_y, row_z):
    low = lanes((8, 128)) < K
    alpha = jnp.where(low, left[3], right[3])
    beta = jnp.where(low, right[3], left[3])
    base = [jnp.where(low, left[d] - right[d], right[d] - left[d]) - beta * lane_u[d] for d in range(3)]
    x_sq = [jnp.square(base[0] + alpha * NODE[a]) for a in range(4)]
    y_sq = [jnp.square(base[1] + alpha * row_y[h]) for h in range(2)]
    z_sq = jnp.square(base[2] + alpha * row_z)
    return tile_from_axes(x_sq, y_sq, z_sq)


def sibling_apply(tile, pair):
    low = lanes((R, 128)) < K
    swapped = pltpu.roll(pair, K, 1)
    stacked = jnp.concatenate(
        [jnp.where(low, swapped, 0.0), jnp.where(low, 0.0, swapped)], axis=0
    )
    high, low_part = halves(stacked)
    t_high, t_low = halves(tile)
    t_high = jnp.concatenate([t_high, t_high], axis=0)
    t_low = jnp.concatenate([t_low, t_low], axis=0)
    out = dot_nt(high, t_high) + dot_nt(high, t_low) + dot_nt(low_part, t_high)
    return jnp.where(low, out[:R], out[R:])


LEVEL_OFFSETS = [0, 128, 192, 224, 240, 248, 252, 254]
PAIR_OFFSETS = [0, 0, 32, 48, 56, 60, 62]


def leaf_kernel(
    x_ref, p_ref, b_ref, t_ref, near_ref,
    send_next, send_prev, coef_ref, lev_ref, root_ref, shape_ref, list_ref,
    pts, shapes,
):
    first_leaf = device_index() * LD
    origin = (first_leaf // 4).astype(F32)
    zero = jnp.zeros((K, P_SIZE), BF16)

    def leaf_pair(c, carry):
        x = x_ref[:, pl.ds(pl.multiple_of(c * 256, 256), 256)]
        weights = jnp.concatenate(
            [
                jnp.concatenate([b_ref[2 * c], zero], axis=1),
                jnp.concatenate([zero, b_ref[2 * c + 1]], axis=1),
            ],
            axis=0,
        )
        coef_ref[c] = dot_nt(x, weights)
        return carry

    lax.fori_loop(0, PAIRS, leaf_pair, 0, unroll=8)

    t_high, t_low = halves(doubled_transfer(t_ref))
    pairs = coef_ref[...]
    for level in range(1, 7):
        pairs = pair_lanes(merge_up(pairs, t_high, t_low))
        lev_ref[pl.ds(PAIR_OFFSETS[level], pairs.shape[0])] = pairs
    root = merge_up(pairs, t_high, t_low)[0]

    for i in range(LD):
        for d in range(3):
            pts[d, i : i + 1, :] = p_ref[d : d + 1, i * P_SIZE : (i + 1) * P_SIZE]
    centers, squares = [], 0.0
    for d in range(3):
        coords = pts[d] - origin if d == 2 else pts[d]
        center = jnp.sum(coords, axis=1, keepdims=True) * (1.0 / P_SIZE)
        centers.append(center)
        squares = squares + jnp.square(coords - center)
    radius = jnp.sqrt(jnp.max(squares, axis=1, keepdims=True))
    lane = lanes((LD, 128))
    shapes[0:LD, :] = jnp.where(
        lane == 0,
        centers[0],
        jnp.where(
            lane == 1,
            centers[1],
            jnp.where(lane == 2, centers[2], jnp.where(lane == 3, radius, 0.0)),
        ),
    )
    count = LD // 2
    for level in range(1, 8):
        source = LEVEL_OFFSETS[level - 1]
        joined = merge_shape_rows(
            shapes[pl.ds(source, count, stride=2), :],
            shapes[pl.ds(source + 1, count, stride=2), :],
        )
        shapes[pl.ds(LEVEL_OFFSETS[level], count), :] = joined
        count //= 2
    shape_rows = jnp.concatenate(
        [jnp.transpose(shapes[0:128, :])[0:8], jnp.transpose(shapes[128:256, :])[0:8]], axis=1
    )
    shape_ref[...] = shape_rows
    root_ref[0:R, :] = root
    root_ref[R : R + 8, :] = jnp.broadcast_to(shapes[254:255, :], (8, 128))

    for send, first_pair, first_group_leaf in ((send_next, PAIRS // 2, LD - 4), (send_prev, 0, 0)):
        send[0 : PAIRS // 2] = coef_ref[pl.ds(first_pair, PAIRS // 2)]
        send[32, 0:8, :] = shape_rows[:, 0:128]
        send[32, 8:32, :] = jnp.zeros((24, 128), F32)
        for k in range(4):
            place = (first_group_leaf + k) * P_SIZE
            send[33 + k] = x_ref[:, place : place + P_SIZE].astype(F32)
            send[32, 8 + 4 * k : 11 + 4 * k, :] = p_ref[:, place : place + P_SIZE]
        for k in range(37, SEND):
            send[k] = jnp.zeros((R, 128), F32)

    lane8 = lanes((8, 128))
    row8 = rows((8, 128))
    offset = jnp.where(near_ref[...] >= 0, near_ref[...] - first_leaf - lane8, 1000)

    def slots_at(delta):
        return jnp.sum(jnp.where(offset == delta, 1.0, 0.0), axis=0, keepdims=True)

    forward = jnp.concatenate([slots_at(delta) for delta in range(8)], axis=0)
    backward = jnp.concatenate(
        [jnp.zeros((1, 128), F32)]
        + [pltpu.roll(slots_at(-delta), 128 - delta, 1) for delta in range(1, 8)],
        axis=0,
    )
    inside = lane8 + row8 < LD
    flags = jnp.where(inside & (forward + backward > 0.0), 1.0, 0.0)
    earlier = jnp.where(rows((128, 128)) < lanes((128, 128)), 1.0, 0.0).astype(BF16)
    place = dot(flags.astype(BF16), earlier)
    totals = jnp.sum(flags, axis=1, keepdims=True)
    before = jnp.full((1, 1), 2.0 * BATCH, F32)
    starts = []
    for delta in range(8):
        starts.append(before)
        before = before + totals[delta : delta + 1, :]
    place = jnp.where(flags > 0.0, place + jnp.concatenate(starts, axis=0), -1.0)
    task_rows = []
    for delta in range(8):
        first = lane8.astype(F32)
        task_rows.append(
            jnp.where(
                row8 == 0,
                first,
                jnp.where(
                    row8 == 1,
                    first + delta,
                    jnp.where(
                        row8 == 2,
                        forward[delta : delta + 1, :],
                        jnp.where(row8 == 3, backward[delta : delta + 1, :], 0.0),
                    ),
                ),
            ).astype(BF16)
        )
    tasks = jnp.concatenate(task_rows, axis=1)
    slot_row = rows((128, 128)).astype(F32)
    for m in range(LIST // 128):
        chosen = jnp.concatenate(
            [
                jnp.where(place[delta : delta + 1, :] == slot_row + 128.0 * m, 1.0, 0.0).astype(BF16)
                for delta in range(8)
            ],
            axis=1,
        )
        part = dot_nt(tasks, chosen)
        part = jnp.where(row8 == 4, before - 2.0 * BATCH, part)
        list_ref[:, m * 128 : (m + 1) * 128] = part.astype(jnp.int32)


def point_features(points8, origin_z):
    row = rows(points8.shape)
    center = jnp.where(row == 2, origin_z + 0.5, 1.0)
    v = jnp.where(row < 3, (points8 - center) * SCALE, 0.0)
    norm = jnp.sum(v * v, axis=0, keepdims=True)
    far = jnp.where(row == 3, norm, jnp.where(row == 4, 1.0, v))
    own = jnp.where(row == 3, 1.0, jnp.where(row == 4, norm, -2.0 * v))
    return far, own


def far_stack(value):
    first, second, third = thirds(value)
    return jnp.concatenate([first, first, first, second, second, third], axis=0)


def own_stack(value):
    first, second, third = thirds(value)
    return jnp.concatenate([first, second, third, first, second, first], axis=0).astype(BF16)


def near_kernel(
    list_ref, shape_ref, x_ref, p_ref, lev_ref, out_ref, couple_ref,
    p8, far_feat, own_feat, dist0, dist1, tile0, tile1,
):
    first_group = device_index() * GROUPS
    p8[...] = jnp.zeros((8, 512), F32)

    def features(g, carry):
        p8[0:3, :] = p_ref[:, pl.ds(pl.multiple_of(g * 512, 512), 512)]
        coords = p8[...]
        origin_z = (first_group + g).astype(F32)
        far, own = point_features(coords, origin_z)
        _, own_up = point_features(coords, origin_z + 1.0)
        far = far_stack(far)
        own = own_stack(own)
        own_up = own_stack(own_up)
        for k in range(4):
            part = slice(k * P_SIZE, (k + 1) * P_SIZE)
            far_feat[4 * g + k] = jnp.transpose(far[:, part]).astype(BF16)
            own_feat[4 * g + k] = own[:, part]
            own_feat[LD + 4 * g + k] = own_up[:, part]
        return carry

    lax.fori_loop(0, GROUPS, features, 0)

    out_ref[...] = x_ref[...].astype(F32)
    for ref in (dist0, dist1, tile0, tile1):
        ref[...] = jnp.zeros(ref.shape, ref.dtype)

    total = list_ref[4, 0]
    steps = (total + BATCH - 1) // BATCH + 2

    def leaf_slice(i):
        return pl.ds(pl.multiple_of(i * P_SIZE, P_SIZE), P_SIZE)

    def phase(n, dist_new, dist_old, tile_new, tile_old):
        results = []
        for u in range(BATCH):
            k = n * BATCH + u
            i, j = list_ref[0, k], list_ref[1, k]
            tile = tile_old[u]
            results.append(
                (
                    i,
                    j,
                    dot(x_ref[:, leaf_slice(j)], tile) * list_ref[2, k].astype(F32),
                    dot_nt(x_ref[:, leaf_slice(i)], tile) * list_ref[3, k].astype(F32),
                )
            )
        for u in range(BATCH):
            k = (n + 2) * BATCH + u
            i, j = list_ref[0, k], list_ref[1, k]
            variant = ((j >> 2) - (i >> 2)) * LD
            dist_new[u] = dot(far_feat[j], own_feat[variant + i])
        for u in range(BATCH):
            tile_new[u] = decay(dist_old[u]).astype(BF16)
        for i, j, to_i, to_j in results:
            out_ref[:, leaf_slice(i)] += to_i
            out_ref[:, leaf_slice(j)] += to_j

    def two_phases(m, carry):
        phase(2 * m, dist0, dist1, tile1, tile0)
        phase(2 * m + 1, dist1, dist0, tile0, tile1)
        return carry

    lax.fori_loop(0, (steps + 1) // 2, two_phases, 0)

    lane_u = lane_nodes()
    row_y, row_z = row_nodes()

    def sibling(pair, cluster):
        left = [shape_ref[d, cluster] * SCALE for d in range(4)]
        right = [shape_ref[d, cluster + 1] * SCALE for d in range(4)]
        tile = sibling_tile(left, right, lane_u, row_y, row_z)
        couple_ref[pair] = sibling_apply(tile, lev_ref[pair])

    def siblings(m, carry):
        for u in range(9):
            pair = 9 * m + u
            sibling(pair, LD + 2 * pair)
        return carry

    lax.fori_loop(0, 7, siblings, 0)


def top_merge_kernel(blocks_ref, t_ref, root_ref, shapes):
    t_high, t_low = halves(doubled_transfer(t_ref))
    n = blocks_ref.shape[0]
    clusters = blocks_ref[:, 0:R, :]
    for k in range(n):
        shift = lanes((1, 128)) == 2
        shapes[k : k + 1, :] = blocks_ref[k, R : R + 1, :] + jnp.where(shift, (k * GROUPS) * 1.0, 0.0)
    source, count = 0, n // 2
    while count >= 1:
        clusters = merge_up(pair_lanes(clusters), t_high, t_low)
        joined = merge_shape_rows(
            shapes[pl.ds(source, count, stride=2), :], shapes[pl.ds(source + 1, count, stride=2), :]
        )
        source += 2 * count
        shapes[pl.ds(source, count), :] = joined
        count //= 2
    root_ref[0:R, :] = clusters[0]
    root_ref[R : R + 8, :] = jnp.broadcast_to(shapes[source : source + 1, :], (8, 128))


def top_down(blocks_ref, member, spacing, incoming, t_high, t_low, pairs_scr, shapes):
    n = blocks_ref.shape[0]
    clusters = blocks_ref[:, 0:R, :]
    for k in range(n):
        shift = lanes((1, 128)) == 2
        shapes[k : k + 1, :] = (
            blocks_ref[k, R : R + 1, :] + jnp.where(shift, (k * spacing) * 1.0, 0.0)
        ) * SCALE
    source, count, pair_source = 0, n // 2, 0
    levels = []
    while count >= 1:
        pairs = pair_lanes(clusters)
        pairs_scr[pl.ds(pair_source, count)] = pairs
        levels.append((source, pair_source))
        if count > 1:
            clusters = merge_up(pairs, t_high, t_low)
            joined = merge_shape_rows(
                shapes[pl.ds(source, count, stride=2), :],
                shapes[pl.ds(source + 1, count, stride=2), :],
            )
            shapes[pl.ds(source + 2 * count, count), :] = joined
        source += 2 * count
        pair_source += count
        count //= 2
    lane_u = lane_nodes()
    row_y, row_z = row_nodes()
    couples = []
    for level, (source, pair_source) in enumerate(levels):
        pair = member >> (level + 1)
        left_row = shapes[pl.ds(source + 2 * pair, 1), :]
        right_row = shapes[pl.ds(source + 2 * pair + 1, 1), :]
        left = [jnp.broadcast_to(left_row[:, d : d + 1], (8, 128)) for d in range(4)]
        right = [jnp.broadcast_to(right_row[:, d : d + 1], (8, 128)) for d in range(4)]
        tile = sibling_tile(left, right, lane_u, row_y, row_z)
        couples.append(sibling_apply(tile, pairs_scr[pair_source + pair]))
    low = lanes((R, 128)) < K
    for level in reversed(range(len(levels))):
        value = couples[level]
        if incoming is not None:
            value = value + push_down(incoming[None], t_high, t_low)[0]
        side = (member >> level) & 1
        keep_low = jnp.where(low, 1, 0) == (1 - side)
        incoming = jnp.where(keep_low, value, 0.0)
    return incoming


def final_kernel(
    near_list, coupling_list, shape_ref,
    near_ref, x_ref, p_ref, b_ref, t_ref, prev_ref, next_ref, coef_ref, couple_ref,
    sub_ref, leaf_ref,
    out_ref,
    pairs_scr, top_shapes, down, leaf_couple, node_tab, high_tab, low_tab,
    halo_shape, sems, p8,
    tile_h0, tile_l0, lhs0, tile_h1, tile_l1, lhs1,
):
    device = device_index()
    first_leaf = device * LD
    lane32 = lanes((R, 128))
    low32 = lane32 < K
    copies = [
        pltpu.make_async_copy(prev_ref.at[32, 0:8], halo_shape.at[0], sems.at[0]),
        pltpu.make_async_copy(next_ref.at[32, 0:8], halo_shape.at[1], sems.at[1]),
    ]
    for copy in copies:
        copy.start()

    t_high, t_low = halves(doubled_transfer(t_ref))
    sub_count = lax.axis_size("sub")
    incoming = top_down(
        leaf_ref, lax.axis_index("leaf"), sub_count * GROUPS, None, t_high, t_low, pairs_scr, top_shapes
    )
    incoming = top_down(
        sub_ref, lax.axis_index("sub"), GROUPS, incoming, t_high, t_low, pairs_scr, top_shapes
    )
    value = couple_ref[pl.ds(PAIR_OFFSETS[6], 1)] + push_down(incoming[None], t_high, t_low)
    for level in range(5, 0, -1):
        n = PAIRS >> level
        value = couple_ref[pl.ds(PAIR_OFFSETS[level], n)] + push_down(
            children_of(value), t_high, t_low
        )
    down[...] = push_down(children_of(value), t_high, t_low)

    p8[...] = jnp.zeros((8, 512), F32)
    out_ref[...] = near_ref[...]
    for halo_ref, group, step in ((prev_ref, 0, -1), (next_ref, GROUPS - 1, 1)):
        origin_z = (device * GROUPS + group).astype(F32)
        span = slice(group * 512, group * 512 + 512)
        p8[0:3, :] = p_ref[:, span]
        _, own = point_features(p8[...], origin_z)
        own = own_stack(own)
        for k in range(4):
            p8[0:3, k * P_SIZE : (k + 1) * P_SIZE] = halo_ref[32, 8 + 4 * k : 11 + 4 * k, :]
        far, _ = point_features(p8[...], origin_z)
        far = far_stack(far)
        for k in range(4):
            far_k = jnp.transpose(far[:, k * P_SIZE : (k + 1) * P_SIZE]).astype(BF16)
            tiles = decay(dot(far_k, own)).astype(BF16)
            x_k = halo_ref[33 + k].astype(BF16)
            target = first_leaf + 4 * (group + step) + k
            products = dot(x_k, tiles)
            for i in range(4):
                leaf = 4 * group + i
                weight = jnp.int32(0)
                for s in range(8):
                    weight = weight + jnp.where(near_list[s, leaf] == target, 1, 0)
                place = slice(leaf * P_SIZE, (leaf + 1) * P_SIZE)
                out_ref[:, place] += products[:, i * P_SIZE : (i + 1) * P_SIZE] * weight.astype(F32)

    def table(first_pair, source_ref, first, count):
        def one(m, carry):
            pair = source_ref[first + m]
            high, low = halves(pair)
            high_tab[0, first_pair + m] = high
            low_tab[0, first_pair + m] = low
            high, low = halves(pltpu.roll(pair, K, 1))
            high_tab[1, first_pair + m] = high
            low_tab[1, first_pair + m] = low
            return carry

        lax.fori_loop(0, count, one, 0, unroll=4)

    table(0, prev_ref, 0, PAIRS // 2)
    table(PAIRS // 2, coef_ref, 0, PAIRS)
    table(PAIRS // 2 + PAIRS, next_ref, 0, PAIRS // 2)
    for swap in range(2):
        high_tab[swap, 2 * PAIRS] = jnp.zeros((R, 128), BF16)
        low_tab[swap, 2 * PAIRS] = jnp.zeros((R, 128), BF16)

    for copy in copies:
        copy.wait()
    lane_u = lane_nodes()
    row8 = rows((8, 128))
    low8 = lanes((8, 128)) < K
    unit8 = jnp.where(row8 == 0, lane_u[0], jnp.where(row8 == 1, lane_u[1], lane_u[2])) * SCALE

    def nodes(first_pair, read, shift, count):
        def one(m, carry):
            left = [read(d, 2 * m) for d in range(4)]
            right = [read(d, 2 * m + 1) for d in range(4)]
            left[2] = left[2] + shift
            right[2] = right[2] + shift

            def column(c):
                return jnp.where(row8 == 0, c[0], jnp.where(row8 == 1, c[1], c[2])) * SCALE

            left_nodes = column(left) + left[3] * unit8
            right_nodes = column(right) + right[3] * unit8
            node_tab[0, first_pair + m] = jnp.where(low8, left_nodes, right_nodes)
            node_tab[1, first_pair + m] = jnp.where(low8, right_nodes, left_nodes)
            return carry

        lax.fori_loop(0, count, one, 0, unroll=4)

    nodes(0, lambda d, k: halo_shape[0, d, HALF + k], -1.0 * GROUPS, PAIRS // 2)
    nodes(PAIRS // 2, lambda d, k: shape_ref[d, k], 0.0, PAIRS)
    nodes(PAIRS // 2 + PAIRS, lambda d, k: halo_shape[1, d, k], 1.0 * GROUPS, PAIRS // 2)

    row_y, row_z = row_nodes()

    def couple_tiles(i, u, tile_h, tile_l, lhs):
        radius = shape_ref[3, i] * SCALE
        center = [shape_ref[d, i] * SCALE for d in range(3)]
        own_x = [center[0] + radius * NODE[a] for a in range(4)]
        own_y = [center[1] + radius * row_y[h] for h in range(2)]
        own_z = center[2] + radius * row_z
        for q in range(4):
            picks = []
            for h in range(2):
                j = coupling_list[2 * q + h, i]
                e = jnp.where(j >= 0, j - first_leaf + HALF, 0)
                swap = (e & 1) ^ h
                picks.append((swap, e >> 1, jnp.where(j >= 0, e >> 1, 2 * PAIRS)))
            (s0, n0, c0), (s1, n1, c1) = picks
            base = jnp.where(low8, node_tab[s0, n0], node_tab[s1, n1])
            bx = jnp.broadcast_to(base[0:1], (8, 128))
            by = jnp.broadcast_to(base[1:2], (8, 128))
            bz = jnp.broadcast_to(base[2:3], (8, 128))
            tile = tile_from_axes(
                [jnp.square(bx - own_x[a]) for a in range(4)],
                [jnp.square(by - own_y[h]) for h in range(2)],
                jnp.square(bz - own_z),
            )
            high, low = halves(tile)
            span = slice(q * 128, (q + 1) * 128)
            tile_h[u, :, span] = high
            tile_l[u, :, span] = low
            lhs[u, 0:R, span] = jnp.where(low32, high_tab[s0, c0], high_tab[s1, c1])
            lhs[u, R : 2 * R, span] = jnp.where(low32, low_tab[s0, c0], low_tab[s1, c1])

    def couple_apply(u, tile_h, tile_l, lhs):
        both = dot_nt(lhs[u], tile_h[u])
        cross = dot_nt(lhs[u, 0:R], tile_l[u])
        return both[0:R] + both[R : 2 * R] + cross

    UNIT = 4

    def couple_phase(n, new, old):
        for v in range(UNIT // 2):
            pair = (n - 1) * (UNIT // 2) + v + 2
            value = jnp.concatenate(
                [couple_apply(2 * v, *old), couple_apply(2 * v + 1, *old)], axis=1
            )
            leaf_couple[pair] = value
        for u in range(UNIT):
            leaf = jnp.minimum(n * UNIT + u, LD - 1)
            couple_tiles(leaf, u, *new)

    buffers = ((tile_h0, tile_l0, lhs0), (tile_h1, tile_l1, lhs1))
    for ref in buffers[1]:
        ref[...] = jnp.zeros(ref.shape, ref.dtype)

    def couple_two(m, carry):
        couple_phase(2 * m, buffers[0], buffers[1])
        couple_phase(2 * m + 1, buffers[1], buffers[0])
        return carry

    lax.fori_loop(0, LD // UNIT // 2 + 1, couple_two, 0)

    zero = jnp.zeros((K, P_SIZE), BF16)

    def finish(c, carry):
        value = (down[c] + leaf_couple[c + 2]).astype(BF16)
        weights = jnp.concatenate(
            [
                jnp.concatenate([b_ref[2 * c], zero], axis=1),
                jnp.concatenate([zero, b_ref[2 * c + 1]], axis=1),
            ],
            axis=0,
        )
        out_ref[:, pl.ds(pl.multiple_of(c * 256, 256), 256)] += dot(value, weights)
        return carry

    lax.fori_loop(0, PAIRS, finish, 0, unroll=8)


def shaped(*shape, dtype=F32):
    return jax.ShapeDtypeStruct(shape, dtype)


def vmem():
    return pl.BlockSpec(memory_space=pltpu.VMEM)


def smem():
    return pl.BlockSpec(memory_space=pltpu.SMEM)


PARAMS = pltpu.CompilerParams(vmem_limit_bytes=VMEM_LIMIT)


def per_device(charges, points, basis, transfer, near_list, coupling_list):
    near_rows = near_list.T
    coupling_rows = coupling_list.T
    n_sub = lax.axis_size("sub")
    n_leaf = lax.axis_size("leaf")
    devices = n_sub * n_leaf
    send_next, send_prev, coef, lev, root, shapes, tasks = pl.pallas_call(
        leaf_kernel,
        name="leaf_up",
        out_shape=(
            shaped(SEND, R, 128),
            shaped(SEND, R, 128),
            shaped(PAIRS, R, 128),
            shaped(PAIRS - 1, R, 128),
            shaped(R + 8, 128),
            shaped(8, 256),
            shaped(8, LIST, dtype=jnp.int32),
        ),
        in_specs=[vmem()] * 5,
        out_specs=[vmem()] * 7,
        scratch_shapes=[pltpu.VMEM((3, LD, 128), F32), pltpu.VMEM((256, 128), F32)],
        compiler_params=PARAMS,
    )(charges, points, basis, transfer, near_rows)

    sub_blocks = lax.all_to_all(
        jnp.broadcast_to(root[None], (n_sub,) + root.shape), "sub", 0, 0, tiled=True
    )
    merged = pl.pallas_call(
        top_merge_kernel,
        name="top_merge",
        out_shape=shaped(R + 8, 128),
        in_specs=[vmem()] * 2,
        out_specs=vmem(),
        scratch_shapes=[pltpu.VMEM((2 * n_sub, 128), F32)],
        compiler_params=PARAMS,
    )(sub_blocks, transfer)
    leaf_blocks = lax.all_to_all(
        jnp.broadcast_to(merged[None], (n_leaf,) + merged.shape), "leaf", 0, 0, tiled=True
    )
    forward = [(i, i + 1) for i in range(devices - 1)]
    backward = [(i + 1, i) for i in range(devices - 1)]
    from_prev = lax.ppermute(send_next, AXES, forward)
    from_next = lax.ppermute(send_prev, AXES, backward)

    near, couple = pl.pallas_call(
        near_kernel,
        name="near_field",
        out_shape=(shaped(R, LD * P_SIZE), shaped(PAIRS - 1, R, 128)),
        in_specs=[smem(), smem(), vmem(), vmem(), vmem()],
        out_specs=[vmem()] * 2,
        scratch_shapes=[
            pltpu.VMEM((8, 512), F32),
            pltpu.VMEM((LD, P_SIZE, FEATS), BF16),
            pltpu.VMEM((2 * LD, FEATS, P_SIZE), BF16),
            pltpu.VMEM((BATCH, 128, 128), F32),
            pltpu.VMEM((BATCH, 128, 128), F32),
            pltpu.VMEM((BATCH, 128, 128), BF16),
            pltpu.VMEM((BATCH, 128, 128), BF16),
        ],
        compiler_params=PARAMS,
        cost_estimate=pl.CostEstimate(
            flops=2 * 460 * 128 * 128 * 128, bytes_accessed=4 << 20, transcendentals=460 * 32768
        ),
    )(tasks, shapes, charges, points, lev)

    n_top = max(n_sub, n_leaf)
    unit = 4
    stages = [
        pltpu.VMEM((unit, K, 512), BF16),
        pltpu.VMEM((unit, K, 512), BF16),
        pltpu.VMEM((unit, 2 * R, 512), BF16),
    ]
    return pl.pallas_call(
        final_kernel,
        name="couple_down",
        out_shape=shaped(R, LD * P_SIZE),
        in_specs=[smem()] * 3 + [vmem()] * 11,
        out_specs=vmem(),
        scratch_shapes=[
            pltpu.VMEM((n_top, R, 128), F32),
            pltpu.VMEM((2 * n_top, 128), F32),
            pltpu.VMEM((PAIRS, R, 128), F32),
            pltpu.VMEM((PAIRS + 8, R, 128), F32),
            pltpu.VMEM((2, 2 * PAIRS, 8, 128), F32),
            pltpu.VMEM((2, 2 * PAIRS + 1, R, 128), BF16),
            pltpu.VMEM((2, 2 * PAIRS + 1, R, 128), BF16),
            pltpu.SMEM((2, 8, 128), F32),
            pltpu.SemaphoreType.DMA((2,)),
            pltpu.VMEM((8, 512), F32),
        ]
        + stages
        + stages,
        compiler_params=PARAMS,
    )(
        near_rows, coupling_rows, shapes,
        near, charges, points, basis, transfer, from_prev, from_next, coef, couple,
        sub_blocks, leaf_blocks,
    )


def solution(mesh):
    in_specs = (
        P(None, AXES),
        P(None, AXES),
        P(AXES, None, None),
        P(),
        P(AXES, None),
        P(AXES, None),
    )
    return jax.shard_map(
        per_device, mesh=mesh, in_specs=in_specs, out_specs=P(None, AXES), check_vma=False
    )
```

time: 669 us -> 120 us (0.18)
  the two profiles are of different devices: /device:TPU:4 before, /device:TPU:31 now
where the time goes in v1:
time: 120 us; the launch traced here: 119 us
  Pallas kernels  77.9 us (65%)
  blocking collectives  26.2 us (22%)
  starting transfers between devices  11.9 us (10%)
  local copies, waits for them, and re-layouts  3.22 us (3%)
    pallas_call x1, Pallas kernels, per_device(): pl.pallas_call(near_kernel, name='near_field', out_shape=(shaped(R, LD *...  36.1 us
    pallas_call x1, Pallas kernels, per_device(): pl.pallas_call(final_kernel, name='couple_down', out_shape=shaped(R, LD *...  31.3 us
    all_to_all x1, blocking collectives, per_device(): lax.all_to_all(jnp.broadcast_to(root[None], (n_sub,) + root.shape), 'sub'...  26.2 us
    pallas_call x1, Pallas kernels, per_device(): pl.pallas_call(leaf_kernel, name='leaf_up', out_shape=(shaped(SEND, R, 12...  8.52 us
    all_to_all x1, starting transfers between devices, per_device(): lax.all_to_all(jnp.broadcast_to(merged[None], (n_leaf,) + merged.shape),...  6.57 us
    ppermute x1, starting transfers between devices, per_device(): from_next = lax.ppermute(send_prev, AXES, backward)  4.03 us
  transfers between devices with their start and end apart: 3, of which 0 were waited for; matrix products, arithmetic and copies ran while one was open for 2% of the time, Pallas kernels for 32%

profile of v1, /device:TPU:31, one launch (start us, length us, event | category | flops | bytes accessed | tf_op | source)
XLA Modules:
  0.0 119.3 jit_solution(13534781616141559610)
XLA Ops:
  0.0 8.5 %leaf_up.1 = (f32[40,32,128]{2,1,0:T(8,128)}, f32[40,32,128]{2,1,0:T(8,128)}, f32[64,32,128]{2,1,0:T(8,128)}, f32[63,32,128]{2,1,0:T(8,128)}, f32[40,128]{1,0:T(...) custom-call(bf16[32,16384]{1,0:T(8,128)(2,1)} %x_ref.5, f32[3,16384]{1,0:T(4,128)} %p_ref.5, bf16[128,64,128]{2,1,0:T(8,128)(2,1)} %b_ref.3, ...), custom_call_target="tpu_custom_call" | custom-call | tf_op jit(solution)/shard_map/leaf_up/pallas_call | solution.py:677
  8.5 1.3 %collective-permute-start = (f32[40,32,128]{2,1,0:T(8,128)}, f32[40,32,128]{2,1,0:T(8,128)S(1)}, u32[]{:S(2)}, u32[]{:S(2)}) collective-permute-start(f32[40,32,128]{2,1,0:T(8,128)} %get-tuple-element.18), channel_id=1, source_target_pairs={{0,1},{1,2},{2,3},{3,4},{4,5},{5,6},{6,7},{7,8},{8,9},{9,10},{10,1... | collective-permute-start | bytes 1966088 | tf_op jit(solution)/shard_map/ppermute | solution.py:712
  9.8 4.0 %collective-permute-start.1 = (f32[40,32,128]{2,1,0:T(8,128)}, f32[40,32,128]{2,1,0:T(8,128)S(1)}, u32[]{:S(2)}, u32[]{:S(2)}) collective-permute-start(f32[40,32,128]{2,1,0:T(8,128)} %get-tuple-element.19), channel_id=1, source_target_pairs={{1,0},{2,1},{3,2},{4,3},{5,4},{6,5},{7,6},{8,7},{9,8},{10,9},{11,1... | collective-permute-start | bytes 1966088 | tf_op jit(solution)/shard_map/ppermute | solution.py:713
  13.8 0.7 broadcast_in_dim.4
  14.6 26.2 %all_to_all.10.blocks_ref.sub_ref = f32[4,40,128]{2,1,0:T(8,128)} all-to-all(f32[4,40,128]{2,1,0:T(8,128)S(1)} %broadcast_in_dim.4), channel_id=1, replica_groups=mesh['leaf'=8,'sub'=4] {'sub'}, dimensions={0} | all-to-all | bytes 163840 | tf_op jit(solution)/shard_map/all_to_all | solution.py:695
  40.8 1.9 %top_merge.1 = f32[40,128]{1,0:T(8,128)} custom-call(f32[4,40,128]{2,1,0:T(8,128)} %all_to_all.10.blocks_ref.sub_ref, f32[2,64,64]{2,1,0:T(8,128)} %t_ref.5), custom_call_target="tpu_custom_call" | custom-call | tf_op jit(solution)/shard_map/top_merge/pallas_call | solution.py:698
  42.7 1.4 %broadcast_in_dim.5 = f32[8,40,128]{2,1,0:T(8,128)} broadcast(f32[40,128]{1,0:T(8,128)} %top_merge.1), dimensions={1,2} | broadcast | bytes 184320 | tf_op jit(solution)/shard_map/broadcast_in_dim | solution.py:708
  44.1 6.6 %all-to-all-start.1 = ((f32[8,40,128]{2,1,0:T(8,128)}), f32[8,40,128]{2,1,0:T(8,128)S(1)}, u32[]{:S(2)}, u32[]{:S(2)}) async-start(f32[8,40,128]{2,1,0:T(8,128)} %broadcast_in_dim.5), calls=%async_computation.1 | async-start | bytes 327680 | tf_op jit(solution)/shard_map/all_to_all | solution.py:707
  50.7 36.1 %near_field.1 = (f32[32,16384]{1,0:T(8,128)}, f32[63,32,128]{2,1,0:T(8,128)}) custom-call(s32[8,896]{1,0:T(8,128)} %get-tuple-element.15.list_ref, f32[8,256]{1,0:T(8,128)} %get-tuple-element.14.shape_ref, bf16[32,16384]{1,0:T(8,128)(2,1)} %x_ref.5, f32[3,16384]{1,0:T(4,128)} %p_ref.5, f32[63,32,128]{2,1,0:T(8,128)} %get-tuple-element.16.lev_ref), custom_call_target="tpu_custom_call" | custom-call | flops 1929379840 | bytes 4194304 | tf_op jit(solution)/shard_map/near_field/pallas_call | solution.py:715
  86.8 0.0 all-to-all-done.1.leaf_ref
  86.8 0.0 copy-start.2
  86.8 0.0 collective-permute-done.prev_ref
  86.8 0.0 copy-start
  86.8 0.0 collective-permute-done.1.next_ref
  86.8 0.0 copy-start.1
  86.9 0.6 copy-done.2
  87.5 0.3 copy-done
  87.7 0.2 copy-done.1
  87.9 31.3 %couple_down.1 = f32[32,16384]{1,0:T(8,128)} custom-call(s32[8,128]{1,0:T(8,128)} %bitcast.3, s32[8,128]{1,0:T(8,128)} %bitcast.4, f32[8,256]{1,0:T(8,128)} %get-tuple-element.14.shape_ref, f32[32,16384]{1,0:T(8,128)} %get-tuple-element.17.near_ref, bf16[32,16384]{1,0:T(8,128)(2,1)} %x_ref.5, f32[3,16384]{1,0:T(4,128)} %p_ref.5, ...), custom_call_target="tpu_custom_call" | custom-call | tf_op jit(solution)/shard_map/couple_down/pallas_call | solution.py:743
Async XLA Ops:
  8.5 78.3 %collective-permute-start = (f32[40,32,128]{2,1,0:T(8,128)}, f32[40,32,128]{2,1,0:T(8,128)S(1)}, u32[]{:S(2)}, u32[]{:S(2)}) collective-permute-start(f32[40,32,128]{2,1,0:T(8,128)} %get-tuple-element.18), channel_id=1, source_target_pairs={{0,1},{1,2},{2,3},{3,4},{4,5},{5,6},{6,7},{7,8},{8,9},{9,10},{10,1... | collective-permute-start | bytes 1966088 | tf_op jit(solution)/shard_map/ppermute | solution.py:712
  9.8 77.0 %collective-permute-start.1 = (f32[40,32,128]{2,1,0:T(8,128)}, f32[40,32,128]{2,1,0:T(8,128)S(1)}, u32[]{:S(2)}, u32[]{:S(2)}) collective-permute-start(f32[40,32,128]{2,1,0:T(8,128)} %get-tuple-element.19), channel_id=1, source_target_pairs={{1,0},{2,1},{3,2},{4,3},{5,4},{6,5},{7,6},{8,7},{9,8},{10,9},{11,1... | collective-permute-start | bytes 1966088 | tf_op jit(solution)/shard_map/ppermute | solution.py:713
  44.1 42.7 %all-to-all-start.1 = ((f32[8,40,128]{2,1,0:T(8,128)}), f32[8,40,128]{2,1,0:T(8,128)S(1)}, u32[]{:S(2)}, u32[]{:S(2)}) async-start(f32[8,40,128]{2,1,0:T(8,128)} %broadcast_in_dim.5), calls=%async_computation.1 | async-start | bytes 327680 | tf_op jit(solution)/shard_map/all_to_all | solution.py:707
  86.8 0.7 copy-start.2
  86.8 0.9 copy-start
  86.8 1.1 copy-start.1

commit v2 on v1

v2 whole, which is shorter than its diff:
```python
import functools
import math

import jax
import jax.numpy as jnp
from jax import lax
from jax.experimental import pallas as pl
from jax.experimental.pallas import tpu as pltpu
from jax.sharding import PartitionSpec as P

P_SIZE = 128
K = 64
R = 32
LD = 128
PAIRS = LD // 2
GROUPS = LD // 4
HALF = LD // 2
NEAR_REACH = 8
FEATS = 64
BATCH = 8
LIST = 896
SEND = 40
SCALE = 0.5 * math.log2(math.e)
NODE = [math.cos((2 * a + 1) * math.pi / 8) for a in range(4)]
AXES = ("leaf", "sub")
F32 = jnp.float32
BF16 = jnp.bfloat16
NT = (((1,), (1,)), ((), ()))
TINY = 1e-30
VMEM_LIMIT = 56 * 1024 * 1024


def lanes(shape):
    return lax.broadcasted_iota(jnp.int32, shape, len(shape) - 1)


def rows(shape):
    return lax.broadcasted_iota(jnp.int32, shape, len(shape) - 2)


def dot(a, b):
    return jnp.dot(a, b, preferred_element_type=F32)


def dot_nt(a, b):
    return lax.dot_general(a, b, NT, preferred_element_type=F32)


def halves(value):
    high = value.astype(BF16)
    return high, (value - high.astype(F32)).astype(BF16)


def thirds(value):
    first = value.astype(BF16).astype(F32)
    rest = value - first
    second = rest.astype(BF16).astype(F32)
    return first, second, rest - second


def unit_node(index):
    return jnp.where(
        index == 0,
        NODE[0],
        jnp.where(index == 1, NODE[1], jnp.where(index == 2, NODE[2], NODE[3])),
    ).astype(F32)


def lane_nodes():
    b = lanes((8, 128)) & 63
    return [unit_node(b >> 4), unit_node((b >> 2) & 3), unit_node(b & 3)]


def row_nodes():
    r = rows((8, 128))
    return [unit_node(r >> 2), unit_node((r >> 2) + 2)], unit_node(r & 3)


def decay(t):
    t = jnp.maximum(t, TINY)
    return jnp.exp2(-(t * lax.rsqrt(t)))


def tile_from_axes(x_sq, y_sq, z_sq):
    yz = [y_sq[0] + z_sq, y_sq[1] + z_sq]
    return decay(jnp.concatenate([x_sq[k // 2] + yz[k % 2] for k in range(8)], axis=0))


def doubled_transfer(t_ref):
    flat = t_ref[...].reshape(2 * K, K)
    return jnp.concatenate([flat, flat], axis=1)


def device_index():
    return lax.axis_index("leaf") * lax.axis_size("sub") + lax.axis_index("sub")


def merge_up(pairs, t_high, t_low):
    n = pairs.shape[0]
    high, low = halves(pairs.reshape(n * R, 128))
    out = dot(high, t_high) + dot(high, t_low) + dot(low, t_high)
    return out.reshape(n, R, 128)


def pair_lanes(clusters):
    n = clusters.shape[0]
    split = clusters.reshape(n // 2, 2, R, 128)
    return jnp.where(lanes((1, R, 128)) < K, split[:, 0], split[:, 1])


def push_down(value, t_high, t_low):
    n = value.shape[0]
    high, low = halves(value.reshape(n * R, 128))
    out = dot_nt(high, t_high) + dot_nt(high, t_low) + dot_nt(low, t_high)
    return out.reshape(n, R, 128)


def children_of(pairs):
    lane = lanes((1, R, 128))
    left = jnp.where(lane < K, pairs, 0.0)
    right = jnp.where(lane < K, 0.0, pairs)
    return jnp.stack([left, right], axis=1).reshape(2 * pairs.shape[0], R, 128)


def merge_shape_rows(left, right):
    lane = lanes(left.shape)
    sep = left - right
    gap = jnp.sqrt(jnp.sum(jnp.where(lane < 3, sep * sep, 0.0), axis=1, keepdims=True))
    radius = jnp.maximum(left, right) + 0.5 * gap
    return jnp.where(lane == 3, radius, jnp.where(lane < 3, 0.5 * (left + right), 0.0))


def sibling_tile(left, right, lane_u, row_y, row_z):
    low = lanes((8, 128)) < K
    alpha = jnp.where(low, left[3], right[3])
    beta = jnp.where(low, right[3], left[3])
    base = [jnp.where(low, left[d] - right[d], right[d] - left[d]) - beta * lane_u[d] for d in range(3)]
    x_sq = [jnp.square(base[0] + alpha * NODE[a]) for a in range(4)]
    y_sq = [jnp.square(base[1] + alpha * row_y[h]) for h in range(2)]
    z_sq = jnp.square(base[2] + alpha * row_z)
    return tile_from_axes(x_sq, y_sq, z_sq)


def sibling_apply(tile, pair):
    low = lanes((R, 128)) < K
    swapped = pltpu.roll(pair, K, 1)
    stacked = jnp.concatenate(
        [jnp.where(low, swapped, 0.0), jnp.where(low, 0.0, swapped)], axis=0
    )
    high, low_part = halves(stacked)
    t_high, t_low = halves(tile)
    t_high = jnp.concatenate([t_high, t_high], axis=0)
    t_low = jnp.concatenate([t_low, t_low], axis=0)
    out = dot_nt(high, t_high) + dot_nt(high, t_low) + dot_nt(low_part, t_high)
    return jnp.where(low, out[:R], out[R:])


LEVEL_OFFSETS = [0, 128, 192, 224, 240, 248, 252, 254]
PAIR_OFFSETS = [0, 0, 32, 48, 56, 60, 62]


def block_diagonal(left, right):
    zero = jnp.zeros(left.shape, left.dtype)
    return jnp.concatenate(
        [jnp.concatenate([left, zero], axis=1), jnp.concatenate([zero, right], axis=1)], axis=0
    )


def leaf_kernel(
    x_ref, p_ref, b_ref, t_ref,
    send_next, send_prev, coef_ref, lev_ref, root_ref, shape_ref,
    pts, shapes, p8,
):
    origin = (device_index() * GROUPS).astype(F32)

    def leaf_pair(c, carry):
        x = x_ref[:, pl.ds(pl.multiple_of(c * 256, 256), 256)]
        coef_ref[c] = dot_nt(x, block_diagonal(b_ref[2 * c], b_ref[2 * c + 1]))
        return carry

    lax.fori_loop(0, PAIRS, leaf_pair, 0, unroll=8)

    t_high, t_low = halves(doubled_transfer(t_ref))
    pairs = coef_ref[...]
    for level in range(1, 7):
        pairs = pair_lanes(merge_up(pairs, t_high, t_low))
        lev_ref[pl.ds(PAIR_OFFSETS[level], pairs.shape[0])] = pairs
    root = merge_up(pairs, t_high, t_low)[0]

    for i in range(LD):
        for d in range(3):
            pts[d, i : i + 1, :] = p_ref[d : d + 1, i * P_SIZE : (i + 1) * P_SIZE]
    centers, squares = [], 0.0
    for d in range(3):
        coords = pts[d] - origin if d == 2 else pts[d]
        center = jnp.sum(coords, axis=1, keepdims=True) * (1.0 / P_SIZE)
        centers.append(center)
        squares = squares + jnp.square(coords - center)
    radius = jnp.sqrt(jnp.max(squares, axis=1, keepdims=True))
    lane = lanes((LD, 128))
    shapes[0:LD, :] = jnp.where(
        lane == 0,
        centers[0],
        jnp.where(
            lane == 1,
            centers[1],
            jnp.where(lane == 2, centers[2], jnp.where(lane == 3, radius, 0.0)),
        ),
    )
    count = LD // 2
    for level in range(1, 8):
        source = LEVEL_OFFSETS[level - 1]
        joined = merge_shape_rows(
            shapes[pl.ds(source, count, stride=2), :],
            shapes[pl.ds(source + 1, count, stride=2), :],
        )
        shapes[pl.ds(LEVEL_OFFSETS[level], count), :] = joined
        count //= 2
    shape_rows = jnp.concatenate(
        [jnp.transpose(shapes[0:128, :])[0:8], jnp.transpose(shapes[128:256, :])[0:8]], axis=1
    )
    shape_ref[...] = shape_rows
    low = lanes((R // 2, 128)) < K
    block = jnp.concatenate(
        [
            jnp.where(low, root[0 : R // 2], root[R // 2 : R]),
            jnp.broadcast_to(shapes[254:255, :], (8, 128)),
        ],
        axis=0,
    )
    root_ref[...] = jnp.broadcast_to(block[None], root_ref.shape)

    p8[...] = jnp.zeros((8, 512), F32)
    for send, first_pair, group in ((send_next, PAIRS // 2, GROUPS - 1), (send_prev, 0, 0)):
        send[0 : PAIRS // 2] = coef_ref[pl.ds(first_pair, PAIRS // 2)].astype(BF16)
        parts = thirds(shape_rows[:, 0:128])
        send[36] = jnp.concatenate(list(parts) + [jnp.zeros((8, 128), F32)], axis=0).astype(BF16)
        p8[0:3, :] = p_ref[:, group * 512 : group * 512 + 512]
        parts = thirds(p8[...])
        for k in range(4):
            span = slice(k * P_SIZE, (k + 1) * P_SIZE)
            send[32 + k] = x_ref[:, group * 512 + k * P_SIZE : group * 512 + (k + 1) * P_SIZE]
        for part in range(3):
            send[37 + part] = jnp.concatenate(
                [parts[part][:, k * P_SIZE : (k + 1) * P_SIZE] for k in range(4)], axis=0
            ).astype(BF16)


def list_kernel(near_ref, list_ref):
    first_leaf = device_index() * LD
    lane8 = lanes((8, 128))
    row8 = rows((8, 128))
    offset = jnp.where(near_ref[...] >= 0, near_ref[...] - first_leaf - lane8, 1000)

    def slots_at(delta):
        return jnp.sum(jnp.where(offset == delta, 1.0, 0.0), axis=0, keepdims=True)

    forward = jnp.concatenate([slots_at(delta) for delta in range(8)], axis=0)
    backward = jnp.concatenate(
        [jnp.zeros((1, 128), F32)]
        + [pltpu.roll(slots_at(-delta), 128 - delta, 1) for delta in range(1, 8)],
        axis=0,
    )
    inside = lane8 + row8 < LD
    flags = jnp.where(inside & (forward + backward > 0.0), 1.0, 0.0)
    earlier = jnp.where(rows((128, 128)) < lanes((128, 128)), 1.0, 0.0).astype(BF16)
    place = dot(flags.astype(BF16), earlier)
    totals = jnp.sum(flags, axis=1, keepdims=True)
    before = jnp.full((1, 1), 2.0 * BATCH, F32)
    starts = []
    for delta in range(8):
        starts.append(before)
        before = before + totals[delta : delta + 1, :]
    place = jnp.where(flags > 0.0, place + jnp.concatenate(starts, axis=0), -1.0)
    task_rows = []
    for delta in range(8):
        first = lane8.astype(F32)
        task_rows.append(
            jnp.where(
                row8 == 0,
                first,
                jnp.where(
                    row8 == 1,
                    first + delta,
                    jnp.where(
                        row8 == 2,
                        forward[delta : delta + 1, :],
                        jnp.where(row8 == 3, backward[delta : delta + 1, :], 0.0),
                    ),
                ),
            ).astype(BF16)
        )
    tasks = jnp.concatenate(task_rows, axis=1)
    slot_row = rows((128, 128)).astype(F32)
    for m in range(LIST // 128):
        chosen = jnp.concatenate(
            [
                jnp.where(place[delta : delta + 1, :] == slot_row + 128.0 * m, 1.0, 0.0).astype(BF16)
                for delta in range(8)
            ],
            axis=1,
        )
        part = dot_nt(tasks, chosen)
        part = jnp.where(row8 == 4, before - 2.0 * BATCH, part)
        list_ref[:, m * 128 : (m + 1) * 128] = part.astype(jnp.int32)


def point_features(points8, origin_z):
    row = rows(points8.shape)
    center = jnp.where(row == 2, origin_z + 0.5, 1.0)
    v = jnp.where(row < 3, (points8 - center) * SCALE, 0.0)
    norm = jnp.sum(v * v, axis=0, keepdims=True)
    far = jnp.where(row == 3, norm, jnp.where(row == 4, 1.0, v))
    own = jnp.where(row == 3, 1.0, jnp.where(row == 4, norm, -2.0 * v))
    return far, own


def far_stack(value):
    first, second, third = thirds(value)
    none = jnp.zeros(value.shape, F32)
    return jnp.concatenate(
        [first, first, first, second, second, third, none, none], axis=0
    ).astype(BF16)


def own_stack(value):
    first, second, third = thirds(value)
    none = jnp.zeros(value.shape, F32)
    return jnp.concatenate(
        [first, second, third, first, second, first, none, none], axis=0
    ).astype(BF16)


def identity():
    return jnp.where(rows((128, 128)) == lanes((128, 128)), 1.0, 0.0).astype(BF16)


def near_kernel(
    list_ref, x_ref, p_ref, out_ref,
    p8, far_feat, own_feat, back, dist0, dist1, tile0, tile1,
):
    first_group = device_index() * GROUPS
    p8[...] = jnp.zeros(p8.shape, F32)
    eye = identity()

    def features(m, carry):
        for v in range(2):
            g = 2 * m + v
            p8[v, 0:3, :] = p_ref[:, pl.ds(pl.multiple_of(g * 512, 512), 512)]
            coords = p8[v]
            origin_z = (first_group + g).astype(F32)
            far, own = point_features(coords, origin_z)
            _, own_up = point_features(coords, origin_z + 1.0)
            far = far_stack(far)
            own = own_stack(own)
            own_up = own_stack(own_up)
            parts = [far[:, k * P_SIZE : (k + 1) * P_SIZE] for k in range(4)]
            for swap in range(2):
                stacked = jnp.concatenate([parts[k ^ swap] for k in range(4)], axis=0)
                turned = dot_nt(eye, stacked).astype(BF16)
                far_feat[swap, 2 * g] = turned[:, 0:128]
                far_feat[swap, 2 * g + 1] = turned[:, 128:256]
            for k in range(4):
                part = slice(k * P_SIZE, (k + 1) * P_SIZE)
                own_feat[4 * g + k] = own[:, part]
                own_feat[LD + 4 * g + k] = own_up[:, part]
        return carry

    lax.fori_loop(0, GROUPS // 2, features, 0)

    out_ref[...] = x_ref[...].astype(F32)
    for ref in (back, dist0, dist1, tile0, tile1):
        ref[...] = jnp.zeros(ref.shape, ref.dtype)

    total = list_ref[4, 0]
    steps = (total + BATCH - 1) // BATCH + 2
    low = lanes((128, 128)) < K

    def leaf_slice(i):
        return pl.ds(pl.multiple_of(i * P_SIZE, P_SIZE), P_SIZE)

    def phase(n, dist_new, dist_old, tile_new, tile_old):
        results = []
        for u in range(BATCH):
            k = n * BATCH + u
            i, j = list_ref[0, k], list_ref[1, k]
            tile = tile_old[u // 2, :, (u % 2) * 128 : (u % 2) * 128 + 128]
            results.append(
                (
                    i,
                    j,
                    dot(x_ref[:, leaf_slice(j)], tile) * list_ref[2, k].astype(F32),
                    dot_nt(x_ref[:, leaf_slice(i)], tile) * list_ref[3, k].astype(F32),
                )
            )
        for u in range(BATCH // 2):
            far, own = [], []
            for h in range(2):
                k = (n + 2) * BATCH + 2 * u + h
                i, j = list_ref[0, k], list_ref[1, k]
                variant = ((j >> 2) - (i >> 2)) * LD
                far.append(far_feat[(j & 1) ^ h, j >> 1])
                own.append(own_feat[variant + i])
            dist_new[u] = dot(jnp.where(low, far[0], far[1]), block_diagonal(own[0], own[1]))
        for u in range(BATCH // 2):
            tile_new[u] = decay(dist_old[u]).astype(BF16)
        for i, j, to_i, to_j in results:
            out_ref[:, leaf_slice(i)] += to_i
            back[:, leaf_slice(j)] += to_j

    def two_phases(m, carry):
        phase(2 * m, dist0, dist1, tile1, tile0)
        phase(2 * m + 1, dist1, dist0, tile0, tile1)
        return carry

    lax.fori_loop(0, (steps + 1) // 2, two_phases, 0)
    out_ref[...] += back[...]


def down_kernel(
    shape_ref, lev_ref, t_ref, root_ref, down_ref, couple, pairs_scr, shapes,
):
    lane_u = lane_nodes()
    row_y, row_z = row_nodes()

    def sibling(pair, cluster):
        left = [shape_ref[d, cluster] * SCALE for d in range(4)]
        right = [shape_ref[d, cluster + 1] * SCALE for d in range(4)]
        tile = sibling_tile(left, right, lane_u, row_y, row_z)
        couple[pair] = sibling_apply(tile, lev_ref[pair])

    def siblings(m, carry):
        for u in range(9):
            pair = 9 * m + u
            sibling(pair, LD + 2 * pair)
        return carry

    lax.fori_loop(0, 7, siblings, 0)

    t_high, t_low = halves(doubled_transfer(t_ref))
    device = device_index()
    n = root_ref.shape[0]
    low = lanes((R, 128)) < K
    for k in range(n):
        shift = lanes((1, 128)) == 2
        shapes[k : k + 1, :] = (
            root_ref[k, R // 2 : R // 2 + 1, :] + jnp.where(shift, (k * GROUPS) * 1.0, 0.0)
        ) * SCALE
    for k in range(n // 2):
        left = root_ref[2 * k, 0 : R // 2, :]
        right = root_ref[2 * k + 1, 0 : R // 2, :]
        left = jnp.concatenate([left, pltpu.roll(left, K, 1)], axis=0)
        right = jnp.concatenate([pltpu.roll(right, K, 1), right], axis=0)
        pairs_scr[k] = jnp.where(low, left, right)
    source, count, pair_source = 0, n // 2, 0
    levels = []
    while count >= 1:
        levels.append((source, pair_source))
        if count > 1:
            pairs = pair_lanes(merge_up(pairs_scr[pl.ds(pair_source, count)], t_high, t_low))
            pairs_scr[pl.ds(pair_source + count, count // 2)] = pairs
            joined = merge_shape_rows(
                shapes[pl.ds(source, count, stride=2), :],
                shapes[pl.ds(source + 1, count, stride=2), :],
            )
            shapes[pl.ds(source + 2 * count, count), :] = joined
        source += 2 * count
        pair_source += count
        count //= 2
    couples = []
    for level, (source, pair_source) in enumerate(levels):
        pair = device >> (level + 1)
        left_row = shapes[pl.ds(source + 2 * pair, 1), :]
        right_row = shapes[pl.ds(source + 2 * pair + 1, 1), :]
        left = [jnp.broadcast_to(left_row[:, d : d + 1], (8, 128)) for d in range(4)]
        right = [jnp.broadcast_to(right_row[:, d : d + 1], (8, 128)) for d in range(4)]
        tile = sibling_tile(left, right, lane_u, row_y, row_z)
        couples.append(sibling_apply(tile, pairs_scr[pair_source + pair]))
    incoming = None
    for level in reversed(range(len(levels))):
        value = couples[level]
        if incoming is not None:
            value = value + push_down(incoming[None], t_high, t_low)[0]
        side = (device >> level) & 1
        keep_low = jnp.where(low, 1, 0) == (1 - side)
        incoming = jnp.where(keep_low, value, 0.0)
    value = couple[pl.ds(PAIR_OFFSETS[6], 1)] + push_down(incoming[None], t_high, t_low)
    for level in range(5, 0, -1):
        n = PAIRS >> level
        value = couple[pl.ds(PAIR_OFFSETS[level], n)] + push_down(
            children_of(value), t_high, t_low
        )
    down_ref[...] = push_down(children_of(value), t_high, t_low)


UNIT = 4


def couple_kernel(
    coupling_list, shape_ref, prev_ref, next_ref, coef_ref,
    leaf_couple,
    node_tab, high_tab, low_tab, halo_rows, halo_shape, sems,
    tile_h0, tile_l0, lhs0, tile_h1, tile_l1, lhs1,
):
    first_leaf = device_index() * LD
    low32 = lanes((R, 128)) < K
    copies = []
    for k, ref in enumerate((prev_ref, next_ref)):
        parts = ref[36].astype(F32)
        halo_rows[k] = parts[0:8] + parts[8:16] + parts[16:24]
        copies.append(pltpu.make_async_copy(halo_rows.at[k], halo_shape.at[k], sems.at[k]))
        copies[k].start()

    def own_table(m, carry):
        pair = coef_ref[m]
        high, low = halves(pair)
        high_tab[0, PAIRS // 2 + m] = high
        low_tab[0, m] = low
        high, low = halves(pltpu.roll(pair, K, 1))
        high_tab[1, PAIRS // 2 + m] = high
        low_tab[1, m] = low
        return carry

    lax.fori_loop(0, PAIRS, own_table, 0, unroll=4)
    for first_pair, ref in ((0, prev_ref), (PAIRS // 2 + PAIRS, next_ref)):

        def halo_table(m, carry):
            pair = ref[m]
            high_tab[0, first_pair + m] = pair
            high_tab[1, first_pair + m] = pltpu.roll(pair.astype(F32), K, 1).astype(BF16)
            return carry

        lax.fori_loop(0, PAIRS // 2, halo_table, 0, unroll=4)
    for swap in range(2):
        high_tab[swap, 2 * PAIRS] = jnp.zeros((R, 128), BF16)
        low_tab[swap, PAIRS] = jnp.zeros((R, 128), BF16)

    lane_u = lane_nodes()
    row8 = rows((8, 128))
    low8 = lanes((8, 128)) < K
    unit8 = jnp.where(row8 == 0, lane_u[0], jnp.where(row8 == 1, lane_u[1], lane_u[2])) * SCALE
    for copy in copies:
        copy.wait()

    def nodes(first_pair, read, shift, count):
        def one(m, carry):
            left = [read(d, 2 * m) for d in range(4)]
            right = [read(d, 2 * m + 1) for d in range(4)]
            left[2] = left[2] + shift
            right[2] = right[2] + shift

            def column(c):
                return jnp.where(row8 == 0, c[0], jnp.where(row8 == 1, c[1], c[2])) * SCALE

            left_nodes = column(left) + left[3] * unit8
            right_nodes = column(right) + right[3] * unit8
            node_tab[0, first_pair + m] = jnp.where(low8, left_nodes, right_nodes)
            node_tab[1, first_pair + m] = jnp.where(low8, right_nodes, left_nodes)
            return carry

        lax.fori_loop(0, count, one, 0, unroll=4)

    nodes(0, lambda d, k: halo_shape[0, d, HALF + k], -1.0 * GROUPS, PAIRS // 2)
    nodes(PAIRS // 2, lambda d, k: shape_ref[d, k], 0.0, PAIRS)
    nodes(PAIRS // 2 + PAIRS, lambda d, k: halo_shape[1, d, k], 1.0 * GROUPS, PAIRS // 2)

    row_y, row_z = row_nodes()

    def couple_tiles(i, u, tile_h, tile_l, lhs):
        radius = shape_ref[3, i] * SCALE
        center = [shape_ref[d, i] * SCALE for d in range(3)]
        own_x = [center[0] + radius * NODE[a] for a in range(4)]
        own_y = [center[1] + radius * row_y[h] for h in range(2)]
        own_z = center[2] + radius * row_z
        for q in range(4):
            picks = []
            for h in range(2):
                j = coupling_list[2 * q + h, i]
                e = jnp.where(j >= 0, j - first_leaf + HALF, 0)
                p = e >> 1
                own = (p >= PAIRS // 2) & (p < PAIRS // 2 + PAIRS) & (j >= 0)
                picks.append(
                    (
                        (e & 1) ^ h,
                        p,
                        jnp.where(j >= 0, p, 2 * PAIRS),
                        jnp.where(own, p - PAIRS // 2, PAIRS),
                    )
                )
            (s0, n0, c0, l0), (s1, n1, c1, l1) = picks
            base = jnp.where(low8, node_tab[s0, n0], node_tab[s1, n1])
            bx = jnp.broadcast_to(base[0:1], (8, 128))
            by = jnp.broadcast_to(base[1:2], (8, 128))
            bz = jnp.broadcast_to(base[2:3], (8, 128))
            tile = tile_from_axes(
                [jnp.square(bx - own_x[a]) for a in range(4)],
                [jnp.square(by - own_y[h]) for h in range(2)],
                jnp.square(bz - own_z),
            )
            high, low = halves(tile)
            span = slice(q * 128, (q + 1) * 128)
            tile_h[u, :, span] = high
            tile_l[u, :, span] = low
            lhs[u, 0:R, span] = jnp.where(low32, high_tab[s0, c0], high_tab[s1, c1])
            lhs[u, R : 2 * R, span] = jnp.where(low32, low_tab[s0, l0], low_tab[s1, l1])

    def couple_apply(u, tile_h, tile_l, lhs):
        both = dot_nt(lhs[u], tile_h[u])
        cross = dot_nt(lhs[u, 0:R], tile_l[u])
        return both[0:R] + both[R : 2 * R] + cross

    def couple_phase(n, new, old):
        for v in range(UNIT // 2):
            pair = (n - 1) * (UNIT // 2) + v + 2
            leaf_couple[pair] = jnp.concatenate(
                [couple_apply(2 * v, *old), couple_apply(2 * v + 1, *old)], axis=1
            )
        for u in range(UNIT):
            leaf = jnp.minimum(n * UNIT + u, LD - 1)
            couple_tiles(leaf, u, *new)

    buffers = ((tile_h0, tile_l0, lhs0), (tile_h1, tile_l1, lhs1))
    for ref in buffers[1]:
        ref[...] = jnp.zeros(ref.shape, ref.dtype)

    def couple_two(m, carry):
        couple_phase(2 * m, buffers[0], buffers[1])
        couple_phase(2 * m + 1, buffers[1], buffers[0])
        return carry

    lax.fori_loop(0, LD // UNIT // 2 + 1, couple_two, 0)


def finish_kernel(
    near_list, near_ref, p_ref, b_ref, prev_ref, next_ref, down_ref, leaf_couple,
    out_ref,
    p8,
):
    device = device_index()
    first_leaf = device * LD

    def finish(c, carry):
        value = (down_ref[c] + leaf_couple[c + 2]).astype(BF16)
        span = pl.ds(pl.multiple_of(c * 256, 256), 256)
        out_ref[:, span] = near_ref[:, span] + dot(
            value, block_diagonal(b_ref[2 * c], b_ref[2 * c + 1])
        )
        return carry

    lax.fori_loop(0, PAIRS, finish, 0, unroll=8)

    p8[...] = jnp.zeros(p8.shape, F32)
    eye = identity()
    for side, (halo_ref, group, step) in enumerate(((prev_ref, 0, -1), (next_ref, GROUPS - 1, 1))):
        origin_z = (device * GROUPS + group).astype(F32)
        p8[side, 0:3, :] = p_ref[:, group * 512 : group * 512 + 512]
        _, own = point_features(p8[side], origin_z)
        own = own_stack(own)
        coords = halo_ref[37].astype(F32) + halo_ref[38].astype(F32) + halo_ref[39].astype(F32)
        for k in range(4):
            far, _ = point_features(coords[8 * k : 8 * k + 8], origin_z)
            far_k = dot_nt(eye, far_stack(far)).astype(BF16)
            tiles = decay(dot(far_k, own)).astype(BF16)
            target = first_leaf + 4 * (group + step) + k
            products = dot(halo_ref[32 + k], tiles)
            for i in range(4):
                leaf = 4 * group + i
                weight = jnp.int32(0)
                for s in range(8):
                    weight = weight + jnp.where(near_list[s, leaf] == target, 1, 0)
                place = slice(leaf * P_SIZE, (leaf + 1) * P_SIZE)
                out_ref[:, place] += products[:, i * P_SIZE : (i + 1) * P_SIZE] * weight.astype(F32)


def shaped(*shape, dtype=F32):
    return jax.ShapeDtypeStruct(shape, dtype)


def vmem():
    return pl.BlockSpec(memory_space=pltpu.VMEM)


def smem():
    return pl.BlockSpec(memory_space=pltpu.SMEM)


PARAMS = pltpu.CompilerParams(vmem_limit_bytes=VMEM_LIMIT)


def per_device(charges, points, basis, transfer, near_list, coupling_list):
    near_rows = near_list.T
    coupling_rows = coupling_list.T
    devices = lax.axis_size("sub") * lax.axis_size("leaf")
    send_next, send_prev, coef, lev, root, shapes = pl.pallas_call(
        leaf_kernel,
        name="leaf_up",
        out_shape=(
            shaped(SEND, R, 128, dtype=BF16),
            shaped(SEND, R, 128, dtype=BF16),
            shaped(PAIRS, R, 128),
            shaped(PAIRS - 1, R, 128),
            shaped(devices, R // 2 + 8, 128),
            shaped(8, 256),
        ),
        in_specs=[vmem()] * 4,
        out_specs=[vmem()] * 6,
        scratch_shapes=[
            pltpu.VMEM((3, LD, 128), F32),
            pltpu.VMEM((256, 128), F32),
            pltpu.VMEM((8, 512), F32),
        ],
        compiler_params=PARAMS,
    )(charges, points, basis, transfer)

    roots = lax.all_to_all(root, AXES, 0, 0, tiled=True)
    forward = [(i, i + 1) for i in range(devices - 1)]
    backward = [(i + 1, i) for i in range(devices - 1)]
    from_prev = lax.ppermute(send_next, AXES, forward)
    from_next = lax.ppermute(send_prev, AXES, backward)

    tasks = pl.pallas_call(
        list_kernel,
        name="near_tasks",
        out_shape=shaped(8, LIST, dtype=jnp.int32),
        in_specs=[vmem()],
        out_specs=vmem(),
        compiler_params=PARAMS,
        cost_estimate=pl.CostEstimate(flops=1 << 24, bytes_accessed=1 << 16, transcendentals=0),
    )(near_rows)
    near = pl.pallas_call(
        near_kernel,
        name="near_field",
        out_shape=shaped(R, LD * P_SIZE),
        in_specs=[smem(), vmem(), vmem()],
        out_specs=vmem(),
        scratch_shapes=[
            pltpu.VMEM((2, 8, 512), F32),
            pltpu.VMEM((2, PAIRS, P_SIZE, 2 * FEATS), BF16),
            pltpu.VMEM((2 * LD, FEATS, P_SIZE), BF16),
            pltpu.VMEM((R, LD * P_SIZE), F32),
            pltpu.VMEM((BATCH // 2, 128, 256), F32),
            pltpu.VMEM((BATCH // 2, 128, 256), F32),
            pltpu.VMEM((BATCH // 2, 128, 256), BF16),
            pltpu.VMEM((BATCH // 2, 128, 256), BF16),
        ],
        compiler_params=PARAMS,
        cost_estimate=pl.CostEstimate(
            flops=2 * 460 * 128 * 128 * 128, bytes_accessed=4 << 20, transcendentals=460 * 32768
        ),
    )(tasks, charges, points)

    down = pl.pallas_call(
        down_kernel,
        name="tree_down",
        out_shape=shaped(PAIRS, R, 128),
        in_specs=[smem()] + [vmem()] * 3,
        out_specs=vmem(),
        scratch_shapes=[
            pltpu.VMEM((PAIRS - 1, R, 128), F32),
            pltpu.VMEM((devices, R, 128), F32),
            pltpu.VMEM((2 * devices, 128), F32),
        ],
        compiler_params=PARAMS,
    )(shapes, lev, transfer, roots)

    stages = [
        pltpu.VMEM((UNIT, K, 512), BF16),
        pltpu.VMEM((UNIT, K, 512), BF16),
        pltpu.VMEM((UNIT, 2 * R, 512), BF16),
    ]
    leaf_couple = pl.pallas_call(
        couple_kernel,
        name="leaf_couple",
        out_shape=shaped(PAIRS + 8, R, 128),
        in_specs=[smem()] * 2 + [vmem()] * 3,
        out_specs=vmem(),
        scratch_shapes=[
            pltpu.VMEM((2, 2 * PAIRS, 8, 128), F32),
            pltpu.VMEM((2, 2 * PAIRS + 1, R, 128), BF16),
            pltpu.VMEM((2, PAIRS + 1, R, 128), BF16),
            pltpu.VMEM((2, 8, 128), F32),
            pltpu.SMEM((2, 8, 128), F32),
            pltpu.SemaphoreType.DMA((2,)),
        ]
        + stages
        + stages,
        compiler_params=PARAMS,
    )(coupling_rows, shapes, from_prev, from_next, coef)

    return pl.pallas_call(
        finish_kernel,
        name="finish",
        out_shape=shaped(R, LD * P_SIZE),
        in_specs=[smem()] + [vmem()] * 7,
        out_specs=vmem(),
        scratch_shapes=[pltpu.VMEM((2, 8, 512), F32)],
        compiler_params=PARAMS,
    )(near_rows, near, points, basis, from_prev, from_next, down, leaf_couple)


def solution(mesh):
    in_specs = (
        P(None, AXES),
        P(None, AXES),
        P(AXES, None, None),
        P(),
        P(AXES, None),
        P(AXES, None),
    )
    return jax.shard_map(
        per_device, mesh=mesh, in_specs=in_specs, out_specs=P(None, AXES), check_vma=False
    )
```

time: 120 us -> 101 us (0.84)
  the two profiles are of different devices: /device:TPU:31 before, /device:TPU:4 now
where the time goes in v2:
time: 101 us
  Pallas kernels  83.6 us (83%)
  starting transfers between devices  15.3 us (15%)
  local copies, waits for them, and re-layouts  1.59 us (2%)
    pallas_call x1, Pallas kernels, per_device(): pl.pallas_call(near_kernel, name='near_field', out_shape=shaped(R, LD * P...  28.5 us
    pallas_call x1, Pallas kernels, per_device(): pl.pallas_call(couple_kernel, name='leaf_couple', out_shape=shaped(PAIRS...  24 us
    pallas_call x1, Pallas kernels, per_device(): pl.pallas_call(down_kernel, name='tree_down', out_shape=shaped(PAIRS, R,...  11.9 us
    pallas_call x1, Pallas kernels, per_device(): pl.pallas_call(finish_kernel, name='finish', out_shape=shaped(R, LD * P_S...  8.82 us
    pallas_call x1, Pallas kernels, per_device(): pl.pallas_call(leaf_kernel, name='leaf_up', out_shape=(shaped(SEND, R, 12...  8.05 us
    all_to_all x1, starting transfers between devices, per_device(): roots = lax.all_to_all(root, AXES, 0, 0, tiled=True)  6.1 us
    ppermute x1, starting transfers between devices, per_device(): from_next = lax.ppermute(send_prev, AXES, backward)  5.78 us
    ppermute x1, starting transfers between devices, per_device(): from_prev = lax.ppermute(send_next, AXES, forward)  3.37 us
  transfers between devices with their start and end apart: 3, of which 0 were waited for; matrix products, arithmetic and copies ran while one was open for 0% of the time, Pallas kernels for 55%

profile of v2, /device:TPU:4, one launch (start us, length us, event | category | flops | bytes accessed | tf_op | source)
XLA Modules:
  0.0 100.5 jit_solution(2885159416466957414)
XLA Ops:
  0.0 8.0 %leaf_up.1 = (bf16[40,32,128]{2,1,0:T(8,128)(2,1)}, bf16[40,32,128]{2,1,0:T(8,128)(2,1)}, f32[64,32,128]{2,1,0:T(8,128)}, f32[63,32,128]{2,1,0:T(8,128)}, f32[32,24,128]{2,1,0:T(8,128)}, /*index=5*/f32[8,256]{1,0:T(8,128)}) custom-call(bf16[32,16384]{1,0:T(8,128)(2,1)} %x_ref.3, f32[3,16384]{1,0:T(4,128)} %p_ref.5, bf16[128,64,128]{2,1,0:T(8,128)(2,1)} %b_ref.3, ...), custom_call_target="tpu_custom_call" | custom-call | tf_op jit(solution)/shard_map/leaf_up/pallas_call | solution.py:694
  8.0 6.1 %all-to-all-start = ((f32[32,24,128]{2,1,0:T(8,128)}), f32[32,24,128]{2,1,0:T(8,128)S(1)}, u32[]{:S(2)}, u32[]{:S(2)}) async-start(f32[32,24,128]{2,1,0:T(8,128)} %get-tuple-element.15), calls=%async_computation | async-start | bytes 786432 | tf_op jit(solution)/shard_map/all_to_all | solution.py:715
  14.2 3.4 %collective-permute-start = (bf16[40,32,128]{2,1,0:T(8,128)(2,1)}, bf16[40,32,128]{2,1,0:T(8,128)(2,1)S(1)}, u32[]{:S(2)}, u32[]{:S(2)}) collective-permute-start(bf16[40,32,128]{2,1,0:T(8,128)(2,1)} %get-tuple-element.11), channel_id=1, source_target_pairs={{0,1},{1,2},{2,3},{3,4},{4,5},{5,6},{6,7},{7,8},{8,9},{9,10},{10,1... | collective-permute-start | bytes 983048 | tf_op jit(solution)/shard_map/ppermute | solution.py:718
  17.5 5.8 %collective-permute-start.1 = (bf16[40,32,128]{2,1,0:T(8,128)(2,1)}, bf16[40,32,128]{2,1,0:T(8,128)(2,1)S(1)}, u32[]{:S(2)}, u32[]{:S(2)}) collective-permute-start(bf16[40,32,128]{2,1,0:T(8,128)(2,1)} %get-tuple-element.12), channel_id=1, source_target_pairs={{1,0},{2,1},{3,2},{4,3},{5,4},{6,5},{7,6},{8,7},{9,8},{10,9},{11,1... | collective-permute-start | bytes 983048 | tf_op jit(solution)/shard_map/ppermute | solution.py:719
  23.3 2.2 %near_tasks.1.list_ref = s32[8,896]{1,0:T(8,128)} custom-call(s32[8,128]{1,0:T(8,128)} %bitcast.3), custom_call_target="tpu_custom_call" | custom-call | flops 16777216 | bytes 65536 | tf_op jit(solution)/shard_map/near_tasks/pallas_call | solution.py:721
  25.6 28.5 %near_field.1.near_ref = f32[32,16384]{1,0:T(8,128)} custom-call(s32[8,896]{1,0:T(8,128)} %near_tasks.1.list_ref, bf16[32,16384]{1,0:T(8,128)(2,1)} %x_ref.3, f32[3,16384]{1,0:T(4,128)} %p_ref.5), custom_call_target="tpu_custom_call" | custom-call | flops 1929379840 | bytes 4194304 | tf_op jit(solution)/shard_map/near_field/pallas_call | solution.py:730
  54.1 0.0 collective-permute-done.prev_ref
  54.1 0.0 copy-start.1
  54.1 0.0 collective-permute-done.1.next_ref
  54.1 0.0 copy-start.2
  54.1 0.7 copy-done.1
  54.9 0.1 copy-done.2
  55.0 24.0 %leaf_couple.1 = f32[72,32,128]{2,1,0:T(8,128)} custom-call(s32[8,128]{1,0:T(8,128)} %bitcast.2, f32[8,256]{1,0:T(8,128)} %get-tuple-element.13.shape_ref, bf16[40,32,128]{2,1,0:T(8,128)(2,1)} %copy-done.1, bf16[40,32,128]{2,1,0:T(8,128)(2,1)} %copy-done.2, f32[64,32,128]{2,1,0:T(8,128)} %get-tuple-element.16.coef_ref), custom_call_target="tpu_custom_call" | custom-call | tf_op jit(solution)/shard_map/leaf_couple/pallas_call | solution.py:771
  79.0 0.0 all-to-all-done.root_ref
  79.0 0.0 copy-start
  79.0 0.7 copy-done
  79.8 11.9 %tree_down.1.down_ref = f32[64,32,128]{2,1,0:T(8,128)} custom-call(f32[8,256]{1,0:T(8,128)} %get-tuple-element.13.shape_ref, f32[63,32,128]{2,1,0:T(8,128)} %get-tuple-element.14.lev_ref, f32[2,64,64]{2,1,0:T(8,128)} %t_ref.3, f32[32,24,128]{2,1,0:T(8,128)} %copy-done), custom_call_target="tpu_custom_call" | custom-call | tf_op jit(solution)/shard_map/tree_down/pallas_call | solution.py:752
  91.7 8.8 %finish.1 = f32[32,16384]{1,0:T(8,128)} custom-call(s32[8,128]{1,0:T(8,128)} %bitcast.4, f32[32,16384]{1,0:T(8,128)} %near_field.1.near_ref, f32[3,16384]{1,0:T(4,128)} %p_ref.5, bf16[128,64,128]{2,1,0:T(8,128)(2,1)} %b_ref.3, bf16[40,32,128]{2,1,0:T(8,128)(2,1)} %copy-done.1, bf16[40,32,128]{2,1,0:T(8,128)(2,1)} %copy-done.2, ...), custom_call_target="tpu_custom_call" | custom-call | tf_op jit(solution)/shard_map/finish/pallas_call | solution.py:790
Async XLA Ops:
  8.0 71.0 %all-to-all-start = ((f32[32,24,128]{2,1,0:T(8,128)}), f32[32,24,128]{2,1,0:T(8,128)S(1)}, u32[]{:S(2)}, u32[]{:S(2)}) async-start(f32[32,24,128]{2,1,0:T(8,128)} %get-tuple-element.15), calls=%async_computation | async-start | bytes 786432 | tf_op jit(solution)/shard_map/all_to_all | solution.py:715
  14.2 39.9 %collective-permute-start = (bf16[40,32,128]{2,1,0:T(8,128)(2,1)}, bf16[40,32,128]{2,1,0:T(8,128)(2,1)S(1)}, u32[]{:S(2)}, u32[]{:S(2)}) collective-permute-start(bf16[40,32,128]{2,1,0:T(8,128)(2,1)} %get-tuple-element.11), channel_id=1, source_target_pairs={{0,1},{1,2},{2,3},{3,4},{4,5},{5,6},{6,7},{7,8},{8,9},{9,10},{10,1... | collective-permute-start | bytes 983048 | tf_op jit(solution)/shard_map/ppermute | solution.py:718
  17.5 36.6 %collective-permute-start.1 = (bf16[40,32,128]{2,1,0:T(8,128)(2,1)}, bf16[40,32,128]{2,1,0:T(8,128)(2,1)S(1)}, u32[]{:S(2)}, u32[]{:S(2)}) collective-permute-start(bf16[40,32,128]{2,1,0:T(8,128)(2,1)} %get-tuple-element.12), channel_id=1, source_target_pairs={{1,0},{2,1},{3,2},{4,3},{5,4},{6,5},{7,6},{8,7},{9,8},{10,9},{11,1... | collective-permute-start | bytes 983048 | tf_op jit(solution)/shard_map/ppermute | solution.py:719
  54.1 0.8 copy-start.1
  54.1 0.9 copy-start.2
  79.0 0.7 copy-start

commit v3 on v2

v3 whole, which is shorter than its diff:
```python
import functools
import math

import jax
import jax.numpy as jnp
from jax import lax
from jax.experimental import pallas as pl
from jax.experimental.pallas import tpu as pltpu
from jax.sharding import PartitionSpec as P

P_SIZE = 128
K = 64
R = 32
LD = 128
PAIRS = LD // 2
GROUPS = LD // 4
TABLE = 257
HALF = LD // 2
NEAR_REACH = 8
FEATS = 64
BATCH = 8
LIST = 896
SEND = 72
SCALE = 0.5 * math.log2(math.e)
NODE = [math.cos((2 * a + 1) * math.pi / 8) for a in range(4)]
AXES = ("leaf", "sub")
F32 = jnp.float32
BF16 = jnp.bfloat16
NT = (((1,), (1,)), ((), ()))
TINY = 1e-30
VMEM_LIMIT = 32 * 1024 * 1024


def lanes(shape):
    return lax.broadcasted_iota(jnp.int32, shape, len(shape) - 1)


def rows(shape):
    return lax.broadcasted_iota(jnp.int32, shape, len(shape) - 2)


def dot(a, b):
    return jnp.dot(a, b, preferred_element_type=F32)


def dot_nt(a, b):
    return lax.dot_general(a, b, NT, preferred_element_type=F32)


def halves(value):
    high = value.astype(BF16)
    return high, (value - high.astype(F32)).astype(BF16)


def thirds(value):
    first = value.astype(BF16).astype(F32)
    rest = value - first
    second = rest.astype(BF16).astype(F32)
    return first, second, rest - second


def unit_node(index):
    return jnp.where(
        index == 0,
        NODE[0],
        jnp.where(index == 1, NODE[1], jnp.where(index == 2, NODE[2], NODE[3])),
    ).astype(F32)


def lane_nodes():
    b = lanes((8, 128)) & 63
    return [unit_node(b >> 4), unit_node((b >> 2) & 3), unit_node(b & 3)]


def row_nodes():
    r = rows((8, 128))
    return [unit_node(r >> 2), unit_node((r >> 2) + 2)], unit_node(r & 3)


def decay(t):
    t = jnp.maximum(t, TINY)
    return jnp.exp2(-(t * lax.rsqrt(t)))


def tile_from_axes(x_sq, y_sq, z_sq):
    yz = [y_sq[0] + z_sq, y_sq[1] + z_sq]
    return decay(jnp.concatenate([x_sq[k // 2] + yz[k % 2] for k in range(8)], axis=0))


def doubled_transfer(t_ref):
    flat = t_ref[...].reshape(2 * K, K)
    return jnp.concatenate([flat, flat], axis=1)


def device_index():
    return lax.axis_index("leaf") * lax.axis_size("sub") + lax.axis_index("sub")


def merge_up(pairs, t_high, t_low):
    n = pairs.shape[0]
    high, low = halves(pairs.reshape(n * R, 128))
    out = dot(high, t_high) + dot(high, t_low) + dot(low, t_high)
    return out.reshape(n, R, 128)


def pair_lanes(clusters):
    n = clusters.shape[0]
    split = clusters.reshape(n // 2, 2, R, 128)
    return jnp.where(lanes((1, R, 128)) < K, split[:, 0], split[:, 1])


def push_down(value, t_high, t_low):
    n = value.shape[0]
    high, low = halves(value.reshape(n * R, 128))
    out = dot_nt(high, t_high) + dot_nt(high, t_low) + dot_nt(low, t_high)
    return out.reshape(n, R, 128)


def children_of(pairs):
    lane = lanes((1, R, 128))
    left = jnp.where(lane < K, pairs, 0.0)
    right = jnp.where(lane < K, 0.0, pairs)
    return jnp.stack([left, right], axis=1).reshape(2 * pairs.shape[0], R, 128)


def merge_shape_rows(left, right):
    lane = lanes(left.shape)
    sep = left - right
    gap = jnp.sqrt(jnp.sum(jnp.where(lane < 3, sep * sep, 0.0), axis=1, keepdims=True))
    radius = jnp.maximum(left, right) + 0.5 * gap
    return jnp.where(lane == 3, radius, jnp.where(lane < 3, 0.5 * (left + right), 0.0))


def sibling_tile(left, right, lane_u, row_y, row_z):
    low = lanes((8, 128)) < K
    alpha = jnp.where(low, left[3], right[3])
    beta = jnp.where(low, right[3], left[3])
    base = [jnp.where(low, left[d] - right[d], right[d] - left[d]) - beta * lane_u[d] for d in range(3)]
    x_sq = [jnp.square(base[0] + alpha * NODE[a]) for a in range(4)]
    y_sq = [jnp.square(base[1] + alpha * row_y[h]) for h in range(2)]
    z_sq = jnp.square(base[2] + alpha * row_z)
    return tile_from_axes(x_sq, y_sq, z_sq)


def sibling_apply(tile, pair):
    low = lanes((R, 128)) < K
    swapped = pltpu.roll(pair, K, 1)
    stacked = jnp.concatenate(
        [jnp.where(low, swapped, 0.0), jnp.where(low, 0.0, swapped)], axis=0
    )
    high, low_part = halves(stacked)
    t_high, t_low = halves(tile)
    t_high = jnp.concatenate([t_high, t_high], axis=0)
    t_low = jnp.concatenate([t_low, t_low], axis=0)
    out = dot_nt(high, t_high) + dot_nt(high, t_low) + dot_nt(low_part, t_high)
    return jnp.where(low, out[:R], out[R:])


LEVEL_OFFSETS = [0, 128, 192, 224, 240, 248, 252, 254]
PAIR_OFFSETS = [0, 0, 32, 48, 56, 60, 62]


def block_diagonal(left, right):
    zero = jnp.zeros(left.shape, left.dtype)
    return jnp.concatenate(
        [jnp.concatenate([left, zero], axis=1), jnp.concatenate([zero, right], axis=1)], axis=0
    )


def leaf_kernel(
    x_ref, p_ref, b_ref, t_ref,
    send_next, send_prev, high_ref, low_ref, lev_ref, root_ref, shape_ref,
    coef, pts, shapes, p8,
):
    origin = (device_index() * GROUPS).astype(F32)
    low32 = lanes((R, 128)) < K

    def leaf_pair(c, carry):
        both = []
        for side in range(2):
            leaf = 2 * c + side
            x = x_ref[:, pl.ds(pl.multiple_of(leaf * P_SIZE, P_SIZE), P_SIZE)]
            weights = b_ref[leaf]
            value = dot_nt(x, jnp.concatenate([weights, weights], axis=0))
            high_ref[leaf], low_ref[leaf] = halves(value)
            both.append(value)
        coef[c] = jnp.where(low32, both[0], both[1])
        return carry

    lax.fori_loop(0, PAIRS, leaf_pair, 0, unroll=8)

    t_high, t_low = halves(doubled_transfer(t_ref))
    pairs = coef[...]
    for level in range(1, 7):
        pairs = pair_lanes(merge_up(pairs, t_high, t_low))
        lev_ref[pl.ds(PAIR_OFFSETS[level], pairs.shape[0])] = pairs
    root = merge_up(pairs, t_high, t_low)[0]

    for i in range(LD):
        for d in range(3):
            pts[d, i : i + 1, :] = p_ref[d : d + 1, i * P_SIZE : (i + 1) * P_SIZE]
    centers, squares = [], 0.0
    for d in range(3):
        coords = (pts[d] - origin if d == 2 else pts[d]) * SCALE
        center = jnp.sum(coords, axis=1, keepdims=True) * (1.0 / P_SIZE)
        centers.append(center)
        squares = squares + jnp.square(coords - center)
    radius = jnp.sqrt(jnp.max(squares, axis=1, keepdims=True))
    lane = lanes((LD, 128))
    shapes[0:LD, :] = jnp.where(
        lane == 0,
        centers[0],
        jnp.where(
            lane == 1,
            centers[1],
            jnp.where(lane == 2, centers[2], jnp.where(lane == 3, radius, 0.0)),
        ),
    )
    count = LD // 2
    for level in range(1, 8):
        source = LEVEL_OFFSETS[level - 1]
        joined = merge_shape_rows(
            shapes[pl.ds(source, count, stride=2), :],
            shapes[pl.ds(source + 1, count, stride=2), :],
        )
        shapes[pl.ds(LEVEL_OFFSETS[level], count), :] = joined
        count //= 2
    shape_rows = jnp.concatenate(
        [jnp.transpose(shapes[0:128, :])[0:8], jnp.transpose(shapes[128:256, :])[0:8]], axis=1
    )
    shape_ref[...] = shape_rows
    low = lanes((R // 2, 128)) < K
    block = jnp.concatenate(
        [
            jnp.where(low, root[0 : R // 2], root[R // 2 : R]),
            jnp.broadcast_to(shapes[254:255, :], (8, 128)),
        ],
        axis=0,
    )
    root_ref[...] = jnp.broadcast_to(block[None], root_ref.shape)

    p8[...] = jnp.zeros((8, 512), F32)
    for send, first_pair, group in ((send_next, PAIRS // 2, GROUPS - 1), (send_prev, 0, 0)):

        def copy_pair(m, carry):
            send[m], send[32 + m] = halves(coef[first_pair + m])
            return carry

        lax.fori_loop(0, PAIRS // 2, copy_pair, 0, unroll=8)
        parts = thirds(shape_rows[:, 0:128])
        send[68] = jnp.concatenate(list(parts) + [jnp.zeros((8, 128), F32)], axis=0).astype(BF16)
        p8[0:3, :] = p_ref[:, group * 512 : group * 512 + 512]
        parts = thirds(p8[...])
        for k in range(4):
            send[64 + k] = x_ref[:, group * 512 + k * P_SIZE : group * 512 + (k + 1) * P_SIZE]
        for part in range(3):
            send[69 + part] = jnp.concatenate(
                [parts[part][:, k * P_SIZE : (k + 1) * P_SIZE] for k in range(4)], axis=0
            ).astype(BF16)


def list_kernel(near_ref, coupling_ref, list_ref, count_ref, index_ref):
    first_leaf = device_index() * LD
    lane8 = lanes((8, 128))
    row8 = rows((8, 128))
    offset = jnp.where(near_ref[...] >= 0, near_ref[...] - first_leaf - lane8, 1000)

    def slots_at(delta):
        return jnp.sum(jnp.where(offset == delta, 1.0, 0.0), axis=0, keepdims=True)

    forward = jnp.concatenate([slots_at(delta) for delta in range(8)], axis=0)
    reverse = jnp.concatenate(
        [jnp.zeros((1, 128), F32)] + [slots_at(-delta) for delta in range(1, 8)], axis=0
    )
    count_ref[0:8, :] = forward
    count_ref[8:16, :] = reverse
    backward = jnp.concatenate(
        [jnp.zeros((1, 128), F32)]
        + [pltpu.roll(reverse[delta : delta + 1, :], 128 - delta, 1) for delta in range(1, 8)],
        axis=0,
    )
    turned = (row8 == 1) & ((lane8 & 3) == 2)
    leaf = lane8.astype(F32)
    other = leaf + row8.astype(F32)
    first = jnp.where(turned, other, leaf)
    second = jnp.where(turned, leaf, other)
    to_first = jnp.where(turned, backward, forward)
    to_second = jnp.where(turned, forward, backward)
    odd = jnp.where(turned, lane8, lane8 + row8) & 1
    wanted = (lane8 + row8 < LD) & (forward + backward > 0.0)
    earlier = jnp.where(rows((128, 128)) < lanes((128, 128)), 1.0, 0.0).astype(BF16)
    place = jnp.full((8, 128), -1.0, F32)
    most = jnp.zeros((1, 1), F32)
    for parity in range(2):
        flags = jnp.where(wanted & (odd == parity), 1.0, 0.0)
        rank = dot(flags.astype(BF16), earlier)
        totals = jnp.sum(flags, axis=1, keepdims=True)
        before = jnp.zeros((1, 1), F32)
        starts = []
        for delta in range(8):
            starts.append(before)
            before = before + totals[delta : delta + 1, :]
        rank = rank + jnp.concatenate(starts, axis=0)
        place = jnp.where(flags > 0.0, 2.0 * rank + (1.0 * BATCH + parity), place)
        most = jnp.maximum(most, before)
    task_rows = []
    for delta in range(8):
        pick = slice(delta, delta + 1)
        task_rows.append(
            jnp.where(
                row8 == 0,
                first[pick],
                jnp.where(
                    row8 == 1,
                    second[pick],
                    jnp.where(
                        row8 == 2, to_first[pick], jnp.where(row8 == 3, to_second[pick], 0.0)
                    ),
                ),
            ).astype(BF16)
        )
    tasks = jnp.concatenate(task_rows, axis=1)
    slot_row = rows((128, 128)).astype(F32)
    for m in range(LIST // 128):
        chosen = jnp.concatenate(
            [
                jnp.where(place[delta : delta + 1, :] == slot_row + 128.0 * m, 1.0, 0.0).astype(BF16)
                for delta in range(8)
            ],
            axis=1,
        )
        part = dot_nt(tasks, chosen)
        part = jnp.where(row8 == 4, 2.0 * most, part)
        list_ref[:, m * 128 : (m + 1) * 128] = part.astype(jnp.int32)

    target = coupling_ref[...]
    reach = target - first_leaf + HALF
    swap = ((reach ^ row8) & 1) * (PAIRS // 2)
    entry = jnp.where(
        reach < HALF,
        LD + (reach >> 1) + swap,
        jnp.where(reach < HALF + LD, reach - HALF, LD + HALF + ((reach - HALF - LD) >> 1) + swap),
    )
    index_ref[0:8, :] = jnp.where(target >= 0, entry, TABLE - 1)
    index_ref[8:16, :] = jnp.where(target >= 0, reach, 0)


def point_features(points8, origin_z):
    row = rows(points8.shape)
    center = jnp.where(row == 2, origin_z + 0.5, 1.0)
    v = jnp.where(row < 3, (points8 - center) * SCALE, 0.0)
    norm = jnp.sum(v * v, axis=0, keepdims=True)
    far = jnp.where(row == 3, norm, jnp.where(row == 4, 1.0, v))
    own = jnp.where(row == 3, 1.0, jnp.where(row == 4, norm, -2.0 * v))
    return far, own


def far_stack(value):
    first, second, third = thirds(value)
    none = jnp.zeros(value.shape, F32)
    return jnp.concatenate(
        [first, first, first, second, second, third, none, none], axis=0
    ).astype(BF16)


def own_stack(value):
    first, second, third = thirds(value)
    none = jnp.zeros(value.shape, F32)
    return jnp.concatenate(
        [first, second, third, first, second, first, none, none], axis=0
    ).astype(BF16)


def identity():
    return jnp.where(rows((128, 128)) == lanes((128, 128)), 1.0, 0.0).astype(BF16)


def near_kernel(
    list_ref, x_ref, p_ref, out_ref,
    p8, far_feat, own_feat, back, tile0, tile1,
):
    first_group = device_index() * GROUPS
    p8[...] = jnp.zeros(p8.shape, F32)
    eye = identity()

    def features(m, carry):
        for v in range(4):
            g = 4 * m + v
            p8[v, 0:3, :] = p_ref[:, pl.ds(pl.multiple_of(g * 512, 512), 512)]
            coords = p8[v]
            origin_z = (first_group + g).astype(F32)
            far, own = point_features(coords, origin_z)
            _, own_up = point_features(coords, origin_z + 1.0)
            far = far_stack(far)
            own = own_stack(own)
            own_up = own_stack(own_up)
            parts = [far[:, k * P_SIZE : (k + 1) * P_SIZE] for k in range(4)]
            turned = dot_nt(eye, jnp.concatenate(parts, axis=0)).astype(BF16)
            far_feat[2 * g] = turned[:, 0:128]
            far_feat[2 * g + 1] = turned[:, 128:256]
            for k in range(4):
                part = slice(k * P_SIZE, (k + 1) * P_SIZE)
                own_feat[4 * g + k] = own[:, part]
                own_feat[LD + 4 * g + k] = own_up[:, part]
        return carry

    lax.fori_loop(0, GROUPS // 4, features, 0)

    out_ref[...] = x_ref[...].astype(F32)
    for ref in (back, tile0, tile1):
        ref[...] = jnp.zeros(ref.shape, ref.dtype)

    total = list_ref[4, 0]
    steps = (total + BATCH - 1) // BATCH + 1
    low = lanes((128, 128)) < K

    def leaf_slice(i):
        return pl.ds(pl.multiple_of(i * P_SIZE, P_SIZE), P_SIZE)

    def phase(n, tile_new, tile_old):
        for u in range(BATCH // 2):
            far, own = [], []
            for h in range(2):
                k = (n + 1) * BATCH + 2 * u + h
                i, j = list_ref[0, k], list_ref[1, k]
                variant = ((j >> 2) - (i >> 2)) * LD
                far.append(far_feat[j >> 1])
                own.append(own_feat[variant + i])
            dist = dot(jnp.where(low, far[0], far[1]), block_diagonal(own[0], own[1]))
            tile_new[u] = decay(dist).astype(BF16)
            for h in range(2):
                k = n * BATCH + 2 * u + h
                i, j = list_ref[0, k], list_ref[1, k]
                tile = tile_old[u, :, h * 128 : h * 128 + 128]
                to_i = dot(x_ref[:, leaf_slice(j)], tile) * list_ref[2, k].astype(F32)
                to_j = dot_nt(x_ref[:, leaf_slice(i)], tile) * list_ref[3, k].astype(F32)
                out_ref[:, leaf_slice(i)] += to_i
                back[:, leaf_slice(j)] += to_j

    def two_phases(m, carry):
        phase(2 * m, tile0, tile1)
        phase(2 * m + 1, tile1, tile0)
        return carry

    lax.fori_loop(0, (steps + 1) // 2, two_phases, 0)
    out_ref[...] += back[...]


def down_kernel(
    shape_ref, lev_ref, t_ref, root_ref, down_ref, couple, pairs_scr, shapes,
):
    lane_u = lane_nodes()
    row_y, row_z = row_nodes()

    def sibling(pair, cluster):
        left = [shape_ref[d, cluster] for d in range(4)]
        right = [shape_ref[d, cluster + 1] for d in range(4)]
        tile = sibling_tile(left, right, lane_u, row_y, row_z)
        couple[pair] = sibling_apply(tile, lev_ref[pair])

    def siblings(m, carry):
        for u in range(21):
            pair = 21 * m + u
            sibling(pair, LD + 2 * pair)
        return carry

    lax.fori_loop(0, 3, siblings, 0)

    t_high, t_low = halves(doubled_transfer(t_ref))
    device = device_index()
    n = root_ref.shape[0]
    low = lanes((R, 128)) < K
    for k in range(n):
        shift = lanes((1, 128)) == 2
        shapes[k : k + 1, :] = (
            root_ref[k, R // 2 : R // 2 + 1, :] + jnp.where(shift, (k * GROUPS) * SCALE, 0.0)
        )
    for k in range(n // 2):
        left = root_ref[2 * k, 0 : R // 2, :]
        right = root_ref[2 * k + 1, 0 : R // 2, :]
        left = jnp.concatenate([left, pltpu.roll(left, K, 1)], axis=0)
        right = jnp.concatenate([pltpu.roll(right, K, 1), right], axis=0)
        pairs_scr[k] = jnp.where(low, left, right)
    source, count, pair_source = 0, n // 2, 0
    levels = []
    while count >= 1:
        levels.append((source, pair_source))
        if count > 1:
            pairs = pair_lanes(merge_up(pairs_scr[pl.ds(pair_source, count)], t_high, t_low))
            pairs_scr[pl.ds(pair_source + count, count // 2)] = pairs
            joined = merge_shape_rows(
                shapes[pl.ds(source, count, stride=2), :],
                shapes[pl.ds(source + 1, count, stride=2), :],
            )
            shapes[pl.ds(source + 2 * count, count), :] = joined
        source += 2 * count
        pair_source += count
        count //= 2
    couples = []
    for level, (source, pair_source) in enumerate(levels):
        pair = device >> (level + 1)
        left_row = shapes[pl.ds(source + 2 * pair, 1), :]
        right_row = shapes[pl.ds(source + 2 * pair + 1, 1), :]
        left = [jnp.broadcast_to(left_row[:, d : d + 1], (8, 128)) for d in range(4)]
        right = [jnp.broadcast_to(right_row[:, d : d + 1], (8, 128)) for d in range(4)]
        tile = sibling_tile(left, right, lane_u, row_y, row_z)
        couples.append(sibling_apply(tile, pairs_scr[pair_source + pair]))
    incoming = None
    for level in reversed(range(len(levels))):
        value = couples[level]
        if incoming is not None:
            value = value + push_down(incoming[None], t_high, t_low)[0]
        side = (device >> level) & 1
        keep_low = jnp.where(low, 1, 0) == (1 - side)
        incoming = jnp.where(keep_low, value, 0.0)
    value = couple[pl.ds(PAIR_OFFSETS[6], 1)] + push_down(incoming[None], t_high, t_low)
    for level in range(5, 0, -1):
        n = PAIRS >> level
        value = couple[pl.ds(PAIR_OFFSETS[level], n)] + push_down(
            children_of(value), t_high, t_low
        )
    down_ref[...] = push_down(children_of(value), t_high, t_low)


UNIT = 4


def couple_kernel(
    entries, shape_ref, prev_ref, next_ref, high_ref, low_ref,
    leaf_couple,
    shape_tab, high_tab, low_tab, halo_rows, halo_shape, sems,
    tile_h0, tile_l0, lhs0, tile_h1, tile_l1, lhs1,
):
    copies = [
        pltpu.make_async_copy(high_ref, high_tab.at[0:LD], sems.at[2]),
        pltpu.make_async_copy(low_ref, low_tab.at[0:LD], sems.at[3]),
    ]
    for k, ref in enumerate((prev_ref, next_ref)):
        parts = ref[68].astype(F32)
        halo_rows[k] = parts[0:8] + parts[8:16] + parts[16:24]
        copies.append(pltpu.make_async_copy(halo_rows.at[k], halo_shape.at[k], sems.at[k]))
    for copy in copies:
        copy.start()
    low32 = lanes((R, 128)) < K
    lane_u = lane_nodes()
    row8 = rows((8, 128))
    low8 = lanes((8, 128)) < K

    def shape_rows(read, k, shift):
        return jnp.where(
            row8 == 0,
            read(0, k),
            jnp.where(row8 == 1, read(1, k), jnp.where(row8 == 2, read(2, k) + shift, read(3, k))),
        )

    def own_nodes(m, carry):
        shape_tab[HALF + m] = shape_rows(lambda d, k: shape_ref[d, k], m, 0.0)
        return carry

    lax.fori_loop(0, LD, own_nodes, 0, unroll=8)
    for copy in copies[2:]:
        copy.wait()
    for side, ref in enumerate((prev_ref, next_ref)):
        first = LD + side * HALF

        def halo_pair(m, carry):
            def read(d, k):
                return halo_shape[side, d, k]

            source = HALF if side == 0 else 0
            place = 0 if side == 0 else HALF + LD
            shift = (2.0 * side - 1.0) * GROUPS * SCALE
            for h in range(2):
                shape_tab[place + 2 * m + h] = shape_rows(read, source + 2 * m + h, shift)
            for tab, place in ((high_tab, m), (low_tab, 32 + m)):
                pair = ref[place]
                tab[first + m] = pair
                tab[first + PAIRS // 2 + m] = pltpu.roll(pair.astype(F32), K, 1).astype(BF16)
            return carry

        lax.fori_loop(0, PAIRS // 2, halo_pair, 0, unroll=4)
    high_tab[TABLE - 1] = jnp.zeros((R, 128), BF16)
    low_tab[TABLE - 1] = jnp.zeros((R, 128), BF16)
    for copy in copies[:2]:
        copy.wait()

    row_y, row_z = row_nodes()

    def couple_tiles(pair, u, tile_h, tile_l, lhs):
        leaves = (2 * pair, 2 * pair + 1)
        own = jnp.where(low8, shape_tab[HALF + leaves[0]], shape_tab[HALF + leaves[1]])
        radius = jnp.broadcast_to(own[3:4], (8, 128))
        own = [jnp.broadcast_to(own[d : d + 1], (8, 128)) + radius * lane_u[d] for d in range(3)]
        for s in range(8):
            e0, e1 = entries[8 + s, leaves[0]], entries[8 + s, leaves[1]]
            far = jnp.where(low8, shape_tab[e0], shape_tab[e1])
            reach = jnp.broadcast_to(far[3:4], (8, 128))
            gap = [own[d] - jnp.broadcast_to(far[d : d + 1], (8, 128)) for d in range(3)]
            tile = tile_from_axes(
                [jnp.square(gap[0] - reach * NODE[b]) for b in range(4)],
                [jnp.square(gap[1] - reach * row_y[h]) for h in range(2)],
                jnp.square(gap[2] - reach * row_z),
            )
            high, low = halves(tile)
            tile_h[u, s * K : (s + 1) * K, :] = high
            tile_l[u, s * K : (s + 1) * K, :] = low
        for q in range(4):
            span = slice(q * 128, (q + 1) * 128)
            for h in range(2):
                e0, e1 = entries[2 * q, leaves[h]], entries[2 * q + 1, leaves[h]]
                lhs[u, h * R : (h + 1) * R, span] = jnp.where(low32, high_tab[e0], high_tab[e1])
                lhs[u, (2 + h) * R : (3 + h) * R, span] = jnp.where(
                    low32, low_tab[e0], low_tab[e1]
                )

    def couple_apply(u, tile_h, tile_l, lhs):
        both = dot(lhs[u], tile_h[u])
        both = both[0 : 2 * R] + both[2 * R : 4 * R] + dot(lhs[u, 0 : 2 * R], tile_l[u])
        return jnp.where(low32, both[0:R], both[R : 2 * R])

    def couple_phase(n, new, old):
        for u in range(UNIT):
            leaf_couple[(n - 1) * UNIT + u + UNIT] = couple_apply(u, *old)
            couple_tiles(jnp.minimum(n * UNIT + u, PAIRS - 1), u, *new)

    buffers = ((tile_h0, tile_l0, lhs0), (tile_h1, tile_l1, lhs1))
    for ref in buffers[1]:
        ref[...] = jnp.zeros(ref.shape, ref.dtype)

    def couple_two(m, carry):
        couple_phase(2 * m, buffers[0], buffers[1])
        couple_phase(2 * m + 1, buffers[1], buffers[0])
        return carry

    lax.fori_loop(0, PAIRS // UNIT // 2 + 1, couple_two, 0)


def finish_kernel(
    counts, near_ref, p_ref, b_ref, prev_ref, next_ref, down_ref, leaf_couple,
    out_ref,
    p8, coords,
):
    device = device_index()

    def finish(c, carry):
        value = (down_ref[c] + leaf_couple[c + UNIT]).astype(BF16)
        span = pl.ds(pl.multiple_of(c * 256, 256), 256)
        out_ref[:, span] = near_ref[:, span] + dot(
            value, block_diagonal(b_ref[2 * c], b_ref[2 * c + 1])
        )
        return carry

    lax.fori_loop(0, PAIRS, finish, 0, unroll=8)

    p8[...] = jnp.zeros(p8.shape, F32)
    eye = identity()
    sides = ((prev_ref, 0), (next_ref, GROUPS - 1))
    for side, (halo_ref, group) in enumerate(sides):
        p8[side, 0:3, :] = p_ref[:, group * 512 : group * 512 + 512]
        coords[side] = halo_ref[69].astype(F32) + halo_ref[70].astype(F32) + halo_ref[71].astype(F32)

    def edge(k, carry):
        for side, (halo_ref, group) in enumerate(sides):
            origin_z = (device * GROUPS + group).astype(F32)
            _, own = point_features(p8[side], origin_z)
            far, _ = point_features(coords[side, pl.ds(pl.multiple_of(8 * k, 8), 8), :], origin_z)
            far = dot_nt(eye, far_stack(far)).astype(BF16)
            tiles = decay(dot(far, own_stack(own))).astype(BF16)
            products = dot(halo_ref[64 + k], tiles)
            for i in range(4):
                delta = (4 + i - k) if side == 0 else (4 + k - i)
                weight = counts[8 * (1 - side) + jnp.clip(delta, 0, 7), 4 * group + i]
                place = slice((4 * group + i) * P_SIZE, (4 * group + i + 1) * P_SIZE)
                out_ref[:, place] += products[:, i * P_SIZE : (i + 1) * P_SIZE] * weight
        return carry

    lax.fori_loop(0, 4, edge, 0)


def shaped(*shape, dtype=F32):
    return jax.ShapeDtypeStruct(shape, dtype)


def vmem():
    return pl.BlockSpec(memory_space=pltpu.VMEM)


def smem():
    return pl.BlockSpec(memory_space=pltpu.SMEM)


PARAMS = pltpu.CompilerParams(vmem_limit_bytes=VMEM_LIMIT)


def per_device(charges, points, basis, transfer, near_list, coupling_list):
    near_rows = near_list.T
    coupling_rows = coupling_list.T
    devices = lax.axis_size("sub") * lax.axis_size("leaf")
    send_next, send_prev, high, low, lev, root, shapes = pl.pallas_call(
        leaf_kernel,
        name="leaf_up",
        out_shape=(
            shaped(SEND, R, 128, dtype=BF16),
            shaped(SEND, R, 128, dtype=BF16),
            shaped(LD, R, 128, dtype=BF16),
            shaped(LD, R, 128, dtype=BF16),
            shaped(PAIRS - 1, R, 128),
            shaped(devices, R // 2 + 8, 128),
            shaped(8, 256),
        ),
        in_specs=[vmem()] * 4,
        out_specs=[vmem()] * 7,
        scratch_shapes=[
            pltpu.VMEM((PAIRS, R, 128), F32),
            pltpu.VMEM((3, LD, 128), F32),
            pltpu.VMEM((256, 128), F32),
            pltpu.VMEM((8, 512), F32),
        ],
        compiler_params=PARAMS,
    )(charges, points, basis, transfer)

    roots = lax.all_to_all(root, AXES, 0, 0, tiled=True)
    forward = [(i, i + 1) for i in range(devices - 1)]
    backward = [(i + 1, i) for i in range(devices - 1)]
    from_prev = lax.ppermute(send_next, AXES, forward)
    from_next = lax.ppermute(send_prev, AXES, backward)

    tasks, counts, entries = pl.pallas_call(
        list_kernel,
        name="lists",
        out_shape=(
            shaped(8, LIST, dtype=jnp.int32),
            shaped(16, 128),
            shaped(16, 128, dtype=jnp.int32),
        ),
        in_specs=[vmem()] * 2,
        out_specs=[vmem()] * 3,
        compiler_params=PARAMS,
        cost_estimate=pl.CostEstimate(flops=1 << 24, bytes_accessed=1 << 16, transcendentals=0),
    )(near_rows, coupling_rows)
    near = pl.pallas_call(
        near_kernel,
        name="near_field",
        out_shape=shaped(R, LD * P_SIZE),
        in_specs=[smem(), vmem(), vmem()],
        out_specs=vmem(),
        scratch_shapes=[
            pltpu.VMEM((4, 8, 512), F32),
            pltpu.VMEM((PAIRS, P_SIZE, 2 * FEATS), BF16),
            pltpu.VMEM((2 * LD, FEATS, P_SIZE), BF16),
            pltpu.VMEM((R, LD * P_SIZE), F32),
            pltpu.VMEM((BATCH // 2, 128, 256), BF16),
            pltpu.VMEM((BATCH // 2, 128, 256), BF16),
        ],
        compiler_params=PARAMS,
        cost_estimate=pl.CostEstimate(
            flops=2 * 460 * 128 * 128 * 128, bytes_accessed=4 << 20, transcendentals=460 * 32768
        ),
    )(tasks, charges, points)

    down = pl.pallas_call(
        down_kernel,
        name="tree_down",
        out_shape=shaped(PAIRS, R, 128),
        in_specs=[smem()] + [vmem()] * 3,
        out_specs=vmem(),
        scratch_shapes=[
            pltpu.VMEM((PAIRS - 1, R, 128), F32),
            pltpu.VMEM((devices, R, 128), F32),
            pltpu.VMEM((2 * devices, 128), F32),
        ],
        compiler_params=PARAMS,
    )(shapes, lev, transfer, roots)

    stages = [
        pltpu.VMEM((UNIT, 512, 128), BF16),
        pltpu.VMEM((UNIT, 512, 128), BF16),
        pltpu.VMEM((UNIT, 4 * R, 512), BF16),
    ]
    leaf_couple = pl.pallas_call(
        couple_kernel,
        name="leaf_couple",
        out_shape=shaped(PAIRS + 2 * UNIT, R, 128),
        in_specs=[smem()] * 2 + [vmem()] * 2 + [pl.BlockSpec(memory_space=pl.ANY)] * 2,
        out_specs=vmem(),
        scratch_shapes=[
            pltpu.VMEM((2 * LD, 8, 128), F32),
            pltpu.VMEM((TABLE, R, 128), BF16),
            pltpu.VMEM((TABLE, R, 128), BF16),
            pltpu.VMEM((2, 8, 128), F32),
            pltpu.SMEM((2, 8, 128), F32),
            pltpu.SemaphoreType.DMA((4,)),
        ]
        + stages
        + stages,
        compiler_params=PARAMS,
    )(entries, shapes, from_prev, from_next, high, low)

    return pl.pallas_call(
        finish_kernel,
        name="finish",
        out_shape=shaped(R, LD * P_SIZE),
        in_specs=[smem()] + [vmem()] * 7,
        out_specs=vmem(),
        scratch_shapes=[pltpu.VMEM((2, 8, 512), F32), pltpu.VMEM((2, R, 128), F32)],
        compiler_params=PARAMS,
    )(counts, near, points, basis, from_prev, from_next, down, leaf_couple)


def solution(mesh):
    in_specs = (
        P(None, AXES),
        P(None, AXES),
        P(AXES, None, None),
        P(),
        P(AXES, None),
        P(AXES, None),
    )
    return jax.shard_map(
        per_device, mesh=mesh, in_specs=in_specs, out_specs=P(None, AXES), check_vma=False
    )
```

time: 101 us -> 100 us (0.990)
  the two profiles are of different devices: /device:TPU:4 before, /device:TPU:0 now
where the time goes in v3:
time: 100 us; the launch traced here: 99.6 us
  Pallas kernels  59.7 us (60%)
  local copies, waits for them, and re-layouts  16.9 us (17%)
  starting transfers between devices  12.3 us (12%)
  waiting for transfers between devices  10.6 us (11%)
    pallas_call x1, Pallas kernels, per_device(): pl.pallas_call(couple_kernel, name='leaf_couple', out_shape=shaped(PAIRS...  18.7 us
    pallas_call x1, Pallas kernels, per_device(): pl.pallas_call(near_kernel, name='near_field', out_shape=shaped(R, LD * P...  17.5 us
    unnamed x42, local copies, waits for them, and re-layouts  16.9 us
    ppermute x1, waiting for transfers between devices, per_device(): from_next = lax.ppermute(send_prev, AXES, backward)  10.6 us
    pallas_call x1, Pallas kernels, per_device(): pl.pallas_call(down_kernel, name='tree_down', out_shape=shaped(PAIRS, R,...  9.94 us
    all_to_all x1, starting transfers between devices, per_device(): roots = lax.all_to_all(root, AXES, 0, 0, tiled=True)  7.41 us
    pallas_call x1, Pallas kernels, per_device(): pl.pallas_call(finish_kernel, name='finish', out_shape=shaped(R, LD * P_S...  6.86 us
    pallas_call x1, Pallas kernels, per_device(): pl.pallas_call(leaf_kernel, name='leaf_up', out_shape=(shaped(SEND, R, 12...  5.67 us
  transfers between devices with their start and end apart: 3, of which 1 were waited for; matrix products, arithmetic and copies ran while one was open for 0% of the time, Pallas kernels for 37%

profile of v3, /device:TPU:0, one launch (start us, length us, event | category | flops | bytes accessed | tf_op | source)
XLA Modules:
  0.0 99.6 jit_solution(7110349537026897838)
XLA Ops:
  0.0 1.6 %copy-done = bf16[128,64,128]{2,1,0:T(8,128)(2,1)S(1)} copy-done((bf16[128,64,128]{2,1,0:T(8,128)(2,1)S(1)}, bf16[128,64,128]{2,1,0:T(8,128)(2,1)}, u32[]{:S(2)}) %copy-start) | copy-done | bytes 2097176
  1.6 1.2 %copy-done.8 = bf16[32,16384]{1,0:T(8,128)(2,1)S(1)} copy-done((bf16[32,16384]{1,0:T(8,128)(2,1)S(1)}, bf16[32,16384]{1,0:T(8,128)(2,1)}, u32[]{:S(2)}) %copy-start.8) | copy-done | bytes 1048600
  2.8 0.9 copy-done.10
  3.8 0.8 copy-done.15
  4.6 5.7 %leaf_up.1 = (bf16[72,32,128]{2,1,0:T(8,128)(2,1)S(1)}, bf16[72,32,128]{2,1,0:T(8,128)(2,1)S(1)}, bf16[128,32,128]{2,1,0:T(8,128)(2,1)S(1)}, bf16[128,32,128]{2,...) custom-call(bf16[32,16384]{1,0:T(8,128)(2,1)S(1)} %copy-done.8, ...), custom_call_target="tpu_custom_call" | custom-call | tf_op jit(solution)/shard_map/leaf_up/pallas_call | solution.py:699
  10.3 1.0 copy-done.12
  12.1 0.8 copy-done.17
  12.9 0.8 copy-done.18
  13.7 7.4 %all-to-all-start = ((f32[32,24,128]{2,1,0:T(8,128)}), f32[32,24,128]{2,1,0:T(8,128)}, u32[]{:S(2)}, u32[]{:S(2)}) async-start(f32[32,24,128]{2,1,0:T(8,128)} %copy-done.14), calls=%async_computation | async-start | bytes 786432 | tf_op jit(solution)/shard_map/all_to_all | solution.py:722
  21.1 3.6 %collective-permute-start = (bf16[72,32,128]{2,1,0:T(8,128)(2,1)}, bf16[72,32,128]{2,1,0:T(8,128)(2,1)S(1)}, u32[]{:S(2)}, u32[]{:S(2)}) collective-permute-start(bf16[72,32,128]{2,1,0:T(8,128)(2,1)} %copy-done.18), channel_id=1, source_target_pairs={{0,1},{1,2},{2,3},{3,4},{4,5},{5,6},{6,7},{7,8},{8,9},{9,10},{10,1... | collective-permute-start | bytes 1769480 | tf_op jit(solution)/shard_map/ppermute | solution.py:725
  24.8 1.3 %collective-permute-start.1 = (bf16[72,32,128]{2,1,0:T(8,128)(2,1)}, bf16[72,32,128]{2,1,0:T(8,128)(2,1)S(1)}, u32[]{:S(2)}, u32[]{:S(2)}) collective-permute-start(bf16[72,32,128]{2,1,0:T(8,128)(2,1)} %copy-done.17), channel_id=1, source_target_pairs={{1,0},{2,1},{3,2},{4,3},{5,4},{6,5},{7,6},{8,7},{9,8},{10,9},{11,1... | collective-permute-start | bytes 1769480 | tf_op jit(solution)/shard_map/ppermute | solution.py:726
  26.1 0.9 lists.1
  27.0 17.5 %near_field.1.near_ref = f32[32,16384]{1,0:T(8,128)S(1)} custom-call(s32[8,896]{1,0:T(8,128)S(1)} %get-tuple-element.16.list_ref, bf16[32,16384]{1,0:T(8,128)(2,1)S(1)} %copy-done.9, f32[3,16384]{1,0:T(4,128)S(1)} %copy-done.11), custom_call_target="tpu_custom_call" | custom-call | flops 1929379840 | bytes 4194304 | tf_op jit(solution)/shard_map/near_field/pallas_call | solution.py:741
  44.6 1.3 %copy-done.6 = f32[32,16384]{1,0:T(8,128)} copy-done((f32[32,16384]{1,0:T(8,128)}, f32[32,16384]{1,0:T(8,128)S(1)}, u32[]{:S(2)}) %copy-start.6) | copy-done | bytes 2097176
  45.9 10.6 %collective-permute-done.1.next_ref = bf16[72,32,128]{2,1,0:T(8,128)(2,1)S(1)} collective-permute-done((bf16[72,32,128]{2,1,0:T(8,128)(2,1)}, bf16[72,32,128]{2,1,0:T(8,128)(2,1)S(1)}, u32[]{:S(2)}, u32[]{:S(2)}) %collective-permute-start.1) | collective-permute-done | bytes 589856 | tf_op jit(solution)/shard_map/ppermute | solution.py:726
  56.5 18.7 %leaf_couple.1 = f32[72,32,128]{2,1,0:T(8,128)S(1)} custom-call(s32[16,128]{1,0:T(8,128)S(1)} %get-tuple-element.22.entries, f32[8,256]{1,0:T(8,128)S(1)} %get-tuple-element.19.shape_ref, bf16[72,32,128]{2,1,0:T(8,128)(2,1)S(1)} %collective-permute-done.prev_ref, bf16[72,32,128]{2,1,0:T(8,128)(2,1)S(1)} %collective-permute-done.1.next_ref, ...), custom_call_target="tpu_custom_call" | custom-call | tf_op jit(solution)/shard_map/leaf_couple/pallas_call | solution.py:780
  75.2 0.8 copy-done.2
  76.9 1.4 %copy-done.13 = f32[63,32,128]{2,1,0:T(8,128)S(1)} copy-done((f32[63,32,128]{2,1,0:T(8,128)S(1)}, f32[63,32,128]{2,1,0:T(8,128)}, u32[]{:S(2)}) %copy-start.13) | copy-done | bytes 1032216
  78.3 0.8 copy-done.16
  79.1 9.9 %tree_down.1.down_ref = f32[64,32,128]{2,1,0:T(8,128)S(1)} custom-call(f32[8,256]{1,0:T(8,128)S(1)} %get-tuple-element.19.shape_ref, f32[63,32,128]{2,1,0:T(8,128)S(1)} %copy-done.13, f32[2,64,64]{2,1,0:T(8,128)S(1)} %copy-done.16, f32[32,24,128]{2,1,0:T(8,128)} %all-to-all-done.root_ref), custom_call_target="tpu_custom_call" | custom-call | tf_op jit(solution)/shard_map/tree_down/pallas_call | solution.py:761
  89.0 1.1 %copy-done.3 = bf16[72,32,128]{2,1,0:T(8,128)(2,1)S(1)} copy-done((bf16[72,32,128]{2,1,0:T(8,128)(2,1)S(1)}, bf16[72,32,128]{2,1,0:T(8,128)(2,1)}, u32[]{:S(2)}) %copy-start.3) | copy-done | bytes 589848
  90.1 1.1 %copy-done.5 = bf16[72,32,128]{2,1,0:T(8,128)(2,1)S(1)} copy-done((bf16[72,32,128]{2,1,0:T(8,128)(2,1)S(1)}, bf16[72,32,128]{2,1,0:T(8,128)(2,1)}, u32[]{:S(2)}) %copy-start.5) | copy-done | bytes 589848
  91.2 1.6 %copy-done.7 = f32[32,16384]{1,0:T(8,128)S(1)} copy-done((f32[32,16384]{1,0:T(8,128)S(1)}, f32[32,16384]{1,0:T(8,128)}, u32[]{:S(2)}) %copy-start.7) | copy-done | bytes 2097176
  92.8 6.9 %finish.1 = f32[32,16384]{1,0:T(8,128)} custom-call(f32[16,128]{1,0:T(8,128)S(1)} %get-tuple-element.15.counts, f32[32,16384]{1,0:T(8,128)S(1)} %copy-done.7, f32[3,16384]{1,0:T(4,128)S(1)} %copy-done.11, bf16[128,64,128]{2,1,0:T(8,128)(2,1)S(1)} %copy-done.1, bf16[72,32,128]{2,1,0:T(8,128)(2,1)S(1)} %copy-done.3, bf16[72,32,128]{2,1,0:T(8,128)(2,1)S(1)} %copy-done.5, ...), custom_call_target="tpu_custom_call" | custom-call | tf_op jit(solution)/shard_map/finish/pallas_call | solution.py:799
  (30 shorter events, 1.6 us)
Async XLA Ops:
  0.0 1.6 %copy-start = (bf16[128,64,128]{2,1,0:T(8,128)(2,1)S(1)}, bf16[128,64,128]{2,1,0:T(8,128)(2,1)}, u32[]{:S(2)}) copy-start(bf16[128,64,128]{2,1,0:T(8,128)(2,1)} %b_ref.3) | copy-start | bytes 6291460
  1.6 1.2 %copy-start.8 = (bf16[32,16384]{1,0:T(8,128)(2,1)S(1)}, bf16[32,16384]{1,0:T(8,128)(2,1)}, u32[]{:S(2)}) copy-start(bf16[32,16384]{1,0:T(8,128)(2,1)} %x_ref.3) | copy-start | bytes 3145732
  2.8 0.9 copy-start.10
  3.8 0.8 copy-start.15
  4.6 21.5 %copy-start.19 = (s32[128,8]{0,1:T(8,128)S(1)}, s32[128,8]{0,1:T(8,128)}, u32[]{:S(2)}) copy-start(s32[128,8]{0,1:T(8,128)} %param.10) | copy-start | bytes 12292
  4.6 21.5 %copy-start.20 = (s32[128,8]{0,1:T(8,128)S(1)}, s32[128,8]{0,1:T(8,128)}, u32[]{:S(2)}) copy-start(s32[128,8]{0,1:T(8,128)} %param.11) | copy-start | bytes 12292
  4.6 22.4 %copy-start.9 = (bf16[32,16384]{1,0:T(8,128)(2,1)S(1)}, bf16[32,16384]{1,0:T(8,128)(2,1)}, u32[]{:S(2)}) copy-start(bf16[32,16384]{1,0:T(8,128)(2,1)} %x_ref.3) | copy-start | bytes 3145732
  4.6 22.4 %copy-start.11 = (f32[3,16384]{1,0:T(4,128)S(1)}, f32[3,16384]{1,0:T(4,128)}, u32[]{:S(2)}) copy-start(f32[3,16384]{1,0:T(4,128)} %p_ref.5) | copy-start | bytes 589828
  10.3 1.0 %copy-start.12 = (f32[63,32,128]{2,1,0:T(8,128)}, f32[63,32,128]{2,1,0:T(8,128)S(1)}, u32[]{:S(2)}) copy-start(f32[63,32,128]{2,1,0:T(8,128)S(1)} %get-tuple-element.20.lev_ref) | copy-start | bytes 3096580
  11.3 0.8 copy-start.14
  12.0 0.8 copy-start.17
  12.9 0.8 copy-start.18
  13.7 63.2 %all-to-all-start = ((f32[32,24,128]{2,1,0:T(8,128)}), f32[32,24,128]{2,1,0:T(8,128)}, u32[]{:S(2)}, u32[]{:S(2)}) async-start(f32[32,24,128]{2,1,0:T(8,128)} %copy-done.14), calls=%async_computation | async-start | bytes 786432 | tf_op jit(solution)/shard_map/all_to_all | solution.py:722
  21.1 24.8 %collective-permute-start = (bf16[72,32,128]{2,1,0:T(8,128)(2,1)}, bf16[72,32,128]{2,1,0:T(8,128)(2,1)S(1)}, u32[]{:S(2)}, u32[]{:S(2)}) collective-permute-start(bf16[72,32,128]{2,1,0:T(8,128)(2,1)} %copy-done.18), channel_id=1, source_target_pairs={{0,1},{1,2},{2,3},{3,4},{4,5},{5,6},{6,7},{7,8},{8,9},{9,10},{10,1... | collective-permute-start | bytes 1769480 | tf_op jit(solution)/shard_map/ppermute | solution.py:725
  24.8 31.7 %collective-permute-start.1 = (bf16[72,32,128]{2,1,0:T(8,128)(2,1)}, bf16[72,32,128]{2,1,0:T(8,128)(2,1)S(1)}, u32[]{:S(2)}, u32[]{:S(2)}) collective-permute-start(bf16[72,32,128]{2,1,0:T(8,128)(2,1)} %copy-done.17), channel_id=1, source_target_pairs={{1,0},{2,1},{3,2},{4,3},{5,4},{6,5},{7,6},{8,7},{9,8},{10,9},{11,1... | collective-permute-start | bytes 1769480 | tf_op jit(solution)/shard_map/ppermute | solution.py:726
  44.6 1.3 %copy-start.6 = (f32[32,16384]{1,0:T(8,128)}, f32[32,16384]{1,0:T(8,128)S(1)}, u32[]{:S(2)}) copy-start(f32[32,16384]{1,0:T(8,128)S(1)} %near_field.1.near_ref) | copy-start | bytes 6291460
  75.2 0.8 copy-start.2
  76.1 0.8 copy-start.4
  76.9 12.2 %copy-start.1 = (bf16[128,64,128]{2,1,0:T(8,128)(2,1)S(1)}, bf16[128,64,128]{2,1,0:T(8,128)(2,1)}, u32[]{:S(2)}) copy-start(bf16[128,64,128]{2,1,0:T(8,128)(2,1)} %b_ref.3) | copy-start | bytes 6291460
  76.9 1.4 %copy-start.13 = (f32[63,32,128]{2,1,0:T(8,128)S(1)}, f32[63,32,128]{2,1,0:T(8,128)}, u32[]{:S(2)}) copy-start(f32[63,32,128]{2,1,0:T(8,128)} %copy-done.12) | copy-start | bytes 3096580
  78.3 0.8 copy-start.16
  89.0 1.1 %copy-start.3 = (bf16[72,32,128]{2,1,0:T(8,128)(2,1)S(1)}, bf16[72,32,128]{2,1,0:T(8,128)(2,1)}, u32[]{:S(2)}) copy-start(bf16[72,32,128]{2,1,0:T(8,128)(2,1)} %copy-done.2) | copy-start | bytes 1769476
  90.1 1.1 %copy-start.5 = (bf16[72,32,128]{2,1,0:T(8,128)(2,1)S(1)}, bf16[72,32,128]{2,1,0:T(8,128)(2,1)}, u32[]{:S(2)}) copy-start(bf16[72,32,128]{2,1,0:T(8,128)(2,1)} %copy-done.4) | copy-start | bytes 1769476
  91.2 1.6 %copy-start.7 = (f32[32,16384]{1,0:T(8,128)S(1)}, f32[32,16384]{1,0:T(8,128)}, u32[]{:S(2)}) copy-start(f32[32,16384]{1,0:T(8,128)} %copy-done.6) | copy-start | bytes 6291460

commit v4 on v3

--- a/solution.py
+++ b/solution.py
@@ -18,7 +18,7 @@
 HALF = LD // 2
 NEAR_REACH = 8
 FEATS = 64
-BATCH = 8
+BATCH = 16
 LIST = 896
 SEND = 72
 SCALE = 0.5 * math.log2(math.e)
@@ -28,7 +28,7 @@
 BF16 = jnp.bfloat16
 NT = (((1,), (1,)), ((), ()))
 TINY = 1e-30
-VMEM_LIMIT = 32 * 1024 * 1024
+VMEM_LIMIT = 56 * 1024 * 1024
 
 
 def lanes(shape):
@@ -175,19 +175,20 @@
     origin = (device_index() * GROUPS).astype(F32)
     low32 = lanes((R, 128)) < K
 
-    def leaf_pair(c, carry):
-        both = []
-        for side in range(2):
-            leaf = 2 * c + side
+    def leaf_pairs(m, carry):
+        values = []
+        for v in range(16):
+            leaf = 16 * m + v
             x = x_ref[:, pl.ds(pl.multiple_of(leaf * P_SIZE, P_SIZE), P_SIZE)]
             weights = b_ref[leaf]
-            value = dot_nt(x, jnp.concatenate([weights, weights], axis=0))
-            high_ref[leaf], low_ref[leaf] = halves(value)
-            both.append(value)
-        coef[c] = jnp.where(low32, both[0], both[1])
+            values.append(dot_nt(x, jnp.concatenate([weights, weights], axis=0)))
+        for v in range(16):
+            high_ref[16 * m + v], low_ref[16 * m + v] = halves(values[v])
+        for v in range(8):
+            coef[8 * m + v] = jnp.where(low32, values[2 * v], values[2 * v + 1])
         return carry
 
-    lax.fori_loop(0, PAIRS, leaf_pair, 0, unroll=8)
+    lax.fori_loop(0, LD // 16, leaf_pairs, 0)
 
     t_high, t_low = halves(doubled_transfer(t_ref))
     pairs = coef[...]
@@ -242,11 +243,13 @@
     p8[...] = jnp.zeros((8, 512), F32)
     for send, first_pair, group in ((send_next, PAIRS // 2, GROUPS - 1), (send_prev, 0, 0)):
 
-        def copy_pair(m, carry):
-            send[m], send[32 + m] = halves(coef[first_pair + m])
+        def copy_pairs(m, carry):
+            parts = [halves(coef[first_pair + 8 * m + v]) for v in range(8)]
+            for v in range(8):
+                send[8 * m + v], send[32 + 8 * m + v] = parts[v]
             return carry
 
-        lax.fori_loop(0, PAIRS // 2, copy_pair, 0, unroll=8)
+        lax.fori_loop(0, PAIRS // 16, copy_pairs, 0)
         parts = thirds(shape_rows[:, 0:128])
         send[68] = jnp.concatenate(list(parts) + [jnp.zeros((8, 128), F32)], axis=0).astype(BF16)
         p8[0:3, :] = p_ref[:, group * 512 : group * 512 + 512]
@@ -377,25 +380,29 @@
 
 def near_kernel(
     list_ref, x_ref, p_ref, out_ref,
-    p8, far_feat, own_feat, back, tile0, tile1,
+    p8, far_feat, own_feat, part1, part2, part3, tile0, tile1,
 ):
     first_group = device_index() * GROUPS
     p8[...] = jnp.zeros(p8.shape, F32)
     eye = identity()
 
     def features(m, carry):
+        loaded = [p_ref[:, pl.ds(pl.multiple_of((4 * m + v) * 512, 512), 512)] for v in range(4)]
         for v in range(4):
-            g = 4 * m + v
-            p8[v, 0:3, :] = p_ref[:, pl.ds(pl.multiple_of(g * 512, 512), 512)]
+            p8[v, 0:3, :] = loaded[v]
+        made = []
+        for v in range(4):
             coords = p8[v]
-            origin_z = (first_group + g).astype(F32)
+            origin_z = (first_group + 4 * m + v).astype(F32)
             far, own = point_features(coords, origin_z)
             _, own_up = point_features(coords, origin_z + 1.0)
             far = far_stack(far)
-            own = own_stack(own)
-            own_up = own_stack(own_up)
             parts = [far[:, k * P_SIZE : (k + 1) * P_SIZE] for k in range(4)]
             turned = dot_nt(eye, jnp.concatenate(parts, axis=0)).astype(BF16)
+            made.append((turned, own_stack(own), own_stack(own_up)))
+        for v in range(4):
+            g = 4 * m + v
+            turned, own, own_up = made[v]
             far_feat[2 * g] = turned[:, 0:128]
             far_feat[2 * g + 1] = turned[:, 128:256]
             for k in range(4):
@@ -407,7 +414,8 @@
     lax.fori_loop(0, GROUPS // 4, features, 0)
 
     out_ref[...] = x_ref[...].astype(F32)
-    for ref in (back, tile0, tile1):
+    parts = (out_ref, part1, part2, part3)
+    for ref in (part1, part2, part3, tile0, tile1):
         ref[...] = jnp.zeros(ref.shape, ref.dtype)
 
     total = list_ref[4, 0]
@@ -418,24 +426,44 @@
         return pl.ds(pl.multiple_of(i * P_SIZE, P_SIZE), P_SIZE)
 
     def phase(n, tile_new, tile_old):
+        far, own, sources, updates = [], [], [], []
+        for u in range(BATCH):
+            k = (n + 1) * BATCH + u
+            i, j = list_ref[0, k], list_ref[1, k]
+            variant = ((j >> 2) - (i >> 2)) * LD
+            far.append(far_feat[j >> 1])
+            own.append(own_feat[variant + i])
+        for u in range(BATCH):
+            k = n * BATCH + u
+            i, j = list_ref[0, k], list_ref[1, k]
+            sources.append((x_ref[:, leaf_slice(j)], x_ref[:, leaf_slice(i)]))
+        tiles = []
         for u in range(BATCH // 2):
-            far, own = [], []
-            for h in range(2):
-                k = (n + 1) * BATCH + 2 * u + h
-                i, j = list_ref[0, k], list_ref[1, k]
-                variant = ((j >> 2) - (i >> 2)) * LD
-                far.append(far_feat[j >> 1])
-                own.append(own_feat[variant + i])
-            dist = dot(jnp.where(low, far[0], far[1]), block_diagonal(own[0], own[1]))
-            tile_new[u] = decay(dist).astype(BF16)
+            pick = jnp.where(low, far[2 * u], far[2 * u + 1])
+            dist = dot(pick, block_diagonal(own[2 * u], own[2 * u + 1]))
+            tiles.append(decay(dist).astype(BF16))
             for h in range(2):
                 k = n * BATCH + 2 * u + h
-                i, j = list_ref[0, k], list_ref[1, k]
                 tile = tile_old[u, :, h * 128 : h * 128 + 128]
-                to_i = dot(x_ref[:, leaf_slice(j)], tile) * list_ref[2, k].astype(F32)
-                to_j = dot_nt(x_ref[:, leaf_slice(i)], tile) * list_ref[3, k].astype(F32)
-                out_ref[:, leaf_slice(i)] += to_i
-                back[:, leaf_slice(j)] += to_j
+                x_j, x_i = sources[2 * u + h]
+                updates.append(
+                    (
+                        dot(x_j, tile) * list_ref[2, k].astype(F32),
+                        dot_nt(x_i, tile) * list_ref[3, k].astype(F32),
+                    )
+                )
+        for u in range(BATCH // 2):
+            tile_new[u] = tiles[u]
+        for u in range(BATCH // 2):
+            places, sums = [], []
+            for h in range(2):
+                k = n * BATCH + 2 * u + h
+                for side in range(2):
+                    place = leaf_slice(list_ref[side, k])
+                    places.append(place)
+                    sums.append(parts[2 * h + side][:, place] + updates[2 * u + h][side])
+            for ref, place, value in zip(parts, places, sums):
+                ref[:, place] = value
 
     def two_phases(m, carry):
         phase(2 * m, tile0, tile1)
@@ -443,7 +471,15 @@
         return carry
 
     lax.fori_loop(0, (steps + 1) // 2, two_phases, 0)
-    out_ref[...] += back[...]
+
+    def total_up(m, carry):
+        place = pl.ds(pl.multiple_of(m * 1024, 1024), 1024)
+        out_ref[:, place] = (out_ref[:, place] + part1[:, place]) + (
+            part2[:, place] + part3[:, place]
+        )
+        return carry
+
+    lax.fori_loop(0, LD * P_SIZE // 1024, total_up, 0)
 
 
 def down_kernel(
@@ -452,28 +488,29 @@
     lane_u = lane_nodes()
     row_y, row_z = row_nodes()
 
-    def sibling(pair, cluster):
-        left = [shape_ref[d, cluster] for d in range(4)]
-        right = [shape_ref[d, cluster + 1] for d in range(4)]
-        tile = sibling_tile(left, right, lane_u, row_y, row_z)
-        couple[pair] = sibling_apply(tile, lev_ref[pair])
-
     def siblings(m, carry):
-        for u in range(21):
-            pair = 21 * m + u
-            sibling(pair, LD + 2 * pair)
+        loaded = [lev_ref[9 * m + u] for u in range(9)]
+        values = []
+        for u in range(9):
+            cluster = LD + 2 * (9 * m + u)
+            left = [shape_ref[d, cluster] for d in range(4)]
+            right = [shape_ref[d, cluster + 1] for d in range(4)]
+            tile = sibling_tile(left, right, lane_u, row_y, row_z)
+            values.append(sibling_apply(tile, loaded[u]))
+        for u in range(9):
+            couple[9 * m + u] = values[u]
         return carry
 
-    lax.fori_loop(0, 3, siblings, 0)
+    lax.fori_loop(0, 7, siblings, 0)
 
     t_high, t_low = halves(doubled_transfer(t_ref))
     device = device_index()
     n = root_ref.shape[0]
     low = lanes((R, 128)) < K
+    shift = lanes((1, 128)) == 2
     for k in range(n):
-        shift = lanes((1, 128)) == 2
-        shapes[k : k + 1, :] = (
-            root_ref[k, R // 2 : R // 2 + 1, :] + jnp.where(shift, (k * GROUPS) * SCALE, 0.0)
+        shapes[k : k + 1, :] = root_ref[k, R // 2 : R // 2 + 1, :] + jnp.where(
+            shift, (k * GROUPS) * SCALE, 0.0
         )
     for k in range(n // 2):
         left = root_ref[2 * k, 0 : R // 2, :]
@@ -522,7 +559,7 @@
     down_ref[...] = push_down(children_of(value), t_high, t_low)
 
 
-UNIT = 4
+UNIT = 2
 
 
 def couple_kernel(
@@ -563,22 +600,27 @@
     for side, ref in enumerate((prev_ref, next_ref)):
         first = LD + side * HALF
 
-        def halo_pair(m, carry):
+        def halo_pairs(m, carry):
             def read(d, k):
                 return halo_shape[side, d, k]
 
+            loaded = [
+                (tab, 4 * m + v, ref[offset + 4 * m + v])
+                for tab, offset in ((high_tab, 0), (low_tab, 32))
+                for v in range(4)
+            ]
+            turned = [pltpu.roll(pair.astype(F32), K, 1).astype(BF16) for _, _, pair in loaded]
             source = HALF if side == 0 else 0
             place = 0 if side == 0 else HALF + LD
             shift = (2.0 * side - 1.0) * GROUPS * SCALE
-            for h in range(2):
-                shape_tab[place + 2 * m + h] = shape_rows(read, source + 2 * m + h, shift)
-            for tab, place in ((high_tab, m), (low_tab, 32 + m)):
-                pair = ref[place]
-                tab[first + m] = pair
-                tab[first + PAIRS // 2 + m] = pltpu.roll(pair.astype(F32), K, 1).astype(BF16)
+            for v in range(8):
+                shape_tab[place + 8 * m + v] = shape_rows(read, source + 8 * m + v, shift)
+            for (tab, pair, value), other in zip(loaded, turned):
+                tab[first + pair] = value
+                tab[first + PAIRS // 2 + pair] = other
             return carry
 
-        lax.fori_loop(0, PAIRS // 2, halo_pair, 0, unroll=4)
+        lax.fori_loop(0, PAIRS // 8, halo_pairs, 0)
     high_tab[TABLE - 1] = jnp.zeros((R, 128), BF16)
     low_tab[TABLE - 1] = jnp.zeros((R, 128), BF16)
     for copy in copies[:2]:
@@ -586,14 +628,26 @@
 
     row_y, row_z = row_nodes()
 
-    def couple_tiles(pair, u, tile_h, tile_l, lhs):
+    def couple_load(pair):
         leaves = (2 * pair, 2 * pair + 1)
         own = jnp.where(low8, shape_tab[HALF + leaves[0]], shape_tab[HALF + leaves[1]])
+        fars = []
+        for s in range(8):
+            e0, e1 = entries[8 + s, leaves[0]], entries[8 + s, leaves[1]]
+            fars.append(jnp.where(low8, shape_tab[e0], shape_tab[e1]))
+        sources = []
+        for tab in (high_tab, low_tab):
+            for h in range(2):
+                for q in range(4):
+                    e0, e1 = entries[2 * q, leaves[h]], entries[2 * q + 1, leaves[h]]
+                    sources.append(jnp.where(low32, tab[e0], tab[e1]))
+        return own, fars, sources
+
+    def couple_tiles(own, fars):
         radius = jnp.broadcast_to(own[3:4], (8, 128))
         own = [jnp.broadcast_to(own[d : d + 1], (8, 128)) + radius * lane_u[d] for d in range(3)]
-        for s in range(8):
-            e0, e1 = entries[8 + s, leaves[0]], entries[8 + s, leaves[1]]
-            far = jnp.where(low8, shape_tab[e0], shape_tab[e1])
+        tiles = []
+        for far in fars:
             reach = jnp.broadcast_to(far[3:4], (8, 128))
             gap = [own[d] - jnp.broadcast_to(far[d : d + 1], (8, 128)) for d in range(3)]
             tile = tile_from_axes(
@@ -601,17 +655,8 @@
                 [jnp.square(gap[1] - reach * row_y[h]) for h in range(2)],
                 jnp.square(gap[2] - reach * row_z),
             )
-            high, low = halves(tile)
-            tile_h[u, s * K : (s + 1) * K, :] = high
-            tile_l[u, s * K : (s + 1) * K, :] = low
-        for q in range(4):
-            span = slice(q * 128, (q + 1) * 128)
-            for h in range(2):
-                e0, e1 = entries[2 * q, leaves[h]], entries[2 * q + 1, leaves[h]]
-                lhs[u, h * R : (h + 1) * R, span] = jnp.where(low32, high_tab[e0], high_tab[e1])
-                lhs[u, (2 + h) * R : (3 + h) * R, span] = jnp.where(
-                    low32, low_tab[e0], low_tab[e1]
-                )
+            tiles.append(halves(tile))
+        return tiles
 
     def couple_apply(u, tile_h, tile_l, lhs):
         both = dot(lhs[u], tile_h[u])
@@ -619,9 +664,21 @@
         return jnp.where(low32, both[0:R], both[R : 2 * R])
 
     def couple_phase(n, new, old):
+        tile_h, tile_l, lhs = new
+        loaded = [couple_load(jnp.minimum(n * UNIT + u, PAIRS - 1)) for u in range(UNIT)]
+        results, made = [], []
         for u in range(UNIT):
-            leaf_couple[(n - 1) * UNIT + u + UNIT] = couple_apply(u, *old)
-            couple_tiles(jnp.minimum(n * UNIT + u, PAIRS - 1), u, *new)
+            results.append(couple_apply(u, *old))
+            made.append(couple_tiles(loaded[u][0], loaded[u][1]))
+        for u in range(UNIT):
+            for k, value in enumerate(loaded[u][2]):
+                r, q = k // 4, k % 4
+                lhs[u, r * R : (r + 1) * R, q * 128 : (q + 1) * 128] = value
+            for s, (high, low) in enumerate(made[u]):
+                tile_h[u, s * K : (s + 1) * K, :] = high
+                tile_l[u, s * K : (s + 1) * K, :] = low
+        for u in range(UNIT):
+            leaf_couple[n * UNIT + u] = results[u]
 
     buffers = ((tile_h0, tile_l0, lhs0), (tile_h1, tile_l1, lhs1))
     for ref in buffers[1]:
@@ -642,15 +699,24 @@
 ):
     device = device_index()
 
-    def finish(c, carry):
-        value = (down_ref[c] + leaf_couple[c + UNIT]).astype(BF16)
-        span = pl.ds(pl.multiple_of(c * 256, 256), 256)
-        out_ref[:, span] = near_ref[:, span] + dot(
-            value, block_diagonal(b_ref[2 * c], b_ref[2 * c + 1])
-        )
+    def finish(m, carry):
+        values = []
+        for v in range(8):
+            c = 8 * m + v
+            value = (down_ref[c] + leaf_couple[c + UNIT]).astype(BF16)
+            span = pl.ds(pl.multiple_of(c * 256, 256), 256)
+            values.append(
+                (
+                    span,
+                    near_ref[:, span]
+                    + dot(value, block_diagonal(b_ref[2 * c], b_ref[2 * c + 1])),
+                )
+            )
+        for span, value in values:
+            out_ref[:, span] = value
         return carry
 
-    lax.fori_loop(0, PAIRS, finish, 0, unroll=8)
+    lax.fori_loop(0, PAIRS // 8, finish, 0)
 
     p8[...] = jnp.zeros(p8.shape, F32)
     eye = identity()
@@ -660,13 +726,18 @@
         coords[side] = halo_ref[69].astype(F32) + halo_ref[70].astype(F32) + halo_ref[71].astype(F32)
 
     def edge(k, carry):
-        for side, (halo_ref, group) in enumerate(sides):
+        loaded = [
+            (halo_ref[64 + k], coords[side, pl.ds(pl.multiple_of(8 * k, 8), 8), :], p8[side])
+            for side, (halo_ref, _) in enumerate(sides)
+        ]
+        for side, (_, group) in enumerate(sides):
+            x_far, far, own = loaded[side]
             origin_z = (device * GROUPS + group).astype(F32)
-            _, own = point_features(p8[side], origin_z)
-            far, _ = point_features(coords[side, pl.ds(pl.multiple_of(8 * k, 8), 8), :], origin_z)
+            _, own = point_features(own, origin_z)
+            far, _ = point_features(far, origin_z)
             far = dot_nt(eye, far_stack(far)).astype(BF16)
             tiles = decay(dot(far, own_stack(own))).astype(BF16)
-            products = dot(halo_ref[64 + k], tiles)
+            products = dot(x_far, tiles)
             for i in range(4):
                 delta = (4 + i - k) if side == 0 else (4 + k - i)
                 weight = counts[8 * (1 - side) + jnp.clip(delta, 0, 7), 4 * group + i]
@@ -749,6 +820,8 @@
             pltpu.VMEM((PAIRS, P_SIZE, 2 * FEATS), BF16),
             pltpu.VMEM((2 * LD, FEATS, P_SIZE), BF16),
             pltpu.VMEM((R, LD * P_SIZE), F32),
+            pltpu.VMEM((R, LD * P_SIZE), F32),
+            pltpu.VMEM((R, LD * P_SIZE), F32),
             pltpu.VMEM((BATCH // 2, 128, 256), BF16),
             pltpu.VMEM((BATCH // 2, 128, 256), BF16),
         ],

time: 100 us -> 95.7 us (0.957)
  local copies, waits for them, and re-layouts: 16.9 us -> 1.57 us
  Pallas kernels: 59.7 us -> 71.9 us
  waiting for transfers between devices: 10.6 us -> 9.52 us
    unnamed x42 -> x6, local copies, waits for them, and re-layouts: 16.9 us -> 1.57 us
    pallas_call x1, Pallas kernels: 5.67 us -> 9.82 us  [per_device(): pl.pallas_call(leaf_kernel, name='leaf_up', out_shape=(shaped(SEND, R, 12...]
    pallas_call x1, Pallas kernels: 6.86 us -> 9.4 us  [per_device(): pl.pallas_call(finish_kernel, name='finish', out_shape=shaped(R, LD * P_S...]
    pallas_call x1, Pallas kernels: 9.94 us -> 11.9 us  [per_device(): pl.pallas_call(down_kernel, name='tree_down', out_shape=shaped(PAIRS, R,...]
    pallas_call x1, Pallas kernels: 0.94 us -> 2.27 us  [per_device(): pl.pallas_call(list_kernel, name='lists', out_shape=(shaped(8, LIST, dtyp...]
    pallas_call x1, Pallas kernels: 18.7 us -> 19.8 us  [per_device(): pl.pallas_call(couple_kernel, name='leaf_couple', out_shape=shaped(PAIRS...]
    pallas_call x1, Pallas kernels: 17.5 us -> 18.6 us  [per_device(): pl.pallas_call(near_kernel, name='near_field', out_shape=shaped(R, LD * P...]
    ppermute x1, waiting for transfers between devices: 10.6 us -> 9.52 us  [per_device(): from_next = lax.ppermute(send_prev, AXES, backward)]
  transfers between devices with their start and end apart: 3 -> 3, of which waited for: 1 -> 1; matrix products, arithmetic and copies ran while one was open for 0% -> 0% of each run, Pallas kernels for 37% -> 43%
where the time goes in v4:
time: 95.7 us; the launch traced here: 95.3 us
  Pallas kernels  71.9 us (75%)
  starting transfers between devices  12.3 us (13%)
  waiting for transfers between devices  9.52 us (10%)
  local copies, waits for them, and re-layouts  1.57 us (2%)
    pallas_call x1, Pallas kernels, per_device(): pl.pallas_call(couple_kernel, name='leaf_couple', out_shape=shaped(PAIRS...  19.8 us
    pallas_call x1, Pallas kernels, per_device(): pl.pallas_call(near_kernel, name='near_field', out_shape=shaped(R, LD * P...  18.6 us
    pallas_call x1, Pallas kernels, per_device(): pl.pallas_call(down_kernel, name='tree_down', out_shape=shaped(PAIRS, R,...  11.9 us
    pallas_call x1, Pallas kernels, per_device(): pl.pallas_call(leaf_kernel, name='leaf_up', out_shape=(shaped(SEND, R, 12...  9.82 us
    ppermute x1, waiting for transfers between devices, per_device(): from_next = lax.ppermute(send_prev, AXES, backward)  9.52 us
    pallas_call x1, Pallas kernels, per_device(): pl.pallas_call(finish_kernel, name='finish', out_shape=shaped(R, LD * P_S...  9.4 us
    all_to_all x1, starting transfers between devices, per_device(): roots = lax.all_to_all(root, AXES, 0, 0, tiled=True)  7.3 us
    ppermute x1, starting transfers between devices, per_device(): from_prev = lax.ppermute(send_next, AXES, forward)  3.71 us
  transfers between devices with their start and end apart: 3, of which 1 were waited for; matrix products, arithmetic and copies ran while one was open for 0% of the time, Pallas kernels for 43%

profile of v4, /device:TPU:0, one launch (start us, length us, event | category | flops | bytes accessed | tf_op | source)
XLA Modules:
  0.0 95.3 jit_solution(14759881508549627000)
XLA Ops:
  0.0 9.8 %leaf_up.1 = (bf16[72,32,128]{2,1,0:T(8,128)(2,1)}, bf16[72,32,128]{2,1,0:T(8,128)(2,1)}, bf16[128,32,128]{2,1,0:T(8,128)(2,1)}, bf16[128,32,128]{2,1,0:T(8,128)...) custom-call(bf16[32,16384]{1,0:T(8,128)(2,1)} %x_ref.3, f32[3,16384]{1,0:T(4,128)} %p_ref.5, ...), custom_call_target="tpu_custom_call" | custom-call | tf_op jit(solution)/shard_map/leaf_up/pallas_call | solution.py:770
  9.8 7.3 %all-to-all-start = ((f32[32,24,128]{2,1,0:T(8,128)}), f32[32,24,128]{2,1,0:T(8,128)S(1)}, u32[]{:S(2)}, u32[]{:S(2)}) async-start(f32[32,24,128]{2,1,0:T(8,128)} %get-tuple-element.21), calls=%async_computation | async-start | bytes 786432 | tf_op jit(solution)/shard_map/all_to_all | solution.py:793
  17.1 3.7 %collective-permute-start = (bf16[72,32,128]{2,1,0:T(8,128)(2,1)}, bf16[72,32,128]{2,1,0:T(8,128)(2,1)S(1)}, u32[]{:S(2)}, u32[]{:S(2)}) collective-permute-start(bf16[72,32,128]{2,1,0:T(8,128)(2,1)} %get-tuple-element.17), channel_id=1, source_target_pairs={{0,1},{1,2},{2,3},{3,4},{4,5},{5,6},{6,7},{7,8},{8,9},{9,10},{10,1... | collective-permute-start | bytes 1769480 | tf_op jit(solution)/shard_map/ppermute | solution.py:796
  20.8 1.3 %collective-permute-start.1 = (bf16[72,32,128]{2,1,0:T(8,128)(2,1)}, bf16[72,32,128]{2,1,0:T(8,128)(2,1)S(1)}, u32[]{:S(2)}, u32[]{:S(2)}) collective-permute-start(bf16[72,32,128]{2,1,0:T(8,128)(2,1)} %get-tuple-element.18), channel_id=1, source_target_pairs={{1,0},{2,1},{3,2},{4,3},{5,4},{6,5},{7,6},{8,7},{9,8},{10,9},{11,1... | collective-permute-start | bytes 1769480 | tf_op jit(solution)/shard_map/ppermute | solution.py:797
  22.1 2.3 %lists.1 = (s32[8,896]{1,0:T(8,128)}, f32[16,128]{1,0:T(8,128)}, s32[16,128]{1,0:T(8,128)}) custom-call(s32[8,128]{1,0:T(8,128)} %bitcast.2, s32[8,128]{1,0:T(8,128)} %bitcast.3), custom_call_target="tpu_custom_call" | custom-call | flops 16777216 | bytes 65536 | tf_op jit(solution)/shard_map/lists/pallas_call | solution.py:799
  24.4 18.6 %near_field.1.near_ref = f32[32,16384]{1,0:T(8,128)} custom-call(s32[8,896]{1,0:T(8,128)} %get-tuple-element.16.list_ref, bf16[32,16384]{1,0:T(8,128)(2,1)} %x_ref.3, f32[3,16384]{1,0:T(4,128)} %p_ref.5), custom_call_target="tpu_custom_call" | custom-call | flops 1929379840 | bytes 4194304 | tf_op jit(solution)/shard_map/near_field/pallas_call | solution.py:812
  43.1 0.0 collective-permute-done.prev_ref
  43.1 0.0 copy-start
  43.1 9.5 %collective-permute-done.1.next_ref = bf16[72,32,128]{2,1,0:T(8,128)(2,1)S(1)} collective-permute-done((bf16[72,32,128]{2,1,0:T(8,128)(2,1)}, bf16[72,32,128]{2,1,0:T(8,128)(2,1)S(1)}, u32[]{:S(2)}, u32[]{:S(2)}) %collective-permute-start.1) | collective-permute-done | bytes 589856 | tf_op jit(solution)/shard_map/ppermute | solution.py:797
  52.6 0.0 copy-start.1
  52.6 0.0 copy-done
  52.6 0.8 copy-done.1
  53.4 19.8 %leaf_couple.1 = f32[68,32,128]{2,1,0:T(8,128)} custom-call(s32[16,128]{1,0:T(8,128)} %get-tuple-element.22.entries, f32[8,256]{1,0:T(8,128)} %get-tuple-element.19.shape_ref, bf16[72,32,128]{2,1,0:T(8,128)(2,1)} %copy-done, bf16[72,32,128]{2,1,0:T(8,128)(2,1)} %copy-done.1, bf16[128,32,128]{2,1,0:T(8,128)(2,1)} %get-tuple-element.23.high_ref, ...), custom_call_target="tpu_custom_call" | custom-call | tf_op jit(solution)/shard_map/leaf_couple/pallas_call | solution.py:853
  73.3 0.0 all-to-all-done.root_ref
  73.3 0.0 copy-start.2
  73.3 0.7 copy-done.2
  74.0 11.9 %tree_down.1.down_ref = f32[64,32,128]{2,1,0:T(8,128)} custom-call(f32[8,256]{1,0:T(8,128)} %get-tuple-element.19.shape_ref, f32[63,32,128]{2,1,0:T(8,128)} %get-tuple-element.20.lev_ref, f32[2,64,64]{2,1,0:T(8,128)} %t_ref.3, f32[32,24,128]{2,1,0:T(8,128)} %copy-done.2), custom_call_target="tpu_custom_call" | custom-call | tf_op jit(solution)/shard_map/tree_down/pallas_call | solution.py:834
  85.9 9.4 %finish.1 = f32[32,16384]{1,0:T(8,128)} custom-call(f32[16,128]{1,0:T(8,128)} %get-tuple-element.15.counts, f32[32,16384]{1,0:T(8,128)} %near_field.1.near_ref, f32[3,16384]{1,0:T(4,128)} %p_ref.5, bf16[128,64,128]{2,1,0:T(8,128)(2,1)} %b_ref.3, bf16[72,32,128]{2,1,0:T(8,128)(2,1)} %copy-done, bf16[72,32,128]{2,1,0:T(8,128)(2,1)} %copy-done.1, ...), custom_call_target="tpu_custom_call" | custom-call | tf_op jit(solution)/shard_map/finish/pallas_call | solution.py:872
Async XLA Ops:
  9.8 63.4 %all-to-all-start = ((f32[32,24,128]{2,1,0:T(8,128)}), f32[32,24,128]{2,1,0:T(8,128)S(1)}, u32[]{:S(2)}, u32[]{:S(2)}) async-start(f32[32,24,128]{2,1,0:T(8,128)} %get-tuple-element.21), calls=%async_computation | async-start | bytes 786432 | tf_op jit(solution)/shard_map/all_to_all | solution.py:793
  17.1 25.9 %collective-permute-start = (bf16[72,32,128]{2,1,0:T(8,128)(2,1)}, bf16[72,32,128]{2,1,0:T(8,128)(2,1)S(1)}, u32[]{:S(2)}, u32[]{:S(2)}) collective-permute-start(bf16[72,32,128]{2,1,0:T(8,128)(2,1)} %get-tuple-element.17), channel_id=1, source_target_pairs={{0,1},{1,2},{2,3},{3,4},{4,5},{5,6},{6,7},{7,8},{8,9},{9,10},{10,1... | collective-permute-start | bytes 1769480 | tf_op jit(solution)/shard_map/ppermute | solution.py:796
  20.8 31.7 %collective-permute-start.1 = (bf16[72,32,128]{2,1,0:T(8,128)(2,1)}, bf16[72,32,128]{2,1,0:T(8,128)(2,1)S(1)}, u32[]{:S(2)}, u32[]{:S(2)}) collective-permute-start(bf16[72,32,128]{2,1,0:T(8,128)(2,1)} %get-tuple-element.18), channel_id=1, source_target_pairs={{1,0},{2,1},{3,2},{4,3},{5,4},{6,5},{7,6},{8,7},{9,8},{10,9},{11,1... | collective-permute-start | bytes 1769480 | tf_op jit(solution)/shard_map/ppermute | solution.py:797
  43.1 9.5 %copy-start = (bf16[72,32,128]{2,1,0:T(8,128)(2,1)}, bf16[72,32,128]{2,1,0:T(8,128)(2,1)S(1)}, u32[]{:S(2)}) copy-start(bf16[72,32,128]{2,1,0:T(8,128)(2,1)S(1)} %collective-permute-done.prev_ref) | copy-start | bytes 1769476
  52.6 0.8 copy-start.1
  73.3 0.7 copy-start.2

commit v5 on v4

--- a/solution.py
+++ b/solution.py
@@ -18,10 +18,10 @@
 HALF = LD // 2
 NEAR_REACH = 8
 FEATS = 64
-BATCH = 16
+BATCH = 8
 LIST = 896
 SEND = 72
-SCALE = 0.5 * math.log2(math.e)
+SCALE = 0.25 * math.log2(math.e)
 NODE = [math.cos((2 * a + 1) * math.pi / 8) for a in range(4)]
 AXES = ("leaf", "sub")
 F32 = jnp.float32
@@ -79,7 +79,9 @@
 
 def decay(t):
     t = jnp.maximum(t, TINY)
-    return jnp.exp2(-(t * lax.rsqrt(t)))
+    r = lax.rsqrt(t.astype(BF16)).astype(F32)
+    s = t * r
+    return jnp.exp2(s * (s * r - 3.0))
 
 
 def tile_from_axes(x_sq, y_sq, z_sq):
@@ -99,7 +101,8 @@
 def merge_up(pairs, t_high, t_low):
     n = pairs.shape[0]
     high, low = halves(pairs.reshape(n * R, 128))
-    out = dot(high, t_high) + dot(high, t_low) + dot(low, t_high)
+    out = dot(high, jnp.concatenate([t_high, t_low], axis=1))
+    out = out[:, 0:128] + out[:, 128:256] + dot(low, t_high)
     return out.reshape(n, R, 128)
 
 
@@ -112,7 +115,8 @@
 def push_down(value, t_high, t_low):
     n = value.shape[0]
     high, low = halves(value.reshape(n * R, 128))
-    out = dot_nt(high, t_high) + dot_nt(high, t_low) + dot_nt(low, t_high)
+    out = dot_nt(high, jnp.concatenate([t_high, t_low], axis=0))
+    out = out[:, 0:128] + out[:, 128:256] + dot_nt(low, t_high)
     return out.reshape(n, R, 128)
 
 
@@ -152,7 +156,8 @@
     t_high, t_low = halves(tile)
     t_high = jnp.concatenate([t_high, t_high], axis=0)
     t_low = jnp.concatenate([t_low, t_low], axis=0)
-    out = dot_nt(high, t_high) + dot_nt(high, t_low) + dot_nt(low_part, t_high)
+    out = dot_nt(high, jnp.concatenate([t_high, t_low], axis=0))
+    out = out[:, 0:128] + out[:, 128:256] + dot_nt(low_part, t_high)
     return jnp.where(low, out[:R], out[R:])
 
 
@@ -566,7 +571,7 @@
     entries, shape_ref, prev_ref, next_ref, high_ref, low_ref,
     leaf_couple,
     shape_tab, high_tab, low_tab, halo_rows, halo_shape, sems,
-    tile_h0, tile_l0, lhs0, tile_h1, tile_l1, lhs1,
+    tiles0, lhs0, tiles1, lhs1,
 ):
     copies = [
         pltpu.make_async_copy(high_ref, high_tab.at[0:LD], sems.at[2]),
@@ -658,13 +663,13 @@
             tiles.append(halves(tile))
         return tiles
 
-    def couple_apply(u, tile_h, tile_l, lhs):
-        both = dot(lhs[u], tile_h[u])
-        both = both[0 : 2 * R] + both[2 * R : 4 * R] + dot(lhs[u, 0 : 2 * R], tile_l[u])
+    def couple_apply(u, tiles, lhs):
+        both = dot(lhs[u], tiles[u])
+        both = both[0 : 2 * R, 0:128] + (both[2 * R : 4 * R, 0:128] + both[0 : 2 * R, 128:256])
         return jnp.where(low32, both[0:R], both[R : 2 * R])
 
     def couple_phase(n, new, old):
-        tile_h, tile_l, lhs = new
+        tiles, lhs = new
         loaded = [couple_load(jnp.minimum(n * UNIT + u, PAIRS - 1)) for u in range(UNIT)]
         results, made = [], []
         for u in range(UNIT):
@@ -675,12 +680,12 @@
                 r, q = k // 4, k % 4
                 lhs[u, r * R : (r + 1) * R, q * 128 : (q + 1) * 128] = value
             for s, (high, low) in enumerate(made[u]):
-                tile_h[u, s * K : (s + 1) * K, :] = high
-                tile_l[u, s * K : (s + 1) * K, :] = low
+                tiles[u, s * K : (s + 1) * K, 0:128] = high
+                tiles[u, s * K : (s + 1) * K, 128:256] = low
         for u in range(UNIT):
             leaf_couple[n * UNIT + u] = results[u]
 
-    buffers = ((tile_h0, tile_l0, lhs0), (tile_h1, tile_l1, lhs1))
+    buffers = ((tiles0, lhs0), (tiles1, lhs1))
     for ref in buffers[1]:
         ref[...] = jnp.zeros(ref.shape, ref.dtype)
 
@@ -846,8 +851,7 @@
     )(shapes, lev, transfer, roots)
 
     stages = [
-        pltpu.VMEM((UNIT, 512, 128), BF16),
-        pltpu.VMEM((UNIT, 512, 128), BF16),
+        pltpu.VMEM((UNIT, 512, 256), BF16),
         pltpu.VMEM((UNIT, 4 * R, 512), BF16),
     ]
     leaf_couple = pl.pallas_call(

time: 95.7 us -> 93.8 us (0.980)
  waiting for transfers between devices: 9.52 us -> 8.31 us
    pallas_call x1, Pallas kernels: 11.9 us -> 9.36 us  [per_device(): pl.pallas_call(down_kernel, name='tree_down', out_shape=shaped(PAIRS, R,...]
    ppermute x1, waiting for transfers between devices: 9.52 us -> 8.3 us  [per_device(): from_next = lax.ppermute(send_prev, AXES, backward)]
    pallas_call x1, Pallas kernels: 18.6 us -> 19.9 us  [per_device(): pl.pallas_call(near_kernel, name='near_field', out_shape=shaped(R, LD * P...]
    pallas_call x1, Pallas kernels: 19.8 us -> 21 us  [per_device(): pl.pallas_call(couple_kernel, name='leaf_couple', out_shape=shaped(PAIRS...]
  transfers between devices with their start and end apart: 3 -> 3, of which waited for: 1 -> 1; matrix products, arithmetic and copies ran while one was open for 0% -> 0% of each run, Pallas kernels for 43% -> 46%
where the time goes in v5:
time: 93.8 us; the launch traced here: 93.4 us
  Pallas kernels  71.1 us (76%)
  starting transfers between devices  12.3 us (13%)
  waiting for transfers between devices  8.31 us (9%)
  local copies, waits for them, and re-layouts  1.57 us (2%)
    pallas_call x1, Pallas kernels, per_device(): pl.pallas_call(couple_kernel, name='leaf_couple', out_shape=shaped(PAIRS...  21 us
    pallas_call x1, Pallas kernels, per_device(): pl.pallas_call(near_kernel, name='near_field', out_shape=shaped(R, LD * P...  19.9 us
    pallas_call x1, Pallas kernels, per_device(): pl.pallas_call(finish_kernel, name='finish', out_shape=shaped(R, LD * P_S...  9.56 us
    pallas_call x1, Pallas kernels, per_device(): pl.pallas_call(down_kernel, name='tree_down', out_shape=shaped(PAIRS, R,...  9.36 us
    pallas_call x1, Pallas kernels, per_device(): pl.pallas_call(leaf_kernel, name='leaf_up', out_shape=(shaped(SEND, R, 12...  9.08 us
    ppermute x1, waiting for transfers between devices, per_device(): from_next = lax.ppermute(send_prev, AXES, backward)  8.3 us
    all_to_all x1, starting transfers between devices, per_device(): roots = lax.all_to_all(root, AXES, 0, 0, tiled=True)  7.3 us
    ppermute x1, starting transfers between devices, per_device(): from_prev = lax.ppermute(send_next, AXES, forward)  3.71 us
  transfers between devices with their start and end apart: 3, of which 1 were waited for; matrix products, arithmetic and copies ran while one was open for 0% of the time, Pallas kernels for 46%

profile of v5, /device:TPU:0, one launch (start us, length us, event | category | flops | bytes accessed | tf_op | source)
XLA Modules:
  0.0 93.4 jit_solution(8885733407420412379)
XLA Ops:
  0.0 9.1 %leaf_up.1 = (bf16[72,32,128]{2,1,0:T(8,128)(2,1)}, bf16[72,32,128]{2,1,0:T(8,128)(2,1)}, bf16[128,32,128]{2,1,0:T(8,128)(2,1)}, bf16[128,32,128]{2,1,0:T(8,128)...) custom-call(bf16[32,16384]{1,0:T(8,128)(2,1)} %x_ref.3, f32[3,16384]{1,0:T(4,128)} %p_ref.5, ...), custom_call_target="tpu_custom_call" | custom-call | tf_op jit(solution)/shard_map/leaf_up/pallas_call | solution.py:775
  9.1 7.3 %all-to-all-start = ((f32[32,24,128]{2,1,0:T(8,128)}), f32[32,24,128]{2,1,0:T(8,128)S(1)}, u32[]{:S(2)}, u32[]{:S(2)}) async-start(f32[32,24,128]{2,1,0:T(8,128)} %get-tuple-element.21), calls=%async_computation | async-start | bytes 786432 | tf_op jit(solution)/shard_map/all_to_all | solution.py:798
  16.4 3.7 %collective-permute-start = (bf16[72,32,128]{2,1,0:T(8,128)(2,1)}, bf16[72,32,128]{2,1,0:T(8,128)(2,1)S(1)}, u32[]{:S(2)}, u32[]{:S(2)}) collective-permute-start(bf16[72,32,128]{2,1,0:T(8,128)(2,1)} %get-tuple-element.17), channel_id=1, source_target_pairs={{0,1},{1,2},{2,3},{3,4},{4,5},{5,6},{6,7},{7,8},{8,9},{9,10},{10,1... | collective-permute-start | bytes 1769480 | tf_op jit(solution)/shard_map/ppermute | solution.py:801
  20.1 1.3 %collective-permute-start.1 = (bf16[72,32,128]{2,1,0:T(8,128)(2,1)}, bf16[72,32,128]{2,1,0:T(8,128)(2,1)S(1)}, u32[]{:S(2)}, u32[]{:S(2)}) collective-permute-start(bf16[72,32,128]{2,1,0:T(8,128)(2,1)} %get-tuple-element.18), channel_id=1, source_target_pairs={{1,0},{2,1},{3,2},{4,3},{5,4},{6,5},{7,6},{8,7},{9,8},{10,9},{11,1... | collective-permute-start | bytes 1769480 | tf_op jit(solution)/shard_map/ppermute | solution.py:802
  21.4 2.3 %lists.1 = (s32[8,896]{1,0:T(8,128)}, f32[16,128]{1,0:T(8,128)}, s32[16,128]{1,0:T(8,128)}) custom-call(s32[8,128]{1,0:T(8,128)} %bitcast.2, s32[8,128]{1,0:T(8,128)} %bitcast.3), custom_call_target="tpu_custom_call" | custom-call | flops 16777216 | bytes 65536 | tf_op jit(solution)/shard_map/lists/pallas_call | solution.py:804
  23.7 19.9 %near_field.1.near_ref = f32[32,16384]{1,0:T(8,128)} custom-call(s32[8,896]{1,0:T(8,128)} %get-tuple-element.16.list_ref, bf16[32,16384]{1,0:T(8,128)(2,1)} %x_ref.3, f32[3,16384]{1,0:T(4,128)} %p_ref.5), custom_call_target="tpu_custom_call" | custom-call | flops 1929379840 | bytes 4194304 | tf_op jit(solution)/shard_map/near_field/pallas_call | solution.py:817
  43.5 0.0 collective-permute-done.prev_ref
  43.5 0.0 copy-start
  43.5 8.3 %collective-permute-done.1.next_ref = bf16[72,32,128]{2,1,0:T(8,128)(2,1)S(1)} collective-permute-done((bf16[72,32,128]{2,1,0:T(8,128)(2,1)}, bf16[72,32,128]{2,1,0:T(8,128)(2,1)S(1)}, u32[]{:S(2)}, u32[]{:S(2)}) %collective-permute-start.1) | collective-permute-done | bytes 589856 | tf_op jit(solution)/shard_map/ppermute | solution.py:802
  51.8 0.0 copy-start.1
  51.8 0.0 copy-done
  51.8 0.8 copy-done.1
  52.7 21.0 %leaf_couple.1 = f32[68,32,128]{2,1,0:T(8,128)} custom-call(s32[16,128]{1,0:T(8,128)} %get-tuple-element.22.entries, f32[8,256]{1,0:T(8,128)} %get-tuple-element.19.shape_ref, bf16[72,32,128]{2,1,0:T(8,128)(2,1)} %copy-done, bf16[72,32,128]{2,1,0:T(8,128)(2,1)} %copy-done.1, bf16[128,32,128]{2,1,0:T(8,128)(2,1)} %get-tuple-element.23.high_ref, ...), custom_call_target="tpu_custom_call" | custom-call | tf_op jit(solution)/shard_map/leaf_couple/pallas_call | solution.py:857
  73.7 0.0 all-to-all-done.root_ref
  73.7 0.0 copy-start.2
  73.7 0.7 copy-done.2
  74.4 9.4 %tree_down.1.down_ref = f32[64,32,128]{2,1,0:T(8,128)} custom-call(f32[8,256]{1,0:T(8,128)} %get-tuple-element.19.shape_ref, f32[63,32,128]{2,1,0:T(8,128)} %get-tuple-element.20.lev_ref, f32[2,64,64]{2,1,0:T(8,128)} %t_ref.3, f32[32,24,128]{2,1,0:T(8,128)} %copy-done.2), custom_call_target="tpu_custom_call" | custom-call | tf_op jit(solution)/shard_map/tree_down/pallas_call | solution.py:839
  83.8 9.6 %finish.1 = f32[32,16384]{1,0:T(8,128)} custom-call(f32[16,128]{1,0:T(8,128)} %get-tuple-element.15.counts, f32[32,16384]{1,0:T(8,128)} %near_field.1.near_ref, f32[3,16384]{1,0:T(4,128)} %p_ref.5, bf16[128,64,128]{2,1,0:T(8,128)(2,1)} %b_ref.3, bf16[72,32,128]{2,1,0:T(8,128)(2,1)} %copy-done, bf16[72,32,128]{2,1,0:T(8,128)(2,1)} %copy-done.1, ...), custom_call_target="tpu_custom_call" | custom-call | tf_op jit(solution)/shard_map/finish/pallas_call | solution.py:876
Async XLA Ops:
  9.1 64.6 %all-to-all-start = ((f32[32,24,128]{2,1,0:T(8,128)}), f32[32,24,128]{2,1,0:T(8,128)S(1)}, u32[]{:S(2)}, u32[]{:S(2)}) async-start(f32[32,24,128]{2,1,0:T(8,128)} %get-tuple-element.21), calls=%async_computation | async-start | bytes 786432 | tf_op jit(solution)/shard_map/all_to_all | solution.py:798
  16.4 27.1 %collective-permute-start = (bf16[72,32,128]{2,1,0:T(8,128)(2,1)}, bf16[72,32,128]{2,1,0:T(8,128)(2,1)S(1)}, u32[]{:S(2)}, u32[]{:S(2)}) collective-permute-start(bf16[72,32,128]{2,1,0:T(8,128)(2,1)} %get-tuple-element.17), channel_id=1, source_target_pairs={{0,1},{1,2},{2,3},{3,4},{4,5},{5,6},{6,7},{7,8},{8,9},{9,10},{10,1... | collective-permute-start | bytes 1769480 | tf_op jit(solution)/shard_map/ppermute | solution.py:801
  20.1 31.7 %collective-permute-start.1 = (bf16[72,32,128]{2,1,0:T(8,128)(2,1)}, bf16[72,32,128]{2,1,0:T(8,128)(2,1)S(1)}, u32[]{:S(2)}, u32[]{:S(2)}) collective-permute-start(bf16[72,32,128]{2,1,0:T(8,128)(2,1)} %get-tuple-element.18), channel_id=1, source_target_pairs={{1,0},{2,1},{3,2},{4,3},{5,4},{6,5},{7,6},{8,7},{9,8},{10,9},{11,1... | collective-permute-start | bytes 1769480 | tf_op jit(solution)/shard_map/ppermute | solution.py:802
  43.5 8.3 %copy-start = (bf16[72,32,128]{2,1,0:T(8,128)(2,1)}, bf16[72,32,128]{2,1,0:T(8,128)(2,1)S(1)}, u32[]{:S(2)}) copy-start(bf16[72,32,128]{2,1,0:T(8,128)(2,1)S(1)} %collective-permute-done.prev_ref) | copy-start | bytes 1769476
  51.8 0.8 copy-start.1
  73.7 0.7 copy-start.2

commit v6 on v5

--- a/solution.py
+++ b/solution.py
@@ -21,13 +21,15 @@
 BATCH = 8
 LIST = 896
 SEND = 72
-SCALE = 0.25 * math.log2(math.e)
+SCALE = 0.5 * math.log2(math.e)
 NODE = [math.cos((2 * a + 1) * math.pi / 8) for a in range(4)]
 AXES = ("leaf", "sub")
 F32 = jnp.float32
 BF16 = jnp.bfloat16
 NT = (((1,), (1,)), ((), ()))
 TINY = 1e-30
+EXP_FIT = [0.9999997512304358, 0.9999730886879146, 0.49952048226020057, 0.16360993458180054, 0.03348150378325188]
+EXP_NEAR = [c * (-math.log(2.0) / 4.0) ** k for k, c in enumerate(EXP_FIT)]
 VMEM_LIMIT = 56 * 1024 * 1024
 
 
@@ -79,9 +81,17 @@
 
 def decay(t):
     t = jnp.maximum(t, TINY)
-    r = lax.rsqrt(t.astype(BF16)).astype(F32)
-    s = t * r
-    return jnp.exp2(s * (s * r - 3.0))
+    return jnp.exp2(-(t * lax.rsqrt(t)))
+
+
+def decay_near(t):
+    t = jnp.maximum(t, TINY)
+    s = t * lax.rsqrt(t)
+    value = EXP_NEAR[4]
+    for coefficient in EXP_NEAR[3::-1]:
+        value = value * s + coefficient
+    value = value * value
+    return value * value
 
 
 def tile_from_axes(x_sq, y_sq, z_sq):
@@ -385,7 +395,7 @@
 
 def near_kernel(
     list_ref, x_ref, p_ref, out_ref,
-    p8, far_feat, own_feat, part1, part2, part3, tile0, tile1,
+    p8, far_feat, own_feat, back, tile0, tile1,
 ):
     first_group = device_index() * GROUPS
     p8[...] = jnp.zeros(p8.shape, F32)
@@ -419,8 +429,7 @@
     lax.fori_loop(0, GROUPS // 4, features, 0)
 
     out_ref[...] = x_ref[...].astype(F32)
-    parts = (out_ref, part1, part2, part3)
-    for ref in (part1, part2, part3, tile0, tile1):
+    for ref in (back, tile0, tile1):
         ref[...] = jnp.zeros(ref.shape, ref.dtype)
 
     total = list_ref[4, 0]
@@ -446,7 +455,9 @@
         for u in range(BATCH // 2):
             pick = jnp.where(low, far[2 * u], far[2 * u + 1])
             dist = dot(pick, block_diagonal(own[2 * u], own[2 * u + 1]))
-            tiles.append(decay(dist).astype(BF16))
+            tiles.append(
+                jnp.concatenate([decay(dist[:, 0:128]), decay_near(dist[:, 128:256])], axis=1).astype(BF16)
+            )
             for h in range(2):
                 k = n * BATCH + 2 * u + h
                 tile = tile_old[u, :, h * 128 : h * 128 + 128]
@@ -459,16 +470,14 @@
                 )
         for u in range(BATCH // 2):
             tile_new[u] = tiles[u]
-        for u in range(BATCH // 2):
-            places, sums = [], []
-            for h in range(2):
-                k = n * BATCH + 2 * u + h
-                for side in range(2):
-                    place = leaf_slice(list_ref[side, k])
-                    places.append(place)
-                    sums.append(parts[2 * h + side][:, place] + updates[2 * u + h][side])
-            for ref, place, value in zip(parts, places, sums):
-                ref[:, place] = value
+        for u in range(BATCH):
+            k = n * BATCH + u
+            to_i = leaf_slice(list_ref[0, k])
+            to_j = leaf_slice(list_ref[1, k])
+            at_i = out_ref[:, to_i] + updates[u][0]
+            at_j = back[:, to_j] + updates[u][1]
+            out_ref[:, to_i] = at_i
+            back[:, to_j] = at_j
 
     def two_phases(m, carry):
         phase(2 * m, tile0, tile1)
@@ -479,9 +488,7 @@
 
     def total_up(m, carry):
         place = pl.ds(pl.multiple_of(m * 1024, 1024), 1024)
-        out_ref[:, place] = (out_ref[:, place] + part1[:, place]) + (
-            part2[:, place] + part3[:, place]
-        )
+        out_ref[:, place] += back[:, place]
         return carry
 
     lax.fori_loop(0, LD * P_SIZE // 1024, total_up, 0)
@@ -825,8 +832,6 @@
             pltpu.VMEM((PAIRS, P_SIZE, 2 * FEATS), BF16),
             pltpu.VMEM((2 * LD, FEATS, P_SIZE), BF16),
             pltpu.VMEM((R, LD * P_SIZE), F32),
-            pltpu.VMEM((R, LD * P_SIZE), F32),
-            pltpu.VMEM((R, LD * P_SIZE), F32),
             pltpu.VMEM((BATCH // 2, 128, 256), BF16),
             pltpu.VMEM((BATCH // 2, 128, 256), BF16),
         ],

time: 93.8 us -> 92.2 us (0.983)
  Pallas kernels: 71.1 us -> 69.4 us
    pallas_call x1, Pallas kernels: 21 us -> 19.6 us  [per_device(): pl.pallas_call(couple_kernel, name='leaf_couple', out_shape=shaped(PAIRS...]
  transfers between devices with their start and end apart: 3 -> 3, of which waited for: 1 -> 1; matrix products, arithmetic and copies ran while one was open for 0% -> 0% of each run, Pallas kernels for 46% -> 45%
where the time goes in v6:
time: 92.2 us; the launch traced here: 91.9 us
  Pallas kernels  69.4 us (75%)
  starting transfers between devices  12.3 us (13%)
  waiting for transfers between devices  8.53 us (9%)
  local copies, waits for them, and re-layouts  1.57 us (2%)
    pallas_call x1, Pallas kernels, per_device(): pl.pallas_call(near_kernel, name='near_field', out_shape=shaped(R, LD * P...  19.6 us
    pallas_call x1, Pallas kernels, per_device(): pl.pallas_call(couple_kernel, name='leaf_couple', out_shape=shaped(PAIRS...  19.6 us
    pallas_call x1, Pallas kernels, per_device(): pl.pallas_call(down_kernel, name='tree_down', out_shape=shaped(PAIRS, R,...  9.44 us
    pallas_call x1, Pallas kernels, per_device(): pl.pallas_call(finish_kernel, name='finish', out_shape=shaped(R, LD * P_S...  9.4 us
    pallas_call x1, Pallas kernels, per_device(): pl.pallas_call(leaf_kernel, name='leaf_up', out_shape=(shaped(SEND, R, 12...  9.08 us
    ppermute x1, waiting for transfers between devices, per_device(): from_next = lax.ppermute(send_prev, AXES, backward)  8.53 us
    all_to_all x1, starting transfers between devices, per_device(): roots = lax.all_to_all(root, AXES, 0, 0, tiled=True)  7.3 us
    ppermute x1, starting transfers between devices, per_device(): from_prev = lax.ppermute(send_next, AXES, forward)  3.71 us
  transfers between devices with their start and end apart: 3, of which 1 were waited for; matrix products, arithmetic and copies ran while one was open for 0% of the time, Pallas kernels for 45%

profile of v6, /device:TPU:0, one launch (start us, length us, event | category | flops | bytes accessed | tf_op | source)
XLA Modules:
  0.0 91.9 jit_solution(13067447359840893748)
XLA Ops:
  0.0 9.1 %leaf_up.1 = (bf16[72,32,128]{2,1,0:T(8,128)(2,1)}, bf16[72,32,128]{2,1,0:T(8,128)(2,1)}, bf16[128,32,128]{2,1,0:T(8,128)(2,1)}, bf16[128,32,128]{2,1,0:T(8,128)...) custom-call(bf16[32,16384]{1,0:T(8,128)(2,1)} %x_ref.3, f32[3,16384]{1,0:T(4,128)} %p_ref.5, ...), custom_call_target="tpu_custom_call" | custom-call | tf_op jit(solution)/shard_map/leaf_up/pallas_call | solution.py:782
  9.1 7.3 %all-to-all-start = ((f32[32,24,128]{2,1,0:T(8,128)}), f32[32,24,128]{2,1,0:T(8,128)S(1)}, u32[]{:S(2)}, u32[]{:S(2)}) async-start(f32[32,24,128]{2,1,0:T(8,128)} %get-tuple-element.21), calls=%async_computation | async-start | bytes 786432 | tf_op jit(solution)/shard_map/all_to_all | solution.py:805
  16.4 3.7 %collective-permute-start = (bf16[72,32,128]{2,1,0:T(8,128)(2,1)}, bf16[72,32,128]{2,1,0:T(8,128)(2,1)S(1)}, u32[]{:S(2)}, u32[]{:S(2)}) collective-permute-start(bf16[72,32,128]{2,1,0:T(8,128)(2,1)} %get-tuple-element.17), channel_id=1, source_target_pairs={{0,1},{1,2},{2,3},{3,4},{4,5},{5,6},{6,7},{7,8},{8,9},{9,10},{10,1... | collective-permute-start | bytes 1769480 | tf_op jit(solution)/shard_map/ppermute | solution.py:808
  20.1 1.3 %collective-permute-start.1 = (bf16[72,32,128]{2,1,0:T(8,128)(2,1)}, bf16[72,32,128]{2,1,0:T(8,128)(2,1)S(1)}, u32[]{:S(2)}, u32[]{:S(2)}) collective-permute-start(bf16[72,32,128]{2,1,0:T(8,128)(2,1)} %get-tuple-element.18), channel_id=1, source_target_pairs={{1,0},{2,1},{3,2},{4,3},{5,4},{6,5},{7,6},{8,7},{9,8},{10,9},{11,1... | collective-permute-start | bytes 1769480 | tf_op jit(solution)/shard_map/ppermute | solution.py:809
  21.4 2.3 %lists.1 = (s32[8,896]{1,0:T(8,128)}, f32[16,128]{1,0:T(8,128)}, s32[16,128]{1,0:T(8,128)}) custom-call(s32[8,128]{1,0:T(8,128)} %bitcast.2, s32[8,128]{1,0:T(8,128)} %bitcast.3), custom_call_target="tpu_custom_call" | custom-call | flops 16777216 | bytes 65536 | tf_op jit(solution)/shard_map/lists/pallas_call | solution.py:811
  23.7 19.6 %near_field.1.near_ref = f32[32,16384]{1,0:T(8,128)} custom-call(s32[8,896]{1,0:T(8,128)} %get-tuple-element.16.list_ref, bf16[32,16384]{1,0:T(8,128)(2,1)} %x_ref.3, f32[3,16384]{1,0:T(4,128)} %p_ref.5), custom_call_target="tpu_custom_call" | custom-call | flops 1929379840 | bytes 4194304 | tf_op jit(solution)/shard_map/near_field/pallas_call | solution.py:824
  43.3 0.0 collective-permute-done.prev_ref
  43.3 0.0 copy-start
  43.3 8.5 %collective-permute-done.1.next_ref = bf16[72,32,128]{2,1,0:T(8,128)(2,1)S(1)} collective-permute-done((bf16[72,32,128]{2,1,0:T(8,128)(2,1)}, bf16[72,32,128]{2,1,0:T(8,128)(2,1)S(1)}, u32[]{:S(2)}, u32[]{:S(2)}) %collective-permute-start.1) | collective-permute-done | bytes 589856 | tf_op jit(solution)/shard_map/ppermute | solution.py:809
  51.8 0.0 copy-start.1
  51.8 0.0 copy-done
  51.8 0.8 copy-done.1
  52.7 19.6 %leaf_couple.1 = f32[68,32,128]{2,1,0:T(8,128)} custom-call(s32[16,128]{1,0:T(8,128)} %get-tuple-element.22.entries, f32[8,256]{1,0:T(8,128)} %get-tuple-element.19.shape_ref, bf16[72,32,128]{2,1,0:T(8,128)(2,1)} %copy-done, bf16[72,32,128]{2,1,0:T(8,128)(2,1)} %copy-done.1, bf16[128,32,128]{2,1,0:T(8,128)(2,1)} %get-tuple-element.23.high_ref, ...), custom_call_target="tpu_custom_call" | custom-call | tf_op jit(solution)/shard_map/leaf_couple/pallas_call | solution.py:862
  72.3 0.0 all-to-all-done.root_ref
  72.3 0.0 copy-start.2
  72.3 0.7 copy-done.2
  73.0 9.4 %tree_down.1.down_ref = f32[64,32,128]{2,1,0:T(8,128)} custom-call(f32[8,256]{1,0:T(8,128)} %get-tuple-element.19.shape_ref, f32[63,32,128]{2,1,0:T(8,128)} %get-tuple-element.20.lev_ref, f32[2,64,64]{2,1,0:T(8,128)} %t_ref.3, f32[32,24,128]{2,1,0:T(8,128)} %copy-done.2), custom_call_target="tpu_custom_call" | custom-call | tf_op jit(solution)/shard_map/tree_down/pallas_call | solution.py:844
  82.5 9.4 %finish.1 = f32[32,16384]{1,0:T(8,128)} custom-call(f32[16,128]{1,0:T(8,128)} %get-tuple-element.15.counts, f32[32,16384]{1,0:T(8,128)} %near_field.1.near_ref, f32[3,16384]{1,0:T(4,128)} %p_ref.5, bf16[128,64,128]{2,1,0:T(8,128)(2,1)} %b_ref.3, bf16[72,32,128]{2,1,0:T(8,128)(2,1)} %copy-done, bf16[72,32,128]{2,1,0:T(8,128)(2,1)} %copy-done.1, ...), custom_call_target="tpu_custom_call" | custom-call | tf_op jit(solution)/shard_map/finish/pallas_call | solution.py:881
Async XLA Ops:
  9.1 63.2 %all-to-all-start = ((f32[32,24,128]{2,1,0:T(8,128)}), f32[32,24,128]{2,1,0:T(8,128)S(1)}, u32[]{:S(2)}, u32[]{:S(2)}) async-start(f32[32,24,128]{2,1,0:T(8,128)} %get-tuple-element.21), calls=%async_computation | async-start | bytes 786432 | tf_op jit(solution)/shard_map/all_to_all | solution.py:805
  16.4 26.9 %collective-permute-start = (bf16[72,32,128]{2,1,0:T(8,128)(2,1)}, bf16[72,32,128]{2,1,0:T(8,128)(2,1)S(1)}, u32[]{:S(2)}, u32[]{:S(2)}) collective-permute-start(bf16[72,32,128]{2,1,0:T(8,128)(2,1)} %get-tuple-element.17), channel_id=1, source_target_pairs={{0,1},{1,2},{2,3},{3,4},{4,5},{5,6},{6,7},{7,8},{8,9},{9,10},{10,1... | collective-permute-start | bytes 1769480 | tf_op jit(solution)/shard_map/ppermute | solution.py:808
  20.1 31.7 %collective-permute-start.1 = (bf16[72,32,128]{2,1,0:T(8,128)(2,1)}, bf16[72,32,128]{2,1,0:T(8,128)(2,1)S(1)}, u32[]{:S(2)}, u32[]{:S(2)}) collective-permute-start(bf16[72,32,128]{2,1,0:T(8,128)(2,1)} %get-tuple-element.18), channel_id=1, source_target_pairs={{1,0},{2,1},{3,2},{4,3},{5,4},{6,5},{7,6},{8,7},{9,8},{10,9},{11,1... | collective-permute-start | bytes 1769480 | tf_op jit(solution)/shard_map/ppermute | solution.py:809
  43.3 8.5 %copy-start = (bf16[72,32,128]{2,1,0:T(8,128)(2,1)}, bf16[72,32,128]{2,1,0:T(8,128)(2,1)S(1)}, u32[]{:S(2)}) copy-start(bf16[72,32,128]{2,1,0:T(8,128)(2,1)S(1)} %collective-permute-done.prev_ref) | copy-start | bytes 1769476
  51.8 0.8 copy-start.1
  72.3 0.7 copy-start.2

commit v7 on v6

--- a/solution.py
+++ b/solution.py
@@ -18,7 +18,7 @@
 HALF = LD // 2
 NEAR_REACH = 8
 FEATS = 64
-BATCH = 8
+BATCH = 16
 LIST = 896
 SEND = 72
 SCALE = 0.5 * math.log2(math.e)
@@ -28,8 +28,6 @@
 BF16 = jnp.bfloat16
 NT = (((1,), (1,)), ((), ()))
 TINY = 1e-30
-EXP_FIT = [0.9999997512304358, 0.9999730886879146, 0.49952048226020057, 0.16360993458180054, 0.03348150378325188]
-EXP_NEAR = [c * (-math.log(2.0) / 4.0) ** k for k, c in enumerate(EXP_FIT)]
 VMEM_LIMIT = 56 * 1024 * 1024
 
 
@@ -82,16 +80,6 @@
 def decay(t):
     t = jnp.maximum(t, TINY)
     return jnp.exp2(-(t * lax.rsqrt(t)))
-
-
-def decay_near(t):
-    t = jnp.maximum(t, TINY)
-    s = t * lax.rsqrt(t)
-    value = EXP_NEAR[4]
-    for coefficient in EXP_NEAR[3::-1]:
-        value = value * s + coefficient
-    value = value * value
-    return value * value
 
 
 def tile_from_axes(x_sq, y_sq, z_sq):
@@ -182,102 +170,7 @@
     )
 
 
-def leaf_kernel(
-    x_ref, p_ref, b_ref, t_ref,
-    send_next, send_prev, high_ref, low_ref, lev_ref, root_ref, shape_ref,
-    coef, pts, shapes, p8,
-):
-    origin = (device_index() * GROUPS).astype(F32)
-    low32 = lanes((R, 128)) < K
-
-    def leaf_pairs(m, carry):
-        values = []
-        for v in range(16):
-            leaf = 16 * m + v
-            x = x_ref[:, pl.ds(pl.multiple_of(leaf * P_SIZE, P_SIZE), P_SIZE)]
-            weights = b_ref[leaf]
-            values.append(dot_nt(x, jnp.concatenate([weights, weights], axis=0)))
-        for v in range(16):
-            high_ref[16 * m + v], low_ref[16 * m + v] = halves(values[v])
-        for v in range(8):
-            coef[8 * m + v] = jnp.where(low32, values[2 * v], values[2 * v + 1])
-        return carry
-
-    lax.fori_loop(0, LD // 16, leaf_pairs, 0)
-
-    t_high, t_low = halves(doubled_transfer(t_ref))
-    pairs = coef[...]
-    for level in range(1, 7):
-        pairs = pair_lanes(merge_up(pairs, t_high, t_low))
-        lev_ref[pl.ds(PAIR_OFFSETS[level], pairs.shape[0])] = pairs
-    root = merge_up(pairs, t_high, t_low)[0]
-
-    for i in range(LD):
-        for d in range(3):
-            pts[d, i : i + 1, :] = p_ref[d : d + 1, i * P_SIZE : (i + 1) * P_SIZE]
-    centers, squares = [], 0.0
-    for d in range(3):
-        coords = (pts[d] - origin if d == 2 else pts[d]) * SCALE
-        center = jnp.sum(coords, axis=1, keepdims=True) * (1.0 / P_SIZE)
-        centers.append(center)
-        squares = squares + jnp.square(coords - center)
-    radius = jnp.sqrt(jnp.max(squares, axis=1, keepdims=True))
-    lane = lanes((LD, 128))
-    shapes[0:LD, :] = jnp.where(
-        lane == 0,
-        centers[0],
-        jnp.where(
-            lane == 1,
-            centers[1],
-            jnp.where(lane == 2, centers[2], jnp.where(lane == 3, radius, 0.0)),
-        ),
-    )
-    count = LD // 2
-    for level in range(1, 8):
-        source = LEVEL_OFFSETS[level - 1]
-        joined = merge_shape_rows(
-            shapes[pl.ds(source, count, stride=2), :],
-            shapes[pl.ds(source + 1, count, stride=2), :],
-        )
-        shapes[pl.ds(LEVEL_OFFSETS[level], count), :] = joined
-        count //= 2
-    shape_rows = jnp.concatenate(
-        [jnp.transpose(shapes[0:128, :])[0:8], jnp.transpose(shapes[128:256, :])[0:8]], axis=1
-    )
-    shape_ref[...] = shape_rows
-    low = lanes((R // 2, 128)) < K
-    block = jnp.concatenate(
-        [
-            jnp.where(low, root[0 : R // 2], root[R // 2 : R]),
-            jnp.broadcast_to(shapes[254:255, :], (8, 128)),
-        ],
-        axis=0,
-    )
-    root_ref[...] = jnp.broadcast_to(block[None], root_ref.shape)
-
-    p8[...] = jnp.zeros((8, 512), F32)
-    for send, first_pair, group in ((send_next, PAIRS // 2, GROUPS - 1), (send_prev, 0, 0)):
-
-        def copy_pairs(m, carry):
-            parts = [halves(coef[first_pair + 8 * m + v]) for v in range(8)]
-            for v in range(8):
-                send[8 * m + v], send[32 + 8 * m + v] = parts[v]
-            return carry
-
-        lax.fori_loop(0, PAIRS // 16, copy_pairs, 0)
-        parts = thirds(shape_rows[:, 0:128])
-        send[68] = jnp.concatenate(list(parts) + [jnp.zeros((8, 128), F32)], axis=0).astype(BF16)
-        p8[0:3, :] = p_ref[:, group * 512 : group * 512 + 512]
-        parts = thirds(p8[...])
-        for k in range(4):
-            send[64 + k] = x_ref[:, group * 512 + k * P_SIZE : group * 512 + (k + 1) * P_SIZE]
-        for part in range(3):
-            send[69 + part] = jnp.concatenate(
-                [parts[part][:, k * P_SIZE : (k + 1) * P_SIZE] for k in range(4)], axis=0
-            ).astype(BF16)
-
-
-def list_kernel(near_ref, coupling_ref, list_ref, count_ref, index_ref):
+def make_lists(near_ref, coupling_ref, list_ref, count_ref, index_ref):
     first_leaf = device_index() * LD
     lane8 = lanes((8, 128))
     row8 = rows((8, 128))
@@ -363,6 +256,135 @@
     index_ref[8:16, :] = jnp.where(target >= 0, reach, 0)
 
 
+CHUNKS = 4
+
+
+def leaf_kernel(
+    x_any, p_ref, b_any, t_ref, near_ref, coupling_ref,
+    send_next, send_prev, high_any, low_any, lev_any, root_ref, shape_ref,
+    list_ref, count_ref, index_ref,
+    x_ref, b_ref, high_ref, low_ref, lev_ref, coef, pts, shapes, p8, sems,
+):
+    leaves = LD // CHUNKS
+    copies = []
+    for c in range(CHUNKS):
+        span = slice(c * leaves * P_SIZE, (c + 1) * leaves * P_SIZE)
+        part = slice(c * leaves, (c + 1) * leaves)
+        copies.append(
+            (
+                pltpu.make_async_copy(x_any.at[:, span], x_ref.at[:, span], sems.at[c]),
+                pltpu.make_async_copy(b_any.at[part], b_ref.at[part], sems.at[CHUNKS + c]),
+            )
+        )
+    for pair in copies:
+        for copy in pair:
+            copy.start()
+    origin = (device_index() * GROUPS).astype(F32)
+    low32 = lanes((R, 128)) < K
+
+    make_lists(near_ref, coupling_ref, list_ref, count_ref, index_ref)
+    for i in range(LD):
+        for d in range(3):
+            pts[d, i : i + 1, :] = p_ref[d : d + 1, i * P_SIZE : (i + 1) * P_SIZE]
+    centers, squares = [], 0.0
+    for d in range(3):
+        coords = (pts[d] - origin if d == 2 else pts[d]) * SCALE
+        center = jnp.sum(coords, axis=1, keepdims=True) * (1.0 / P_SIZE)
+        centers.append(center)
+        squares = squares + jnp.square(coords - center)
+    radius = jnp.sqrt(jnp.max(squares, axis=1, keepdims=True))
+    lane = lanes((LD, 128))
+    shapes[0:LD, :] = jnp.where(
+        lane == 0,
+        centers[0],
+        jnp.where(
+            lane == 1,
+            centers[1],
+            jnp.where(lane == 2, centers[2], jnp.where(lane == 3, radius, 0.0)),
+        ),
+    )
+    count = LD // 2
+    for level in range(1, 8):
+        source = LEVEL_OFFSETS[level - 1]
+        joined = merge_shape_rows(
+            shapes[pl.ds(source, count, stride=2), :],
+            shapes[pl.ds(source + 1, count, stride=2), :],
+        )
+        shapes[pl.ds(LEVEL_OFFSETS[level], count), :] = joined
+        count //= 2
+    shape_rows = jnp.concatenate(
+        [jnp.transpose(shapes[0:128, :])[0:8], jnp.transpose(shapes[128:256, :])[0:8]], axis=1
+    )
+    shape_ref[...] = shape_rows
+
+    def leaf_pairs(m, carry):
+        values = []
+        for v in range(16):
+            leaf = 16 * m + v
+            x = x_ref[:, pl.ds(pl.multiple_of(leaf * P_SIZE, P_SIZE), P_SIZE)]
+            weights = b_ref[leaf]
+            values.append(dot_nt(x, jnp.concatenate([weights, weights], axis=0)))
+        for v in range(16):
+            high_ref[16 * m + v], low_ref[16 * m + v] = halves(values[v])
+        for v in range(8):
+            coef[8 * m + v] = jnp.where(low32, values[2 * v], values[2 * v + 1])
+        return carry
+
+    for c in range(CHUNKS):
+        for copy in copies[c]:
+            copy.wait()
+        steps = leaves // 16
+        lax.fori_loop(c * steps, (c + 1) * steps, leaf_pairs, 0)
+    leaving = [
+        pltpu.make_async_copy(high_ref, high_any, sems.at[2 * CHUNKS]),
+        pltpu.make_async_copy(low_ref, low_any, sems.at[2 * CHUNKS + 1]),
+    ]
+    for copy in leaving:
+        copy.start()
+
+    t_high, t_low = halves(doubled_transfer(t_ref))
+    pairs = coef[...]
+    for level in range(1, 7):
+        pairs = pair_lanes(merge_up(pairs, t_high, t_low))
+        lev_ref[pl.ds(PAIR_OFFSETS[level], pairs.shape[0])] = pairs
+    leaving.append(pltpu.make_async_copy(lev_ref, lev_any, sems.at[2 * CHUNKS + 2]))
+    leaving[2].start()
+    root = merge_up(pairs, t_high, t_low)[0]
+
+    low = lanes((R // 2, 128)) < K
+    block = jnp.concatenate(
+        [
+            jnp.where(low, root[0 : R // 2], root[R // 2 : R]),
+            jnp.broadcast_to(shapes[254:255, :], (8, 128)),
+        ],
+        axis=0,
+    )
+    root_ref[...] = jnp.broadcast_to(block[None], root_ref.shape)
+
+    p8[...] = jnp.zeros((8, 512), F32)
+    for send, first_pair, group in ((send_next, PAIRS // 2, GROUPS - 1), (send_prev, 0, 0)):
+
+        def copy_pairs(m, carry):
+            parts = [halves(coef[first_pair + 8 * m + v]) for v in range(8)]
+            for v in range(8):
+                send[8 * m + v], send[32 + 8 * m + v] = parts[v]
+            return carry
+
+        lax.fori_loop(0, PAIRS // 16, copy_pairs, 0)
+        parts = thirds(shape_rows[:, 0:128])
+        send[68] = jnp.concatenate(list(parts) + [jnp.zeros((8, 128), F32)], axis=0).astype(BF16)
+        p8[0:3, :] = p_ref[:, group * 512 : group * 512 + 512]
+        parts = thirds(p8[...])
+        for k in range(4):
+            send[64 + k] = x_ref[:, group * 512 + k * P_SIZE : group * 512 + (k + 1) * P_SIZE]
+        for part in range(3):
+            send[69 + part] = jnp.concatenate(
+                [parts[part][:, k * P_SIZE : (k + 1) * P_SIZE] for k in range(4)], axis=0
+            ).astype(BF16)
+    for copy in leaving:
+        copy.wait()
+
+
 def point_features(points8, origin_z):
     row = rows(points8.shape)
     center = jnp.where(row == 2, origin_z + 0.5, 1.0)
@@ -395,7 +417,7 @@
 
 def near_kernel(
     list_ref, x_ref, p_ref, out_ref,
-    p8, far_feat, own_feat, back, tile0, tile1,
+    p8, far_feat, own_feat, tile0, tile1,
 ):
     first_group = device_index() * GROUPS
     p8[...] = jnp.zeros(p8.shape, F32)
@@ -429,7 +451,7 @@
     lax.fori_loop(0, GROUPS // 4, features, 0)
 
     out_ref[...] = x_ref[...].astype(F32)
-    for ref in (back, tile0, tile1):
+    for ref in (tile0, tile1):
         ref[...] = jnp.zeros(ref.shape, ref.dtype)
 
     total = list_ref[4, 0]
@@ -455,9 +477,7 @@
         for u in range(BATCH // 2):
             pick = jnp.where(low, far[2 * u], far[2 * u + 1])
             dist = dot(pick, block_diagonal(own[2 * u], own[2 * u + 1]))
-            tiles.append(
-                jnp.concatenate([decay(dist[:, 0:128]), decay_near(dist[:, 128:256])], axis=1).astype(BF16)
-            )
+            tiles.append(decay(dist).astype(BF16))
             for h in range(2):
                 k = n * BATCH + 2 * u + h
                 tile = tile_old[u, :, h * 128 : h * 128 + 128]
@@ -474,10 +494,8 @@
             k = n * BATCH + u
             to_i = leaf_slice(list_ref[0, k])
             to_j = leaf_slice(list_ref[1, k])
-            at_i = out_ref[:, to_i] + updates[u][0]
-            at_j = back[:, to_j] + updates[u][1]
-            out_ref[:, to_i] = at_i
-            back[:, to_j] = at_j
+            out_ref[:, to_i] += updates[u][0]
+            out_ref[:, to_j] += updates[u][1]
 
     def two_phases(m, carry):
         phase(2 * m, tile0, tile1)
@@ -486,17 +504,8 @@
 
     lax.fori_loop(0, (steps + 1) // 2, two_phases, 0)
 
-    def total_up(m, carry):
-        place = pl.ds(pl.multiple_of(m * 1024, 1024), 1024)
-        out_ref[:, place] += back[:, place]
-        return carry
-
-    lax.fori_loop(0, LD * P_SIZE // 1024, total_up, 0)
-
-
-def down_kernel(
-    shape_ref, lev_ref, t_ref, root_ref, down_ref, couple, pairs_scr, shapes,
-):
+
+def tree_down(shape_ref, lev_ref, t_ref, root_ref, down_ref, couple, pairs_scr, shapes):
     lane_u = lane_nodes()
     row_y, row_z = row_nodes()
 
@@ -574,16 +583,12 @@
 UNIT = 2
 
 
-def couple_kernel(
-    entries, shape_ref, prev_ref, next_ref, high_ref, low_ref,
-    leaf_couple,
+def couple_leaves(
+    entries, shape_ref, prev_ref, next_ref, table_copies, leaf_couple,
     shape_tab, high_tab, low_tab, halo_rows, halo_shape, sems,
     tiles0, lhs0, tiles1, lhs1,
 ):
-    copies = [
-        pltpu.make_async_copy(high_ref, high_tab.at[0:LD], sems.at[2]),
-        pltpu.make_async_copy(low_ref, low_tab.at[0:LD], sems.at[3]),
-    ]
+    copies = []
     for k, ref in enumerate((prev_ref, next_ref)):
         parts = ref[68].astype(F32)
         halo_rows[k] = parts[0:8] + parts[8:16] + parts[16:24]
@@ -607,7 +612,7 @@
         return carry
 
     lax.fori_loop(0, LD, own_nodes, 0, unroll=8)
-    for copy in copies[2:]:
+    for copy in copies:
         copy.wait()
     for side, ref in enumerate((prev_ref, next_ref)):
         first = LD + side * HALF
@@ -635,7 +640,7 @@
         lax.fori_loop(0, PAIRS // 8, halo_pairs, 0)
     high_tab[TABLE - 1] = jnp.zeros((R, 128), BF16)
     low_tab[TABLE - 1] = jnp.zeros((R, 128), BF16)
-    for copy in copies[:2]:
+    for copy in table_copies:
         copy.wait()
 
     row_y, row_z = row_nodes()
@@ -704,10 +709,8 @@
     lax.fori_loop(0, PAIRS // UNIT // 2 + 1, couple_two, 0)
 
 
-def finish_kernel(
-    counts, near_ref, p_ref, b_ref, prev_ref, next_ref, down_ref, leaf_couple,
-    out_ref,
-    p8, coords,
+def finish_leaves(
+    counts, p_ref, b_ref, prev_ref, next_ref, down_ref, leaf_couple, out_ref, p8, coords
 ):
     device = device_index()
 
@@ -720,7 +723,7 @@
             values.append(
                 (
                     span,
-                    near_ref[:, span]
+                    out_ref[:, span]
                     + dot(value, block_diagonal(b_ref[2 * c], b_ref[2 * c + 1])),
                 )
             )
@@ -760,6 +763,45 @@
     lax.fori_loop(0, 4, edge, 0)
 
 
+def final_kernel(
+    entries, shape_ref, counts,
+    p_ref, t_ref,
+    near_any, b_any, prev_any, next_any, high_any, low_any, lev_any, root_any,
+    out_ref,
+    b_ref, prev_ref, next_ref, lev_ref, root_ref, down, leaf_couple,
+    couple, pairs_scr, shapes, shape_tab, high_tab, low_tab, halo_rows, halo_shape,
+    tiles0, lhs0, tiles1, lhs1, p8, coords, sems, halo_sems,
+):
+    moves = (
+        (lev_any, lev_ref),
+        (root_any, root_ref),
+        (prev_any, prev_ref),
+        (next_any, next_ref),
+        (high_any, high_tab.at[0:LD]),
+        (low_any, low_tab.at[0:LD]),
+        (b_any, b_ref),
+        (near_any, out_ref),
+    )
+    copies = [pltpu.make_async_copy(a, b, sems.at[k]) for k, (a, b) in enumerate(moves)]
+    for copy in copies:
+        copy.start()
+    copies[0].wait()
+    copies[1].wait()
+    tree_down(shape_ref, lev_ref, t_ref, root_ref, down, couple, pairs_scr, shapes)
+    copies[2].wait()
+    copies[3].wait()
+    couple_leaves(
+        entries, shape_ref, prev_ref, next_ref, copies[4:6], leaf_couple,
+        shape_tab, high_tab, low_tab, halo_rows, halo_shape, halo_sems,
+        tiles0, lhs0, tiles1, lhs1,
+    )
+    copies[6].wait()
+    copies[7].wait()
+    finish_leaves(
+        counts, p_ref, b_ref, prev_ref, next_ref, down, leaf_couple, out_ref, p8, coords
+    )
+
+
 def shaped(*shape, dtype=F32):
     return jax.ShapeDtypeStruct(shape, dtype)
 
@@ -770,6 +812,10 @@
 
 def smem():
     return pl.BlockSpec(memory_space=pltpu.SMEM)
+
+
+def anywhere():
+    return pl.BlockSpec(memory_space=pl.ANY)
 
 
 PARAMS = pltpu.CompilerParams(vmem_limit_bytes=VMEM_LIMIT)
@@ -779,7 +825,7 @@
     near_rows = near_list.T
     coupling_rows = coupling_list.T
     devices = lax.axis_size("sub") * lax.axis_size("leaf")
-    send_next, send_prev, high, low, lev, root, shapes = pl.pallas_call(
+    send_next, send_prev, high, low, lev, root, shapes, tasks, counts, entries = pl.pallas_call(
         leaf_kernel,
         name="leaf_up",
         out_shape=(
@@ -790,17 +836,26 @@
             shaped(PAIRS - 1, R, 128),
             shaped(devices, R // 2 + 8, 128),
             shaped(8, 256),
+            shaped(8, LIST, dtype=jnp.int32),
+            shaped(16, 128),
+            shaped(16, 128, dtype=jnp.int32),
         ),
-        in_specs=[vmem()] * 4,
-        out_specs=[vmem()] * 7,
+        in_specs=[anywhere(), vmem(), anywhere(), vmem(), vmem(), vmem()],
+        out_specs=[vmem()] * 2 + [anywhere()] * 3 + [vmem()] * 5,
         scratch_shapes=[
+            pltpu.VMEM((R, LD * P_SIZE), BF16),
+            pltpu.VMEM((LD, K, P_SIZE), BF16),
+            pltpu.VMEM((LD, R, 128), BF16),
+            pltpu.VMEM((LD, R, 128), BF16),
+            pltpu.VMEM((PAIRS - 1, R, 128), F32),
             pltpu.VMEM((PAIRS, R, 128), F32),
             pltpu.VMEM((3, LD, 128), F32),
             pltpu.VMEM((256, 128), F32),
             pltpu.VMEM((8, 512), F32),
+            pltpu.SemaphoreType.DMA((2 * CHUNKS + 3,)),
         ],
         compiler_params=PARAMS,
-    )(charges, points, basis, transfer)
+    )(charges, points, basis, transfer, near_rows, coupling_rows)
 
     roots = lax.all_to_all(root, AXES, 0, 0, tiled=True)
     forward = [(i, i + 1) for i in range(devices - 1)]
@@ -808,19 +863,6 @@
     from_prev = lax.ppermute(send_next, AXES, forward)
     from_next = lax.ppermute(send_prev, AXES, backward)
 
-    tasks, counts, entries = pl.pallas_call(
-        list_kernel,
-        name="lists",
-        out_shape=(
-            shaped(8, LIST, dtype=jnp.int32),
-            shaped(16, 128),
-            shaped(16, 128, dtype=jnp.int32),
-        ),
-        in_specs=[vmem()] * 2,
-        out_specs=[vmem()] * 3,
-        compiler_params=PARAMS,
-        cost_estimate=pl.CostEstimate(flops=1 << 24, bytes_accessed=1 << 16, transcendentals=0),
-    )(near_rows, coupling_rows)
     near = pl.pallas_call(
         near_kernel,
         name="near_field",
@@ -831,7 +873,6 @@
             pltpu.VMEM((4, 8, 512), F32),
             pltpu.VMEM((PAIRS, P_SIZE, 2 * FEATS), BF16),
             pltpu.VMEM((2 * LD, FEATS, P_SIZE), BF16),
-            pltpu.VMEM((R, LD * P_SIZE), F32),
             pltpu.VMEM((BATCH // 2, 128, 256), BF16),
             pltpu.VMEM((BATCH // 2, 128, 256), BF16),
         ],
@@ -841,52 +882,46 @@
         ),
     )(tasks, charges, points)
 
-    down = pl.pallas_call(
-        down_kernel,
-        name="tree_down",
-        out_shape=shaped(PAIRS, R, 128),
-        in_specs=[smem()] + [vmem()] * 3,
-        out_specs=vmem(),
-        scratch_shapes=[
-            pltpu.VMEM((PAIRS - 1, R, 128), F32),
-            pltpu.VMEM((devices, R, 128), F32),
-            pltpu.VMEM((2 * devices, 128), F32),
-        ],
-        compiler_params=PARAMS,
-    )(shapes, lev, transfer, roots)
-
     stages = [
         pltpu.VMEM((UNIT, 512, 256), BF16),
         pltpu.VMEM((UNIT, 4 * R, 512), BF16),
     ]
-    leaf_couple = pl.pallas_call(
-        couple_kernel,
-        name="leaf_couple",
-        out_shape=shaped(PAIRS + 2 * UNIT, R, 128),
-        in_specs=[smem()] * 2 + [vmem()] * 2 + [pl.BlockSpec(memory_space=pl.ANY)] * 2,
+    return pl.pallas_call(
+        final_kernel,
+        name="tree_couple_finish",
+        out_shape=shaped(R, LD * P_SIZE),
+        in_specs=[smem()] * 3 + [vmem()] * 2 + [anywhere()] * 8,
         out_specs=vmem(),
         scratch_shapes=[
+            pltpu.VMEM((LD, K, P_SIZE), BF16),
+            pltpu.VMEM((SEND, R, 128), BF16),
+            pltpu.VMEM((SEND, R, 128), BF16),
+            pltpu.VMEM((PAIRS - 1, R, 128), F32),
+            pltpu.VMEM((devices, R // 2 + 8, 128), F32),
+            pltpu.VMEM((PAIRS, R, 128), F32),
+            pltpu.VMEM((PAIRS + 2 * UNIT, R, 128), F32),
+            pltpu.VMEM((PAIRS - 1, R, 128), F32),
+            pltpu.VMEM((devices, R, 128), F32),
+            pltpu.VMEM((2 * devices, 128), F32),
             pltpu.VMEM((2 * LD, 8, 128), F32),
             pltpu.VMEM((TABLE, R, 128), BF16),
             pltpu.VMEM((TABLE, R, 128), BF16),
             pltpu.VMEM((2, 8, 128), F32),
             pltpu.SMEM((2, 8, 128), F32),
-            pltpu.SemaphoreType.DMA((4,)),
         ]
         + stages
-        + stages,
+        + stages
+        + [
+            pltpu.VMEM((2, 8, 512), F32),
+            pltpu.VMEM((2, R, 128), F32),
+            pltpu.SemaphoreType.DMA((8,)),
+            pltpu.SemaphoreType.DMA((2,)),
+        ],
         compiler_params=PARAMS,
-    )(entries, shapes, from_prev, from_next, high, low)
-
-    return pl.pallas_call(
-        finish_kernel,
-        name="finish",
-        out_shape=shaped(R, LD * P_SIZE),
-        in_specs=[smem()] + [vmem()] * 7,
-        out_specs=vmem(),
-        scratch_shapes=[pltpu.VMEM((2, 8, 512), F32), pltpu.VMEM((2, R, 128), F32)],
-        compiler_params=PARAMS,
-    )(counts, near, points, basis, from_prev, from_next, down, leaf_couple)
+    )(
+        entries, shapes, counts, points, transfer,
+        near, basis, from_prev, from_next, high, low, lev, roots,
+    )
 
 
 def solution(mesh):

time: 92.2 us -> 86.1 us (0.934)
  Pallas kernels: 69.4 us -> 60.1 us
  waiting for transfers between devices: 8.53 us -> 12.4 us
    pallas_call x4 -> x1, Pallas kernels: 40.7 us -> 33 us  [per_device(): pl.pallas_call(final_kernel, name='tree_couple_finish', out_shape=shaped(...]
    ppermute x1, waiting for transfers between devices: 8.53 us -> 12.4 us  [per_device(): from_next = lax.ppermute(send_prev, AXES, backward)]
    pallas_call x1, Pallas kernels: 19.6 us -> 18 us  [per_device(): pl.pallas_call(near_kernel, name='near_field', out_shape=shaped(R, LD * P...]
  transfers between devices with their start and end apart: 3 -> 3, of which waited for: 1 -> 1; matrix products, arithmetic and copies ran while one was open for 0% -> 0% of each run, Pallas kernels for 45% -> 21%
where the time goes in v7:
time: 86.1 us; the launch traced here: 85.8 us
  Pallas kernels  60.1 us (70%)
  waiting for transfers between devices  12.4 us (14%)
  starting transfers between devices  12.3 us (14%)
  local copies, waits for them, and re-layouts  0.97 us (1%)
    pallas_call x1, Pallas kernels, per_device(): pl.pallas_call(final_kernel, name='tree_couple_finish', out_shape=shaped(...  33 us
    pallas_call x1, Pallas kernels, per_device(): pl.pallas_call(near_kernel, name='near_field', out_shape=shaped(R, LD * P...  18 us
    ppermute x1, waiting for transfers between devices, per_device(): from_next = lax.ppermute(send_prev, AXES, backward)  12.4 us
    pallas_call x1, Pallas kernels, per_device(): pl.pallas_call(leaf_kernel, name='leaf_up', out_shape=(shaped(SEND, R, 12...  9.05 us
    all_to_all x1, starting transfers between devices, per_device(): roots = lax.all_to_all(root, AXES, 0, 0, tiled=True)  7.3 us
    ppermute x1, starting transfers between devices, per_device(): from_prev = lax.ppermute(send_next, AXES, forward)  3.71 us
  transfers between devices with their start and end apart: 3, of which 1 were waited for; matrix products, arithmetic and copies ran while one was open for 0% of the time, Pallas kernels for 21%

profile of v7, /device:TPU:0, one launch (start us, length us, event | category | flops | bytes accessed | tf_op | source)
XLA Modules:
  0.0 85.8 jit_solution(7926869603697348157)
XLA Ops:
  0.0 9.1 %leaf_up.1 = (bf16[72,32,128]{2,1,0:T(8,128)(2,1)}, bf16[72,32,128]{2,1,0:T(8,128)(2,1)}, bf16[128,32,128]{2,1,0:T(8,128)(2,1)}, bf16[128,32,128]{2,1,0:T(8,128)...) custom-call(bf16[32,16384]{1,0:T(8,128)(2,1)} %x_ref.1, ...), custom_call_target="tpu_custom_call" | custom-call | tf_op jit(solution)/shard_map/leaf_up/pallas_call | solution.py:828
  9.1 7.3 %all-to-all-start = ((f32[32,24,128]{2,1,0:T(8,128)}), f32[32,24,128]{2,1,0:T(8,128)S(1)}, u32[]{:S(2)}, u32[]{:S(2)}) async-start(f32[32,24,128]{2,1,0:T(8,128)} %get-tuple-element.24), calls=%async_computation | async-start | bytes 786432 | tf_op jit(solution)/shard_map/all_to_all | solution.py:860
  16.4 3.7 %collective-permute-start = (bf16[72,32,128]{2,1,0:T(8,128)(2,1)}, bf16[72,32,128]{2,1,0:T(8,128)(2,1)S(1)}, u32[]{:S(2)}, u32[]{:S(2)}) collective-permute-start(bf16[72,32,128]{2,1,0:T(8,128)(2,1)} %get-tuple-element.19), channel_id=1, source_target_pairs={{0,1},{1,2},{2,3},{3,4},{4,5},{5,6},{6,7},{7,8},{8,9},{9,10},{10,1... | collective-permute-start | bytes 1769480 | tf_op jit(solution)/shard_map/ppermute | solution.py:863
  20.1 1.3 %collective-permute-start.1 = (bf16[72,32,128]{2,1,0:T(8,128)(2,1)}, bf16[72,32,128]{2,1,0:T(8,128)(2,1)S(1)}, u32[]{:S(2)}, u32[]{:S(2)}) collective-permute-start(bf16[72,32,128]{2,1,0:T(8,128)(2,1)} %get-tuple-element.20), channel_id=1, source_target_pairs={{1,0},{2,1},{3,2},{4,3},{5,4},{6,5},{7,6},{8,7},{9,8},{10,9},{11,1... | collective-permute-start | bytes 1769480 | tf_op jit(solution)/shard_map/ppermute | solution.py:864
  21.4 18.0 %near_field.1.near_any = f32[32,16384]{1,0:T(8,128)} custom-call(s32[8,896]{1,0:T(8,128)} %get-tuple-element.18.list_ref, bf16[32,16384]{1,0:T(8,128)(2,1)} %x_ref.1, f32[3,16384]{1,0:T(4,128)} %p_ref.5), custom_call_target="tpu_custom_call" | custom-call | flops 1929379840 | bytes 4194304 | tf_op jit(solution)/shard_map/near_field/pallas_call | solution.py:866
  39.4 0.0 collective-permute-done.prev_any
  39.4 0.0 copy-start.1
  39.4 12.4 %collective-permute-done.1.next_any = bf16[72,32,128]{2,1,0:T(8,128)(2,1)S(1)} collective-permute-done((bf16[72,32,128]{2,1,0:T(8,128)(2,1)}, bf16[72,32,128]{2,1,0:T(8,128)(2,1)S(1)}, u32[]{:S(2)}, u32[]{:S(2)}) %collective-permute-start.1) | collective-permute-done | bytes 589856 | tf_op jit(solution)/shard_map/ppermute | solution.py:864
  51.8 0.0 copy-start.2
  51.8 0.0 all-to-all-done.root_any
  51.8 0.0 copy-start
  51.8 0.0 copy-done.1
  51.8 0.8 copy-done.2
  52.7 0.1 copy-done
  52.8 33.0 %tree_couple_finish.1 = f32[32,16384]{1,0:T(8,128)} custom-call(s32[16,128]{1,0:T(8,128)} %get-tuple-element.15.entries, f32[8,256]{1,0:T(8,128)} %get-tuple-element.16.shape_ref, f32[16,128]{1,0:T(8,128)} %get-tuple-element.17.counts, f32[3,16384]{1,0:T(4,128)} %p_ref.5, f32[2,64,64]{2,1,0:T(8,128)} %t_ref.3, f32[32,16384]{1,0:T(8,128)} %near_field.1.near_any, ...), custom_call_target="tpu_custom_call" | custom-call | tf_op jit(solution)/shard_map/tree_couple_finish/pallas_call | solution.py:889
Async XLA Ops:
  9.1 42.8 %all-to-all-start = ((f32[32,24,128]{2,1,0:T(8,128)}), f32[32,24,128]{2,1,0:T(8,128)S(1)}, u32[]{:S(2)}, u32[]{:S(2)}) async-start(f32[32,24,128]{2,1,0:T(8,128)} %get-tuple-element.24), calls=%async_computation | async-start | bytes 786432 | tf_op jit(solution)/shard_map/all_to_all | solution.py:860
  16.4 23.0 %collective-permute-start = (bf16[72,32,128]{2,1,0:T(8,128)(2,1)}, bf16[72,32,128]{2,1,0:T(8,128)(2,1)S(1)}, u32[]{:S(2)}, u32[]{:S(2)}) collective-permute-start(bf16[72,32,128]{2,1,0:T(8,128)(2,1)} %get-tuple-element.19), channel_id=1, source_target_pairs={{0,1},{1,2},{2,3},{3,4},{4,5},{5,6},{6,7},{7,8},{8,9},{9,10},{10,1... | collective-permute-start | bytes 1769480 | tf_op jit(solution)/shard_map/ppermute | solution.py:863
  20.1 31.7 %collective-permute-start.1 = (bf16[72,32,128]{2,1,0:T(8,128)(2,1)}, bf16[72,32,128]{2,1,0:T(8,128)(2,1)S(1)}, u32[]{:S(2)}, u32[]{:S(2)}) collective-permute-start(bf16[72,32,128]{2,1,0:T(8,128)(2,1)} %get-tuple-element.20), channel_id=1, source_target_pairs={{1,0},{2,1},{3,2},{4,3},{5,4},{6,5},{7,6},{8,7},{9,8},{10,9},{11,1... | collective-permute-start | bytes 1769480 | tf_op jit(solution)/shard_map/ppermute | solution.py:864
  39.4 12.4 %copy-start.1 = (bf16[72,32,128]{2,1,0:T(8,128)(2,1)}, bf16[72,32,128]{2,1,0:T(8,128)(2,1)S(1)}, u32[]{:S(2)}) copy-start(bf16[72,32,128]{2,1,0:T(8,128)(2,1)S(1)} %collective-permute-done.prev_any) | copy-start | bytes 1769476
  51.8 0.8 copy-start.2
  51.8 1.0 %copy-start = (f32[32,24,128]{2,1,0:T(8,128)}, f32[32,24,128]{2,1,0:T(8,128)S(1)}, u32[]{:S(2)}) copy-start(f32[32,24,128]{2,1,0:T(8,128)S(1)} %all-to-all-done.root_any) | copy-start | bytes 1179652

commit v8 on v7

--- a/solution.py
+++ b/solution.py
@@ -478,14 +478,16 @@
             pick = jnp.where(low, far[2 * u], far[2 * u + 1])
             dist = dot(pick, block_diagonal(own[2 * u], own[2 * u + 1]))
             tiles.append(decay(dist).astype(BF16))
+            weights = block_diagonal(tile_old[u, :, 0:128], tile_old[u, :, 128:256])
+            to_i = dot(jnp.concatenate([sources[2 * u][0], sources[2 * u + 1][0]], axis=1), weights)
+            to_j = dot_nt(jnp.concatenate([sources[2 * u][1], sources[2 * u + 1][1]], axis=1), weights)
             for h in range(2):
                 k = n * BATCH + 2 * u + h
-                tile = tile_old[u, :, h * 128 : h * 128 + 128]
-                x_j, x_i = sources[2 * u + h]
+                span = slice(h * 128, (h + 1) * 128)
                 updates.append(
                     (
-                        dot(x_j, tile) * list_ref[2, k].astype(F32),
-                        dot_nt(x_i, tile) * list_ref[3, k].astype(F32),
+                        to_i[:, span] * list_ref[2, k].astype(F32),
+                        to_j[:, span] * list_ref[3, k].astype(F32),
                     )
                 )
         for u in range(BATCH // 2):
@@ -580,7 +582,7 @@
     down_ref[...] = push_down(children_of(value), t_high, t_low)
 
 
-UNIT = 2
+UNIT = 4
 
 
 def couple_leaves(
@@ -645,26 +647,24 @@
 
     row_y, row_z = row_nodes()
 
-    def couple_load(pair):
+    def couple_tiles(pair, u, tiles, lhs):
         leaves = (2 * pair, 2 * pair + 1)
+        for q in range(4):
+            span = slice(q * 128, (q + 1) * 128)
+            for h in range(2):
+                e0, e1 = entries[2 * q, leaves[h]], entries[2 * q + 1, leaves[h]]
+                lhs[u, h * R : (h + 1) * R, span] = jnp.where(low32, high_tab[e0], high_tab[e1])
+                lhs[u, (2 + h) * R : (3 + h) * R, span] = jnp.where(
+                    low32, low_tab[e0], low_tab[e1]
+                )
         own = jnp.where(low8, shape_tab[HALF + leaves[0]], shape_tab[HALF + leaves[1]])
+        radius = jnp.broadcast_to(own[3:4], (8, 128))
+        own = [jnp.broadcast_to(own[d : d + 1], (8, 128)) + radius * lane_u[d] for d in range(3)]
         fars = []
         for s in range(8):
             e0, e1 = entries[8 + s, leaves[0]], entries[8 + s, leaves[1]]
             fars.append(jnp.where(low8, shape_tab[e0], shape_tab[e1]))
-        sources = []
-        for tab in (high_tab, low_tab):
-            for h in range(2):
-                for q in range(4):
-                    e0, e1 = entries[2 * q, leaves[h]], entries[2 * q + 1, leaves[h]]
-                    sources.append(jnp.where(low32, tab[e0], tab[e1]))
-        return own, fars, sources
-
-    def couple_tiles(own, fars):
-        radius = jnp.broadcast_to(own[3:4], (8, 128))
-        own = [jnp.broadcast_to(own[d : d + 1], (8, 128)) + radius * lane_u[d] for d in range(3)]
-        tiles = []
-        for far in fars:
+        for s, far in enumerate(fars):
             reach = jnp.broadcast_to(far[3:4], (8, 128))
             gap = [own[d] - jnp.broadcast_to(far[d : d + 1], (8, 128)) for d in range(3)]
             tile = tile_from_axes(
@@ -672,8 +672,9 @@
                 [jnp.square(gap[1] - reach * row_y[h]) for h in range(2)],
                 jnp.square(gap[2] - reach * row_z),
             )
-            tiles.append(halves(tile))
-        return tiles
+            high, low = halves(tile)
+            tiles[u, s * K : (s + 1) * K, 0:128] = high
+            tiles[u, s * K : (s + 1) * K, 128:256] = low
 
     def couple_apply(u, tiles, lhs):
         both = dot(lhs[u], tiles[u])
@@ -681,21 +682,9 @@
         return jnp.where(low32, both[0:R], both[R : 2 * R])
 
     def couple_phase(n, new, old):
-        tiles, lhs = new
-        loaded = [couple_load(jnp.minimum(n * UNIT + u, PAIRS - 1)) for u in range(UNIT)]
-        results, made = [], []
         for u in range(UNIT):
-            results.append(couple_apply(u, *old))
-            made.append(couple_tiles(loaded[u][0], loaded[u][1]))
-        for u in range(UNIT):
-            for k, value in enumerate(loaded[u][2]):
-                r, q = k // 4, k % 4
-                lhs[u, r * R : (r + 1) * R, q * 128 : (q + 1) * 128] = value
-            for s, (high, low) in enumerate(made[u]):
-                tiles[u, s * K : (s + 1) * K, 0:128] = high
-                tiles[u, s * K : (s + 1) * K, 128:256] = low
-        for u in range(UNIT):
-            leaf_couple[n * UNIT + u] = results[u]
+            couple_tiles(jnp.minimum(n * UNIT + u, PAIRS - 1), u, *new)
+            leaf_couple[n * UNIT + u] = couple_apply(u, *old)
 
     buffers = ((tiles0, lhs0), (tiles1, lhs1))
     for ref in buffers[1]:
@@ -763,40 +752,45 @@
     lax.fori_loop(0, 4, edge, 0)
 
 
+def tree_kernel(
+    shape_ref, t_ref, lev_ref, root_any, down_ref, root_ref, couple, pairs_scr, shapes, sems
+):
+    copy = pltpu.make_async_copy(root_any, root_ref, sems.at[0])
+    copy.start()
+    copy.wait()
+    tree_down(shape_ref, lev_ref, t_ref, root_ref, down_ref, couple, pairs_scr, shapes)
+
+
 def final_kernel(
     entries, shape_ref, counts,
-    p_ref, t_ref,
-    near_any, b_any, prev_any, next_any, high_any, low_any, lev_any, root_any,
+    p_ref,
+    near_any, b_any, prev_any, next_any, high_any, low_any, down_any,
     out_ref,
-    b_ref, prev_ref, next_ref, lev_ref, root_ref, down, leaf_couple,
-    couple, pairs_scr, shapes, shape_tab, high_tab, low_tab, halo_rows, halo_shape,
+    b_ref, prev_ref, next_ref, down, leaf_couple,
+    shape_tab, high_tab, low_tab, halo_rows, halo_shape,
     tiles0, lhs0, tiles1, lhs1, p8, coords, sems, halo_sems,
 ):
     moves = (
-        (lev_any, lev_ref),
-        (root_any, root_ref),
         (prev_any, prev_ref),
         (next_any, next_ref),
         (high_any, high_tab.at[0:LD]),
         (low_any, low_tab.at[0:LD]),
         (b_any, b_ref),
         (near_any, out_ref),
+        (down_any, down),
     )
     copies = [pltpu.make_async_copy(a, b, sems.at[k]) for k, (a, b) in enumerate(moves)]
     for copy in copies:
         copy.start()
     copies[0].wait()
     copies[1].wait()
-    tree_down(shape_ref, lev_ref, t_ref, root_ref, down, couple, pairs_scr, shapes)
-    copies[2].wait()
-    copies[3].wait()
     couple_leaves(
-        entries, shape_ref, prev_ref, next_ref, copies[4:6], leaf_couple,
+        entries, shape_ref, prev_ref, next_ref, copies[2:4], leaf_couple,
         shape_tab, high_tab, low_tab, halo_rows, halo_shape, halo_sems,
         tiles0, lhs0, tiles1, lhs1,
     )
-    copies[6].wait()
-    copies[7].wait()
+    for copy in copies[4:]:
+        copy.wait()
     finish_leaves(
         counts, p_ref, b_ref, prev_ref, next_ref, down, leaf_couple, out_ref, p8, coords
     )
@@ -882,27 +876,40 @@
         ),
     )(tasks, charges, points)
 
+    near, roots = lax.optimization_barrier((near, roots))
     stages = [
         pltpu.VMEM((UNIT, 512, 256), BF16),
         pltpu.VMEM((UNIT, 4 * R, 512), BF16),
     ]
+    down = pl.pallas_call(
+        tree_kernel,
+        name="tree_down",
+        out_shape=shaped(PAIRS, R, 128),
+        in_specs=[smem(), vmem(), vmem(), anywhere()],
+        out_specs=vmem(),
+        scratch_shapes=[
+            pltpu.VMEM((devices, R // 2 + 8, 128), F32),
+            pltpu.VMEM((PAIRS - 1, R, 128), F32),
+            pltpu.VMEM((devices, R, 128), F32),
+            pltpu.VMEM((2 * devices, 128), F32),
+            pltpu.SemaphoreType.DMA((1,)),
+        ],
+        compiler_params=PARAMS,
+    )(shapes, transfer, lev, roots)
+    from_prev, from_next, down = lax.optimization_barrier((from_prev, from_next, down))
+
     return pl.pallas_call(
         final_kernel,
-        name="tree_couple_finish",
+        name="couple_finish",
         out_shape=shaped(R, LD * P_SIZE),
-        in_specs=[smem()] * 3 + [vmem()] * 2 + [anywhere()] * 8,
+        in_specs=[smem()] * 3 + [vmem()] + [anywhere()] * 7,
         out_specs=vmem(),
         scratch_shapes=[
             pltpu.VMEM((LD, K, P_SIZE), BF16),
             pltpu.VMEM((SEND, R, 128), BF16),
             pltpu.VMEM((SEND, R, 128), BF16),
-            pltpu.VMEM((PAIRS - 1, R, 128), F32),
-            pltpu.VMEM((devices, R // 2 + 8, 128), F32),
             pltpu.VMEM((PAIRS, R, 128), F32),
             pltpu.VMEM((PAIRS + 2 * UNIT, R, 128), F32),
-            pltpu.VMEM((PAIRS - 1, R, 128), F32),
-            pltpu.VMEM((devices, R, 128), F32),
-            pltpu.VMEM((2 * devices, 128), F32),
             pltpu.VMEM((2 * LD, 8, 128), F32),
             pltpu.VMEM((TABLE, R, 128), BF16),
             pltpu.VMEM((TABLE, R, 128), BF16),
@@ -914,13 +921,13 @@
         + [
             pltpu.VMEM((2, 8, 512), F32),
             pltpu.VMEM((2, R, 128), F32),
-            pltpu.SemaphoreType.DMA((8,)),
+            pltpu.SemaphoreType.DMA((7,)),
             pltpu.SemaphoreType.DMA((2,)),
         ],
         compiler_params=PARAMS,
     )(
-        entries, shapes, counts, points, transfer,
-        near, basis, from_prev, from_next, high, low, lev, roots,
+        entries, shapes, counts, points,
+        near, basis, from_prev, from_next, high, low, down,
     )
 
 

time: 86.1 us -> 82.7 us (0.961)
  the two profiles are of different devices: /device:TPU:0 before, /device:TPU:2 now
where the time goes in v8:
time: 82.7 us; the launch traced here: 82.3 us
  Pallas kernels  66 us (80%)
  starting transfers between devices  14.4 us (17%)
  local copies, waits for them, and re-layouts  1.81 us (2%)
    pallas_call x1, Pallas kernels, per_device(): pl.pallas_call(final_kernel, name='couple_finish', out_shape=shaped(R, LD...  25.4 us
    pallas_call x1, Pallas kernels, per_device(): pl.pallas_call(near_kernel, name='near_field', out_shape=shaped(R, LD * P...  21.3 us
    pallas_call x1, Pallas kernels, per_device(): pl.pallas_call(tree_kernel, name='tree_down', out_shape=shaped(PAIRS, R,...  10.3 us
    pallas_call x1, Pallas kernels, per_device(): pl.pallas_call(leaf_kernel, name='leaf_up', out_shape=(shaped(SEND, R, 12...  9.04 us
    all_to_all x1, starting transfers between devices, per_device(): roots = lax.all_to_all(root, AXES, 0, 0, tiled=True)  6.13 us
    ppermute x1, starting transfers between devices, per_device(): from_next = lax.ppermute(send_prev, AXES, backward)  4.88 us
    ppermute x1, starting transfers between devices, per_device(): from_prev = lax.ppermute(send_next, AXES, forward)  3.37 us
    unnamed x6, local copies, waits for them, and re-layouts  1.81 us
  transfers between devices with their start and end apart: 3, of which 0 were waited for; matrix products, arithmetic and copies ran while one was open for 0% of the time, Pallas kernels for 38%

profile of v8, /device:TPU:2, one launch (start us, length us, event | category | flops | bytes accessed | tf_op | source)
XLA Modules:
  0.0 82.3 jit_solution(1382375826987141760)
XLA Ops:
  0.0 9.0 %leaf_up.1 = (bf16[72,32,128]{2,1,0:T(8,128)(2,1)}, bf16[72,32,128]{2,1,0:T(8,128)(2,1)}, bf16[128,32,128]{2,1,0:T(8,128)(2,1)}, bf16[128,32,128]{2,1,0:T(8,128)...) custom-call(bf16[32,16384]{1,0:T(8,128)(2,1)} %x_ref.1, ...), custom_call_target="tpu_custom_call" | custom-call | tf_op jit(solution)/shard_map/leaf_up/pallas_call | solution.py:822
  9.0 6.1 %all-to-all-start = ((f32[32,24,128]{2,1,0:T(8,128)}), f32[32,24,128]{2,1,0:T(8,128)S(1)}, u32[]{:S(2)}, u32[]{:S(2)}) async-start(f32[32,24,128]{2,1,0:T(8,128)} %get-tuple-element.24), calls=%async_computation | async-start | bytes 786432 | tf_op jit(solution)/shard_map/all_to_all | solution.py:854
  15.2 3.4 %collective-permute-start = (bf16[72,32,128]{2,1,0:T(8,128)(2,1)}, bf16[72,32,128]{2,1,0:T(8,128)(2,1)S(1)}, u32[]{:S(2)}, u32[]{:S(2)}) collective-permute-start(bf16[72,32,128]{2,1,0:T(8,128)(2,1)} %get-tuple-element.26), channel_id=1, source_target_pairs={{0,1},{1,2},{2,3},{3,4},{4,5},{5,6},{6,7},{7,8},{8,9},{9,10},{10,1... | collective-permute-start | bytes 1769480 | tf_op jit(solution)/shard_map/ppermute | solution.py:857
  18.6 4.9 %collective-permute-start.1 = (bf16[72,32,128]{2,1,0:T(8,128)(2,1)}, bf16[72,32,128]{2,1,0:T(8,128)(2,1)S(1)}, u32[]{:S(2)}, u32[]{:S(2)}) collective-permute-start(bf16[72,32,128]{2,1,0:T(8,128)(2,1)} %get-tuple-element.27), channel_id=1, source_target_pairs={{1,0},{2,1},{3,2},{4,3},{5,4},{6,5},{7,6},{8,7},{9,8},{10,9},{11,1... | collective-permute-start | bytes 1769480 | tf_op jit(solution)/shard_map/ppermute | solution.py:858
  23.5 21.3 %near_field.1.near_any = f32[32,16384]{1,0:T(8,128)} custom-call(s32[8,896]{1,0:T(8,128)} %get-tuple-element.23.list_ref, bf16[32,16384]{1,0:T(8,128)(2,1)} %x_ref.1, f32[3,16384]{1,0:T(4,128)} %p_ref.5), custom_call_target="tpu_custom_call" | custom-call | flops 1929379840 | bytes 4194304 | tf_op jit(solution)/shard_map/near_field/pallas_call | solution.py:860
  44.8 0.0 all-to-all-done.root_any
  44.8 0.0 copy-start
  44.8 0.8 copy-done
  45.5 10.3 %tree_down.1.down_any = f32[64,32,128]{2,1,0:T(8,128)} custom-call(f32[8,256]{1,0:T(8,128)} %get-tuple-element.21.shape_ref, f32[2,64,64]{2,1,0:T(8,128)} %t_ref.3, f32[63,32,128]{2,1,0:T(8,128)} %get-tuple-element.28.lev_ref, f32[32,24,128]{2,1,0:T(8,128)} %copy-done), custom_call_target="tpu_custom_call" | custom-call | tf_op jit(solution)/shard_map/tree_down/pallas_call | solution.py:884
  55.9 0.0 collective-permute-done.prev_any
  55.9 0.0 copy-start.1
  55.9 0.0 collective-permute-done.1.next_any
  55.9 0.0 copy-start.2
  55.9 0.8 copy-done.1
  56.7 0.2 copy-done.2
  57.0 25.4 %couple_finish.1 = f32[32,16384]{1,0:T(8,128)} custom-call(s32[16,128]{1,0:T(8,128)} %get-tuple-element.20.entries, f32[8,256]{1,0:T(8,128)} %get-tuple-element.21.shape_ref, f32[16,128]{1,0:T(8,128)} %get-tuple-element.22.counts, f32[3,16384]{1,0:T(4,128)} %p_ref.5, f32[32,16384]{1,0:T(8,128)} %near_field.1.near_any, bf16[128,64,128]{2,1,0:T(8,128)(2,1)} %b_any.3, ...), custom_call_target="tpu_custom_call" | custom-call | tf_op jit(solution)/shard_map/couple_finish/pallas_call | solution.py:901
Async XLA Ops:
  9.0 35.7 %all-to-all-start = ((f32[32,24,128]{2,1,0:T(8,128)}), f32[32,24,128]{2,1,0:T(8,128)S(1)}, u32[]{:S(2)}, u32[]{:S(2)}) async-start(f32[32,24,128]{2,1,0:T(8,128)} %get-tuple-element.24), calls=%async_computation | async-start | bytes 786432 | tf_op jit(solution)/shard_map/all_to_all | solution.py:854
  15.2 40.7 %collective-permute-start = (bf16[72,32,128]{2,1,0:T(8,128)(2,1)}, bf16[72,32,128]{2,1,0:T(8,128)(2,1)S(1)}, u32[]{:S(2)}, u32[]{:S(2)}) collective-permute-start(bf16[72,32,128]{2,1,0:T(8,128)(2,1)} %get-tuple-element.26), channel_id=1, source_target_pairs={{0,1},{1,2},{2,3},{3,4},{4,5},{5,6},{6,7},{7,8},{8,9},{9,10},{10,1... | collective-permute-start | bytes 1769480 | tf_op jit(solution)/shard_map/ppermute | solution.py:857
  18.6 37.3 %collective-permute-start.1 = (bf16[72,32,128]{2,1,0:T(8,128)(2,1)}, bf16[72,32,128]{2,1,0:T(8,128)(2,1)S(1)}, u32[]{:S(2)}, u32[]{:S(2)}) collective-permute-start(bf16[72,32,128]{2,1,0:T(8,128)(2,1)} %get-tuple-element.27), channel_id=1, source_target_pairs={{1,0},{2,1},{3,2},{4,3},{5,4},{6,5},{7,6},{8,7},{9,8},{10,9},{11,1... | collective-permute-start | bytes 1769480 | tf_op jit(solution)/shard_map/ppermute | solution.py:858
  44.8 0.8 copy-start
  55.9 0.8 %copy-start.1 = (bf16[72,32,128]{2,1,0:T(8,128)(2,1)}, bf16[72,32,128]{2,1,0:T(8,128)(2,1)S(1)}, u32[]{:S(2)}) copy-start(bf16[72,32,128]{2,1,0:T(8,128)(2,1)S(1)} %collective-permute-done.prev_any) | copy-start | bytes 1769476
  55.9 1.1 %copy-start.2 = (bf16[72,32,128]{2,1,0:T(8,128)(2,1)}, bf16[72,32,128]{2,1,0:T(8,128)(2,1)S(1)}, u32[]{:S(2)}) copy-start(bf16[72,32,128]{2,1,0:T(8,128)(2,1)S(1)} %collective-permute-done.1.next_any) | copy-start | bytes 1769476

commit v9 on v8

--- a/solution.py
+++ b/solution.py
@@ -29,6 +29,7 @@
 NT = (((1,), (1,)), ((), ()))
 TINY = 1e-30
 VMEM_LIMIT = 56 * 1024 * 1024
+SMALL_LIMIT = 40 * 1024 * 1024
 
 
 def lanes(shape):
@@ -78,13 +79,17 @@
 
 
 def decay(t):
-    t = jnp.maximum(t, TINY)
+    return decay_positive(jnp.maximum(t, TINY))
+
+
+def decay_positive(t):
     return jnp.exp2(-(t * lax.rsqrt(t)))
 
 
 def tile_from_axes(x_sq, y_sq, z_sq):
+    z_sq = z_sq + TINY
     yz = [y_sq[0] + z_sq, y_sq[1] + z_sq]
-    return decay(jnp.concatenate([x_sq[k // 2] + yz[k % 2] for k in range(8)], axis=0))
+    return decay_positive(jnp.concatenate([x_sq[k // 2] + yz[k % 2] for k in range(8)], axis=0))
 
 
 def doubled_transfer(t_ref):
@@ -110,19 +115,20 @@
     return jnp.where(lanes((1, R, 128)) < K, split[:, 0], split[:, 1])
 
 
-def push_down(value, t_high, t_low):
+def down_weights(doubled):
+    low = lanes(doubled.shape) < K
+    both = jnp.concatenate(
+        [jnp.where(low, doubled, 0.0), jnp.where(low, 0.0, doubled)], axis=0
+    )
+    return halves(both)
+
+
+def push_down(value, w_high, w_low):
     n = value.shape[0]
     high, low = halves(value.reshape(n * R, 128))
-    out = dot_nt(high, jnp.concatenate([t_high, t_low], axis=0))
-    out = out[:, 0:128] + out[:, 128:256] + dot_nt(low, t_high)
-    return out.reshape(n, R, 128)
-
-
-def children_of(pairs):
-    lane = lanes((1, R, 128))
-    left = jnp.where(lane < K, pairs, 0.0)
-    right = jnp.where(lane < K, 0.0, pairs)
-    return jnp.stack([left, right], axis=1).reshape(2 * pairs.shape[0], R, 128)
+    out = dot_nt(high, w_high) + dot_nt(high, w_low) + dot_nt(low, w_high)
+    out = out.reshape(n, R, 256)
+    return jnp.stack([out[:, :, 0:128], out[:, :, 128:256]], axis=1).reshape(2 * n, R, 128)
 
 
 def merge_shape_rows(left, right):
@@ -145,18 +151,16 @@
 
 
 def sibling_apply(tile, pair):
-    low = lanes((R, 128)) < K
-    swapped = pltpu.roll(pair, K, 1)
-    stacked = jnp.concatenate(
-        [jnp.where(low, swapped, 0.0), jnp.where(low, 0.0, swapped)], axis=0
-    )
-    high, low_part = halves(stacked)
-    t_high, t_low = halves(tile)
-    t_high = jnp.concatenate([t_high, t_high], axis=0)
-    t_low = jnp.concatenate([t_low, t_low], axis=0)
-    out = dot_nt(high, jnp.concatenate([t_high, t_low], axis=0))
-    out = out[:, 0:128] + out[:, 128:256] + dot_nt(low_part, t_high)
-    return jnp.where(low, out[:R], out[R:])
+    low = lanes((K, 128)) < K
+    zero = jnp.zeros((K, 128), BF16)
+    weights = []
+    for part in halves(tile):
+        weights.append(
+            jnp.concatenate([jnp.where(low, part, zero), jnp.where(low, zero, part)], axis=0)
+        )
+    high, low_part = halves(pltpu.roll(pair, K, 1))
+    out = dot_nt(high, jnp.concatenate(weights, axis=0))
+    return out[:, 0:128] + out[:, 128:256] + dot_nt(low_part, weights[0])
 
 
 LEVEL_OFFSETS = [0, 128, 192, 224, 240, 248, 252, 254]
@@ -416,9 +420,11 @@
 
 
 def near_kernel(
-    list_ref, x_ref, p_ref, out_ref,
-    p8, far_feat, own_feat, tile0, tile1,
+    list_ref, x_any, p_ref, out_ref,
+    x_ref, sems, p8, far_feat, own_feat, tile0, tile1,
 ):
+    copy = pltpu.make_async_copy(x_any, x_ref, sems.at[0])
+    copy.start()
     first_group = device_index() * GROUPS
     p8[...] = jnp.zeros(p8.shape, F32)
     eye = identity()
@@ -450,6 +456,7 @@
 
     lax.fori_loop(0, GROUPS // 4, features, 0)
 
+    copy.wait()
     out_ref[...] = x_ref[...].astype(F32)
     for ref in (tile0, tile1):
         ref[...] = jnp.zeros(ref.shape, ref.dtype)
@@ -526,7 +533,9 @@
 
     lax.fori_loop(0, 7, siblings, 0)
 
-    t_high, t_low = halves(doubled_transfer(t_ref))
+    doubled = doubled_transfer(t_ref)
+    t_high, t_low = halves(doubled)
+    w_high, w_low = down_weights(doubled)
     device = device_index()
     n = root_ref.shape[0]
     low = lanes((R, 128)) < K
@@ -569,17 +578,17 @@
     for level in reversed(range(len(levels))):
         value = couples[level]
         if incoming is not None:
-            value = value + push_down(incoming[None], t_high, t_low)[0]
+            pushed = push_down(incoming[None], w_high, w_low)
+            value = value + (pushed[0] + pushed[1])
         side = (device >> level) & 1
         keep_low = jnp.where(low, 1, 0) == (1 - side)
         incoming = jnp.where(keep_low, value, 0.0)
-    value = couple[pl.ds(PAIR_OFFSETS[6], 1)] + push_down(incoming[None], t_high, t_low)
+    pushed = push_down(incoming[None], w_high, w_low)
+    value = couple[pl.ds(PAIR_OFFSETS[6], 1)] + (pushed[0:1] + pushed[1:2])
     for level in range(5, 0, -1):
         n = PAIRS >> level
-        value = couple[pl.ds(PAIR_OFFSETS[level], n)] + push_down(
-            children_of(value), t_high, t_low
-        )
-    down_ref[...] = push_down(children_of(value), t_high, t_low)
+        value = couple[pl.ds(PAIR_OFFSETS[level], n)] + push_down(value, w_high, w_low)
+    down_ref[...] = push_down(value, w_high, w_low)
 
 
 UNIT = 4
@@ -731,7 +740,7 @@
 
     def edge(k, carry):
         loaded = [
-            (halo_ref[64 + k], coords[side, pl.ds(pl.multiple_of(8 * k, 8), 8), :], p8[side])
+            (halo_ref[64 + k], coords[side, 8 * k : 8 * k + 8, :], p8[side])
             for side, (halo_ref, _) in enumerate(sides)
         ]
         for side, (_, group) in enumerate(sides):
@@ -744,29 +753,37 @@
             products = dot(x_far, tiles)
             for i in range(4):
                 delta = (4 + i - k) if side == 0 else (4 + k - i)
-                weight = counts[8 * (1 - side) + jnp.clip(delta, 0, 7), 4 * group + i]
+                weight = counts[8 * (1 - side) + delta, 4 * group + i]
                 place = slice((4 * group + i) * P_SIZE, (4 * group + i + 1) * P_SIZE)
                 out_ref[:, place] += products[:, i * P_SIZE : (i + 1) * P_SIZE] * weight
         return carry
 
-    lax.fori_loop(0, 4, edge, 0)
+    for k in range(4):
+        edge(k, 0)
 
 
 def tree_kernel(
-    shape_ref, t_ref, lev_ref, root_any, down_ref, root_ref, couple, pairs_scr, shapes, sems
+    shape_ref, t_any, lev_any, root_any, down_ref,
+    t_ref, lev_ref, root_ref, couple, pairs_scr, shapes, sems,
 ):
-    copy = pltpu.make_async_copy(root_any, root_ref, sems.at[0])
-    copy.start()
-    copy.wait()
+    copies = [
+        pltpu.make_async_copy(lev_any, lev_ref, sems.at[0]),
+        pltpu.make_async_copy(root_any, root_ref, sems.at[1]),
+        pltpu.make_async_copy(t_any, t_ref, sems.at[2]),
+    ]
+    for copy in copies:
+        copy.start()
+    for copy in copies:
+        copy.wait()
     tree_down(shape_ref, lev_ref, t_ref, root_ref, down_ref, couple, pairs_scr, shapes)
 
 
 def final_kernel(
     entries, shape_ref, counts,
-    p_ref,
+    p_any,
     near_any, b_any, prev_any, next_any, high_any, low_any, down_any,
     out_ref,
-    b_ref, prev_ref, next_ref, down, leaf_couple,
+    p_ref, b_ref, prev_ref, next_ref, down, leaf_couple,
     shape_tab, high_tab, low_tab, halo_rows, halo_shape,
     tiles0, lhs0, tiles1, lhs1, p8, coords, sems, halo_sems,
 ):
@@ -778,6 +795,7 @@
         (b_any, b_ref),
         (near_any, out_ref),
         (down_any, down),
+        (p_any, p_ref),
     )
     copies = [pltpu.make_async_copy(a, b, sems.at[k]) for k, (a, b) in enumerate(moves)]
     for copy in copies:
@@ -812,7 +830,12 @@
     return pl.BlockSpec(memory_space=pl.ANY)
 
 
+def pinned():
+    return pl.BlockSpec(memory_space=pltpu.HBM)
+
+
 PARAMS = pltpu.CompilerParams(vmem_limit_bytes=VMEM_LIMIT)
+SMALL = pltpu.CompilerParams(vmem_limit_bytes=SMALL_LIMIT)
 
 
 def per_device(charges, points, basis, transfer, near_list, coupling_list):
@@ -834,8 +857,8 @@
             shaped(16, 128),
             shaped(16, 128, dtype=jnp.int32),
         ),
-        in_specs=[anywhere(), vmem(), anywhere(), vmem(), vmem(), vmem()],
-        out_specs=[vmem()] * 2 + [anywhere()] * 3 + [vmem()] * 5,
+        in_specs=[pinned(), vmem(), pinned(), vmem(), vmem(), vmem()],
+        out_specs=[vmem()] * 2 + [pinned()] * 3 + [vmem()] * 5,
         scratch_shapes=[
             pltpu.VMEM((R, LD * P_SIZE), BF16),
             pltpu.VMEM((LD, K, P_SIZE), BF16),
@@ -861,9 +884,11 @@
         near_kernel,
         name="near_field",
         out_shape=shaped(R, LD * P_SIZE),
-        in_specs=[smem(), vmem(), vmem()],
+        in_specs=[smem(), pinned(), vmem()],
         out_specs=vmem(),
         scratch_shapes=[
+            pltpu.VMEM((R, LD * P_SIZE), BF16),
+            pltpu.SemaphoreType.DMA((1,)),
             pltpu.VMEM((4, 8, 512), F32),
             pltpu.VMEM((PAIRS, P_SIZE, 2 * FEATS), BF16),
             pltpu.VMEM((2 * LD, FEATS, P_SIZE), BF16),
@@ -885,16 +910,18 @@
         tree_kernel,
         name="tree_down",
         out_shape=shaped(PAIRS, R, 128),
-        in_specs=[smem(), vmem(), vmem(), anywhere()],
+        in_specs=[smem(), pinned(), pinned(), anywhere()],
         out_specs=vmem(),
         scratch_shapes=[
+            pltpu.VMEM((2, K, K), F32),
+            pltpu.VMEM((PAIRS - 1, R, 128), F32),
             pltpu.VMEM((devices, R // 2 + 8, 128), F32),
             pltpu.VMEM((PAIRS - 1, R, 128), F32),
             pltpu.VMEM((devices, R, 128), F32),
             pltpu.VMEM((2 * devices, 128), F32),
-            pltpu.SemaphoreType.DMA((1,)),
+            pltpu.SemaphoreType.DMA((3,)),
         ],
-        compiler_params=PARAMS,
+        compiler_params=SMALL,
     )(shapes, transfer, lev, roots)
     from_prev, from_next, down = lax.optimization_barrier((from_prev, from_next, down))
 
@@ -902,9 +929,10 @@
         final_kernel,
         name="couple_finish",
         out_shape=shaped(R, LD * P_SIZE),
-        in_specs=[smem()] * 3 + [vmem()] + [anywhere()] * 7,
+        in_specs=[smem()] * 3 + [pinned()] * 3 + [anywhere()] * 2 + [pinned()] * 3,
         out_specs=vmem(),
         scratch_shapes=[
+            pltpu.VMEM((3, LD * P_SIZE), F32),
             pltpu.VMEM((LD, K, P_SIZE), BF16),
             pltpu.VMEM((SEND, R, 128), BF16),
             pltpu.VMEM((SEND, R, 128), BF16),
@@ -921,10 +949,10 @@
         + [
             pltpu.VMEM((2, 8, 512), F32),
             pltpu.VMEM((2, R, 128), F32),
-            pltpu.SemaphoreType.DMA((7,)),
+            pltpu.SemaphoreType.DMA((8,)),
             pltpu.SemaphoreType.DMA((2,)),
         ],
-        compiler_params=PARAMS,
+        compiler_params=SMALL,
     )(
         entries, shapes, counts, points,
         near, basis, from_prev, from_next, high, low, down,

time: 82.7 us -> 84 us (1.016)
  the two profiles are of different devices: /device:TPU:2 before, /device:TPU:31 now
where the time goes in v9:
time: 84 us; the launch traced here: 82.6 us
  Pallas kernels  65.2 us (78%)
  starting transfers between devices  12.3 us (15%)
  local copies, waits for them, and re-layouts  5.04 us (6%)
    pallas_call x1, Pallas kernels, per_device(): pl.pallas_call(final_kernel, name='couple_finish', out_shape=shaped(R, LD...  24.1 us
    pallas_call x1, Pallas kernels, per_device(): pl.pallas_call(near_kernel, name='near_field', out_shape=shaped(R, LD * P...  23.6 us
    pallas_call x1, Pallas kernels, per_device(): pl.pallas_call(leaf_kernel, name='leaf_up', out_shape=(shaped(SEND, R, 12...  9.05 us
    pallas_call x1, Pallas kernels, per_device(): pl.pallas_call(tree_kernel, name='tree_down', out_shape=shaped(PAIRS, R,...  8.47 us
    all_to_all x1, starting transfers between devices, per_device(): roots = lax.all_to_all(root, AXES, 0, 0, tiled=True)  6.15 us
    unnamed x20, local copies, waits for them, and re-layouts  5.04 us
    ppermute x1, starting transfers between devices, per_device(): from_next = lax.ppermute(send_prev, AXES, backward)  4.82 us
  transfers between devices with their start and end apart: 3, of which 0 were waited for; matrix products, arithmetic and copies ran while one was open for 0% of the time, Pallas kernels for 39%

profile of v9, /device:TPU:31, one launch (start us, length us, event | category | flops | bytes accessed | tf_op | source)
XLA Modules:
  0.0 82.6 jit_solution(13522617380408478391)
XLA Ops:
  0.0 9.0 %leaf_up.1 = (bf16[72,32,128]{2,1,0:T(8,128)(2,1)}, bf16[72,32,128]{2,1,0:T(8,128)(2,1)}, bf16[128,32,128]{2,1,0:T(8,128)(2,1)}, bf16[128,32,128]{2,1,0:T(8,128)...) custom-call(bf16[32,16384]{1,0:T(8,128)(2,1)} %x_any.3, ...), custom_call_target="tpu_custom_call" | custom-call | tf_op jit(solution)/shard_map/leaf_up/pallas_call | solution.py:845
  9.1 6.2 %all-to-all-start = ((f32[32,24,128]{2,1,0:T(8,128)}), f32[32,24,128]{2,1,0:T(8,128)S(1)}, u32[]{:S(2)}, u32[]{:S(2)}) async-start(f32[32,24,128]{2,1,0:T(8,128)} %get-tuple-element.24), calls=%async_computation | async-start | bytes 786432 | tf_op jit(solution)/shard_map/all_to_all | solution.py:877
  15.2 1.3 %collective-permute-start = (bf16[72,32,128]{2,1,0:T(8,128)(2,1)}, bf16[72,32,128]{2,1,0:T(8,128)(2,1)}, u32[]{:S(2)}, u32[]{:S(2)}) collective-permute-start(bf16[72,32,128]{2,1,0:T(8,128)(2,1)} %get-tuple-element.26), channel_id=1, source_target_pairs={{0,1},{1,2},{2,3},{3,4},{4,5},{5,6},{6,7},{7,8},{8,9},{9,10},{10,1... | collective-permute-start | bytes 1769480 | tf_op jit(solution)/shard_map/ppermute | solution.py:880
  16.5 4.8 %collective-permute-start.1 = (bf16[72,32,128]{2,1,0:T(8,128)(2,1)}, bf16[72,32,128]{2,1,0:T(8,128)(2,1)}, u32[]{:S(2)}, u32[]{:S(2)}) collective-permute-start(bf16[72,32,128]{2,1,0:T(8,128)(2,1)} %get-tuple-element.27), channel_id=1, source_target_pairs={{1,0},{2,1},{3,2},{4,3},{5,4},{6,5},{7,6},{8,7},{9,8},{10,9},{11,1... | collective-permute-start | bytes 1769480 | tf_op jit(solution)/shard_map/ppermute | solution.py:881
  21.3 23.6 %near_field.1.near_any = f32[32,16384]{1,0:T(8,128)} custom-call(s32[8,896]{1,0:T(8,128)} %get-tuple-element.23.list_ref, bf16[32,16384]{1,0:T(8,128)(2,1)} %x_any.3, f32[3,16384]{1,0:T(4,128)} %p_any.1), custom_call_target="tpu_custom_call" | custom-call | flops 1929379840 | bytes 4194304 | tf_op jit(solution)/shard_map/near_field/pallas_call | solution.py:883
  44.9 0.0 copy-start
  45.0 0.0 all-to-all-done.root_any
  45.0 0.0 copy-start.4
  45.0 0.0 copy-done.7
  45.0 0.0 copy-start.5
  45.0 1.4 %copy-done.5 = f32[63,32,128]{2,1,0:T(8,128)S(1)} copy-done((f32[63,32,128]{2,1,0:T(8,128)S(1)}, f32[63,32,128]{2,1,0:T(8,128)}, u32[]{:S(2)}) %copy-start.5) | copy-done | bytes 1032216
  46.4 0.8 %copy-done.6 = f32[2,64,64]{2,1,0:T(8,128)S(1)} copy-done((f32[2,64,64]{2,1,0:T(8,128)S(1)}, f32[2,64,64]{2,1,0:T(8,128)}, u32[]{:S(2)}) %copy-start.6) | copy-done | bytes 32792
  47.2 8.5 %tree_down.1.down_any = f32[64,32,128]{2,1,0:T(8,128)S(1)} custom-call(f32[8,256]{1,0:T(8,128)S(1)} %copy-done.7, f32[2,64,64]{2,1,0:T(8,128)S(1)} %copy-done.6, f32[63,32,128]{2,1,0:T(8,128)S(1)} %copy-done.5, f32[32,24,128]{2,1,0:T(8,128)S(1)} %all-to-all-done.root_any), custom_call_target="tpu_custom_call" | custom-call | tf_op jit(solution)/shard_map/tree_down/pallas_call | solution.py:909
  55.7 0.0 collective-permute-done.prev_any
  55.7 0.0 collective-permute-done.1.next_any
  55.7 0.0 copy-done.2
  55.7 0.0 copy-done.8
  55.7 0.0 copy-done
  55.7 0.0 copy-done.4
  55.7 0.0 copy-done.9
  55.7 0.0 copy-start.1
  55.8 1.6 %copy-done.1 = f32[32,16384]{1,0:T(8,128)S(1)} copy-done((f32[32,16384]{1,0:T(8,128)S(1)}, f32[32,16384]{1,0:T(8,128)}, u32[]{:S(2)}) %copy-start.1) | copy-done | bytes 2097176
  57.3 1.2 %copy-done.3 = bf16[128,32,128]{2,1,0:T(8,128)(2,1)S(1)} copy-done((bf16[128,32,128]{2,1,0:T(8,128)(2,1)S(1)}, bf16[128,32,128]{2,1,0:T(8,128)(2,1)}, u32[]{:S(2)}) %copy-start.3) | copy-done | bytes 1048600
  58.6 24.1 %couple_finish.1 = f32[32,16384]{1,0:T(8,128)} custom-call(s32[16,128]{1,0:T(8,128)S(1)} %copy-done.9, f32[8,256]{1,0:T(8,128)S(1)} %copy-done.7, f32[16,128]{1,0:T(8,128)S(1)} %copy-done.8, f32[3,16384]{1,0:T(4,128)S(1)} %copy-done.4, f32[32,16384]{1,0:T(8,128)S(1)} %copy-done.1, bf16[128,64,128]{2,1,0:T(8,128)(2,1)S(1)} %copy-done, ...), custom_call_target="tpu_custom_call" | custom-call | tf_op jit(solution)/shard_map/couple_finish/pallas_call | solution.py:928
  (6 shorter events, 0.0 us)
Async XLA Ops:
  9.1 35.9 %all-to-all-start = ((f32[32,24,128]{2,1,0:T(8,128)}), f32[32,24,128]{2,1,0:T(8,128)S(1)}, u32[]{:S(2)}, u32[]{:S(2)}) async-start(f32[32,24,128]{2,1,0:T(8,128)} %get-tuple-element.24), calls=%async_computation | async-start | bytes 786432 | tf_op jit(solution)/shard_map/all_to_all | solution.py:877
  15.2 40.5 %collective-permute-start = (bf16[72,32,128]{2,1,0:T(8,128)(2,1)}, bf16[72,32,128]{2,1,0:T(8,128)(2,1)}, u32[]{:S(2)}, u32[]{:S(2)}) collective-permute-start(bf16[72,32,128]{2,1,0:T(8,128)(2,1)} %get-tuple-element.26), channel_id=1, source_target_pairs={{0,1},{1,2},{2,3},{3,4},{4,5},{5,6},{6,7},{7,8},{8,9},{9,10},{10,1... | collective-permute-start | bytes 1769480 | tf_op jit(solution)/shard_map/ppermute | solution.py:880
  16.5 39.2 %collective-permute-start.1 = (bf16[72,32,128]{2,1,0:T(8,128)(2,1)}, bf16[72,32,128]{2,1,0:T(8,128)(2,1)}, u32[]{:S(2)}, u32[]{:S(2)}) collective-permute-start(bf16[72,32,128]{2,1,0:T(8,128)(2,1)} %get-tuple-element.27), channel_id=1, source_target_pairs={{1,0},{2,1},{3,2},{4,3},{5,4},{6,5},{7,6},{8,7},{9,8},{10,9},{11,1... | collective-permute-start | bytes 1769480 | tf_op jit(solution)/shard_map/ppermute | solution.py:881
  21.3 23.6 %copy-start.7 = (f32[8,256]{1,0:T(8,128)S(1)}, f32[8,256]{1,0:T(8,128)}, u32[]{:S(2)}) copy-start(f32[8,256]{1,0:T(8,128)} %get-tuple-element.21.shape_ref) | copy-start | bytes 24580
  21.3 34.4 %copy-start.2 = (bf16[128,32,128]{2,1,0:T(8,128)(2,1)S(1)}, bf16[128,32,128]{2,1,0:T(8,128)(2,1)}, u32[]{:S(2)}) copy-start(bf16[128,32,128]{2,1,0:T(8,128)(2,1)} %get-tuple-element.32.high_any) | copy-start | bytes 3145732
  21.3 34.4 %copy-start.8 = (f32[16,128]{1,0:T(8,128)S(1)}, f32[16,128]{1,0:T(8,128)}, u32[]{:S(2)}) copy-start(f32[16,128]{1,0:T(8,128)} %get-tuple-element.22.counts) | copy-start | bytes 24580
  44.9 10.8 %copy-start = (bf16[128,64,128]{2,1,0:T(8,128)(2,1)S(1)}, bf16[128,64,128]{2,1,0:T(8,128)(2,1)}, u32[]{:S(2)}) copy-start(bf16[128,64,128]{2,1,0:T(8,128)(2,1)} %b_any.3) | copy-start | bytes 6291460
  45.0 10.8 %copy-start.4 = (f32[3,16384]{1,0:T(4,128)S(1)}, f32[3,16384]{1,0:T(4,128)}, u32[]{:S(2)}) copy-start(f32[3,16384]{1,0:T(4,128)} %p_any.1) | copy-start | bytes 589828
  45.0 1.4 %copy-start.5 = (f32[63,32,128]{2,1,0:T(8,128)S(1)}, f32[63,32,128]{2,1,0:T(8,128)}, u32[]{:S(2)}) copy-start(f32[63,32,128]{2,1,0:T(8,128)} %get-tuple-element.28.lev_any) | copy-start | bytes 3096580
  46.4 0.8 %copy-start.6 = (f32[2,64,64]{2,1,0:T(8,128)S(1)}, f32[2,64,64]{2,1,0:T(8,128)}, u32[]{:S(2)}) copy-start(f32[2,64,64]{2,1,0:T(8,128)} %t_any.1) | copy-start | bytes 98308
  47.2 8.5 %copy-start.9 = (s32[16,128]{1,0:T(8,128)S(1)}, s32[16,128]{1,0:T(8,128)}, u32[]{:S(2)}) copy-start(s32[16,128]{1,0:T(8,128)} %get-tuple-element.20.entries) | copy-start | bytes 24580
  55.7 1.6 %copy-start.1 = (f32[32,16384]{1,0:T(8,128)S(1)}, f32[32,16384]{1,0:T(8,128)}, u32[]{:S(2)}) copy-start(f32[32,16384]{1,0:T(8,128)} %near_field.1.near_any) | copy-start | bytes 6291460
  57.3 1.2 %copy-start.3 = (bf16[128,32,128]{2,1,0:T(8,128)(2,1)S(1)}, bf16[128,32,128]{2,1,0:T(8,128)(2,1)}, u32[]{:S(2)}) copy-start(bf16[128,32,128]{2,1,0:T(8,128)(2,1)} %get-tuple-element.33.low_any) | copy-start | bytes 3145732

commit v10 on v9

--- a/solution.py
+++ b/solution.py
@@ -19,6 +19,7 @@
 NEAR_REACH = 8
 FEATS = 64
 BATCH = 16
+SIBLINGS = 4
 LIST = 896
 SEND = 72
 SCALE = 0.5 * math.log2(math.e)
@@ -28,8 +29,7 @@
 BF16 = jnp.bfloat16
 NT = (((1,), (1,)), ((), ()))
 TINY = 1e-30
-VMEM_LIMIT = 56 * 1024 * 1024
-SMALL_LIMIT = 40 * 1024 * 1024
+VMEM_LIMIT = 64 * 1024 * 1024
 
 
 def lanes(shape):
@@ -363,7 +363,7 @@
         ],
         axis=0,
     )
-    root_ref[...] = jnp.broadcast_to(block[None], root_ref.shape)
+    root_ref[...] = block
 
     p8[...] = jnp.zeros((8, 512), F32)
     for send, first_pair, group in ((send_next, PAIRS // 2, GROUPS - 1), (send_prev, 0, 0)):
@@ -420,11 +420,16 @@
 
 
 def near_kernel(
-    list_ref, x_any, p_ref, out_ref,
-    x_ref, sems, p8, far_feat, own_feat, tile0, tile1,
+    list_ref, shape_ref, x_any, p_ref, lev_any,
+    out_ref, couple_ref,
+    x_ref, lev_ref, sems, p8, far_feat, own_feat, tile0, tile1,
 ):
-    copy = pltpu.make_async_copy(x_any, x_ref, sems.at[0])
-    copy.start()
+    copies = [
+        pltpu.make_async_copy(x_any, x_ref, sems.at[0]),
+        pltpu.make_async_copy(lev_any, lev_ref, sems.at[1]),
+    ]
+    for copy in copies:
+        copy.start()
     first_group = device_index() * GROUPS
     p8[...] = jnp.zeros(p8.shape, F32)
     eye = identity()
@@ -456,7 +461,8 @@
 
     lax.fori_loop(0, GROUPS // 4, features, 0)
 
-    copy.wait()
+    for copy in copies:
+        copy.wait()
     out_ref[...] = x_ref[...].astype(F32)
     for ref in (tile0, tile1):
         ref[...] = jnp.zeros(ref.shape, ref.dtype)
@@ -468,8 +474,13 @@
     def leaf_slice(i):
         return pl.ds(pl.multiple_of(i * P_SIZE, P_SIZE), P_SIZE)
 
-    def phase(n, tile_new, tile_old):
+    lane_u = lane_nodes()
+    row_y, row_z = row_nodes()
+
+    def phase(n, tile_new, tile_old, pairs):
         far, own, sources, updates = [], [], [], []
+        siblings = [jnp.minimum(pairs * n + v, PAIRS - 2) for v in range(pairs)]
+        levels = [lev_ref[pair] for pair in siblings]
         for u in range(BATCH):
             k = (n + 1) * BATCH + u
             i, j = list_ref[0, k], list_ref[1, k]
@@ -497,6 +508,13 @@
                         to_j[:, span] * list_ref[3, k].astype(F32),
                     )
                 )
+        for pair, level in zip(siblings, levels):
+            cluster = LD + 2 * pair
+            left = [shape_ref[d, cluster] for d in range(4)]
+            right = [shape_ref[d, cluster + 1] for d in range(4)]
+            couple_ref[pair] = sibling_apply(
+                sibling_tile(left, right, lane_u, row_y, row_z), level
+            )
         for u in range(BATCH // 2):
             tile_new[u] = tiles[u]
         for u in range(BATCH):
@@ -506,32 +524,19 @@
             out_ref[:, to_i] += updates[u][0]
             out_ref[:, to_j] += updates[u][1]
 
-    def two_phases(m, carry):
-        phase(2 * m, tile0, tile1)
-        phase(2 * m + 1, tile1, tile0)
+    def two_phases(pairs, m, carry):
+        phase(2 * m, tile0, tile1, pairs)
+        phase(2 * m + 1, tile1, tile0, pairs)
         return carry
 
-    lax.fori_loop(0, (steps + 1) // 2, two_phases, 0)
-
-
-def tree_down(shape_ref, lev_ref, t_ref, root_ref, down_ref, couple, pairs_scr, shapes):
+    rides = PAIRS // (2 * SIBLINGS)
+    lax.fori_loop(0, rides, functools.partial(two_phases, SIBLINGS), 0)
+    lax.fori_loop(rides, (steps + 1) // 2, functools.partial(two_phases, 0), 0)
+
+
+def tree_down(t_ref, root_ref, down_ref, couple, pairs_scr, shapes):
     lane_u = lane_nodes()
     row_y, row_z = row_nodes()
-
-    def siblings(m, carry):
-        loaded = [lev_ref[9 * m + u] for u in range(9)]
-        values = []
-        for u in range(9):
-            cluster = LD + 2 * (9 * m + u)
-            left = [shape_ref[d, cluster] for d in range(4)]
-            right = [shape_ref[d, cluster + 1] for d in range(4)]
-            tile = sibling_tile(left, right, lane_u, row_y, row_z)
-            values.append(sibling_apply(tile, loaded[u]))
-        for u in range(9):
-            couple[9 * m + u] = values[u]
-        return carry
-
-    lax.fori_loop(0, 7, siblings, 0)
 
     doubled = doubled_transfer(t_ref)
     t_high, t_low = halves(doubled)
@@ -762,40 +767,19 @@
         edge(k, 0)
 
 
-def tree_kernel(
-    shape_ref, t_any, lev_any, root_any, down_ref,
-    t_ref, lev_ref, root_ref, couple, pairs_scr, shapes, sems,
-):
-    copies = [
-        pltpu.make_async_copy(lev_any, lev_ref, sems.at[0]),
-        pltpu.make_async_copy(root_any, root_ref, sems.at[1]),
-        pltpu.make_async_copy(t_any, t_ref, sems.at[2]),
-    ]
-    for copy in copies:
-        copy.start()
-    for copy in copies:
-        copy.wait()
-    tree_down(shape_ref, lev_ref, t_ref, root_ref, down_ref, couple, pairs_scr, shapes)
-
-
-def final_kernel(
-    entries, shape_ref, counts,
-    p_any,
-    near_any, b_any, prev_any, next_any, high_any, low_any, down_any,
-    out_ref,
-    p_ref, b_ref, prev_ref, next_ref, down, leaf_couple,
+def couple_kernel(
+    entries, shape_ref,
+    prev_any, next_any, high_any, low_any,
+    leaf_couple,
+    prev_ref, next_ref,
     shape_tab, high_tab, low_tab, halo_rows, halo_shape,
-    tiles0, lhs0, tiles1, lhs1, p8, coords, sems, halo_sems,
+    tiles0, lhs0, tiles1, lhs1, sems, halo_sems,
 ):
     moves = (
         (prev_any, prev_ref),
         (next_any, next_ref),
         (high_any, high_tab.at[0:LD]),
         (low_any, low_tab.at[0:LD]),
-        (b_any, b_ref),
-        (near_any, out_ref),
-        (down_any, down),
-        (p_any, p_ref),
     )
     copies = [pltpu.make_async_copy(a, b, sems.at[k]) for k, (a, b) in enumerate(moves)]
     for copy in copies:
@@ -807,7 +791,33 @@
         shape_tab, high_tab, low_tab, halo_rows, halo_shape, halo_sems,
         tiles0, lhs0, tiles1, lhs1,
     )
-    for copy in copies[4:]:
+
+
+def final_kernel(
+    counts,
+    t_any, root_any, couple_any, b_any, couple_leaf_any, near_any, prev_any, next_any, p_any,
+    out_ref,
+    t_ref, root_ref, couple, b_ref, leaf_couple, prev_ref, next_ref, p_ref,
+    down, pairs_scr, shapes, p8, coords, sems,
+):
+    moves = (
+        (t_any, t_ref),
+        (root_any, root_ref),
+        (couple_any, couple),
+        (b_any, b_ref),
+        (couple_leaf_any, leaf_couple),
+        (near_any, out_ref),
+        (prev_any, prev_ref),
+        (next_any, next_ref),
+        (p_any, p_ref),
+    )
+    copies = [pltpu.make_async_copy(a, b, sems.at[k]) for k, (a, b) in enumerate(moves)]
+    for copy in copies:
+        copy.start()
+    for copy in copies[0:3]:
+        copy.wait()
+    tree_down(t_ref, root_ref, down, couple, pairs_scr, shapes)
+    for copy in copies[3:]:
         copy.wait()
     finish_leaves(
         counts, p_ref, b_ref, prev_ref, next_ref, down, leaf_couple, out_ref, p8, coords
@@ -830,12 +840,7 @@
     return pl.BlockSpec(memory_space=pl.ANY)
 
 
-def pinned():
-    return pl.BlockSpec(memory_space=pltpu.HBM)
-
-
 PARAMS = pltpu.CompilerParams(vmem_limit_bytes=VMEM_LIMIT)
-SMALL = pltpu.CompilerParams(vmem_limit_bytes=SMALL_LIMIT)
 
 
 def per_device(charges, points, basis, transfer, near_list, coupling_list):
@@ -851,14 +856,14 @@
             shaped(LD, R, 128, dtype=BF16),
             shaped(LD, R, 128, dtype=BF16),
             shaped(PAIRS - 1, R, 128),
-            shaped(devices, R // 2 + 8, 128),
+            shaped(R // 2 + 8, 128),
             shaped(8, 256),
             shaped(8, LIST, dtype=jnp.int32),
             shaped(16, 128),
             shaped(16, 128, dtype=jnp.int32),
         ),
-        in_specs=[pinned(), vmem(), pinned(), vmem(), vmem(), vmem()],
-        out_specs=[vmem()] * 2 + [pinned()] * 3 + [vmem()] * 5,
+        in_specs=[anywhere(), vmem(), anywhere(), vmem(), vmem(), vmem()],
+        out_specs=[vmem()] * 2 + [anywhere()] * 3 + [vmem()] * 5,
         scratch_shapes=[
             pltpu.VMEM((R, LD * P_SIZE), BF16),
             pltpu.VMEM((LD, K, P_SIZE), BF16),
@@ -874,21 +879,22 @@
         compiler_params=PARAMS,
     )(charges, points, basis, transfer, near_rows, coupling_rows)
 
-    roots = lax.all_to_all(root, AXES, 0, 0, tiled=True)
+    roots = lax.all_gather(root, AXES, axis=0)
     forward = [(i, i + 1) for i in range(devices - 1)]
     backward = [(i + 1, i) for i in range(devices - 1)]
     from_prev = lax.ppermute(send_next, AXES, forward)
     from_next = lax.ppermute(send_prev, AXES, backward)
 
-    near = pl.pallas_call(
+    near, couple = pl.pallas_call(
         near_kernel,
         name="near_field",
-        out_shape=shaped(R, LD * P_SIZE),
-        in_specs=[smem(), pinned(), vmem()],
-        out_specs=vmem(),
+        out_shape=(shaped(R, LD * P_SIZE), shaped(PAIRS - 1, R, 128)),
+        in_specs=[smem(), smem(), anywhere(), vmem(), anywhere()],
+        out_specs=[vmem()] * 2,
         scratch_shapes=[
             pltpu.VMEM((R, LD * P_SIZE), BF16),
-            pltpu.SemaphoreType.DMA((1,)),
+            pltpu.VMEM((PAIRS - 1, R, 128), F32),
+            pltpu.SemaphoreType.DMA((2,)),
             pltpu.VMEM((4, 8, 512), F32),
             pltpu.VMEM((PAIRS, P_SIZE, 2 * FEATS), BF16),
             pltpu.VMEM((2 * LD, FEATS, P_SIZE), BF16),
@@ -899,45 +905,22 @@
         cost_estimate=pl.CostEstimate(
             flops=2 * 460 * 128 * 128 * 128, bytes_accessed=4 << 20, transcendentals=460 * 32768
         ),
-    )(tasks, charges, points)
-
-    near, roots = lax.optimization_barrier((near, roots))
+    )(tasks, shapes, charges, points, lev)
+
+    near, from_prev, from_next = lax.optimization_barrier((near, from_prev, from_next))
     stages = [
         pltpu.VMEM((UNIT, 512, 256), BF16),
         pltpu.VMEM((UNIT, 4 * R, 512), BF16),
     ]
-    down = pl.pallas_call(
-        tree_kernel,
-        name="tree_down",
-        out_shape=shaped(PAIRS, R, 128),
-        in_specs=[smem(), pinned(), pinned(), anywhere()],
+    leaf_couple = pl.pallas_call(
+        couple_kernel,
+        name="leaf_couple",
+        out_shape=shaped(PAIRS + 2 * UNIT, R, 128),
+        in_specs=[smem()] * 2 + [anywhere()] * 4,
         out_specs=vmem(),
         scratch_shapes=[
-            pltpu.VMEM((2, K, K), F32),
-            pltpu.VMEM((PAIRS - 1, R, 128), F32),
-            pltpu.VMEM((devices, R // 2 + 8, 128), F32),
-            pltpu.VMEM((PAIRS - 1, R, 128), F32),
-            pltpu.VMEM((devices, R, 128), F32),
-            pltpu.VMEM((2 * devices, 128), F32),
-            pltpu.SemaphoreType.DMA((3,)),
-        ],
-        compiler_params=SMALL,
-    )(shapes, transfer, lev, roots)
-    from_prev, from_next, down = lax.optimization_barrier((from_prev, from_next, down))
-
-    return pl.pallas_call(
-        final_kernel,
-        name="couple_finish",
-        out_shape=shaped(R, LD * P_SIZE),
-        in_specs=[smem()] * 3 + [pinned()] * 3 + [anywhere()] * 2 + [pinned()] * 3,
-        out_specs=vmem(),
-        scratch_shapes=[
-            pltpu.VMEM((3, LD * P_SIZE), F32),
-            pltpu.VMEM((LD, K, P_SIZE), BF16),
             pltpu.VMEM((SEND, R, 128), BF16),
             pltpu.VMEM((SEND, R, 128), BF16),
-            pltpu.VMEM((PAIRS, R, 128), F32),
-            pltpu.VMEM((PAIRS + 2 * UNIT, R, 128), F32),
             pltpu.VMEM((2 * LD, 8, 128), F32),
             pltpu.VMEM((TABLE, R, 128), BF16),
             pltpu.VMEM((TABLE, R, 128), BF16),
@@ -946,17 +929,38 @@
         ]
         + stages
         + stages
-        + [
+        + [pltpu.SemaphoreType.DMA((4,)), pltpu.SemaphoreType.DMA((2,))],
+        compiler_params=PARAMS,
+        cost_estimate=pl.CostEstimate(
+            flops=2 * 1024 * 64 * 64 * 32 * 3, bytes_accessed=6 << 20, transcendentals=1024 * 8192
+        ),
+    )(entries, shapes, from_prev, from_next, high, low)
+
+    leaf_couple, roots = lax.optimization_barrier((leaf_couple, roots))
+    return pl.pallas_call(
+        final_kernel,
+        name="tree_finish",
+        out_shape=shaped(R, LD * P_SIZE),
+        in_specs=[smem()] + [anywhere()] * 9,
+        out_specs=vmem(),
+        scratch_shapes=[
+            pltpu.VMEM((2, K, K), F32),
+            pltpu.VMEM((devices, R // 2 + 8, 128), F32),
+            pltpu.VMEM((PAIRS - 1, R, 128), F32),
+            pltpu.VMEM((LD, K, P_SIZE), BF16),
+            pltpu.VMEM((PAIRS + 2 * UNIT, R, 128), F32),
+            pltpu.VMEM((SEND, R, 128), BF16),
+            pltpu.VMEM((SEND, R, 128), BF16),
+            pltpu.VMEM((3, LD * P_SIZE), F32),
+            pltpu.VMEM((PAIRS, R, 128), F32),
+            pltpu.VMEM((devices, R, 128), F32),
+            pltpu.VMEM((2 * devices, 128), F32),
             pltpu.VMEM((2, 8, 512), F32),
             pltpu.VMEM((2, R, 128), F32),
-            pltpu.SemaphoreType.DMA((8,)),
-            pltpu.SemaphoreType.DMA((2,)),
+            pltpu.SemaphoreType.DMA((9,)),
         ],
-        compiler_params=SMALL,
-    )(
-        entries, shapes, counts, points,
-        near, basis, from_prev, from_next, high, low, down,
-    )
+        compiler_params=PARAMS,
+    )(counts, transfer, roots, couple, basis, leaf_couple, near, from_prev, from_next, points)
 
 
 def solution(mesh):

time: 84 us -> 150 us (1.79)
  the two profiles are of different devices: /device:TPU:31 before, /device:TPU:0 now
where the time goes in v10:
time: 150 us
  blocking collectives  81.9 us (55%)
  Pallas kernels  61.2 us (41%)
  starting transfers between devices  7.04 us (5%)
    all_gather x1, blocking collectives, per_device(): roots = lax.all_gather(root, AXES, axis=0)  81.9 us
    pallas_call x1, Pallas kernels, per_device(): pl.pallas_call(near_kernel, name='near_field', out_shape=(shaped(R, LD *...  21 us
    pallas_call x1, Pallas kernels, per_device(): pl.pallas_call(couple_kernel, name='leaf_couple', out_shape=shaped(PAIRS...  19.4 us
    pallas_call x1, Pallas kernels, per_device(): pl.pallas_call(final_kernel, name='tree_finish', out_shape=shaped(R, LD *...  11.8 us
    pallas_call x1, Pallas kernels, per_device(): pl.pallas_call(leaf_kernel, name='leaf_up', out_shape=(shaped(SEND, R, 12...  8.98 us
    ppermute x1, starting transfers between devices, per_device(): from_prev = lax.ppermute(send_next, AXES, forward)  5.76 us
  transfers between devices with their start and end apart: 2, of which 0 were waited for; matrix products, arithmetic and copies ran while one was open for 0% of the time, Pallas kernels for 14%

profile of v10, /device:TPU:0, one launch (start us, length us, event | category | flops | bytes accessed | tf_op | source)
XLA Modules:
  0.0 150.2 jit_solution(14508830544785698954)
XLA Ops:
  0.0 9.0 %leaf_up.1 = (bf16[72,32,128]{2,1,0:T(8,128)(2,1)}, bf16[72,32,128]{2,1,0:T(8,128)(2,1)}, bf16[128,32,128]{2,1,0:T(8,128)(2,1)}, bf16[128,32,128]{2,1,0:T(8,128)...) custom-call(bf16[32,16384]{1,0:T(8,128)(2,1)} %x_any.3, ...), custom_call_target="tpu_custom_call" | custom-call | tf_op jit(solution)/shard_map/leaf_up/pallas_call | solution.py:850
  9.0 5.8 %collective-permute-start = (bf16[72,32,128]{2,1,0:T(8,128)(2,1)}, bf16[72,32,128]{2,1,0:T(8,128)(2,1)}, u32[]{:S(2)}, u32[]{:S(2)}) collective-permute-start(bf16[72,32,128]{2,1,0:T(8,128)(2,1)} %get-tuple-element.28), channel_id=1, source_target_pairs={{0,1},{1,2},{2,3},{3,4},{4,5},{5,6},{6,7},{7,8},{8,9},{9,10},{10,1... | collective-permute-start | bytes 1769480 | tf_op jit(solution)/shard_map/ppermute | solution.py:885
  14.8 1.3 collective-permute-start.1
  16.0 21.0 %near_field.1 = (f32[32,16384]{1,0:T(8,128)}, f32[63,32,128]{2,1,0:T(8,128)}) custom-call(s32[8,896]{1,0:T(8,128)} %get-tuple-element.25.list_ref, f32[8,256]{1,0:T(8,128)} %get-tuple-element.24.shape_ref, bf16[32,16384]{1,0:T(8,128)(2,1)} %x_any.3, f32[3,16384]{1,0:T(4,128)} %p_any.1, f32[63,32,128]{2,1,0:T(8,128)} %get-tuple-element.26.lev_any), custom_call_target="tpu_custom_call" | custom-call | flops 1929379840 | bytes 4194304 | tf_op jit(solution)/shard_map/near_field/pallas_call | solution.py:888
  37.1 81.9 %all-gather = f32[768,128]{1,0:T(8,128)} all-gather(f32[24,128]{1,0:T(8,128)} %get-tuple-element.34), channel_id=2, replica_groups=mesh['leaf'=8,'sub'=4] {'leaf','sub'}, dimensions={0}, use_global_device_ids=true | all-gather | bytes 405504 | tf_op jit(solution)/shard_map/all_gather | solution.py:882
  118.9 0.0 collective-permute-done.prev_any
  118.9 0.0 collective-permute-done.1.next_any
  118.9 19.4 %leaf_couple.1.couple_leaf_any = f32[72,32,128]{2,1,0:T(8,128)} custom-call(s32[16,128]{1,0:T(8,128)} %get-tuple-element.23.entries, f32[8,256]{1,0:T(8,128)} %get-tuple-element.24.shape_ref, bf16[72,32,128]{2,1,0:T(8,128)(2,1)} %collective-permute-done.prev_any, bf16[72,32,128]{2,1,0:T(8,128)(2,1)} %collective-permute-done.1.next_any, ...), custom_call_target="tpu_custom_call" | custom-call | flops 805306368 | bytes 6291456 | tf_op jit(solution)/shard_map/leaf_couple/pallas_call | solution.py:915
  138.3 11.8 %tree_finish.1 = f32[32,16384]{1,0:T(8,128)} custom-call(f32[16,128]{1,0:T(8,128)} %get-tuple-element.22.counts, f32[2,64,64]{2,1,0:T(8,128)} %t_any.1, f32[32,24,128]{2,1,0:T(8,128)} %bitcast.3, f32[63,32,128]{2,1,0:T(8,128)} %get-tuple-element.36.couple_any, bf16[128,64,128]{2,1,0:T(8,128)(2,1)} %b_any.3, f32[72,32,128]{2,1,0:T(8,128)} %leaf_couple.1.couple_leaf_any, ...), custom_call_target="tpu_custom_call" | custom-call | tf_op jit(solution)/shard_map/tree_finish/pallas_call | solution.py:940
Async XLA Ops:
  9.0 109.9 %collective-permute-start = (bf16[72,32,128]{2,1,0:T(8,128)(2,1)}, bf16[72,32,128]{2,1,0:T(8,128)(2,1)}, u32[]{:S(2)}, u32[]{:S(2)}) collective-permute-start(bf16[72,32,128]{2,1,0:T(8,128)(2,1)} %get-tuple-element.28), channel_id=1, source_target_pairs={{0,1},{1,2},{2,3},{3,4},{4,5},{5,6},{6,7},{7,8},{8,9},{9,10},{10,1... | collective-permute-start | bytes 1769480 | tf_op jit(solution)/shard_map/ppermute | solution.py:885
  14.8 104.2 %collective-permute-start.1 = (bf16[72,32,128]{2,1,0:T(8,128)(2,1)}, bf16[72,32,128]{2,1,0:T(8,128)(2,1)}, u32[]{:S(2)}, u32[]{:S(2)}) collective-permute-start(bf16[72,32,128]{2,1,0:T(8,128)(2,1)} %get-tuple-element.29), channel_id=1, source_target_pairs={{1,0},{2,1},{3,2},{4,3},{5,4},{6,5},{7,6},{8,7},{9,8},{10,9},{11,1... | collective-permute-start | bytes 1769480 | tf_op jit(solution)/shard_map/ppermute | solution.py:886

commit v11 on v10

--- a/solution.py
+++ b/solution.py
@@ -287,6 +287,31 @@
     low32 = lanes((R, 128)) < K
 
     make_lists(near_ref, coupling_ref, list_ref, count_ref, index_ref)
+    def leaf_pairs(m, carry):
+        values = []
+        for v in range(16):
+            leaf = 16 * m + v
+            x = x_ref[:, pl.ds(pl.multiple_of(leaf * P_SIZE, P_SIZE), P_SIZE)]
+            weights = b_ref[leaf]
+            values.append(dot_nt(x, jnp.concatenate([weights, weights], axis=0)))
+        for v in range(16):
+            high_ref[16 * m + v], low_ref[16 * m + v] = halves(values[v])
+        for v in range(8):
+            coef[8 * m + v] = jnp.where(low32, values[2 * v], values[2 * v + 1])
+        return carry
+
+    for c in range(CHUNKS):
+        for copy in copies[c]:
+            copy.wait()
+        steps = leaves // 16
+        lax.fori_loop(c * steps, (c + 1) * steps, leaf_pairs, 0)
+    leaving = [
+        pltpu.make_async_copy(high_ref, high_any, sems.at[2 * CHUNKS]),
+        pltpu.make_async_copy(low_ref, low_any, sems.at[2 * CHUNKS + 1]),
+    ]
+    for copy in leaving:
+        copy.start()
+
     for i in range(LD):
         for d in range(3):
             pts[d, i : i + 1, :] = p_ref[d : d + 1, i * P_SIZE : (i + 1) * P_SIZE]
@@ -320,32 +345,6 @@
         [jnp.transpose(shapes[0:128, :])[0:8], jnp.transpose(shapes[128:256, :])[0:8]], axis=1
     )
     shape_ref[...] = shape_rows
-
-    def leaf_pairs(m, carry):
-        values = []
-        for v in range(16):
-            leaf = 16 * m + v
-            x = x_ref[:, pl.ds(pl.multiple_of(leaf * P_SIZE, P_SIZE), P_SIZE)]
-            weights = b_ref[leaf]
-            values.append(dot_nt(x, jnp.concatenate([weights, weights], axis=0)))
-        for v in range(16):
-            high_ref[16 * m + v], low_ref[16 * m + v] = halves(values[v])
-        for v in range(8):
-            coef[8 * m + v] = jnp.where(low32, values[2 * v], values[2 * v + 1])
-        return carry
-
-    for c in range(CHUNKS):
-        for copy in copies[c]:
-            copy.wait()
-        steps = leaves // 16
-        lax.fori_loop(c * steps, (c + 1) * steps, leaf_pairs, 0)
-    leaving = [
-        pltpu.make_async_copy(high_ref, high_any, sems.at[2 * CHUNKS]),
-        pltpu.make_async_copy(low_ref, low_any, sems.at[2 * CHUNKS + 1]),
-    ]
-    for copy in leaving:
-        copy.start()
-
     t_high, t_low = halves(doubled_transfer(t_ref))
     pairs = coef[...]
     for level in range(1, 7):
@@ -363,7 +362,7 @@
         ],
         axis=0,
     )
-    root_ref[...] = block
+    root_ref[...] = jnp.broadcast_to(block[None], root_ref.shape)
 
     p8[...] = jnp.zeros((8, 512), F32)
     for send, first_pair, group in ((send_next, PAIRS // 2, GROUPS - 1), (send_prev, 0, 0)):
@@ -435,21 +434,21 @@
     eye = identity()
 
     def features(m, carry):
-        loaded = [p_ref[:, pl.ds(pl.multiple_of((4 * m + v) * 512, 512), 512)] for v in range(4)]
-        for v in range(4):
+        loaded = [p_ref[:, pl.ds(pl.multiple_of((8 * m + v) * 512, 512), 512)] for v in range(8)]
+        for v in range(8):
             p8[v, 0:3, :] = loaded[v]
         made = []
-        for v in range(4):
+        for v in range(8):
             coords = p8[v]
-            origin_z = (first_group + 4 * m + v).astype(F32)
+            origin_z = (first_group + 8 * m + v).astype(F32)
             far, own = point_features(coords, origin_z)
             _, own_up = point_features(coords, origin_z + 1.0)
             far = far_stack(far)
             parts = [far[:, k * P_SIZE : (k + 1) * P_SIZE] for k in range(4)]
             turned = dot_nt(eye, jnp.concatenate(parts, axis=0)).astype(BF16)
             made.append((turned, own_stack(own), own_stack(own_up)))
-        for v in range(4):
-            g = 4 * m + v
+        for v in range(8):
+            g = 8 * m + v
             turned, own, own_up = made[v]
             far_feat[2 * g] = turned[:, 0:128]
             far_feat[2 * g + 1] = turned[:, 128:256]
@@ -459,7 +458,7 @@
                 own_feat[LD + 4 * g + k] = own_up[:, part]
         return carry
 
-    lax.fori_loop(0, GROUPS // 4, features, 0)
+    lax.fori_loop(0, GROUPS // 8, features, 0)
 
     for copy in copies:
         copy.wait()
@@ -712,11 +711,7 @@
     lax.fori_loop(0, PAIRS // UNIT // 2 + 1, couple_two, 0)
 
 
-def finish_leaves(
-    counts, p_ref, b_ref, prev_ref, next_ref, down_ref, leaf_couple, out_ref, p8, coords
-):
-    device = device_index()
-
+def finish_leaves(b_ref, down_ref, leaf_couple, out_ref, border):
     def finish(m, carry):
         values = []
         for v in range(8):
@@ -735,6 +730,14 @@
         return carry
 
     lax.fori_loop(0, PAIRS // 8, finish, 0)
+    for side, group in enumerate((0, GROUPS - 1)):
+        for i in range(4):
+            leaf = 4 * group + i
+            out_ref[:, leaf * P_SIZE : (leaf + 1) * P_SIZE] += border[4 * side + i]
+
+
+def border_blocks(counts, p_ref, prev_ref, next_ref, border, p8, coords):
+    device = device_index()
 
     p8[...] = jnp.zeros(p8.shape, F32)
     eye = identity()
@@ -743,7 +746,8 @@
         p8[side, 0:3, :] = p_ref[:, group * 512 : group * 512 + 512]
         coords[side] = halo_ref[69].astype(F32) + halo_ref[70].astype(F32) + halo_ref[71].astype(F32)
 
-    def edge(k, carry):
+    sums = [[0.0] * 4, [0.0] * 4]
+    for k in range(4):
         loaded = [
             (halo_ref[64 + k], coords[side, 8 * k : 8 * k + 8, :], p8[side])
             for side, (halo_ref, _) in enumerate(sides)
@@ -759,12 +763,10 @@
             for i in range(4):
                 delta = (4 + i - k) if side == 0 else (4 + k - i)
                 weight = counts[8 * (1 - side) + delta, 4 * group + i]
-                place = slice((4 * group + i) * P_SIZE, (4 * group + i + 1) * P_SIZE)
-                out_ref[:, place] += products[:, i * P_SIZE : (i + 1) * P_SIZE] * weight
-        return carry
-
-    for k in range(4):
-        edge(k, 0)
+                sums[side][i] = sums[side][i] + products[:, i * P_SIZE : (i + 1) * P_SIZE] * weight
+    for side in range(2):
+        for i in range(4):
+            border[4 * side + i] = sums[side][i]
 
 
 def couple_kernel(
@@ -798,30 +800,29 @@
     t_any, root_any, couple_any, b_any, couple_leaf_any, near_any, prev_any, next_any, p_any,
     out_ref,
     t_ref, root_ref, couple, b_ref, leaf_couple, prev_ref, next_ref, p_ref,
-    down, pairs_scr, shapes, p8, coords, sems,
+    down, pairs_scr, shapes, p8, coords, border, sems,
 ):
     moves = (
         (t_any, t_ref),
         (root_any, root_ref),
         (couple_any, couple),
+        (prev_any.at[64:SEND], prev_ref.at[64:SEND]),
+        (next_any.at[64:SEND], next_ref.at[64:SEND]),
+        (p_any, p_ref),
         (b_any, b_ref),
         (couple_leaf_any, leaf_couple),
         (near_any, out_ref),
-        (prev_any, prev_ref),
-        (next_any, next_ref),
-        (p_any, p_ref),
     )
     copies = [pltpu.make_async_copy(a, b, sems.at[k]) for k, (a, b) in enumerate(moves)]
     for copy in copies:
         copy.start()
-    for copy in copies[0:3]:
+    for copy in copies[0:6]:
         copy.wait()
+    border_blocks(counts, p_ref, prev_ref, next_ref, border, p8, coords)
     tree_down(t_ref, root_ref, down, couple, pairs_scr, shapes)
-    for copy in copies[3:]:
+    for copy in copies[6:]:
         copy.wait()
-    finish_leaves(
-        counts, p_ref, b_ref, prev_ref, next_ref, down, leaf_couple, out_ref, p8, coords
-    )
+    finish_leaves(b_ref, down, leaf_couple, out_ref, border)
 
 
 def shaped(*shape, dtype=F32):
@@ -856,7 +857,7 @@
             shaped(LD, R, 128, dtype=BF16),
             shaped(LD, R, 128, dtype=BF16),
             shaped(PAIRS - 1, R, 128),
-            shaped(R // 2 + 8, 128),
+            shaped(devices, R // 2 + 8, 128),
             shaped(8, 256),
             shaped(8, LIST, dtype=jnp.int32),
             shaped(16, 128),
@@ -879,7 +880,7 @@
         compiler_params=PARAMS,
     )(charges, points, basis, transfer, near_rows, coupling_rows)
 
-    roots = lax.all_gather(root, AXES, axis=0)
+    roots = lax.all_to_all(root, AXES, 0, 0, tiled=True)
     forward = [(i, i + 1) for i in range(devices - 1)]
     backward = [(i + 1, i) for i in range(devices - 1)]
     from_prev = lax.ppermute(send_next, AXES, forward)
@@ -895,7 +896,7 @@
             pltpu.VMEM((R, LD * P_SIZE), BF16),
             pltpu.VMEM((PAIRS - 1, R, 128), F32),
             pltpu.SemaphoreType.DMA((2,)),
-            pltpu.VMEM((4, 8, 512), F32),
+            pltpu.VMEM((8, 8, 512), F32),
             pltpu.VMEM((PAIRS, P_SIZE, 2 * FEATS), BF16),
             pltpu.VMEM((2 * LD, FEATS, P_SIZE), BF16),
             pltpu.VMEM((BATCH // 2, 128, 256), BF16),
@@ -957,6 +958,7 @@
             pltpu.VMEM((2 * devices, 128), F32),
             pltpu.VMEM((2, 8, 512), F32),
             pltpu.VMEM((2, R, 128), F32),
+            pltpu.VMEM((8, R, 128), F32),
             pltpu.SemaphoreType.DMA((9,)),
         ],
         compiler_params=PARAMS,

time: 150 us -> 83.6 us (0.56)
  blocking collectives: 81.9 us -> 0 us
  waiting for transfers between devices: 0.01 us -> 9.24 us
  starting transfers between devices: 7.04 us -> 13.1 us
    all_gather x1 -> x0, blocking collectives: 81.9 us -> none  [per_device(): roots = lax.all_gather(root, AXES, axis=0)]
    ppermute x1, waiting for transfers between devices: 0.01 us -> 9.24 us  [per_device(): from_next = lax.ppermute(send_prev, AXES, backward)]
    all_to_all x0 -> x1, starting transfers between devices: none -> 7.42 us  [per_device(): roots = lax.all_to_all(root, AXES, 0, 0, tiled=True)]
  transfers between devices with their start and end apart: 2 -> 3, of which waited for: 0 -> 1; matrix products, arithmetic and copies ran while one was open for 0% -> 0% of each run, Pallas kernels for 14% -> 48%
where the time goes in v11:
time: 83.6 us; the launch traced here: 83.1 us
  Pallas kernels  60.7 us (73%)
  starting transfers between devices  13.1 us (16%)
  waiting for transfers between devices  9.24 us (11%)
    pallas_call x1, Pallas kernels, per_device(): pl.pallas_call(near_kernel, name='near_field', out_shape=(shaped(R, LD *...  20.5 us
    pallas_call x1, Pallas kernels, per_device(): pl.pallas_call(couple_kernel, name='leaf_couple', out_shape=shaped(PAIRS...  19.4 us
    pallas_call x1, Pallas kernels, per_device(): pl.pallas_call(final_kernel, name='tree_finish', out_shape=shaped(R, LD *...  11.7 us
    ppermute x1, waiting for transfers between devices, per_device(): from_next = lax.ppermute(send_prev, AXES, backward)  9.24 us
    pallas_call x1, Pallas kernels, per_device(): pl.pallas_call(leaf_kernel, name='leaf_up', out_shape=(shaped(SEND, R, 12...  9.06 us
    all_to_all x1, starting transfers between devices, per_device(): roots = lax.all_to_all(root, AXES, 0, 0, tiled=True)  7.42 us
    ppermute x1, starting transfers between devices, per_device(): from_prev = lax.ppermute(send_next, AXES, forward)  4.45 us
  transfers between devices with their start and end apart: 3, of which 1 were waited for; matrix products, arithmetic and copies ran while one was open for 0% of the time, Pallas kernels for 48%

profile of v11, /device:TPU:0, one launch (start us, length us, event | category | flops | bytes accessed | tf_op | source)
XLA Modules:
  0.0 83.1 jit_solution(12020637601846651357)
XLA Ops:
  0.0 9.1 %leaf_up.1 = (bf16[72,32,128]{2,1,0:T(8,128)(2,1)}, bf16[72,32,128]{2,1,0:T(8,128)(2,1)}, bf16[128,32,128]{2,1,0:T(8,128)(2,1)}, bf16[128,32,128]{2,1,0:T(8,128)...) custom-call(bf16[32,16384]{1,0:T(8,128)(2,1)} %x_any.3, ...), custom_call_target="tpu_custom_call" | custom-call | tf_op jit(solution)/shard_map/leaf_up/pallas_call | solution.py:851
  9.1 7.4 %all-to-all-start = ((f32[32,24,128]{2,1,0:T(8,128)}), f32[32,24,128]{2,1,0:T(8,128)}, u32[]{:S(2)}, u32[]{:S(2)}) async-start(f32[32,24,128]{2,1,0:T(8,128)} %get-tuple-element.34), calls=%async_computation | async-start | bytes 786432 | tf_op jit(solution)/shard_map/all_to_all | solution.py:883
  16.5 4.5 %collective-permute-start = (bf16[72,32,128]{2,1,0:T(8,128)(2,1)}, bf16[72,32,128]{2,1,0:T(8,128)(2,1)}, u32[]{:S(2)}, u32[]{:S(2)}) collective-permute-start(bf16[72,32,128]{2,1,0:T(8,128)(2,1)} %get-tuple-element.28), channel_id=1, source_target_pairs={{0,1},{1,2},{2,3},{3,4},{4,5},{5,6},{6,7},{7,8},{8,9},{9,10},{10,1... | collective-permute-start | bytes 1769480 | tf_op jit(solution)/shard_map/ppermute | solution.py:886
  20.9 1.3 %collective-permute-start.1 = (bf16[72,32,128]{2,1,0:T(8,128)(2,1)}, bf16[72,32,128]{2,1,0:T(8,128)(2,1)}, u32[]{:S(2)}, u32[]{:S(2)}) collective-permute-start(bf16[72,32,128]{2,1,0:T(8,128)(2,1)} %get-tuple-element.29), channel_id=1, source_target_pairs={{1,0},{2,1},{3,2},{4,3},{5,4},{6,5},{7,6},{8,7},{9,8},{10,9},{11,1... | collective-permute-start | bytes 1769480 | tf_op jit(solution)/shard_map/ppermute | solution.py:887
  22.2 20.5 %near_field.1 = (f32[32,16384]{1,0:T(8,128)}, f32[63,32,128]{2,1,0:T(8,128)}) custom-call(s32[8,896]{1,0:T(8,128)} %get-tuple-element.25.list_ref, f32[8,256]{1,0:T(8,128)} %get-tuple-element.24.shape_ref, bf16[32,16384]{1,0:T(8,128)(2,1)} %x_any.3, f32[3,16384]{1,0:T(4,128)} %p_any.1, f32[63,32,128]{2,1,0:T(8,128)} %get-tuple-element.26.lev_any), custom_call_target="tpu_custom_call" | custom-call | flops 1929379840 | bytes 4194304 | tf_op jit(solution)/shard_map/near_field/pallas_call | solution.py:889
  42.7 0.0 collective-permute-done.prev_any
  42.7 9.2 %collective-permute-done.1.next_any = bf16[72,32,128]{2,1,0:T(8,128)(2,1)} collective-permute-done((bf16[72,32,128]{2,1,0:T(8,128)(2,1)}, bf16[72,32,128]{2,1,0:T(8,128)(2,1)}, u32[]{:S(2)}, u32[]{:S(2)}) %collective-permute-start.1) | collective-permute-done | bytes 589856 | tf_op jit(solution)/shard_map/ppermute | solution.py:887
  52.0 19.4 %leaf_couple.1.couple_leaf_any = f32[72,32,128]{2,1,0:T(8,128)} custom-call(s32[16,128]{1,0:T(8,128)} %get-tuple-element.23.entries, f32[8,256]{1,0:T(8,128)} %get-tuple-element.24.shape_ref, bf16[72,32,128]{2,1,0:T(8,128)(2,1)} %collective-permute-done.prev_any, bf16[72,32,128]{2,1,0:T(8,128)(2,1)} %collective-permute-done.1.next_any, ...), custom_call_target="tpu_custom_call" | custom-call | flops 805306368 | bytes 6291456 | tf_op jit(solution)/shard_map/leaf_couple/pallas_call | solution.py:916
  71.3 0.0 all-to-all-done.root_any
  71.4 11.7 %tree_finish.1 = f32[32,16384]{1,0:T(8,128)} custom-call(f32[16,128]{1,0:T(8,128)} %get-tuple-element.22.counts, f32[2,64,64]{2,1,0:T(8,128)} %t_any.1, f32[32,24,128]{2,1,0:T(8,128)} %all-to-all-done.root_any, f32[63,32,128]{2,1,0:T(8,128)} %get-tuple-element.36.couple_any, bf16[128,64,128]{2,1,0:T(8,128)(2,1)} %b_any.3, ...), custom_call_target="tpu_custom_call" | custom-call | tf_op jit(solution)/shard_map/tree_finish/pallas_call | solution.py:941
Async XLA Ops:
  9.1 62.3 %all-to-all-start = ((f32[32,24,128]{2,1,0:T(8,128)}), f32[32,24,128]{2,1,0:T(8,128)}, u32[]{:S(2)}, u32[]{:S(2)}) async-start(f32[32,24,128]{2,1,0:T(8,128)} %get-tuple-element.34), calls=%async_computation | async-start | bytes 786432 | tf_op jit(solution)/shard_map/all_to_all | solution.py:883
  16.5 26.2 %collective-permute-start = (bf16[72,32,128]{2,1,0:T(8,128)(2,1)}, bf16[72,32,128]{2,1,0:T(8,128)(2,1)}, u32[]{:S(2)}, u32[]{:S(2)}) collective-permute-start(bf16[72,32,128]{2,1,0:T(8,128)(2,1)} %get-tuple-element.28), channel_id=1, source_target_pairs={{0,1},{1,2},{2,3},{3,4},{4,5},{5,6},{6,7},{7,8},{8,9},{9,10},{10,1... | collective-permute-start | bytes 1769480 | tf_op jit(solution)/shard_map/ppermute | solution.py:886
  20.9 31.0 %collective-permute-start.1 = (bf16[72,32,128]{2,1,0:T(8,128)(2,1)}, bf16[72,32,128]{2,1,0:T(8,128)(2,1)}, u32[]{:S(2)}, u32[]{:S(2)}) collective-permute-start(bf16[72,32,128]{2,1,0:T(8,128)(2,1)} %get-tuple-element.29), channel_id=1, source_target_pairs={{1,0},{2,1},{3,2},{4,3},{5,4},{6,5},{7,6},{8,7},{9,8},{10,9},{11,1... | collective-permute-start | bytes 1769480 | tf_op jit(solution)/shard_map/ppermute | solution.py:887

commit v12 on v11

--- a/solution.py
+++ b/solution.py
@@ -265,9 +265,9 @@
 
 def leaf_kernel(
     x_any, p_ref, b_any, t_ref, near_ref, coupling_ref,
-    send_next, send_prev, high_any, low_any, lev_any, root_ref, shape_ref,
+    next_any, prev_any, high_any, low_any, lev_any, root_ref, shape_ref,
     list_ref, count_ref, index_ref,
-    x_ref, b_ref, high_ref, low_ref, lev_ref, coef, pts, shapes, p8, sems,
+    send_next, send_prev, x_ref, b_ref, high_ref, low_ref, lev_ref, coef, pts, shapes, p8, sems,
 ):
     leaves = LD // CHUNKS
     copies = []
@@ -289,21 +289,21 @@
     make_lists(near_ref, coupling_ref, list_ref, count_ref, index_ref)
     def leaf_pairs(m, carry):
         values = []
-        for v in range(16):
-            leaf = 16 * m + v
+        for v in range(32):
+            leaf = 32 * m + v
             x = x_ref[:, pl.ds(pl.multiple_of(leaf * P_SIZE, P_SIZE), P_SIZE)]
             weights = b_ref[leaf]
             values.append(dot_nt(x, jnp.concatenate([weights, weights], axis=0)))
+        for v in range(32):
+            high_ref[32 * m + v], low_ref[32 * m + v] = halves(values[v])
         for v in range(16):
-            high_ref[16 * m + v], low_ref[16 * m + v] = halves(values[v])
-        for v in range(8):
-            coef[8 * m + v] = jnp.where(low32, values[2 * v], values[2 * v + 1])
+            coef[16 * m + v] = jnp.where(low32, values[2 * v], values[2 * v + 1])
         return carry
 
     for c in range(CHUNKS):
         for copy in copies[c]:
             copy.wait()
-        steps = leaves // 16
+        steps = leaves // 32
         lax.fori_loop(c * steps, (c + 1) * steps, leaf_pairs, 0)
     leaving = [
         pltpu.make_async_copy(high_ref, high_any, sems.at[2 * CHUNKS]),
@@ -345,25 +345,6 @@
         [jnp.transpose(shapes[0:128, :])[0:8], jnp.transpose(shapes[128:256, :])[0:8]], axis=1
     )
     shape_ref[...] = shape_rows
-    t_high, t_low = halves(doubled_transfer(t_ref))
-    pairs = coef[...]
-    for level in range(1, 7):
-        pairs = pair_lanes(merge_up(pairs, t_high, t_low))
-        lev_ref[pl.ds(PAIR_OFFSETS[level], pairs.shape[0])] = pairs
-    leaving.append(pltpu.make_async_copy(lev_ref, lev_any, sems.at[2 * CHUNKS + 2]))
-    leaving[2].start()
-    root = merge_up(pairs, t_high, t_low)[0]
-
-    low = lanes((R // 2, 128)) < K
-    block = jnp.concatenate(
-        [
-            jnp.where(low, root[0 : R // 2], root[R // 2 : R]),
-            jnp.broadcast_to(shapes[254:255, :], (8, 128)),
-        ],
-        axis=0,
-    )
-    root_ref[...] = jnp.broadcast_to(block[None], root_ref.shape)
-
     p8[...] = jnp.zeros((8, 512), F32)
     for send, first_pair, group in ((send_next, PAIRS // 2, GROUPS - 1), (send_prev, 0, 0)):
 
@@ -384,6 +365,29 @@
             send[69 + part] = jnp.concatenate(
                 [parts[part][:, k * P_SIZE : (k + 1) * P_SIZE] for k in range(4)], axis=0
             ).astype(BF16)
+    for k, (send, out) in enumerate(((send_next, next_any), (send_prev, prev_any))):
+        leaving.append(pltpu.make_async_copy(send, out, sems.at[2 * CHUNKS + 3 + k]))
+        leaving[-1].start()
+
+    t_high, t_low = halves(doubled_transfer(t_ref))
+    pairs = coef[...]
+    for level in range(1, 7):
+        pairs = pair_lanes(merge_up(pairs, t_high, t_low))
+        lev_ref[pl.ds(PAIR_OFFSETS[level], pairs.shape[0])] = pairs
+    leaving.append(pltpu.make_async_copy(lev_ref, lev_any, sems.at[2 * CHUNKS + 2]))
+    leaving[-1].start()
+    root = merge_up(pairs, t_high, t_low)[0]
+
+    low = lanes((R // 2, 128)) < K
+    block = jnp.concatenate(
+        [
+            jnp.where(low, root[0 : R // 2], root[R // 2 : R]),
+            jnp.broadcast_to(shapes[254:255, :], (8, 128)),
+        ],
+        axis=0,
+    )
+    root_ref[...] = jnp.broadcast_to(block[None], root_ref.shape)
+
     for copy in leaving:
         copy.wait()
 
@@ -434,21 +438,21 @@
     eye = identity()
 
     def features(m, carry):
-        loaded = [p_ref[:, pl.ds(pl.multiple_of((8 * m + v) * 512, 512), 512)] for v in range(8)]
-        for v in range(8):
+        loaded = [p_ref[:, pl.ds(pl.multiple_of((16 * m + v) * 512, 512), 512)] for v in range(16)]
+        for v in range(16):
             p8[v, 0:3, :] = loaded[v]
         made = []
-        for v in range(8):
+        for v in range(16):
             coords = p8[v]
-            origin_z = (first_group + 8 * m + v).astype(F32)
+            origin_z = (first_group + 16 * m + v).astype(F32)
             far, own = point_features(coords, origin_z)
             _, own_up = point_features(coords, origin_z + 1.0)
             far = far_stack(far)
             parts = [far[:, k * P_SIZE : (k + 1) * P_SIZE] for k in range(4)]
             turned = dot_nt(eye, jnp.concatenate(parts, axis=0)).astype(BF16)
             made.append((turned, own_stack(own), own_stack(own_up)))
-        for v in range(8):
-            g = 8 * m + v
+        for v in range(16):
+            g = 16 * m + v
             turned, own, own_up = made[v]
             far_feat[2 * g] = turned[:, 0:128]
             far_feat[2 * g + 1] = turned[:, 128:256]
@@ -458,7 +462,7 @@
                 own_feat[LD + 4 * g + k] = own_up[:, part]
         return carry
 
-    lax.fori_loop(0, GROUPS // 8, features, 0)
+    lax.fori_loop(0, GROUPS // 16, features, 0)
 
     for copy in copies:
         copy.wait()
@@ -595,7 +599,7 @@
     down_ref[...] = push_down(value, w_high, w_low)
 
 
-UNIT = 4
+UNIT = 8
 
 
 def couple_leaves(
@@ -629,30 +633,28 @@
     lax.fori_loop(0, LD, own_nodes, 0, unroll=8)
     for copy in copies:
         copy.wait()
-    for side, ref in enumerate((prev_ref, next_ref)):
-        first = LD + side * HALF
-
-        def halo_pairs(m, carry):
-            def read(d, k):
-                return halo_shape[side, d, k]
-
-            loaded = [
-                (tab, 4 * m + v, ref[offset + 4 * m + v])
-                for tab, offset in ((high_tab, 0), (low_tab, 32))
-                for v in range(4)
-            ]
-            turned = [pltpu.roll(pair.astype(F32), K, 1).astype(BF16) for _, _, pair in loaded]
+    def halo_pairs(m, carry):
+        loaded = [
+            (tab, LD + side * HALF + 4 * m + v, ref[offset + 4 * m + v])
+            for side, ref in enumerate((prev_ref, next_ref))
+            for tab, offset in ((high_tab, 0), (low_tab, 32))
+            for v in range(4)
+        ]
+        turned = [pltpu.roll(pair.astype(F32), K, 1).astype(BF16) for _, _, pair in loaded]
+        for side in range(2):
             source = HALF if side == 0 else 0
             place = 0 if side == 0 else HALF + LD
             shift = (2.0 * side - 1.0) * GROUPS * SCALE
             for v in range(8):
-                shape_tab[place + 8 * m + v] = shape_rows(read, source + 8 * m + v, shift)
-            for (tab, pair, value), other in zip(loaded, turned):
-                tab[first + pair] = value
-                tab[first + PAIRS // 2 + pair] = other
-            return carry
-
-        lax.fori_loop(0, PAIRS // 8, halo_pairs, 0)
+                shape_tab[place + 8 * m + v] = shape_rows(
+                    lambda d, k: halo_shape[side, d, k], source + 8 * m + v, shift
+                )
+        for (tab, pair, value), other in zip(loaded, turned):
+            tab[pair] = value
+            tab[PAIRS // 2 + pair] = other
+        return carry
+
+    lax.fori_loop(0, PAIRS // 8, halo_pairs, 0)
     high_tab[TABLE - 1] = jnp.zeros((R, 128), BF16)
     low_tab[TABLE - 1] = jnp.zeros((R, 128), BF16)
     for copy in table_copies:
@@ -696,7 +698,7 @@
 
     def couple_phase(n, new, old):
         for u in range(UNIT):
-            couple_tiles(jnp.minimum(n * UNIT + u, PAIRS - 1), u, *new)
+            couple_tiles(n * UNIT + u, u, *new)
             leaf_couple[n * UNIT + u] = couple_apply(u, *old)
 
     buffers = ((tiles0, lhs0), (tiles1, lhs1))
@@ -708,14 +710,16 @@
         couple_phase(2 * m + 1, buffers[1], buffers[0])
         return carry
 
-    lax.fori_loop(0, PAIRS // UNIT // 2 + 1, couple_two, 0)
+    lax.fori_loop(0, PAIRS // UNIT // 2, couple_two, 0)
+    for u in range(UNIT):
+        leaf_couple[PAIRS + u] = couple_apply(u, *buffers[1])
 
 
 def finish_leaves(b_ref, down_ref, leaf_couple, out_ref, border):
     def finish(m, carry):
         values = []
-        for v in range(8):
-            c = 8 * m + v
+        for v in range(16):
+            c = 16 * m + v
             value = (down_ref[c] + leaf_couple[c + UNIT]).astype(BF16)
             span = pl.ds(pl.multiple_of(c * 256, 256), 256)
             values.append(
@@ -729,7 +733,7 @@
             out_ref[:, span] = value
         return carry
 
-    lax.fori_loop(0, PAIRS // 8, finish, 0)
+    lax.fori_loop(0, PAIRS // 16, finish, 0)
     for side, group in enumerate((0, GROUPS - 1)):
         for i in range(4):
             leaf = 4 * group + i
@@ -769,58 +773,48 @@
             border[4 * side + i] = sums[side][i]
 
 
-def couple_kernel(
-    entries, shape_ref,
-    prev_any, next_any, high_any, low_any,
-    leaf_couple,
-    prev_ref, next_ref,
+def tree_kernel(
+    t_any, root_any, couple_any, down_ref, t_ref, root_ref, couple, pairs_scr, shapes, sems
+):
+    moves = ((t_any, t_ref), (root_any, root_ref), (couple_any, couple))
+    copies = [pltpu.make_async_copy(a, b, sems.at[k]) for k, (a, b) in enumerate(moves)]
+    for copy in copies:
+        copy.start()
+    for copy in copies:
+        copy.wait()
+    tree_down(t_ref, root_ref, down_ref, couple, pairs_scr, shapes)
+
+
+def final_kernel(
+    entries, shape_ref, counts,
+    prev_any, next_any, p_any, high_any, low_any, b_any, near_any, down_any,
+    out_ref,
+    prev_ref, next_ref, p_ref, b_ref, down, leaf_couple,
     shape_tab, high_tab, low_tab, halo_rows, halo_shape,
-    tiles0, lhs0, tiles1, lhs1, sems, halo_sems,
+    tiles0, lhs0, tiles1, lhs1, p8, coords, border, sems, halo_sems,
 ):
     moves = (
         (prev_any, prev_ref),
         (next_any, next_ref),
+        (p_any, p_ref),
         (high_any, high_tab.at[0:LD]),
         (low_any, low_tab.at[0:LD]),
+        (b_any, b_ref),
+        (near_any, out_ref),
+        (down_any, down),
     )
     copies = [pltpu.make_async_copy(a, b, sems.at[k]) for k, (a, b) in enumerate(moves)]
     for copy in copies:
         copy.start()
-    copies[0].wait()
-    copies[1].wait()
+    for copy in copies[0:3]:
+        copy.wait()
+    border_blocks(counts, p_ref, prev_ref, next_ref, border, p8, coords)
     couple_leaves(
-        entries, shape_ref, prev_ref, next_ref, copies[2:4], leaf_couple,
+        entries, shape_ref, prev_ref, next_ref, copies[3:5], leaf_couple,
         shape_tab, high_tab, low_tab, halo_rows, halo_shape, halo_sems,
         tiles0, lhs0, tiles1, lhs1,
     )
-
-
-def final_kernel(
-    counts,
-    t_any, root_any, couple_any, b_any, couple_leaf_any, near_any, prev_any, next_any, p_any,
-    out_ref,
-    t_ref, root_ref, couple, b_ref, leaf_couple, prev_ref, next_ref, p_ref,
-    down, pairs_scr, shapes, p8, coords, border, sems,
-):
-    moves = (
-        (t_any, t_ref),
-        (root_any, root_ref),
-        (couple_any, couple),
-        (prev_any.at[64:SEND], prev_ref.at[64:SEND]),
-        (next_any.at[64:SEND], next_ref.at[64:SEND]),
-        (p_any, p_ref),
-        (b_any, b_ref),
-        (couple_leaf_any, leaf_couple),
-        (near_any, out_ref),
-    )
-    copies = [pltpu.make_async_copy(a, b, sems.at[k]) for k, (a, b) in enumerate(moves)]
-    for copy in copies:
-        copy.start()
-    for copy in copies[0:6]:
-        copy.wait()
-    border_blocks(counts, p_ref, prev_ref, next_ref, border, p8, coords)
-    tree_down(t_ref, root_ref, down, couple, pairs_scr, shapes)
-    for copy in copies[6:]:
+    for copy in copies[5:]:
         copy.wait()
     finish_leaves(b_ref, down, leaf_couple, out_ref, border)
 
@@ -864,8 +858,10 @@
             shaped(16, 128, dtype=jnp.int32),
         ),
         in_specs=[anywhere(), vmem(), anywhere(), vmem(), vmem(), vmem()],
-        out_specs=[vmem()] * 2 + [anywhere()] * 3 + [vmem()] * 5,
+        out_specs=[anywhere()] * 5 + [vmem()] * 5,
         scratch_shapes=[
+            pltpu.VMEM((SEND, R, 128), BF16),
+            pltpu.VMEM((SEND, R, 128), BF16),
             pltpu.VMEM((R, LD * P_SIZE), BF16),
             pltpu.VMEM((LD, K, P_SIZE), BF16),
             pltpu.VMEM((LD, R, 128), BF16),
@@ -875,7 +871,7 @@
             pltpu.VMEM((3, LD, 128), F32),
             pltpu.VMEM((256, 128), F32),
             pltpu.VMEM((8, 512), F32),
-            pltpu.SemaphoreType.DMA((2 * CHUNKS + 3,)),
+            pltpu.SemaphoreType.DMA((2 * CHUNKS + 5,)),
         ],
         compiler_params=PARAMS,
     )(charges, points, basis, transfer, near_rows, coupling_rows)
@@ -896,7 +892,7 @@
             pltpu.VMEM((R, LD * P_SIZE), BF16),
             pltpu.VMEM((PAIRS - 1, R, 128), F32),
             pltpu.SemaphoreType.DMA((2,)),
-            pltpu.VMEM((8, 8, 512), F32),
+            pltpu.VMEM((16, 8, 512), F32),
             pltpu.VMEM((PAIRS, P_SIZE, 2 * FEATS), BF16),
             pltpu.VMEM((2 * LD, FEATS, P_SIZE), BF16),
             pltpu.VMEM((BATCH // 2, 128, 256), BF16),
@@ -908,20 +904,42 @@
         ),
     )(tasks, shapes, charges, points, lev)
 
-    near, from_prev, from_next = lax.optimization_barrier((near, from_prev, from_next))
+    near, roots = lax.optimization_barrier((near, roots))
+    down = pl.pallas_call(
+        tree_kernel,
+        name="tree_down",
+        out_shape=shaped(PAIRS, R, 128),
+        in_specs=[anywhere()] * 3,
+        out_specs=vmem(),
+        scratch_shapes=[
+            pltpu.VMEM((2, K, K), F32),
+            pltpu.VMEM((devices, R // 2 + 8, 128), F32),
+            pltpu.VMEM((PAIRS - 1, R, 128), F32),
+            pltpu.VMEM((devices, R, 128), F32),
+            pltpu.VMEM((2 * devices, 128), F32),
+            pltpu.SemaphoreType.DMA((3,)),
+        ],
+        compiler_params=PARAMS,
+    )(transfer, roots, couple)
+    from_prev, from_next, down = lax.optimization_barrier((from_prev, from_next, down))
+
     stages = [
         pltpu.VMEM((UNIT, 512, 256), BF16),
         pltpu.VMEM((UNIT, 4 * R, 512), BF16),
     ]
-    leaf_couple = pl.pallas_call(
-        couple_kernel,
-        name="leaf_couple",
-        out_shape=shaped(PAIRS + 2 * UNIT, R, 128),
-        in_specs=[smem()] * 2 + [anywhere()] * 4,
+    return pl.pallas_call(
+        final_kernel,
+        name="couple_finish",
+        out_shape=shaped(R, LD * P_SIZE),
+        in_specs=[smem()] * 3 + [anywhere()] * 8,
         out_specs=vmem(),
         scratch_shapes=[
             pltpu.VMEM((SEND, R, 128), BF16),
             pltpu.VMEM((SEND, R, 128), BF16),
+            pltpu.VMEM((3, LD * P_SIZE), F32),
+            pltpu.VMEM((LD, K, P_SIZE), BF16),
+            pltpu.VMEM((PAIRS, R, 128), F32),
+            pltpu.VMEM((PAIRS + UNIT, R, 128), F32),
             pltpu.VMEM((2 * LD, 8, 128), F32),
             pltpu.VMEM((TABLE, R, 128), BF16),
             pltpu.VMEM((TABLE, R, 128), BF16),
@@ -930,39 +948,18 @@
         ]
         + stages
         + stages
-        + [pltpu.SemaphoreType.DMA((4,)), pltpu.SemaphoreType.DMA((2,))],
-        compiler_params=PARAMS,
-        cost_estimate=pl.CostEstimate(
-            flops=2 * 1024 * 64 * 64 * 32 * 3, bytes_accessed=6 << 20, transcendentals=1024 * 8192
-        ),
-    )(entries, shapes, from_prev, from_next, high, low)
-
-    leaf_couple, roots = lax.optimization_barrier((leaf_couple, roots))
-    return pl.pallas_call(
-        final_kernel,
-        name="tree_finish",
-        out_shape=shaped(R, LD * P_SIZE),
-        in_specs=[smem()] + [anywhere()] * 9,
-        out_specs=vmem(),
-        scratch_shapes=[
-            pltpu.VMEM((2, K, K), F32),
-            pltpu.VMEM((devices, R // 2 + 8, 128), F32),
-            pltpu.VMEM((PAIRS - 1, R, 128), F32),
-            pltpu.VMEM((LD, K, P_SIZE), BF16),
-            pltpu.VMEM((PAIRS + 2 * UNIT, R, 128), F32),
-            pltpu.VMEM((SEND, R, 128), BF16),
-            pltpu.VMEM((SEND, R, 128), BF16),
-            pltpu.VMEM((3, LD * P_SIZE), F32),
-            pltpu.VMEM((PAIRS, R, 128), F32),
-            pltpu.VMEM((devices, R, 128), F32),
-            pltpu.VMEM((2 * devices, 128), F32),
+        + [
             pltpu.VMEM((2, 8, 512), F32),
             pltpu.VMEM((2, R, 128), F32),
             pltpu.VMEM((8, R, 128), F32),
-            pltpu.SemaphoreType.DMA((9,)),
+            pltpu.SemaphoreType.DMA((8,)),
+            pltpu.SemaphoreType.DMA((2,)),
         ],
         compiler_params=PARAMS,
-    )(counts, transfer, roots, couple, basis, leaf_couple, near, from_prev, from_next, points)
+    )(
+        entries, shapes, counts,
+        from_prev, from_next, points, high, low, basis, near, down,
+    )
 
 
 def solution(mesh):

time: 83.6 us -> 75.2 us (0.90); the launches traced: 83.1 us -> 73.7 us
  waiting for transfers between devices: 9.24 us -> 3.22 us
  Pallas kernels: 60.7 us -> 57.2 us
    ppermute x1, waiting for transfers between devices: 9.24 us -> 3.22 us  [per_device(): from_next = lax.ppermute(send_prev, AXES, backward)]
    pallas_call x2, Pallas kernels: 31.1 us -> 28.1 us  [the longest x1 21.8 us: per_device(): pl.pallas_call(final_kernel, name='couple_finish', out_shape=shaped(R, LD...]
  transfers between devices with their start and end apart: 3 -> 3, of which waited for: 1 -> 1; matrix products, arithmetic and copies ran while one was open for 0% -> 0% of each run, Pallas kernels for 48% -> 36%
where the time goes in v12:
time: 75.2 us; the launch traced here: 73.7 us
  Pallas kernels  57.2 us (76%)
  starting transfers between devices  13.1 us (17%)
  waiting for transfers between devices  3.22 us (4%)
    pallas_call x1, Pallas kernels, per_device(): pl.pallas_call(final_kernel, name='couple_finish', out_shape=shaped(R, LD...  21.8 us
    pallas_call x1, Pallas kernels, per_device(): pl.pallas_call(near_kernel, name='near_field', out_shape=(shaped(R, LD *...  20.2 us
    pallas_call x1, Pallas kernels, per_device(): pl.pallas_call(leaf_kernel, name='leaf_up', out_shape=(shaped(SEND, R, 12...  8.85 us
    all_to_all x1, starting transfers between devices, per_device(): roots = lax.all_to_all(root, AXES, 0, 0, tiled=True)  7.42 us
    pallas_call x1, Pallas kernels, per_device(): pl.pallas_call(tree_kernel, name='tree_down', out_shape=shaped(PAIRS, R,...  6.27 us
    ppermute x1, starting transfers between devices, per_device(): from_prev = lax.ppermute(send_next, AXES, forward)  4.44 us
    ppermute x1, waiting for transfers between devices, per_device(): from_next = lax.ppermute(send_prev, AXES, backward)  3.22 us
  transfers between devices with their start and end apart: 3, of which 1 were waited for; matrix products, arithmetic and copies ran while one was open for 0% of the time, Pallas kernels for 36%

profile of v12, /device:TPU:0, one launch (start us, length us, event | category | flops | bytes accessed | tf_op | source)
XLA Modules:
  0.0 73.7 jit_solution(7850465787803645274)
XLA Ops:
  0.0 8.8 %leaf_up.1 = (bf16[72,32,128]{2,1,0:T(8,128)(2,1)}, bf16[72,32,128]{2,1,0:T(8,128)(2,1)}, bf16[128,32,128]{2,1,0:T(8,128)(2,1)}, bf16[128,32,128]{2,1,0:T(8,128)...) custom-call(bf16[32,16384]{1,0:T(8,128)(2,1)} %x_any.3, ...), custom_call_target="tpu_custom_call" | custom-call | tf_op jit(solution)/shard_map/leaf_up/pallas_call | solution.py:845
  8.9 7.4 %all-to-all-start = ((f32[32,24,128]{2,1,0:T(8,128)}), f32[32,24,128]{2,1,0:T(8,128)}, u32[]{:S(2)}, u32[]{:S(2)}) async-start(f32[32,24,128]{2,1,0:T(8,128)} %get-tuple-element.30), calls=%async_computation | async-start | bytes 786432 | tf_op jit(solution)/shard_map/all_to_all | solution.py:879
  16.3 4.4 %collective-permute-start = (bf16[72,32,128]{2,1,0:T(8,128)(2,1)}, bf16[72,32,128]{2,1,0:T(8,128)(2,1)}, u32[]{:S(2)}, u32[]{:S(2)}) collective-permute-start(bf16[72,32,128]{2,1,0:T(8,128)(2,1)} %get-tuple-element.25), channel_id=1, source_target_pairs={{0,1},{1,2},{2,3},{3,4},{4,5},{5,6},{6,7},{7,8},{8,9},{9,10},{10,1... | collective-permute-start | bytes 1769480 | tf_op jit(solution)/shard_map/ppermute | solution.py:882
  20.7 1.3 %collective-permute-start.1 = (bf16[72,32,128]{2,1,0:T(8,128)(2,1)}, bf16[72,32,128]{2,1,0:T(8,128)(2,1)}, u32[]{:S(2)}, u32[]{:S(2)}) collective-permute-start(bf16[72,32,128]{2,1,0:T(8,128)(2,1)} %get-tuple-element.26), channel_id=1, source_target_pairs={{1,0},{2,1},{3,2},{4,3},{5,4},{6,5},{7,6},{8,7},{9,8},{10,9},{11,1... | collective-permute-start | bytes 1769480 | tf_op jit(solution)/shard_map/ppermute | solution.py:883
  22.0 20.2 %near_field.1 = (f32[32,16384]{1,0:T(8,128)}, f32[63,32,128]{2,1,0:T(8,128)}) custom-call(s32[8,896]{1,0:T(8,128)} %get-tuple-element.27.list_ref, f32[8,256]{1,0:T(8,128)} %get-tuple-element.23.shape_ref, bf16[32,16384]{1,0:T(8,128)(2,1)} %x_any.3, f32[3,16384]{1,0:T(4,128)} %p_any.1, f32[63,32,128]{2,1,0:T(8,128)} %get-tuple-element.28.lev_any), custom_call_target="tpu_custom_call" | custom-call | flops 1929379840 | bytes 4194304 | tf_op jit(solution)/shard_map/near_field/pallas_call | solution.py:885
  42.2 0.0 all-to-all-done.root_any
  42.2 6.3 %tree_down.1.down_any = f32[64,32,128]{2,1,0:T(8,128)} custom-call(f32[2,64,64]{2,1,0:T(8,128)} %t_any.1, f32[32,24,128]{2,1,0:T(8,128)} %all-to-all-done.root_any, f32[63,32,128]{2,1,0:T(8,128)} %get-tuple-element.32.couple_any), custom_call_target="tpu_custom_call" | custom-call | tf_op jit(solution)/shard_map/tree_down/pallas_call | solution.py:908
  48.5 0.0 collective-permute-done.prev_any
  48.5 3.2 %collective-permute-done.1.next_any = bf16[72,32,128]{2,1,0:T(8,128)(2,1)} collective-permute-done((bf16[72,32,128]{2,1,0:T(8,128)(2,1)}, bf16[72,32,128]{2,1,0:T(8,128)(2,1)}, u32[]{:S(2)}, u32[]{:S(2)}) %collective-permute-start.1) | collective-permute-done | bytes 589856 | tf_op jit(solution)/shard_map/ppermute | solution.py:883
  51.8 21.8 %couple_finish.1 = f32[32,16384]{1,0:T(8,128)} custom-call(s32[16,128]{1,0:T(8,128)} %get-tuple-element.22.entries, f32[8,256]{1,0:T(8,128)} %get-tuple-element.23.shape_ref, f32[16,128]{1,0:T(8,128)} %get-tuple-element.24.counts, bf16[72,32,128]{2,1,0:T(8,128)(2,1)} %collective-permute-done.prev_any, bf16[72,32,128]{2,1,0:T(8,128)(2,1)} %collective-permute-done.1.next_any, ...), custom_call_target="tpu_custom_call" | custom-call | tf_op jit(solution)/shard_map/couple_finish/pallas_call | solution.py:930
Async XLA Ops:
  8.9 33.4 %all-to-all-start = ((f32[32,24,128]{2,1,0:T(8,128)}), f32[32,24,128]{2,1,0:T(8,128)}, u32[]{:S(2)}, u32[]{:S(2)}) async-start(f32[32,24,128]{2,1,0:T(8,128)} %get-tuple-element.30), calls=%async_computation | async-start | bytes 786432 | tf_op jit(solution)/shard_map/all_to_all | solution.py:879
  16.3 32.2 %collective-permute-start = (bf16[72,32,128]{2,1,0:T(8,128)(2,1)}, bf16[72,32,128]{2,1,0:T(8,128)(2,1)}, u32[]{:S(2)}, u32[]{:S(2)}) collective-permute-start(bf16[72,32,128]{2,1,0:T(8,128)(2,1)} %get-tuple-element.25), channel_id=1, source_target_pairs={{0,1},{1,2},{2,3},{3,4},{4,5},{5,6},{6,7},{7,8},{8,9},{9,10},{10,1... | collective-permute-start | bytes 1769480 | tf_op jit(solution)/shard_map/ppermute | solution.py:882
  20.7 31.0 %collective-permute-start.1 = (bf16[72,32,128]{2,1,0:T(8,128)(2,1)}, bf16[72,32,128]{2,1,0:T(8,128)(2,1)}, u32[]{:S(2)}, u32[]{:S(2)}) collective-permute-start(bf16[72,32,128]{2,1,0:T(8,128)(2,1)} %get-tuple-element.26), channel_id=1, source_target_pairs={{1,0},{2,1},{3,2},{4,3},{5,4},{6,5},{7,6},{8,7},{9,8},{10,9},{11,1... | collective-permute-start | bytes 1769480 | tf_op jit(solution)/shard_map/ppermute | solution.py:883

commit v13 on v12

--- a/solution.py
+++ b/solution.py
@@ -19,8 +19,8 @@
 NEAR_REACH = 8
 FEATS = 64
 BATCH = 16
-SIBLINGS = 4
-LIST = 896
+SIBLINGS = 6
+LIST = 1536
 SEND = 72
 SCALE = 0.5 * math.log2(math.e)
 NODE = [math.cos((2 * a + 1) * math.pi / 8) for a in range(4)]
@@ -194,7 +194,11 @@
         + [pltpu.roll(reverse[delta : delta + 1, :], 128 - delta, 1) for delta in range(1, 8)],
         axis=0,
     )
-    turned = (row8 == 1) & ((lane8 & 3) == 2)
+    wanted = (lane8 + row8 < LD) & (forward + backward > 0.0)
+    mutual = (forward > 0.0) & (backward > 0.0)
+    turned = ((row8 == 1) & ((lane8 & 3) == 2) & mutual) | (
+        (forward == 0.0) & (backward > 0.0)
+    )
     leaf = lane8.astype(F32)
     other = leaf + row8.astype(F32)
     first = jnp.where(turned, other, leaf)
@@ -202,22 +206,31 @@
     to_first = jnp.where(turned, backward, forward)
     to_second = jnp.where(turned, forward, backward)
     odd = jnp.where(turned, lane8, lane8 + row8) & 1
-    wanted = (lane8 + row8 < LD) & (forward + backward > 0.0)
     earlier = jnp.where(rows((128, 128)) < lanes((128, 128)), 1.0, 0.0).astype(BF16)
     place = jnp.full((8, 128), -1.0, F32)
-    most = jnp.zeros((1, 1), F32)
-    for parity in range(2):
-        flags = jnp.where(wanted & (odd == parity), 1.0, 0.0)
-        rank = dot(flags.astype(BF16), earlier)
-        totals = jnp.sum(flags, axis=1, keepdims=True)
-        before = jnp.zeros((1, 1), F32)
-        starts = []
-        for delta in range(8):
-            starts.append(before)
-            before = before + totals[delta : delta + 1, :]
-        rank = rank + jnp.concatenate(starts, axis=0)
-        place = jnp.where(flags > 0.0, 2.0 * rank + (1.0 * BATCH + parity), place)
-        most = jnp.maximum(most, before)
+    batches = jnp.zeros((1, 1), jnp.int32)
+    ends = []
+    for kind in range(2):
+        most = jnp.zeros((1, 1), F32)
+        for parity in range(2):
+            chosen = wanted & (odd == parity) & (mutual if kind == 0 else jnp.logical_not(mutual))
+            flags = jnp.where(chosen, 1.0, 0.0)
+            rank = dot(flags.astype(BF16), earlier)
+            totals = jnp.sum(flags, axis=1, keepdims=True)
+            before = jnp.zeros((1, 1), F32)
+            starts = []
+            for delta in range(8):
+                starts.append(before)
+                before = before + totals[delta : delta + 1, :]
+            rank = rank + jnp.concatenate(starts, axis=0)
+            base = (batches + 1).astype(F32) * BATCH + parity
+            place = jnp.where(flags > 0.0, 2.0 * rank + base, place)
+            most = jnp.maximum(most, before)
+        needed = (2 * most.astype(jnp.int32) + BATCH - 1) // BATCH
+        batches = batches + needed
+        if kind == 0:
+            batches = batches | 1
+        ends.append(batches)
     task_rows = []
     for delta in range(8):
         pick = slice(delta, delta + 1)
@@ -236,7 +249,9 @@
         )
     tasks = jnp.concatenate(task_rows, axis=1)
     slot_row = rows((128, 128)).astype(F32)
-    for m in range(LIST // 128):
+    limit = (ends[1][0, 0] + 4) * BATCH
+
+    def fill(m):
         chosen = jnp.concatenate(
             [
                 jnp.where(place[delta : delta + 1, :] == slot_row + 128.0 * m, 1.0, 0.0).astype(BF16)
@@ -245,8 +260,14 @@
             axis=1,
         )
         part = dot_nt(tasks, chosen)
-        part = jnp.where(row8 == 4, 2.0 * most, part)
-        list_ref[:, m * 128 : (m + 1) * 128] = part.astype(jnp.int32)
+        part = part.astype(jnp.int32)
+        part = jnp.where(row8 == 4, ends[0], jnp.where(row8 == 5, ends[1], part))
+        list_ref[:, m * 128 : (m + 1) * 128] = part
+
+    for m in range(4):
+        fill(m)
+    for m in range(4, LIST // 128):
+        pl.when(m * 128 < limit)(functools.partial(fill, m))
 
     target = coupling_ref[...]
     reach = target - first_leaf + HALF
@@ -447,19 +468,21 @@
             origin_z = (first_group + 16 * m + v).astype(F32)
             far, own = point_features(coords, origin_z)
             _, own_up = point_features(coords, origin_z + 1.0)
+            _, own_down = point_features(coords, origin_z - 1.0)
             far = far_stack(far)
             parts = [far[:, k * P_SIZE : (k + 1) * P_SIZE] for k in range(4)]
             turned = dot_nt(eye, jnp.concatenate(parts, axis=0)).astype(BF16)
-            made.append((turned, own_stack(own), own_stack(own_up)))
+            made.append((turned, own_stack(own), own_stack(own_up), own_stack(own_down)))
         for v in range(16):
             g = 16 * m + v
-            turned, own, own_up = made[v]
+            turned, own, own_up, own_down = made[v]
             far_feat[2 * g] = turned[:, 0:128]
             far_feat[2 * g + 1] = turned[:, 128:256]
             for k in range(4):
                 part = slice(k * P_SIZE, (k + 1) * P_SIZE)
                 own_feat[4 * g + k] = own[:, part]
                 own_feat[LD + 4 * g + k] = own_up[:, part]
+                own_feat[2 * LD + 4 * g + k] = own_down[:, part]
         return carry
 
     lax.fori_loop(0, GROUPS // 16, features, 0)
@@ -470,8 +493,8 @@
     for ref in (tile0, tile1):
         ref[...] = jnp.zeros(ref.shape, ref.dtype)
 
-    total = list_ref[4, 0]
-    steps = (total + BATCH - 1) // BATCH + 1
+    mutual_phases = list_ref[4, 0] + 1
+    all_phases = list_ref[5, 0] + 1
     low = lanes((128, 128)) < K
 
     def leaf_slice(i):
@@ -480,14 +503,15 @@
     lane_u = lane_nodes()
     row_y, row_z = row_nodes()
 
-    def phase(n, tile_new, tile_old, pairs):
+    def phase(n, tile_new, tile_old, pairs, sides):
         far, own, sources, updates = [], [], [], []
         siblings = [jnp.minimum(pairs * n + v, PAIRS - 2) for v in range(pairs)]
         levels = [lev_ref[pair] for pair in siblings]
         for u in range(BATCH):
             k = (n + 1) * BATCH + u
             i, j = list_ref[0, k], list_ref[1, k]
-            variant = ((j >> 2) - (i >> 2)) * LD
+            step = (j >> 2) - (i >> 2)
+            variant = jnp.where(step < 0, 2, step) * LD
             far.append(far_feat[j >> 1])
             own.append(own_feat[variant + i])
         for u in range(BATCH):
@@ -501,14 +525,18 @@
             tiles.append(decay(dist).astype(BF16))
             weights = block_diagonal(tile_old[u, :, 0:128], tile_old[u, :, 128:256])
             to_i = dot(jnp.concatenate([sources[2 * u][0], sources[2 * u + 1][0]], axis=1), weights)
-            to_j = dot_nt(jnp.concatenate([sources[2 * u][1], sources[2 * u + 1][1]], axis=1), weights)
+            to_j = None
+            if sides == 2:
+                to_j = dot_nt(
+                    jnp.concatenate([sources[2 * u][1], sources[2 * u + 1][1]], axis=1), weights
+                )
             for h in range(2):
                 k = n * BATCH + 2 * u + h
                 span = slice(h * 128, (h + 1) * 128)
                 updates.append(
                     (
                         to_i[:, span] * list_ref[2, k].astype(F32),
-                        to_j[:, span] * list_ref[3, k].astype(F32),
+                        to_j[:, span] * list_ref[3, k].astype(F32) if sides == 2 else None,
                     )
                 )
         for pair, level in zip(siblings, levels):
@@ -525,16 +553,19 @@
             to_i = leaf_slice(list_ref[0, k])
             to_j = leaf_slice(list_ref[1, k])
             out_ref[:, to_i] += updates[u][0]
-            out_ref[:, to_j] += updates[u][1]
-
-    def two_phases(pairs, m, carry):
-        phase(2 * m, tile0, tile1, pairs)
-        phase(2 * m + 1, tile1, tile0, pairs)
+            if sides == 2:
+                out_ref[:, to_j] += updates[u][1]
+
+    def two_phases(pairs, sides, m, carry):
+        phase(2 * m, tile0, tile1, pairs, sides)
+        phase(2 * m + 1, tile1, tile0, pairs, sides)
         return carry
 
-    rides = PAIRS // (2 * SIBLINGS)
-    lax.fori_loop(0, rides, functools.partial(two_phases, SIBLINGS), 0)
-    lax.fori_loop(rides, (steps + 1) // 2, functools.partial(two_phases, 0), 0)
+    rides = -(-(PAIRS - 1) // (2 * SIBLINGS))
+    middle = mutual_phases // 2
+    lax.fori_loop(0, rides, functools.partial(two_phases, SIBLINGS, 2), 0)
+    lax.fori_loop(rides, middle, functools.partial(two_phases, 0, 2), 0)
+    lax.fori_loop(middle, (all_phases + 1) // 2, functools.partial(two_phases, 0, 1), 0)
 
 
 def tree_down(t_ref, root_ref, down_ref, couple, pairs_scr, shapes):
@@ -894,7 +925,7 @@
             pltpu.SemaphoreType.DMA((2,)),
             pltpu.VMEM((16, 8, 512), F32),
             pltpu.VMEM((PAIRS, P_SIZE, 2 * FEATS), BF16),
-            pltpu.VMEM((2 * LD, FEATS, P_SIZE), BF16),
+            pltpu.VMEM((3 * LD, FEATS, P_SIZE), BF16),
             pltpu.VMEM((BATCH // 2, 128, 256), BF16),
             pltpu.VMEM((BATCH // 2, 128, 256), BF16),
         ],

time: 75.2 us -> 74.1 us (0.985); the launches traced: 73.7 us -> 73.7 us
  Pallas kernels: 57.2 us -> 56.2 us
  waiting for transfers between devices: 3.22 us -> 4.08 us
    ppermute x1, waiting for transfers between devices: 3.22 us -> 4.07 us  [per_device(): from_next = lax.ppermute(send_prev, AXES, backward)]
    pallas_call x1, Pallas kernels: 20.2 us -> 19.4 us  [per_device(): pl.pallas_call(near_kernel, name='near_field', out_shape=(shaped(R, LD *...]
  transfers between devices with their start and end apart: 3 -> 3, of which waited for: 1 -> 1; matrix products, arithmetic and copies ran while one was open for 0% -> 0% of each run, Pallas kernels for 36% -> 35%
where the time goes in v13:
time: 74.1 us; the launch traced here: 73.7 us
  Pallas kernels  56.2 us (76%)
  starting transfers between devices  13.1 us (18%)
  waiting for transfers between devices  4.08 us (6%)
    pallas_call x1, Pallas kernels, per_device(): pl.pallas_call(final_kernel, name='couple_finish', out_shape=shaped(R, LD...  21.8 us
    pallas_call x1, Pallas kernels, per_device(): pl.pallas_call(near_kernel, name='near_field', out_shape=(shaped(R, LD *...  19.4 us
    pallas_call x1, Pallas kernels, per_device(): pl.pallas_call(leaf_kernel, name='leaf_up', out_shape=(shaped(SEND, R, 12...  8.79 us
    all_to_all x1, starting transfers between devices, per_device(): roots = lax.all_to_all(root, AXES, 0, 0, tiled=True)  7.41 us
    pallas_call x1, Pallas kernels, per_device(): pl.pallas_call(tree_kernel, name='tree_down', out_shape=shaped(PAIRS, R,...  6.27 us
    ppermute x1, starting transfers between devices, per_device(): from_prev = lax.ppermute(send_next, AXES, forward)  4.44 us
    ppermute x1, waiting for transfers between devices, per_device(): from_next = lax.ppermute(send_prev, AXES, backward)  4.07 us
  transfers between devices with their start and end apart: 3, of which 1 were waited for; matrix products, arithmetic and copies ran while one was open for 0% of the time, Pallas kernels for 35%

profile of v13, /device:TPU:0, one launch (start us, length us, event | category | flops | bytes accessed | tf_op | source)
XLA Modules:
  0.0 73.7 jit_solution(4626384402998893442)
XLA Ops:
  0.0 8.8 %leaf_up.1 = (bf16[72,32,128]{2,1,0:T(8,128)(2,1)}, bf16[72,32,128]{2,1,0:T(8,128)(2,1)}, bf16[128,32,128]{2,1,0:T(8,128)(2,1)}, bf16[128,32,128]{2,1,0:T(8,128)...) custom-call(bf16[32,16384]{1,0:T(8,128)(2,1)} %x_any.3, ...), custom_call_target="tpu_custom_call" | custom-call | tf_op jit(solution)/shard_map/leaf_up/pallas_call | solution.py:876
  8.8 7.4 %all-to-all-start = ((f32[32,24,128]{2,1,0:T(8,128)}), f32[32,24,128]{2,1,0:T(8,128)}, u32[]{:S(2)}, u32[]{:S(2)}) async-start(f32[32,24,128]{2,1,0:T(8,128)} %get-tuple-element.30), calls=%async_computation | async-start | bytes 786432 | tf_op jit(solution)/shard_map/all_to_all | solution.py:910
  16.2 4.4 %collective-permute-start = (bf16[72,32,128]{2,1,0:T(8,128)(2,1)}, bf16[72,32,128]{2,1,0:T(8,128)(2,1)}, u32[]{:S(2)}, u32[]{:S(2)}) collective-permute-start(bf16[72,32,128]{2,1,0:T(8,128)(2,1)} %get-tuple-element.25), channel_id=1, source_target_pairs={{0,1},{1,2},{2,3},{3,4},{4,5},{5,6},{6,7},{7,8},{8,9},{9,10},{10,1... | collective-permute-start | bytes 1769480 | tf_op jit(solution)/shard_map/ppermute | solution.py:913
  20.7 1.3 %collective-permute-start.1 = (bf16[72,32,128]{2,1,0:T(8,128)(2,1)}, bf16[72,32,128]{2,1,0:T(8,128)(2,1)}, u32[]{:S(2)}, u32[]{:S(2)}) collective-permute-start(bf16[72,32,128]{2,1,0:T(8,128)(2,1)} %get-tuple-element.26), channel_id=1, source_target_pairs={{1,0},{2,1},{3,2},{4,3},{5,4},{6,5},{7,6},{8,7},{9,8},{10,9},{11,1... | collective-permute-start | bytes 1769480 | tf_op jit(solution)/shard_map/ppermute | solution.py:914
  21.9 19.4 %near_field.1 = (f32[32,16384]{1,0:T(8,128)}, f32[63,32,128]{2,1,0:T(8,128)}) custom-call(s32[8,1536]{1,0:T(8,128)} %get-tuple-element.27.list_ref, f32[8,256]{1,0:T(8,128)} %get-tuple-element.23.shape_ref, bf16[32,16384]{1,0:T(8,128)(2,1)} %x_any.3, f32[3,16384]{1,0:T(4,128)} %p_any.1, f32[63,32,128]{2,1,0:T(8,128)} %get-tuple-element.28.lev_any), custom_call_target="tpu_custom_call" | custom-call | flops 1929379840 | bytes 4194304 | tf_op jit(solution)/shard_map/near_field/pallas_call | solution.py:916
  41.3 0.0 all-to-all-done.root_any
  41.3 6.3 %tree_down.1.down_any = f32[64,32,128]{2,1,0:T(8,128)} custom-call(f32[2,64,64]{2,1,0:T(8,128)} %t_any.1, f32[32,24,128]{2,1,0:T(8,128)} %all-to-all-done.root_any, f32[63,32,128]{2,1,0:T(8,128)} %get-tuple-element.32.couple_any), custom_call_target="tpu_custom_call" | custom-call | tf_op jit(solution)/shard_map/tree_down/pallas_call | solution.py:939
  47.6 0.0 collective-permute-done.prev_any
  47.6 4.1 %collective-permute-done.1.next_any = bf16[72,32,128]{2,1,0:T(8,128)(2,1)} collective-permute-done((bf16[72,32,128]{2,1,0:T(8,128)(2,1)}, bf16[72,32,128]{2,1,0:T(8,128)(2,1)}, u32[]{:S(2)}, u32[]{:S(2)}) %collective-permute-start.1) | collective-permute-done | bytes 589856 | tf_op jit(solution)/shard_map/ppermute | solution.py:914
  51.7 21.8 %couple_finish.1 = f32[32,16384]{1,0:T(8,128)} custom-call(s32[16,128]{1,0:T(8,128)} %get-tuple-element.22.entries, f32[8,256]{1,0:T(8,128)} %get-tuple-element.23.shape_ref, f32[16,128]{1,0:T(8,128)} %get-tuple-element.24.counts, bf16[72,32,128]{2,1,0:T(8,128)(2,1)} %collective-permute-done.prev_any, bf16[72,32,128]{2,1,0:T(8,128)(2,1)} %collective-permute-done.1.next_any, ...), custom_call_target="tpu_custom_call" | custom-call | tf_op jit(solution)/shard_map/couple_finish/pallas_call | solution.py:961
Async XLA Ops:
  8.8 32.5 %all-to-all-start = ((f32[32,24,128]{2,1,0:T(8,128)}), f32[32,24,128]{2,1,0:T(8,128)}, u32[]{:S(2)}, u32[]{:S(2)}) async-start(f32[32,24,128]{2,1,0:T(8,128)} %get-tuple-element.30), calls=%async_computation | async-start | bytes 786432 | tf_op jit(solution)/shard_map/all_to_all | solution.py:910
  16.2 31.4 %collective-permute-start = (bf16[72,32,128]{2,1,0:T(8,128)(2,1)}, bf16[72,32,128]{2,1,0:T(8,128)(2,1)}, u32[]{:S(2)}, u32[]{:S(2)}) collective-permute-start(bf16[72,32,128]{2,1,0:T(8,128)(2,1)} %get-tuple-element.25), channel_id=1, source_target_pairs={{0,1},{1,2},{2,3},{3,4},{4,5},{5,6},{6,7},{7,8},{8,9},{9,10},{10,1... | collective-permute-start | bytes 1769480 | tf_op jit(solution)/shard_map/ppermute | solution.py:913
  20.7 31.0 %collective-permute-start.1 = (bf16[72,32,128]{2,1,0:T(8,128)(2,1)}, bf16[72,32,128]{2,1,0:T(8,128)(2,1)}, u32[]{:S(2)}, u32[]{:S(2)}) collective-permute-start(bf16[72,32,128]{2,1,0:T(8,128)(2,1)} %get-tuple-element.26), channel_id=1, source_target_pairs={{1,0},{2,1},{3,2},{4,3},{5,4},{6,5},{7,6},{8,7},{9,8},{10,9},{11,1... | collective-permute-start | bytes 1769480 | tf_op jit(solution)/shard_map/ppermute | solution.py:914

commit v14 on v13

--- a/solution.py
+++ b/solution.py
@@ -746,7 +746,7 @@
         leaf_couple[PAIRS + u] = couple_apply(u, *buffers[1])
 
 
-def finish_leaves(b_ref, down_ref, leaf_couple, out_ref, border):
+def finish_leaves(b_ref, down_ref, leaf_couple, out_ref, border, out_any, sems):
     def finish(m, carry):
         values = []
         for v in range(16):
@@ -764,11 +764,22 @@
             out_ref[:, span] = value
         return carry
 
-    lax.fori_loop(0, PAIRS // 16, finish, 0)
-    for side, group in enumerate((0, GROUPS - 1)):
-        for i in range(4):
-            leaf = 4 * group + i
-            out_ref[:, leaf * P_SIZE : (leaf + 1) * P_SIZE] += border[4 * side + i]
+    parts = PAIRS // 16
+    leaving = []
+    for c in range(parts):
+        lax.fori_loop(c, c + 1, finish, 0)
+        for side, (part, group) in enumerate(((0, 0), (parts - 1, GROUPS - 1))):
+            if c == part:
+                for i in range(4):
+                    leaf = 4 * group + i
+                    out_ref[:, leaf * P_SIZE : (leaf + 1) * P_SIZE] += border[4 * side + i]
+        span = slice(c * 16 * 256, (c + 1) * 16 * 256)
+        leaving.append(
+            pltpu.make_async_copy(out_ref.at[:, span], out_any.at[:, span], sems.at[c])
+        )
+        leaving[c].start()
+    for copy in leaving:
+        copy.wait()
 
 
 def border_blocks(counts, p_ref, prev_ref, next_ref, border, p8, coords):
@@ -819,10 +830,10 @@
 def final_kernel(
     entries, shape_ref, counts,
     prev_any, next_any, p_any, high_any, low_any, b_any, near_any, down_any,
-    out_ref,
-    prev_ref, next_ref, p_ref, b_ref, down, leaf_couple,
+    out_any,
+    out_ref, prev_ref, next_ref, p_ref, b_ref, down, leaf_couple,
     shape_tab, high_tab, low_tab, halo_rows, halo_shape,
-    tiles0, lhs0, tiles1, lhs1, p8, coords, border, sems, halo_sems,
+    tiles0, lhs0, tiles1, lhs1, p8, coords, border, sems, halo_sems, out_sems,
 ):
     moves = (
         (prev_any, prev_ref),
@@ -847,7 +858,7 @@
     )
     for copy in copies[5:]:
         copy.wait()
-    finish_leaves(b_ref, down, leaf_couple, out_ref, border)
+    finish_leaves(b_ref, down, leaf_couple, out_ref, border, out_any, out_sems)
 
 
 def shaped(*shape, dtype=F32):
@@ -963,8 +974,9 @@
         name="couple_finish",
         out_shape=shaped(R, LD * P_SIZE),
         in_specs=[smem()] * 3 + [anywhere()] * 8,
-        out_specs=vmem(),
+        out_specs=anywhere(),
         scratch_shapes=[
+            pltpu.VMEM((R, LD * P_SIZE), F32),
             pltpu.VMEM((SEND, R, 128), BF16),
             pltpu.VMEM((SEND, R, 128), BF16),
             pltpu.VMEM((3, LD * P_SIZE), F32),
@@ -985,6 +997,7 @@
             pltpu.VMEM((8, R, 128), F32),
             pltpu.SemaphoreType.DMA((8,)),
             pltpu.SemaphoreType.DMA((2,)),
+            pltpu.SemaphoreType.DMA((PAIRS // 16,)),
         ],
         compiler_params=PARAMS,
     )(

time: 74.1 us -> 73.4 us (level)
  Pallas kernels: 56.2 us -> 55.4 us
    pallas_call x1, Pallas kernels: 21.8 us -> 21 us  [per_device(): pl.pallas_call(final_kernel, name='couple_finish', out_shape=shaped(R, LD...]
where the time goes in v14:
time: 73.4 us; the launch traced here: 72.8 us
  Pallas kernels  55.4 us (75%)
  starting transfers between devices  13.1 us (18%)
  waiting for transfers between devices  4.08 us (6%)
    pallas_call x1, Pallas kernels, per_device(): pl.pallas_call(final_kernel, name='couple_finish', out_shape=shaped(R, LD...  21 us
    pallas_call x1, Pallas kernels, per_device(): pl.pallas_call(near_kernel, name='near_field', out_shape=(shaped(R, LD *...  19.4 us
    pallas_call x1, Pallas kernels, per_device(): pl.pallas_call(leaf_kernel, name='leaf_up', out_shape=(shaped(SEND, R, 12...  8.79 us
    all_to_all x1, starting transfers between devices, per_device(): roots = lax.all_to_all(root, AXES, 0, 0, tiled=True)  7.41 us
    pallas_call x1, Pallas kernels, per_device(): pl.pallas_call(tree_kernel, name='tree_down', out_shape=shaped(PAIRS, R,...  6.27 us
    ppermute x1, starting transfers between devices, per_device(): from_prev = lax.ppermute(send_next, AXES, forward)  4.44 us
    ppermute x1, waiting for transfers between devices, per_device(): from_next = lax.ppermute(send_prev, AXES, backward)  4.07 us
  transfers between devices with their start and end apart: 3, of which 1 were waited for; matrix products, arithmetic and copies ran while one was open for 0% of the time, Pallas kernels for 35%

profile of v14, /device:TPU:0, one launch (start us, length us, event | category | flops | bytes accessed | tf_op | source)
XLA Modules:
  0.0 72.8 jit_solution(3745883179009449631)
XLA Ops:
  0.0 8.8 %leaf_up.1 = (bf16[72,32,128]{2,1,0:T(8,128)(2,1)}, bf16[72,32,128]{2,1,0:T(8,128)(2,1)}, bf16[128,32,128]{2,1,0:T(8,128)(2,1)}, bf16[128,32,128]{2,1,0:T(8,128)...) custom-call(bf16[32,16384]{1,0:T(8,128)(2,1)} %x_any.3, ...), custom_call_target="tpu_custom_call" | custom-call | tf_op jit(solution)/shard_map/leaf_up/pallas_call | solution.py:887
  8.8 7.4 %all-to-all-start = ((f32[32,24,128]{2,1,0:T(8,128)}), f32[32,24,128]{2,1,0:T(8,128)}, u32[]{:S(2)}, u32[]{:S(2)}) async-start(f32[32,24,128]{2,1,0:T(8,128)} %get-tuple-element.30), calls=%async_computation | async-start | bytes 786432 | tf_op jit(solution)/shard_map/all_to_all | solution.py:921
  16.2 4.4 %collective-permute-start = (bf16[72,32,128]{2,1,0:T(8,128)(2,1)}, bf16[72,32,128]{2,1,0:T(8,128)(2,1)}, u32[]{:S(2)}, u32[]{:S(2)}) collective-permute-start(bf16[72,32,128]{2,1,0:T(8,128)(2,1)} %get-tuple-element.25), channel_id=1, source_target_pairs={{0,1},{1,2},{2,3},{3,4},{4,5},{5,6},{6,7},{7,8},{8,9},{9,10},{10,1... | collective-permute-start | bytes 1769480 | tf_op jit(solution)/shard_map/ppermute | solution.py:924
  20.7 1.3 %collective-permute-start.1 = (bf16[72,32,128]{2,1,0:T(8,128)(2,1)}, bf16[72,32,128]{2,1,0:T(8,128)(2,1)}, u32[]{:S(2)}, u32[]{:S(2)}) collective-permute-start(bf16[72,32,128]{2,1,0:T(8,128)(2,1)} %get-tuple-element.26), channel_id=1, source_target_pairs={{1,0},{2,1},{3,2},{4,3},{5,4},{6,5},{7,6},{8,7},{9,8},{10,9},{11,1... | collective-permute-start | bytes 1769480 | tf_op jit(solution)/shard_map/ppermute | solution.py:925
  21.9 19.4 %near_field.1 = (f32[32,16384]{1,0:T(8,128)}, f32[63,32,128]{2,1,0:T(8,128)}) custom-call(s32[8,1536]{1,0:T(8,128)} %get-tuple-element.27.list_ref, f32[8,256]{1,0:T(8,128)} %get-tuple-element.23.shape_ref, bf16[32,16384]{1,0:T(8,128)(2,1)} %x_any.3, f32[3,16384]{1,0:T(4,128)} %p_any.1, f32[63,32,128]{2,1,0:T(8,128)} %get-tuple-element.28.lev_any), custom_call_target="tpu_custom_call" | custom-call | flops 1929379840 | bytes 4194304 | tf_op jit(solution)/shard_map/near_field/pallas_call | solution.py:927
  41.3 0.0 all-to-all-done.root_any
  41.3 6.3 %tree_down.1.down_any = f32[64,32,128]{2,1,0:T(8,128)} custom-call(f32[2,64,64]{2,1,0:T(8,128)} %t_any.1, f32[32,24,128]{2,1,0:T(8,128)} %all-to-all-done.root_any, f32[63,32,128]{2,1,0:T(8,128)} %get-tuple-element.32.couple_any), custom_call_target="tpu_custom_call" | custom-call | tf_op jit(solution)/shard_map/tree_down/pallas_call | solution.py:950
  47.6 0.0 collective-permute-done.prev_any
  47.6 4.1 %collective-permute-done.1.next_any = bf16[72,32,128]{2,1,0:T(8,128)(2,1)} collective-permute-done((bf16[72,32,128]{2,1,0:T(8,128)(2,1)}, bf16[72,32,128]{2,1,0:T(8,128)(2,1)}, u32[]{:S(2)}, u32[]{:S(2)}) %collective-permute-start.1) | collective-permute-done | bytes 589856 | tf_op jit(solution)/shard_map/ppermute | solution.py:925
  51.7 21.0 %couple_finish.1 = f32[32,16384]{1,0:T(8,128)} custom-call(s32[16,128]{1,0:T(8,128)} %get-tuple-element.22.entries, f32[8,256]{1,0:T(8,128)} %get-tuple-element.23.shape_ref, f32[16,128]{1,0:T(8,128)} %get-tuple-element.24.counts, bf16[72,32,128]{2,1,0:T(8,128)(2,1)} %collective-permute-done.prev_any, bf16[72,32,128]{2,1,0:T(8,128)(2,1)} %collective-permute-done.1.next_any, ...), custom_call_target="tpu_custom_call" | custom-call | tf_op jit(solution)/shard_map/couple_finish/pallas_call | solution.py:972
Async XLA Ops:
  8.8 32.5 %all-to-all-start = ((f32[32,24,128]{2,1,0:T(8,128)}), f32[32,24,128]{2,1,0:T(8,128)}, u32[]{:S(2)}, u32[]{:S(2)}) async-start(f32[32,24,128]{2,1,0:T(8,128)} %get-tuple-element.30), calls=%async_computation | async-start | bytes 786432 | tf_op jit(solution)/shard_map/all_to_all | solution.py:921
  16.2 31.4 %collective-permute-start = (bf16[72,32,128]{2,1,0:T(8,128)(2,1)}, bf16[72,32,128]{2,1,0:T(8,128)(2,1)}, u32[]{:S(2)}, u32[]{:S(2)}) collective-permute-start(bf16[72,32,128]{2,1,0:T(8,128)(2,1)} %get-tuple-element.25), channel_id=1, source_target_pairs={{0,1},{1,2},{2,3},{3,4},{4,5},{5,6},{6,7},{7,8},{8,9},{9,10},{10,1... | collective-permute-start | bytes 1769480 | tf_op jit(solution)/shard_map/ppermute | solution.py:924
  20.7 31.0 %collective-permute-start.1 = (bf16[72,32,128]{2,1,0:T(8,128)(2,1)}, bf16[72,32,128]{2,1,0:T(8,128)(2,1)}, u32[]{:S(2)}, u32[]{:S(2)}) collective-permute-start(bf16[72,32,128]{2,1,0:T(8,128)(2,1)} %get-tuple-element.26), channel_id=1, source_target_pairs={{1,0},{2,1},{3,2},{4,3},{5,4},{6,5},{7,6},{8,7},{9,8},{10,9},{11,1... | collective-permute-start | bytes 1769480 | tf_op jit(solution)/shard_map/ppermute | solution.py:925

commit v15 on v14

--- a/solution.py
+++ b/solution.py
@@ -445,8 +445,8 @@
 
 def near_kernel(
     list_ref, shape_ref, x_any, p_ref, lev_any,
-    out_ref, couple_ref,
-    x_ref, lev_ref, sems, p8, far_feat, own_feat, tile0, tile1,
+    out_ref, couple_any,
+    couple_ref, x_ref, lev_ref, sems, p8, far_feat, own_feat, tile0, tile1,
 ):
     copies = [
         pltpu.make_async_copy(x_any, x_ref, sems.at[0]),
@@ -564,8 +564,11 @@
     rides = -(-(PAIRS - 1) // (2 * SIBLINGS))
     middle = mutual_phases // 2
     lax.fori_loop(0, rides, functools.partial(two_phases, SIBLINGS, 2), 0)
+    leaving = pltpu.make_async_copy(couple_ref, couple_any, sems.at[2])
+    leaving.start()
     lax.fori_loop(rides, middle, functools.partial(two_phases, 0, 2), 0)
     lax.fori_loop(middle, (all_phases + 1) // 2, functools.partial(two_phases, 0, 1), 0)
+    leaving.wait()
 
 
 def tree_down(t_ref, root_ref, down_ref, couple, pairs_scr, shapes):
@@ -661,7 +664,7 @@
         shape_tab[HALF + m] = shape_rows(lambda d, k: shape_ref[d, k], m, 0.0)
         return carry
 
-    lax.fori_loop(0, LD, own_nodes, 0, unroll=8)
+    lax.fori_loop(0, LD, own_nodes, 0, unroll=32)
     for copy in copies:
         copy.wait()
     def halo_pairs(m, carry):
@@ -929,11 +932,12 @@
         name="near_field",
         out_shape=(shaped(R, LD * P_SIZE), shaped(PAIRS - 1, R, 128)),
         in_specs=[smem(), smem(), anywhere(), vmem(), anywhere()],
-        out_specs=[vmem()] * 2,
+        out_specs=[vmem(), anywhere()],
         scratch_shapes=[
+            pltpu.VMEM((PAIRS - 1, R, 128), F32),
             pltpu.VMEM((R, LD * P_SIZE), BF16),
             pltpu.VMEM((PAIRS - 1, R, 128), F32),
-            pltpu.SemaphoreType.DMA((2,)),
+            pltpu.SemaphoreType.DMA((3,)),
             pltpu.VMEM((16, 8, 512), F32),
             pltpu.VMEM((PAIRS, P_SIZE, 2 * FEATS), BF16),
             pltpu.VMEM((3 * LD, FEATS, P_SIZE), BF16),

time: 73.4 us -> 73.2 us (level)
  no operation moved by 1% of the time
where the time goes in v15:
time: 73.2 us; the launch traced here: 72.8 us
  Pallas kernels  55 us (75%)
  starting transfers between devices  13.1 us (18%)
  waiting for transfers between devices  4.36 us (6%)
    pallas_call x1, Pallas kernels, per_device(): pl.pallas_call(final_kernel, name='couple_finish', out_shape=shaped(R, LD...  20.9 us
    pallas_call x1, Pallas kernels, per_device(): pl.pallas_call(near_kernel, name='near_field', out_shape=(shaped(R, LD *...  19.1 us
    pallas_call x1, Pallas kernels, per_device(): pl.pallas_call(leaf_kernel, name='leaf_up', out_shape=(shaped(SEND, R, 12...  8.79 us
    all_to_all x1, starting transfers between devices, per_device(): roots = lax.all_to_all(root, AXES, 0, 0, tiled=True)  7.41 us
    pallas_call x1, Pallas kernels, per_device(): pl.pallas_call(tree_kernel, name='tree_down', out_shape=shaped(PAIRS, R,...  6.27 us
    ppermute x1, starting transfers between devices, per_device(): from_prev = lax.ppermute(send_next, AXES, forward)  4.44 us
    ppermute x1, waiting for transfers between devices, per_device(): from_next = lax.ppermute(send_prev, AXES, backward)  4.36 us
  transfers between devices with their start and end apart: 3, of which 1 were waited for; matrix products, arithmetic and copies ran while one was open for 0% of the time, Pallas kernels for 35%

profile of v15, /device:TPU:0, one launch (start us, length us, event | category | flops | bytes accessed | tf_op | source)
XLA Modules:
  0.0 72.8 jit_solution(14312636335704136095)
XLA Ops:
  0.0 8.8 %leaf_up.1 = (bf16[72,32,128]{2,1,0:T(8,128)(2,1)}, bf16[72,32,128]{2,1,0:T(8,128)(2,1)}, bf16[128,32,128]{2,1,0:T(8,128)(2,1)}, bf16[128,32,128]{2,1,0:T(8,128)...) custom-call(bf16[32,16384]{1,0:T(8,128)(2,1)} %x_any.3, ...), custom_call_target="tpu_custom_call" | custom-call | tf_op jit(solution)/shard_map/leaf_up/pallas_call | solution.py:890
  8.8 7.4 %all-to-all-start = ((f32[32,24,128]{2,1,0:T(8,128)}), f32[32,24,128]{2,1,0:T(8,128)}, u32[]{:S(2)}, u32[]{:S(2)}) async-start(f32[32,24,128]{2,1,0:T(8,128)} %get-tuple-element.30), calls=%async_computation | async-start | bytes 786432 | tf_op jit(solution)/shard_map/all_to_all | solution.py:924
  16.2 4.4 %collective-permute-start = (bf16[72,32,128]{2,1,0:T(8,128)(2,1)}, bf16[72,32,128]{2,1,0:T(8,128)(2,1)}, u32[]{:S(2)}, u32[]{:S(2)}) collective-permute-start(bf16[72,32,128]{2,1,0:T(8,128)(2,1)} %get-tuple-element.25), channel_id=1, source_target_pairs={{0,1},{1,2},{2,3},{3,4},{4,5},{5,6},{6,7},{7,8},{8,9},{9,10},{10,1... | collective-permute-start | bytes 1769480 | tf_op jit(solution)/shard_map/ppermute | solution.py:927
  20.7 1.3 %collective-permute-start.1 = (bf16[72,32,128]{2,1,0:T(8,128)(2,1)}, bf16[72,32,128]{2,1,0:T(8,128)(2,1)}, u32[]{:S(2)}, u32[]{:S(2)}) collective-permute-start(bf16[72,32,128]{2,1,0:T(8,128)(2,1)} %get-tuple-element.26), channel_id=1, source_target_pairs={{1,0},{2,1},{3,2},{4,3},{5,4},{6,5},{7,6},{8,7},{9,8},{10,9},{11,1... | collective-permute-start | bytes 1769480 | tf_op jit(solution)/shard_map/ppermute | solution.py:928
  21.9 19.1 %near_field.1 = (f32[32,16384]{1,0:T(8,128)}, f32[63,32,128]{2,1,0:T(8,128)}) custom-call(s32[8,1536]{1,0:T(8,128)} %get-tuple-element.27.list_ref, f32[8,256]{1,0:T(8,128)} %get-tuple-element.23.shape_ref, bf16[32,16384]{1,0:T(8,128)(2,1)} %x_any.3, f32[3,16384]{1,0:T(4,128)} %p_any.1, f32[63,32,128]{2,1,0:T(8,128)} %get-tuple-element.28.lev_any), custom_call_target="tpu_custom_call" | custom-call | flops 1929379840 | bytes 4194304 | tf_op jit(solution)/shard_map/near_field/pallas_call | solution.py:930
  41.0 0.0 all-to-all-done.root_any
  41.0 6.3 %tree_down.1.down_any = f32[64,32,128]{2,1,0:T(8,128)} custom-call(f32[2,64,64]{2,1,0:T(8,128)} %t_any.1, f32[32,24,128]{2,1,0:T(8,128)} %all-to-all-done.root_any, f32[63,32,128]{2,1,0:T(8,128)} %get-tuple-element.32.couple_any), custom_call_target="tpu_custom_call" | custom-call | tf_op jit(solution)/shard_map/tree_down/pallas_call | solution.py:954
  47.3 0.0 collective-permute-done.prev_any
  47.3 4.4 %collective-permute-done.1.next_any = bf16[72,32,128]{2,1,0:T(8,128)(2,1)} collective-permute-done((bf16[72,32,128]{2,1,0:T(8,128)(2,1)}, bf16[72,32,128]{2,1,0:T(8,128)(2,1)}, u32[]{:S(2)}, u32[]{:S(2)}) %collective-permute-start.1) | collective-permute-done | bytes 589856 | tf_op jit(solution)/shard_map/ppermute | solution.py:928
  51.7 20.9 %couple_finish.1 = f32[32,16384]{1,0:T(8,128)} custom-call(s32[16,128]{1,0:T(8,128)} %get-tuple-element.22.entries, f32[8,256]{1,0:T(8,128)} %get-tuple-element.23.shape_ref, f32[16,128]{1,0:T(8,128)} %get-tuple-element.24.counts, bf16[72,32,128]{2,1,0:T(8,128)(2,1)} %collective-permute-done.prev_any, bf16[72,32,128]{2,1,0:T(8,128)(2,1)} %collective-permute-done.1.next_any, ...), custom_call_target="tpu_custom_call" | custom-call | tf_op jit(solution)/shard_map/couple_finish/pallas_call | solution.py:976
Async XLA Ops:
  8.8 32.2 %all-to-all-start = ((f32[32,24,128]{2,1,0:T(8,128)}), f32[32,24,128]{2,1,0:T(8,128)}, u32[]{:S(2)}, u32[]{:S(2)}) async-start(f32[32,24,128]{2,1,0:T(8,128)} %get-tuple-element.30), calls=%async_computation | async-start | bytes 786432 | tf_op jit(solution)/shard_map/all_to_all | solution.py:924
  16.2 31.1 %collective-permute-start = (bf16[72,32,128]{2,1,0:T(8,128)(2,1)}, bf16[72,32,128]{2,1,0:T(8,128)(2,1)}, u32[]{:S(2)}, u32[]{:S(2)}) collective-permute-start(bf16[72,32,128]{2,1,0:T(8,128)(2,1)} %get-tuple-element.25), channel_id=1, source_target_pairs={{0,1},{1,2},{2,3},{3,4},{4,5},{5,6},{6,7},{7,8},{8,9},{9,10},{10,1... | collective-permute-start | bytes 1769480 | tf_op jit(solution)/shard_map/ppermute | solution.py:927
  20.7 31.0 %collective-permute-start.1 = (bf16[72,32,128]{2,1,0:T(8,128)(2,1)}, bf16[72,32,128]{2,1,0:T(8,128)(2,1)}, u32[]{:S(2)}, u32[]{:S(2)}) collective-permute-start(bf16[72,32,128]{2,1,0:T(8,128)(2,1)} %get-tuple-element.26), channel_id=1, source_target_pairs={{1,0},{2,1},{3,2},{4,3},{5,4},{6,5},{7,6},{8,7},{9,8},{10,9},{11,1... | collective-permute-start | bytes 1769480 | tf_op jit(solution)/shard_map/ppermute | solution.py:928
